TPU v7x, 32 devices: a whole 2x2x4 slice. The times are simulated.
32 devices in a mesh: item: 4 (over y, x), cent: 8 (over z, core).
Axes of the slice: x: 2, y: 2, z: 4, core: 2. Of those that a mesh axis runs over, the one named last changes fastest.
Arguments:
- vectors: bfloat16 [3072, 1024], P('item'), may hold values from -256 to 256, as said below
- centroids: bfloat16 [8192, 1024], P('cent'), may hold values from -6 to 6, as said below
Outputs:
- centroids_next: bfloat16 [8192, 1024], P(('cent', 'item'))
- log_norm: float32 [3072], P('item')
Inputs may be any that keep to these rules, and one draw needn't show every extreme that they name: vectors hold finite values. `centroids`: centroid entries are independent.
All inputs are finite; a program needn't handle non-finite values.
Results may differ from a plain program's by a relative error of at most 0.0085.
Values may be sent and summed in bfloat16 or wider, within the bound.
No kernel may reach another device: no remote copies, remote signals or barrier semaphores. Data moves between devices by JAX's collectives and lax.ppermute only.
A program may use at most 64 MiB of HBM per device.

v0:
```python
import math

import jax
import jax.numpy as jnp
from jax import lax
from jax.sharding import PartitionSpec as P

ITERS = 2


BETA = 3.0


def local_logits(vectors, rows, scale):
    raw = lax.dot_general(
        vectors, rows, (((1,), (1,)), ((), ())), preferred_element_type=jnp.float32
    )
    sqnorm = jnp.sum(jnp.square(rows.astype(jnp.float32)), axis=1)
    return scale * (raw - 0.5 * sqnorm[None, :])


def normalize(logits):
    local_peak = jnp.max(logits, axis=1)
    peak = lax.pmax(local_peak, "cent")
    expo = jnp.exp(logits - peak[:, None])
    total = lax.psum(jnp.sum(expo, axis=1), "cent")
    resp = (expo / total[:, None]).astype(jnp.bfloat16)
    return (resp, peak + jnp.log(total))


def weighted(resp, vectors):
    return lax.dot_general(
        resp, vectors, (((0,), (0,)), ((), ())), preferred_element_type=jnp.float32
    )


def update(sums, old_rows, mass):
    return ((sums + old_rows.astype(jnp.float32)) / (mass + 1.0)[:, None]).astype(jnp.bfloat16)


def shards(vectors, centroids):
    rows_per = centroids.shape[0] // lax.axis_size("item")
    offset = lax.axis_index("item") * rows_per
    scale = BETA / math.sqrt(vectors.shape[1])
    old_rows = lax.dynamic_slice_in_dim(centroids, offset, rows_per, 0)
    logits = local_logits(vectors, centroids, scale)
    result = old_rows
    log_norm = jnp.zeros((vectors.shape[0],), jnp.float32)
    for step in range(ITERS):
        resp, log_norm = normalize(logits)
        mass = lax.psum(jnp.sum(resp.astype(jnp.float32), axis=0), "item")
        own_mass = lax.dynamic_slice_in_dim(mass, offset, rows_per, 0)

        def term_rows():
            return weighted(resp, vectors)

        if step + 1 < ITERS:
            sums = lax.psum_scatter(
                term_rows().astype(jnp.bfloat16), "item", scatter_dimension=0, tiled=True
            ).astype(jnp.float32)
            fresh = update(sums, old_rows, own_mass)
            logits = local_logits(vectors, lax.all_gather(fresh, "item", axis=0, tiled=True), scale)
            old_rows = fresh
        else:
            sums = lax.psum_scatter(
                term_rows().astype(jnp.bfloat16), "item", scatter_dimension=0, tiled=True
            ).astype(jnp.float32)
            result = update(sums, old_rows, own_mass)
    return (result, log_norm)


def solution(mesh):
    in_specs = (P("item", None), P("cent", None))
    out_specs = (P(("cent", "item"), None), P("item"))
    return jax.shard_map(shards, mesh=mesh, in_specs=in_specs, out_specs=out_specs, check_vma=False)
```

profile of v0, /device:TPU:0, one launch (start us, length us, event | category | flops | bytes accessed | tf_op | source)
XLA Modules:
  0.0 213.2 jit_solution(459155258263598386)
XLA Ops:
  7.2 2.2 %multiply_reduce_fusion.1 = f32[1024]{0:T(1024)S(1)} fusion(bf16[1024,1024]{1,0:T(8,128)(2,1)} %param.3), kind=kLoop, calls=%fused_computation.1 | loop fusion | flops 3144704 | bytes 2101248 | tf_op jit(solution)/shard_map/reduce_sum | solution.py:18
  9.4 5.1 %fusion = (f32[768]{0:T(1024)S(1)}, f32[768,1024]{1,0:T(8,128)}) fusion(f32[1024]{0:T(1024)S(1)} %broadcast_multiply_fusion.1, bf16[768,1024]{1,0:T(8,128)(2,1)S(1)} %copy-done, bf16[1024,1024]{1,0:T(8,128)(2,1)} %param.3), kind=kOutput, calls=%fused_computation.10 | convolution fusion | flops 1612971264 | bytes 6822912 | tf_op jit(solution)/shard_map/dot_general | solution.py:15
  14.5 18.1 %pmax.14 = f32[768]{0:T(1024)S(1)} all-reduce(f32[768]{0:T(1024)S(1)} %get-tuple-element.6), channel_id=1, replica_groups=mesh['item'=4,'cent'=8] {'cent'}, use_global_device_ids=true, to_apply=%region_2.0 | all-reduce | flops 768 | bytes 6144 | tf_op jit(solution)/shard_map/pmax | solution.py:24
  32.6 2.6 %fusion.2 = f32[768]{0:T(1024)S(1)} fusion(f32[768,1024]{1,0:T(8,128)} %get-tuple-element.7, f32[768]{0:T(1024)S(1)} %pmax.14, f32[1024]{0:T(1024)S(1)} %broadcast_multiply_fusion.1), kind=kLoop, calls=%fused_computation.12 | loop fusion | flops 3144960 | bytes 3155968 | tf_op jit(solution)/shard_map/reduce_sum | solution.py:26
  35.2 13.6 %psum.28 = f32[768]{0:T(1024)S(1)} all-reduce(f32[768]{0:T(1024)S(1)} %fusion.2), channel_id=1, replica_groups=mesh['item'=4,'cent'=8] {'cent'}, use_global_device_ids=true, to_apply=%region_4.0 | all-reduce | flops 768 | bytes 6144 | tf_op jit(solution)/shard_map/psum | solution.py:26
  48.8 2.7 %convert_reduce_fusion.1 = (f32[1024]{0:T(1024)S(1)}, bf16[768,1024]{1,0:T(8,128)(2,1)S(1)}) fusion(f32[768]{0:T(1024)S(1)} %psum.28, f32[768]{0:T(1024)S(1)} %pmax.14, f32[768,1024]{1,0:T(8,128)} %get-tuple-element.7, f32[1024]{0:T(1024)S(1)} %broadcast_multiply_fusion.1), kind=kLoop, calls=%fused_computation.6 | loop fusion | flops 5504000 | bytes 4732928 | tf_op jit(solution)/shard_map/reduce_sum | solution.py:51
  51.5 3.2 %convolution_convert_fusion.1 = bf16[1024,1024]{1,0:T(8,128)(2,1)} fusion(bf16[768,1024]{1,0:T(8,128)(2,1)S(1)} %get-tuple-element.5, bf16[768,1024]{1,0:T(8,128)(2,1)S(1)} %copy-done), kind=kOutput, calls=%fused_computation.15 | convolution fusion | flops 1611661312 | bytes 5242880 | tf_op jit(solution)/shard_map/dot_general | solution.py:32
  54.8 10.0 %psum.29 = f32[1024]{0:T(1024)S(1)} all-reduce(f32[1024]{0:T(1024)S(1)} %get-tuple-element.4), channel_id=1, replica_groups=mesh['item'=4,'cent'=8] {'item'}, use_global_device_ids=true, to_apply=%region_7.0 | all-reduce | flops 1024 | bytes 8192 | tf_op jit(solution)/shard_map/psum | solution.py:51
  64.9 0.1 dynamic-slice_add_fusion.1
  64.9 23.4 %reduce-scatter.3.cloned.1.call-done = bf16[256,1024]{1,0:T(8,128)(2,1)} async-done(((bf16[1024,1024]{1,0:T(8,128)(2,1)}), bf16[256,1024]{1,0:T(8,128)(2,1)}) %reduce-scatter.3.cloned.1.call-update) | async-done | bytes 524304 | tf_op jit(solution)/shard_map/reduce_scatter | solution.py:58
  88.4 2.2 %divide_convert_fusion.3 = bf16[256,1024]{1,0:T(8,128)(2,1)} fusion(bf16[256,1024]{1,0:T(8,128)(2,1)} %reduce-scatter.3.cloned.1.call-done, f32[256]{0:T(256)S(1)} %dynamic-slice_add_fusion.1, bf16[1024,1024]{1,0:T(8,128)(2,1)} %param.3, s32[]{:T(128)S(6)} %select_n.2), kind=kLoop, calls=%fused_computation.17 | loop fusion | flops 1310720 | bytes 1573892 | tf_op jit(solution)/shard_map/convert_element_type | solution.py:38
  90.7 35.6 %all-gather.2.cloned.1.call-done = bf16[1024,1024]{1,0:T(8,128)(2,1)} async-done(((bf16[256,1024]{1,0:T(8,128)(2,1)}), bf16[1024,1024]{1,0:T(8,128)(2,1)}) %all-gather.2.cloned.1.call-update) | async-done | bytes 2097168 | tf_op jit(solution)/shard_map/all_gather | solution.py:62
  126.3 2.1 multiply_reduce_fusion
  128.4 5.1 %fusion.1 = (f32[768]{0:T(1024)S(1)}, f32[1024,768]{1,0:T(8,128)}) fusion(f32[1024]{0:T(1024)S(1)} %broadcast_multiply_fusion, bf16[1024,1024]{1,0:T(8,128)(2,1)} %all-gather.2.cloned.1.call-done, bf16[768,1024]{1,0:T(8,128)(2,1)S(1)} %copy-done), kind=kOutput, calls=%fused_computation.11 | convolution fusion | flops 1612971264 | bytes 6822912 | tf_op jit(solution)/shard_map/dot_general | solution.py:15
  133.4 16.3 %pmax.15 = f32[768]{0:T(1024)S(1)} all-reduce(f32[768]{0:T(1024)S(1)} %get-tuple-element.8), channel_id=1, replica_groups=mesh['item'=4,'cent'=8] {'cent'}, use_global_device_ids=true, to_apply=%region_10.0 | all-reduce | flops 768 | bytes 6144 | tf_op jit(solution)/shard_map/pmax | solution.py:24
  149.8 2.6 %fusion.3 = f32[768]{0:T(1024)S(1)} fusion(f32[1024,768]{1,0:T(8,128)} %get-tuple-element.9, f32[768]{0:T(1024)S(1)} %pmax.15, f32[1024]{0:T(1024)S(1)} %broadcast_multiply_fusion), kind=kLoop, calls=%fused_computation.13 | loop fusion | flops 3144960 | bytes 3155968 | tf_op jit(solution)/shard_map/reduce_sum | solution.py:26
  152.4 13.6 %psum.30 = f32[768]{0:T(1024)S(1)} all-reduce(f32[768]{0:T(1024)S(1)} %fusion.3), channel_id=1, replica_groups=mesh['item'=4,'cent'=8] {'cent'}, use_global_device_ids=true, to_apply=%region_12.0 | all-reduce | flops 768 | bytes 6144 | tf_op jit(solution)/shard_map/psum | solution.py:26
  166.0 2.8 %convert_reduce_fusion = (f32[1024]{0:T(1024)S(1)}, bf16[1024,768]{1,0:T(8,128)(2,1)S(1)}) fusion(f32[768]{0:T(1024)S(1)} %psum.30, f32[768]{0:T(1024)S(1)} %pmax.15, f32[1024,768]{1,0:T(8,128)} %get-tuple-element.9, f32[1024]{0:T(1024)S(1)} %broadcast_multiply_fusion), kind=kLoop, calls=%fused_computation.2 | loop fusion | flops 5504000 | bytes 4732928 | tf_op jit(solution)/shard_map/reduce_sum | solution.py:51
  168.8 3.2 %convolution_convert_fusion = bf16[1024,1024]{1,0:T(8,128)(2,1)} fusion(bf16[1024,768]{1,0:T(8,128)(2,1)S(1)} %get-tuple-element.3, bf16[768,1024]{1,0:T(8,128)(2,1)S(1)} %copy-done), kind=kOutput, calls=%fused_computation.14 | convolution fusion | flops 1611661312 | bytes 5242880 | tf_op jit(solution)/shard_map/dot_general | solution.py:32
  172.0 9.1 %psum.31 = f32[1024]{0:T(1024)S(1)} all-reduce(f32[1024]{0:T(1024)S(1)} %get-tuple-element.2), channel_id=1, replica_groups=mesh['item'=4,'cent'=8] {'item'}, use_global_device_ids=true, to_apply=%region_15.0 | all-reduce | flops 1024 | bytes 8192 | tf_op jit(solution)/shard_map/psum | solution.py:51
  181.1 0.1 dynamic-slice_add_fusion
  181.1 0.6 log_add_fusion
  181.7 22.8 %reduce-scatter.5.cloned.1.call-done = bf16[256,1024]{1,0:T(8,128)(2,1)} async-done(((bf16[1024,1024]{1,0:T(8,128)(2,1)}), bf16[256,1024]{1,0:T(8,128)(2,1)}) %reduce-scatter.5.cloned.1.call-update) | async-done | bytes 524304 | tf_op jit(solution)/shard_map/reduce_scatter | solution.py:65
  204.6 2.0 divide_convert_fusion.2
  (12 shorter events, 0.2 us)
Async XLA Ops:
  7.2 2.3 %copy-start = (bf16[768,1024]{1,0:T(8,128)(2,1)S(1)}, bf16[768,1024]{1,0:T(8,128)(2,1)}, u32[]{:S(2)}) copy-start(bf16[768,1024]{1,0:T(8,128)(2,1)} %param.2) | copy-start | bytes 4718596
  7.2 81.2 %reduce-scatter.3.cloned.1.call-start = ((), (), s32[]{:S(2)}) async-start(), calls=%async_computation.2 | async-start | bytes 2621440 | tf_op jit(solution)/shard_map/reduce_scatter | solution.py:58
  54.8 71.5 %all-gather.2.cloned.1.call-start = ((), (), s32[]{:S(2)}) async-start(), calls=%async_computation.3 | async-start | bytes 2621440 | tf_op jit(solution)/shard_map/all_gather | solution.py:62
  90.6 114.0 %reduce-scatter.5.cloned.1.call-start = ((), (), s32[]{:S(2)}) async-start(), calls=%async_computation.4 | async-start | bytes 2621440 | tf_op jit(solution)/shard_map/reduce_scatter | solution.py:65
  168.8 35.8 %copy-start.1 = (bf16[256,1024]{1,0:T(8,128)(2,1)S(1)}, bf16[256,1024]{1,0:T(8,128)(2,1)}, u32[]{:S(2)}) copy-start(bf16[256,1024]{1,0:T(8,128)(2,1)} %divide_convert_fusion.3) | copy-start | bytes 1572868
Sparse Core Ops, SparseCore 0:
  54.9 33.4 reduce-scatter.2
  90.9 35.2 all-gather.1
  172.1 32.4 reduce-scatter.4
where the time goes:
time: 214 us; the launch traced here: 213 us
  waiting for transfers between devices  81.9 us (38%)
  blocking collectives  80.7 us (38%)
  other arithmetic  20 us (9%)
  matrix products  16.5 us (8%)
  between operations  13.8 us (6%)
    reduce_scatter x2, waiting for transfers between devices, shards(): lax.psum_scatter(term_rows().astype(jnp.bfloat16), 'item', scatter_dimens...  46.3 us
    all_gather x1, waiting for transfers between devices, shards(): lax.all_gather(fresh, 'item', axis=0, tiled=True)  35.6 us
    pmax x2, blocking collectives, normalize(): peak = lax.pmax(local_peak, 'cent')  34.4 us
    psum x2, blocking collectives, normalize(): total = lax.psum(jnp.sum(expo, axis=1), 'cent')  27.2 us
    psum x2, blocking collectives, shards(): mass = lax.psum(jnp.sum(resp.astype(jnp.float32), axis=0), 'item')  19.1 us
    dot_general x2, matrix products, local_logits(): lax.dot_general(vectors, rows, (((1,), (1,)), ((), ())), preferred_elemen...  10.2 us
    dot_general x2, matrix products, weighted(): lax.dot_general(resp, vectors, (((0,), (0,)), ((), ())), preferred_elemen...  6.37 us
    reduce_sum x2, other arithmetic, shards(): mass = lax.psum(jnp.sum(resp.astype(jnp.float32), axis=0), 'item')  5.57 us
  transfers between devices with their start and end apart: 3, of which 3 were waited for; matrix products, arithmetic and copies ran while one was open for 0% of the time, Pallas kernels for 0%

commit v1 on v0

v1 whole, which is shorter than its diff:
```python
import functools
import math

import jax
import jax.numpy as jnp
from jax import lax
from jax.experimental import pallas as pl
from jax.experimental.pallas import tpu as pltpu
from jax.sharding import PartitionSpec as P

BETA = 3.0
BOTH = ("item", "cent")
VMEM_LIMIT = 56 * 1024 * 1024
NT = (((1,), (1,)), ((), ()))
NN = (((1,), (0,)), ((), ()))
SMALL = 2 * 1024 * 1024


def scores(rows, vectors, scale):
    raw = lax.dot_general(rows, vectors, NT, preferred_element_type=jnp.float32)
    sqnorm = jnp.sum(jnp.square(rows.astype(jnp.float32)), axis=1, keepdims=True)
    return scale * (raw - 0.5 * sqnorm)


def merge(parts, axis):
    peak = jnp.max(parts, axis=axis, keepdims=True)
    total = jnp.sum(jnp.exp(parts - peak), axis=axis, keepdims=True)
    return jnp.squeeze(peak + jnp.log(total), axis)


def partial_kernel(scale, v_ref, c_ref, out_ref, peak, total):
    step = pl.program_id(0)

    @pl.when(step == 0)
    def _():
        peak[...] = jnp.full_like(peak, -jnp.inf)
        total[...] = jnp.zeros_like(total)

    logits = scores(c_ref[...], v_ref[...], scale)
    top = jnp.maximum(peak[...], jnp.max(logits, axis=0, keepdims=True))
    total[...] = total[...] * jnp.exp(peak[...] - top) + jnp.sum(
        jnp.exp(logits - top), axis=0, keepdims=True
    )
    peak[...] = top

    @pl.when(step == pl.num_programs(0) - 1)
    def _():
        out_ref[...] = peak[...] + jnp.log(total[...])


def partial(vectors, centroids, scale):
    nv, dim = vectors.shape
    k = centroids.shape[0]
    rows = min(256, k)
    return pl.pallas_call(
        functools.partial(partial_kernel, scale),
        grid=(k // rows,),
        in_specs=[
            pl.BlockSpec((nv, dim), lambda i: (0, 0)),
            pl.BlockSpec((rows, dim), lambda i: (i, 0)),
        ],
        out_specs=pl.BlockSpec((1, nv), lambda i: (0, 0)),
        out_shape=jax.ShapeDtypeStruct((1, nv), jnp.float32),
        scratch_shapes=[pltpu.VMEM((1, nv), jnp.float32)] * 2,
        compiler_params=pltpu.CompilerParams(vmem_limit_bytes=24 * 1024 * 1024),
        cost_estimate=pl.CostEstimate(
            flops=2 * nv * k * dim, bytes_accessed=2 * (nv + k) * dim, transcendentals=nv * k
        ),
        name="partial_lse",
    )(vectors, centroids)


def block_of(plan, place):
    if plan["exchange"]:
        return lax.axis_index("item") ^ place
    return place


def fetches(plan, pieces, table, sems):
    nv = plan["nv"]
    core = lax.rem(lax.axis_index("cent"), 2)
    result = []
    for place, entries in enumerate(plan["blocks"]):
        base = block_of(plan, place) * nv
        copies = []
        for piece, start, half, offset, rows in entries:
            if half is None:
                lead = 0
            else:
                lead = (core if half else 1 - core) * (nv // 2)
            dst = pl.multiple_of(base + lead + offset, 64)
            src = pieces[piece]
            if start is not None:
                src = src.at[pl.ds(start, rows), :]
            copies.append(pltpu.make_async_copy(src, table.at[pl.ds(dst, rows), :], sems.at[len(copies), place]))
        result.append(copies)
    return result


def first_kernel(plan, scale, lse_ref, c_ref, *refs):
    n = plan["pieces"]
    pieces = refs[:n]
    new_ref, expo_ref, peak_ref, part_ref, table, own, lse, total, mass, sems, own_sem = refs[n:]
    nv, rows = plan["nv"], new_ref.shape[0]
    copies = fetches(plan, pieces, table, sems)
    start = pl.multiple_of(lax.axis_index("item") * rows, rows)
    own_copy = pltpu.make_async_copy(c_ref.at[pl.ds(start, rows), :], own, own_sem)
    own_copy.start()
    for block in copies:
        for copy in block:
            copy.start()
    lse[...] = merge(lse_ref[...], plan["merge_first"]).reshape(lse.shape)
    own_copy.wait()
    for place, block in enumerate(copies):
        for copy in block:
            copy.wait()
        index = block_of(plan, place)
        vectors = table[pl.ds(pl.multiple_of(index * nv, nv), nv), :]
        logits = scores(own[...], vectors, scale)
        resp = jnp.exp(logits - lse[pl.ds(index, 1), :]).astype(jnp.bfloat16)
        term = lax.dot_general(resp, vectors, NN, preferred_element_type=jnp.float32)
        weight = jnp.sum(resp.astype(jnp.float32), axis=1, keepdims=True)
        if place == 0:
            total[...] = term
            mass[...] = weight
        else:
            total[...] += term
            mass[...] += weight
    new_ref[...] = ((total[...] + own[...].astype(jnp.float32)) / (mass[...] + 1.0)).astype(jnp.bfloat16)
    for place in range(len(copies)):
        index = block_of(plan, place)
        vectors = table[pl.ds(pl.multiple_of(index * nv, nv), nv), :]
        logits = scores(new_ref[...], vectors, scale)
        peak = jnp.max(logits, axis=0, keepdims=True)
        expo = jnp.exp(logits - peak)
        expo_ref[place] = expo
        peak_ref[pl.ds(index, 1), :] = peak
        part_ref[pl.ds(index, 1), :] = peak + jnp.log(jnp.sum(expo, axis=0, keepdims=True))


def last_kernel(plan, lse_ref, old_ref, expo_ref, peak_ref, *refs):
    n = plan["pieces"]
    pieces = refs[:n]
    new_ref, norm_ref, table, lse, total, mass, sems = refs[n:]
    nv = plan["nv"]
    copies = fetches(plan, pieces, table, sems)
    for block in copies:
        for copy in block:
            copy.start()
    lse[...] = merge(lse_ref[...], plan["merge_last"]).reshape(lse.shape)
    norm_ref[...] = lse[pl.ds(lax.axis_index("item"), 1), :]
    for place, block in enumerate(copies):
        for copy in block:
            copy.wait()
        index = block_of(plan, place)
        vectors = table[pl.ds(pl.multiple_of(index * nv, nv), nv), :]
        factor = jnp.exp(peak_ref[pl.ds(index, 1), :] - lse[pl.ds(index, 1), :])
        resp = (expo_ref[place] * factor).astype(jnp.bfloat16)
        term = lax.dot_general(resp, vectors, NN, preferred_element_type=jnp.float32)
        weight = jnp.sum(resp.astype(jnp.float32), axis=1, keepdims=True)
        if place == 0:
            total[...] = term
            mass[...] = weight
        else:
            total[...] += term
            mass[...] += weight
    new_ref[...] = ((total[...] + old_ref[...].astype(jnp.float32)) / (mass[...] + 1.0)).astype(jnp.bfloat16)


def send(value, items, cents, item_of, cent_of):
    pairs = [
        (i * cents + c, item_of(i) * cents + cent_of(c)) for i in range(items) for c in range(cents)
    ]
    return lax.ppermute(value, BOTH, pairs)


def gather_vectors(vectors, items, cents):
    nv = vectors.shape[0]
    if items != 4:
        table = lax.all_gather(vectors, "item", axis=0, tiled=True)
        blocks = [[(0, i * nv, None, 0, nv)] for i in range(items)]
        return [table], dict(nv=nv, pieces=1, exchange=False, blocks=blocks)
    quarter = nv // 4
    core = lax.rem(lax.axis_index("cent"), 2)
    q = [lax.dynamic_slice_in_dim(vectors, core * (nv // 2) + s * quarter, quarter, 0) for s in range(2)]
    go = functools.partial(send, items=items, cents=cents)
    stay = lambda c: c
    over_x = lambda v: go(v, item_of=lambda i: i ^ 1, cent_of=stay)
    over_y = lambda v: go(v, item_of=lambda i: i ^ 2, cent_of=stay)
    over_core = lambda v: go(v, item_of=lambda i: i, cent_of=lambda c: c ^ 1)
    x1, y0 = over_x(q[1]), over_y(q[0])
    x0, y1 = over_x(q[0]), over_y(q[1])
    d0, d1 = over_x(y0), over_y(x1)
    pieces = [vectors]
    blocks = [[(0, None, None, 0, nv)]]
    for pair in ((x0, x1), (y0, y1), (d0, d1)):
        entries = []
        for s, value in enumerate(pair):
            entries.append((len(pieces), None, True, s * quarter, quarter))
            pieces.append(value)
            entries.append((len(pieces), None, False, s * quarter, quarter))
            pieces.append(over_core(value))
        blocks.append(entries)
    return pieces, dict(nv=nv, pieces=len(pieces), exchange=True, blocks=blocks)


def shards(vectors, centroids):
    items, cents = lax.axis_size("item"), lax.axis_size("cent")
    nv, dim = vectors.shape
    rows = centroids.shape[0] // items
    scale = BETA / math.sqrt(dim)
    pieces, plan = gather_vectors(vectors, items, cents)

    part = partial(vectors, centroids, scale)
    parts = lax.all_gather(part, BOTH, axis=0, tiled=True).reshape(items, cents, nv)
    plan["merge_first"] = 1
    deep = max(len(b) for b in plan["blocks"])
    table_scratch = pltpu.VMEM((items * nv, dim), jnp.bfloat16)
    any_spec = pl.BlockSpec(memory_space=pl.ANY)
    vmem = pl.BlockSpec(memory_space=pltpu.VMEM)
    flops = 2 * items * nv * rows * dim
    params = pltpu.CompilerParams(vmem_limit_bytes=VMEM_LIMIT)
    fresh, expo, peak, part = pl.pallas_call(
        functools.partial(first_kernel, plan, scale),
        in_specs=[vmem, any_spec] + [any_spec] * len(pieces),
        out_specs=[vmem] * 4,
        out_shape=[
            jax.ShapeDtypeStruct((rows, dim), jnp.bfloat16),
            jax.ShapeDtypeStruct((items, rows, nv), jnp.float32),
            jax.ShapeDtypeStruct((items, nv), jnp.float32),
            jax.ShapeDtypeStruct((items, nv), jnp.float32),
        ],
        scratch_shapes=[
            table_scratch,
            pltpu.VMEM((rows, dim), jnp.bfloat16),
            pltpu.VMEM((items, nv), jnp.float32),
            pltpu.VMEM((rows, dim), jnp.float32),
            pltpu.VMEM((rows, 1), jnp.float32),
            pltpu.SemaphoreType.DMA((deep, items)),
            pltpu.SemaphoreType.DMA,
        ],
        compiler_params=params,
        cost_estimate=pl.CostEstimate(
            flops=3 * flops, bytes_accessed=2 * items * nv * dim, transcendentals=2 * items * nv * rows
        ),
        name="first_iteration",
    )(parts, centroids, *pieces)

    if items * cents * part.size * 4 <= SMALL:
        parts = lax.all_gather(part, BOTH, axis=0, tiled=False)
    else:
        part = merge(lax.all_gather(part, "cent", axis=0, tiled=False), 0)
        parts = lax.all_gather(part, "item", axis=0, tiled=False)
    plan["merge_last"] = 0
    result, norm = pl.pallas_call(
        functools.partial(last_kernel, plan),
        in_specs=[vmem, vmem, vmem, vmem] + [any_spec] * len(pieces),
        out_specs=[vmem] * 2,
        out_shape=[
            jax.ShapeDtypeStruct((rows, dim), jnp.bfloat16),
            jax.ShapeDtypeStruct((1, nv), jnp.float32),
        ],
        scratch_shapes=[
            table_scratch,
            pltpu.VMEM((items, nv), jnp.float32),
            pltpu.VMEM((rows, dim), jnp.float32),
            pltpu.VMEM((rows, 1), jnp.float32),
            pltpu.SemaphoreType.DMA((deep, items)),
        ],
        compiler_params=params,
        cost_estimate=pl.CostEstimate(flops=flops, bytes_accessed=2 * items * nv * dim, transcendentals=0),
        name="last_iteration",
    )(parts, fresh, expo, peak, *pieces)
    return (result, norm.reshape(nv))


def solution(mesh):
    in_specs = (P("item", None), P("cent", None))
    out_specs = (P(("cent", "item"), None), P("item"))
    return jax.shard_map(shards, mesh=mesh, in_specs=in_specs, out_specs=out_specs, check_vma=False)
```

time: 214 us -> 146 us (0.68)
  waiting for transfers between devices: 81.9 us -> 23.1 us
  Pallas kernels: 0 us -> 22.8 us
  other arithmetic: 20 us -> 1.27 us
  matrix products: 16.5 us -> 0 us
  between operations: 13.8 us -> 0.81 us
  starting transfers between devices: 0.12 us -> 7.81 us
  local copies, waits for them, and re-layouts: 0.02 us -> 6.24 us
  blocking collectives: 80.7 us -> 83.4 us
    all_gather x0 -> x2, blocking collectives: none -> 83.4 us  [the longest x1 42.1 us: shards(): lax.all_gather(part, BOTH, axis=0, tiled=True).reshape(items, cents, nv)]
    psum x4 -> x0, blocking collectives: 46.3 us -> none  [the longest x2 27.2 us: normalize(): total = lax.psum(jnp.sum(expo, axis=1), 'cent')]
    reduce_scatter x2 -> x0, waiting for transfers between devices: 46.3 us -> none  [shards(): lax.psum_scatter(term_rows().astype(jnp.bfloat16), 'item', scatter_dimens...]
    all_gather x1 -> x0, waiting for transfers between devices: 35.6 us -> none  [shards(): lax.all_gather(fresh, 'item', axis=0, tiled=True)]
    pmax x2 -> x0, blocking collectives: 34.4 us -> none  [normalize(): peak = lax.pmax(local_peak, 'cent')]
    ppermute x0 -> x12, waiting for transfers between devices: none -> 23.1 us  [send(): return lax.ppermute(value, BOTH, pairs)]
    pallas_call x0 -> x3, Pallas kernels: none -> 22.8 us  [the longest x1 12.9 us: shards(): pl.pallas_call(functools.partial(first_kernel, plan, scale), in_specs=[vm...]
    dot_general x4 -> x0, matrix products: 16.5 us -> none  [the longest x2 10.2 us: local_logits(): lax.dot_general(vectors, rows, (((1,), (1,)), ((), ())), preferred_elemen...]
  transfers between devices with their start and end apart: 3 -> 12, of which waited for: 3 -> 5; matrix products, arithmetic and copies ran while one was open for 0% -> 0% of each run, Pallas kernels for 0% -> 2%
where the time goes in v1:
time: 146 us; the launch traced here: 145 us
  blocking collectives  83.4 us (57%)
  waiting for transfers between devices  23.1 us (16%)
  Pallas kernels  22.8 us (16%)
  starting transfers between devices  7.81 us (5%)
  local copies, waits for them, and re-layouts  6.24 us (4%)
    all_gather x1, blocking collectives, shards(): lax.all_gather(part, BOTH, axis=0, tiled=True).reshape(items, cents, nv)  42.1 us
    all_gather x1, blocking collectives, shards(): parts = lax.all_gather(part, BOTH, axis=0, tiled=False)  41.3 us
    ppermute x12, waiting for transfers between devices, send(): return lax.ppermute(value, BOTH, pairs)  23.1 us
    pallas_call x1, Pallas kernels, shards(): pl.pallas_call(functools.partial(first_kernel, plan, scale), in_specs=[vm...  12.9 us
    ppermute x12, starting transfers between devices, send(): return lax.ppermute(value, BOTH, pairs)  7.81 us
    pallas_call x1, Pallas kernels, shards(): pl.pallas_call(functools.partial(last_kernel, plan), in_specs=[vmem, vmem...  6.61 us
    unnamed x29, local copies, waits for them, and re-layouts  5.07 us
    pallas_call x1, Pallas kernels, partial(): pl.pallas_call(functools.partial(partial_kernel, scale), grid=(k // rows,...  3.33 us
  transfers between devices with their start and end apart: 12, of which 5 were waited for; matrix products, arithmetic and copies ran while one was open for 0% of the time, Pallas kernels for 2%

profile of v1, /device:TPU:0, one launch (start us, length us, event | category | flops | bytes accessed | tf_op | source)
XLA Modules:
  0.0 145.4 jit_solution(12684603830492660638)
XLA Ops:
  0.6 1.2 constant_dynamic-slice_fusion
  1.8 3.0 %collective-permute-start.6 = (bf16[192,1024]{1,0:T(8,128)(2,1)S(1)}, bf16[192,1024]{1,0:T(8,128)(2,1)S(1)}, u32[]{:S(2)}, u32[]{:S(2)}) collective-permute-start(bf16[192,1024]{1,0:T(8,128)(2,1)S(1)} %get-tuple-element.14), channel_id=1, source_target_pairs={{0,16},{1,17},{2,18},{3,19},{4,20},{5,21},{6,22},{7,23},{8,24},{9,... | collective-permute-start | bytes 1179656 | tf_op jit(solution)/shard_map/ppermute | solution.py:174
  4.9 1.5 %collective-permute-start.2 = (bf16[192,1024]{1,0:T(8,128)(2,1)S(1)}, bf16[192,1024]{1,0:T(8,128)(2,1)S(1)}, u32[]{:S(2)}, u32[]{:S(2)}) collective-permute-start(bf16[192,1024]{1,0:T(8,128)(2,1)S(1)} %get-tuple-element.14), channel_id=1, source_target_pairs={{0,8},{1,9},{2,10},{3,11},{4,12},{5,13},{6,14},{7,15},{8,0},{9,1},... | collective-permute-start | bytes 1179656 | tf_op jit(solution)/shard_map/ppermute | solution.py:174
  6.3 0.5 collective-permute-start.4
  7.0 7.8 %collective-permute-done.6.refs_7_ = bf16[192,1024]{1,0:T(8,128)(2,1)S(1)} collective-permute-done((bf16[192,1024]{1,0:T(8,128)(2,1)S(1)}, bf16[192,1024]{1,0:T(8,128)(2,1)S(1)}, u32[]{:S(2)}, u32[]{:S(2)}) %collective-permute-start.6) | collective-permute-done | bytes 393248 | tf_op jit(solution)/shard_map/ppermute | solution.py:174
  14.8 2.1 %collective-permute-done.2.refs_3_ = bf16[192,1024]{1,0:T(8,128)(2,1)S(1)} collective-permute-done((bf16[192,1024]{1,0:T(8,128)(2,1)S(1)}, bf16[192,1024]{1,0:T(8,128)(2,1)S(1)}, u32[]{:S(2)}, u32[]{:S(2)}) %collective-permute-start.2) | collective-permute-done | bytes 393248 | tf_op jit(solution)/shard_map/ppermute | solution.py:174
  16.9 6.3 %collective-permute-done.4.refs_5_ = bf16[192,1024]{1,0:T(8,128)(2,1)S(1)} collective-permute-done((bf16[192,1024]{1,0:T(8,128)(2,1)S(1)}, bf16[192,1024]{1,0:T(8,128)(2,1)S(1)}, u32[]{:S(2)}, u32[]{:S(2)}) %collective-permute-start.4) | collective-permute-done | bytes 393248 | tf_op jit(solution)/shard_map/ppermute | solution.py:174
  23.2 2.0 %collective-permute-start.8 = (bf16[192,1024]{1,0:T(8,128)(2,1)S(1)}, bf16[192,1024]{1,0:T(8,128)(2,1)S(1)}, u32[]{:S(2)}, u32[]{:S(2)}) collective-permute-start(bf16[192,1024]{1,0:T(8,128)(2,1)S(1)} %collective-permute-done.4.refs_5_), channel_id=1, source_target_pairs={{0,8},{1,9},{2,10},{3,11},{4,12},{5,13},{6,14},{7,15},{8,0},{9,1},... | collective-permute-start | bytes 1179656 | tf_op jit(solution)/shard_map/ppermute | solution.py:174
  25.3 0.5 collective-permute-start.5
  25.9 5.0 %collective-permute-done.10.refs_11_ = bf16[192,1024]{1,0:T(8,128)(2,1)S(1)} collective-permute-done((bf16[192,1024]{1,0:T(8,128)(2,1)S(1)}, bf16[192,1024]{1,0:T(8,128)(2,1)S(1)}, u32[]{:S(2)}, u32[]{:S(2)}) %collective-permute-start.10) | collective-permute-done | bytes 393248 | tf_op jit(solution)/shard_map/ppermute | solution.py:174
  30.8 1.9 %collective-permute-done.8.refs_9_ = bf16[192,1024]{1,0:T(8,128)(2,1)S(1)} collective-permute-done((bf16[192,1024]{1,0:T(8,128)(2,1)S(1)}, bf16[192,1024]{1,0:T(8,128)(2,1)S(1)}, u32[]{:S(2)}, u32[]{:S(2)}) %collective-permute-start.8) | collective-permute-done | bytes 393248 | tf_op jit(solution)/shard_map/ppermute | solution.py:174
  32.7 1.5 %copy-done = bf16[768,1024]{1,0:T(8,128)(2,1)S(1)} copy-done((bf16[768,1024]{1,0:T(8,128)(2,1)S(1)}, bf16[768,1024]{1,0:T(8,128)(2,1)}, u32[]{:S(2)}) %copy-start) | copy-done | bytes 1572888
  34.3 1.6 %copy-done.1 = bf16[1024,1024]{1,0:T(8,128)(2,1)S(1)} copy-done((bf16[1024,1024]{1,0:T(8,128)(2,1)S(1)}, bf16[1024,1024]{1,0:T(8,128)(2,1)}, u32[]{:S(2)}) %copy-start.1) | copy-done | bytes 2097176
  35.8 3.3 %partial_lse.1 = f32[1,768]{1,0:T(1,128)S(1)} custom-call(bf16[768,1024]{1,0:T(8,128)(2,1)S(1)} %copy-done, bf16[1024,1024]{1,0:T(8,128)(2,1)S(1)} %copy-done.1), custom_call_target="tpu_custom_call" | custom-call | flops 1610612736 | bytes 3670016 | tf_op jit(solution)/shard_map/partial_lse/pallas_call | solution.py:55
  39.3 42.1 %all-gather.1 = f32[32,1,768]{2,1,0:T(1,128)S(1)} all-gather(f32[1,1,768]{2,1,0:T(1,128)S(1)} %bitcast.5), channel_id=1, replica_groups=mesh['item'=4,'cent'=8] {'item','cent'}, dimensions={0}, use_global_device_ids=true | all-gather | bytes 101376 | tf_op jit(solution)/shard_map/all_gather | solution.py:215
  81.3 0.6 copy.6
  82.1 0.7 copy-done.9
  82.8 0.2 copy-done.10
  83.0 0.2 copy-done.12
  83.2 0.1 copy-done.13
  83.3 12.9 %first_iteration.1 = (bf16[256,1024]{1,0:T(8,128)(2,1)}, f32[4,256,768]{2,1,0:T(8,128)}, f32[4,768]{1,0:T(4,128)}, f32[4,768]{1,0:T(4,128)}) custom-call(f32[4,8,768]{2,1,0:T(8,128)} %bitcast.6, bf16[1024,1024]{1,0:T(8,128)(2,1)} %c_ref.3, bf16[768,1024]{1,0:T(8,128)(2,1)} %refs_0_.3, bf16[192,1024]{1,0:T(8,128)(2,1)} %copy-done.5, ...), custom_call_target="tpu_custom_call" | custom-call | flops 4831838208 | bytes 6291456 | tf_op jit(solution)/shard_map/first_iteration/pallas_call | solution.py:223
  96.2 41.3 %all-gather.2.lse_ref = f32[32,4,768]{2,1,0:T(4,128)} all-gather(f32[1,4,768]{2,1,0:T(4,128)} %bitcast.7), channel_id=2, replica_groups=mesh['item'=4,'cent'=8] {'item','cent'}, dimensions={0}, use_global_device_ids=true | all-gather | bytes 405504 | tf_op jit(solution)/shard_map/all_gather | solution.py:250
  137.5 6.6 %last_iteration.1 = (bf16[256,1024]{1,0:T(8,128)(2,1)}, f32[1,768]{1,0:T(1,128)}) custom-call(f32[32,4,768]{2,1,0:T(4,128)} %all-gather.2.lse_ref, bf16[256,1024]{1,0:T(8,128)(2,1)} %get-tuple-element.9.old_ref, f32[4,256,768]{2,1,0:T(8,128)} %get-tuple-element.10.expo_ref, f32[4,768]{1,0:T(4,128)} %get-tuple-element.11.peak_ref, bf16[768,1024]{1,0:T(8,128)(2,1)} %refs_0_.3, ...), custom_call_target="tpu_custom_call" | custom-call | flops 1610612736 | bytes 6291456 | tf_op jit(solution)/shard_map/last_iteration/pallas_call | solution.py:255
  144.1 1.3 reduce
  (36 shorter events, 0.4 us)
Async XLA Ops:
  1.8 13.0 %collective-permute-start.6 = (bf16[192,1024]{1,0:T(8,128)(2,1)S(1)}, bf16[192,1024]{1,0:T(8,128)(2,1)S(1)}, u32[]{:S(2)}, u32[]{:S(2)}) collective-permute-start(bf16[192,1024]{1,0:T(8,128)(2,1)S(1)} %get-tuple-element.14), channel_id=1, source_target_pairs={{0,16},{1,17},{2,18},{3,19},{4,20},{5,21},{6,22},{7,23},{8,24},{9,... | collective-permute-start | bytes 1179656 | tf_op jit(solution)/shard_map/ppermute | solution.py:174
  4.9 12.0 %collective-permute-start.2 = (bf16[192,1024]{1,0:T(8,128)(2,1)S(1)}, bf16[192,1024]{1,0:T(8,128)(2,1)S(1)}, u32[]{:S(2)}, u32[]{:S(2)}) collective-permute-start(bf16[192,1024]{1,0:T(8,128)(2,1)S(1)} %get-tuple-element.14), channel_id=1, source_target_pairs={{0,8},{1,9},{2,10},{3,11},{4,12},{5,13},{6,14},{7,15},{8,0},{9,1},... | collective-permute-start | bytes 1179656 | tf_op jit(solution)/shard_map/ppermute | solution.py:174
  6.3 16.9 %collective-permute-start.4 = (bf16[192,1024]{1,0:T(8,128)(2,1)S(1)}, bf16[192,1024]{1,0:T(8,128)(2,1)S(1)}, u32[]{:S(2)}, u32[]{:S(2)}) collective-permute-start(bf16[192,1024]{1,0:T(8,128)(2,1)S(1)} %get-tuple-element.15), channel_id=1, source_target_pairs={{0,16},{1,17},{2,18},{3,19},{4,20},{5,21},{6,22},{7,23},{8,24},{9,... | collective-permute-start | bytes 1179656 | tf_op jit(solution)/shard_map/ppermute | solution.py:174
  6.8 18.4 %collective-permute-start = (bf16[192,1024]{1,0:T(8,128)(2,1)S(1)}, bf16[192,1024]{1,0:T(8,128)(2,1)S(1)}, u32[]{:S(2)}, u32[]{:S(2)}) collective-permute-start(bf16[192,1024]{1,0:T(8,128)(2,1)S(1)} %get-tuple-element.15), channel_id=1, source_target_pairs={{0,8},{1,9},{2,10},{3,11},{4,12},{5,13},{6,14},{7,15},{8,0},{9,1},... | collective-permute-start | bytes 1179656 | tf_op jit(solution)/shard_map/ppermute | solution.py:174
  14.8 24.4 %copy-start.2 = (bf16[192,1024]{1,0:T(8,128)(2,1)}, bf16[192,1024]{1,0:T(8,128)(2,1)S(1)}, u32[]{:S(2)}) copy-start(bf16[192,1024]{1,0:T(8,128)(2,1)S(1)} %collective-permute-done.6.refs_7_) | copy-start | bytes 1179652
  14.8 11.0 %collective-permute-start.7 = (bf16[192,1024]{1,0:T(8,128)(2,1)S(1)}, bf16[192,1024]{1,0:T(8,128)(2,1)S(1)}, u32[]{:S(2)}, u32[]{:S(2)}) collective-permute-start(bf16[192,1024]{1,0:T(8,128)(2,1)S(1)} %collective-permute-done.6.refs_7_), channel_id=1, source_target_pairs={{0,1},{1,0},{2,3},{3,2},{4,5},{5,4},{6,7},{7,6},{8,9},{9,8},{10,11... | collective-permute-start | bytes 1179656 | tf_op jit(solution)/shard_map/ppermute | solution.py:174
  16.9 22.3 %copy-start.3 = (bf16[192,1024]{1,0:T(8,128)(2,1)}, bf16[192,1024]{1,0:T(8,128)(2,1)S(1)}, u32[]{:S(2)}) copy-start(bf16[192,1024]{1,0:T(8,128)(2,1)S(1)} %collective-permute-done.2.refs_3_) | copy-start | bytes 1179652
  16.9 13.9 %collective-permute-start.10 = (bf16[192,1024]{1,0:T(8,128)(2,1)S(1)}, bf16[192,1024]{1,0:T(8,128)(2,1)S(1)}, u32[]{:S(2)}, u32[]{:S(2)}) collective-permute-start(bf16[192,1024]{1,0:T(8,128)(2,1)S(1)} %collective-permute-done.2.refs_3_), channel_id=1, source_target_pairs={{0,16},{1,17},{2,18},{3,19},{4,20},{5,21},{6,22},{7,23},{8,24},{9,... | collective-permute-start | bytes 1179656 | tf_op jit(solution)/shard_map/ppermute | solution.py:174
  23.2 16.0 %copy-start.4 = (bf16[192,1024]{1,0:T(8,128)(2,1)}, bf16[192,1024]{1,0:T(8,128)(2,1)S(1)}, u32[]{:S(2)}) copy-start(bf16[192,1024]{1,0:T(8,128)(2,1)S(1)} %collective-permute-done.4.refs_5_) | copy-start | bytes 1179652
  23.2 9.5 %collective-permute-start.8 = (bf16[192,1024]{1,0:T(8,128)(2,1)S(1)}, bf16[192,1024]{1,0:T(8,128)(2,1)S(1)}, u32[]{:S(2)}, u32[]{:S(2)}) collective-permute-start(bf16[192,1024]{1,0:T(8,128)(2,1)S(1)} %collective-permute-done.4.refs_5_), channel_id=1, source_target_pairs={{0,8},{1,9},{2,10},{3,11},{4,12},{5,13},{6,14},{7,15},{8,0},{9,1},... | collective-permute-start | bytes 1179656 | tf_op jit(solution)/shard_map/ppermute | solution.py:174
  25.3 56.7 %collective-permute-start.3 = (bf16[192,1024]{1,0:T(8,128)(2,1)S(1)}, bf16[192,1024]{1,0:T(8,128)(2,1)S(1)}, u32[]{:S(2)}, u32[]{:S(2)}) collective-permute-start(bf16[192,1024]{1,0:T(8,128)(2,1)S(1)} %collective-permute-done.2.refs_3_), channel_id=1, source_target_pairs={{0,1},{1,0},{2,3},{3,2},{4,5},{5,4},{6,7},{7,6},{8,9},{9,8},{10,11... | collective-permute-start | bytes 1179656 | tf_op jit(solution)/shard_map/ppermute | solution.py:174
  25.3 14.0 %copy-start.5 = (bf16[192,1024]{1,0:T(8,128)(2,1)}, bf16[192,1024]{1,0:T(8,128)(2,1)S(1)}, u32[]{:S(2)}) copy-start(bf16[192,1024]{1,0:T(8,128)(2,1)S(1)} %collective-permute-done.refs_1_) | copy-start | bytes 1179652
  25.3 56.7 %collective-permute-start.5 = (bf16[192,1024]{1,0:T(8,128)(2,1)S(1)}, bf16[192,1024]{1,0:T(8,128)(2,1)S(1)}, u32[]{:S(2)}, u32[]{:S(2)}) collective-permute-start(bf16[192,1024]{1,0:T(8,128)(2,1)S(1)} %collective-permute-done.4.refs_5_), channel_id=1, source_target_pairs={{0,1},{1,0},{2,3},{3,2},{4,5},{5,4},{6,7},{7,6},{8,9},{9,8},{10,11... | collective-permute-start | bytes 1179656 | tf_op jit(solution)/shard_map/ppermute | solution.py:174
  25.8 13.5 %copy-start.6 = (bf16[192,1024]{1,0:T(8,128)(2,1)}, bf16[192,1024]{1,0:T(8,128)(2,1)S(1)}, u32[]{:S(2)}) copy-start(bf16[192,1024]{1,0:T(8,128)(2,1)S(1)} %collective-permute-done.7.refs_8_) | copy-start | bytes 1179652
  25.8 56.2 %collective-permute-start.1 = (bf16[192,1024]{1,0:T(8,128)(2,1)S(1)}, bf16[192,1024]{1,0:T(8,128)(2,1)S(1)}, u32[]{:S(2)}, u32[]{:S(2)}) collective-permute-start(bf16[192,1024]{1,0:T(8,128)(2,1)S(1)} %collective-permute-done.refs_1_), channel_id=1, source_target_pairs={{0,1},{1,0},{2,3},{3,2},{4,5},{5,4},{6,7},{7,6},{8,9},{9,8},{10,11... | collective-permute-start | bytes 1179656 | tf_op jit(solution)/shard_map/ppermute | solution.py:174
  30.8 8.4 %copy-start.7 = (bf16[192,1024]{1,0:T(8,128)(2,1)}, bf16[192,1024]{1,0:T(8,128)(2,1)S(1)}, u32[]{:S(2)}) copy-start(bf16[192,1024]{1,0:T(8,128)(2,1)S(1)} %collective-permute-done.10.refs_11_) | copy-start | bytes 1179652
  30.8 51.2 %collective-permute-start.11 = (bf16[192,1024]{1,0:T(8,128)(2,1)S(1)}, bf16[192,1024]{1,0:T(8,128)(2,1)S(1)}, u32[]{:S(2)}, u32[]{:S(2)}) collective-permute-start(bf16[192,1024]{1,0:T(8,128)(2,1)S(1)} %collective-permute-done.10.refs_11_), channel_id=1, source_target_pairs={{0,1},{1,0},{2,3},{3,2},{4,5},{5,4},{6,7},{7,6},{8,9},{9,8},{10,11... | collective-permute-start | bytes 1179656 | tf_op jit(solution)/shard_map/ppermute | solution.py:174
  32.7 6.5 %copy-start.8 = (bf16[192,1024]{1,0:T(8,128)(2,1)}, bf16[192,1024]{1,0:T(8,128)(2,1)S(1)}, u32[]{:S(2)}) copy-start(bf16[192,1024]{1,0:T(8,128)(2,1)S(1)} %collective-permute-done.8.refs_9_) | copy-start | bytes 1179652
  32.7 49.4 %collective-permute-start.9 = (bf16[192,1024]{1,0:T(8,128)(2,1)S(1)}, bf16[192,1024]{1,0:T(8,128)(2,1)S(1)}, u32[]{:S(2)}, u32[]{:S(2)}) collective-permute-start(bf16[192,1024]{1,0:T(8,128)(2,1)S(1)} %collective-permute-done.8.refs_9_), channel_id=1, source_target_pairs={{0,1},{1,0},{2,3},{3,2},{4,5},{5,4},{6,7},{7,6},{8,9},{9,8},{10,11... | collective-permute-start | bytes 1179656 | tf_op jit(solution)/shard_map/ppermute | solution.py:174
  32.7 1.6 %copy-start = (bf16[768,1024]{1,0:T(8,128)(2,1)S(1)}, bf16[768,1024]{1,0:T(8,128)(2,1)}, u32[]{:S(2)}) copy-start(bf16[768,1024]{1,0:T(8,128)(2,1)} %refs_0_.3) | copy-start | bytes 4718596
  34.3 1.6 %copy-start.1 = (bf16[1024,1024]{1,0:T(8,128)(2,1)S(1)}, bf16[1024,1024]{1,0:T(8,128)(2,1)}, u32[]{:S(2)}) copy-start(bf16[1024,1024]{1,0:T(8,128)(2,1)} %c_ref.3) | copy-start | bytes 6291460
  82.0 1.0 copy-start.11
  82.0 1.2 copy-start.12
  82.1 1.3 copy-start.13
  (2 other events, 1.7 us)

commit v2 on v0

v2 whole, which is shorter than its diff:
```python
import functools
import math

import jax
import jax.numpy as jnp
from jax import lax
from jax.experimental import pallas as pl
from jax.experimental.pallas import tpu as pltpu
from jax.sharding import PartitionSpec as P

BETA = 3.0
BOTH = ("item", "cent")
MIB = 1024 * 1024
NT = (((1,), (1,)), ((), ()))
NN = (((1,), (0,)), ((), ()))


def scores(rows, vectors, scale):
    raw = lax.dot_general(rows, vectors, NT, preferred_element_type=jnp.float32)
    sqnorm = jnp.sum(jnp.square(rows.astype(jnp.float32)), axis=1, keepdims=True)
    return scale * (raw - 0.5 * sqnorm)


def merge(parts):
    peak = functools.reduce(jnp.maximum, parts)
    terms = [jnp.exp(p - peak) for p in parts]
    while len(terms) > 1:
        terms = [sum(terms[i : i + 2]) for i in range(0, len(terms), 2)]
    return peak + jnp.log(terms[0])


def partial_kernel(scale, v_ref, c_ref, out_ref, peak, total):
    step = pl.program_id(0)

    @pl.when(step == 0)
    def _():
        peak[...] = jnp.full_like(peak, -jnp.inf)
        total[...] = jnp.zeros_like(total)

    logits = scores(c_ref[...], v_ref[...], scale)
    top = jnp.maximum(peak[...], jnp.max(logits, axis=0, keepdims=True))
    total[...] = total[...] * jnp.exp(peak[...] - top) + jnp.sum(
        jnp.exp(logits - top), axis=0, keepdims=True
    )
    peak[...] = top

    @pl.when(step == pl.num_programs(0) - 1)
    def _():
        out_ref[...] = peak[...] + jnp.log(total[...])


def in_hbm(value):
    return pltpu.with_memory_space_constraint(value, pltpu.HBM)


def in_vmem(value):
    return pltpu.with_memory_space_constraint(value, pltpu.VMEM)


def partial(vectors, centroids, scale):
    nv, dim = vectors.shape
    k = centroids.shape[0]
    rows = min(256, k)
    return pl.pallas_call(
        functools.partial(partial_kernel, scale),
        grid=(k // rows,),
        in_specs=[
            pl.BlockSpec((nv, dim), lambda i: (0, 0)),
            pl.BlockSpec((rows, dim), lambda i: (i, 0)),
        ],
        out_specs=pl.BlockSpec((1, nv), lambda i: (0, 0)),
        out_shape=jax.ShapeDtypeStruct((1, nv), jnp.float32),
        scratch_shapes=[pltpu.VMEM((1, nv), jnp.float32)] * 2,
        compiler_params=pltpu.CompilerParams(vmem_limit_bytes=16 * MIB),
        cost_estimate=pl.CostEstimate(
            flops=2 * nv * k * dim, bytes_accessed=2 * (nv + k) * dim, transcendentals=nv * k
        ),
        name="partial_lse",
    )(in_hbm(vectors), in_hbm(centroids))


def fetches(nv, blocks, pieces, table, sems):
    core = lax.rem(lax.axis_index("cent"), 2)
    result = []
    for place, entries in enumerate(blocks):
        copies = []
        for piece, start, mine, offset, rows in entries:
            lead = 0 if mine is None else (core if mine else 1 - core) * (nv // 2)
            dst = pl.multiple_of(place * nv + lead + offset, 64)
            src = pieces[piece] if start is None else pieces[piece].at[pl.ds(start, rows), :]
            copies.append(pltpu.make_async_copy(src, table.at[pl.ds(dst, rows), :], sems.at[len(copies), place]))
        result.append(copies)
    return result


def weigh(resp, vectors):
    term = lax.dot_general(resp, vectors, NN, preferred_element_type=jnp.float32)
    return term, jnp.sum(resp.astype(jnp.float32), axis=1, keepdims=True)


def updated(total, mass, old):
    return ((total + old.astype(jnp.float32)) / (mass + 1.0)).astype(jnp.bfloat16)


def open_kernel(plan, scale, c_ref, *refs):
    nv, blocks = plan["nv"], plan["early"]
    lse, refs = refs[: len(blocks)], refs[len(blocks) :]
    pieces, refs = refs[: plan["n_early"]], refs[plan["n_early"] :]
    table, own, total, mass, sems, own_sem = refs
    rows = own.shape[0]
    start = pl.multiple_of(lax.axis_index("item") * rows, rows)
    own_copy = pltpu.make_async_copy(c_ref.at[pl.ds(start, rows), :], own, own_sem)
    own_copy.start()
    copies = fetches(nv, blocks, pieces, table, sems)
    for block in copies:
        for copy in block:
            copy.start()
    own_copy.wait()
    for place, block in enumerate(copies):
        for copy in block:
            copy.wait()
        vectors = table[pl.ds(place * nv, nv), :]
        resp = jnp.exp(scores(own[...], vectors, scale) - lse[place][...]).astype(jnp.bfloat16)
        term, weight = weigh(resp, vectors)
        total[...] = term if place == 0 else total[...] + term
        mass[...] = weight if place == 0 else mass[...] + weight


def close_kernel(plan, scale, early, own, total, mass, *refs):
    nv, blocks, first = plan["nv"], plan["late"], len(plan["early"])
    lse, refs = refs[: len(blocks)], refs[len(blocks) :]
    pieces, refs = refs[: plan["n_late"]], refs[plan["n_late"] :]
    new_ref, expo_ref, peak_ref, part_ref = refs[:4]
    late = sems = None
    if blocks:
        late, sems = refs[4:]
        copies = fetches(nv, blocks, pieces, late, sems)
        for block in copies:
            for copy in block:
                copy.start()
        sums, weights = total[...], mass[...]
        for place, block in enumerate(copies):
            for copy in block:
                copy.wait()
            vectors = late[pl.ds(place * nv, nv), :]
            resp = jnp.exp(scores(own[...], vectors, scale) - lse[place][...]).astype(jnp.bfloat16)
            term, weight = weigh(resp, vectors)
            sums, weights = sums + term, weights + weight
        new_ref[...] = updated(sums, weights, own[...])
    else:
        new_ref[...] = updated(total[...], mass[...], own[...])
    for place in range(first + len(blocks)):
        vectors = early[pl.ds(place * nv, nv), :] if place < first else late[pl.ds((place - first) * nv, nv), :]
        logits = scores(new_ref[...], vectors, scale)
        peak = jnp.max(logits, axis=0, keepdims=True)
        expo = jnp.exp(logits - peak)
        expo_ref[place] = expo
        peak_ref[pl.ds(place, 1), :] = peak
        part_ref[pl.ds(place, 1), :] = peak + jnp.log(jnp.sum(expo, axis=0, keepdims=True))


def last_kernel(plan, old_ref, expo_ref, peak_ref, *refs):
    nv, n = plan["nv"], plan["n_parts"]
    first, second = len(plan["early"]), len(plan["late"])
    parts, refs = refs[:n], refs[n:]
    early, refs = refs[0], refs[1:]
    late = refs[0] if second else None
    new_ref, norm_ref, total, mass = refs[1:] if second else refs
    for place in range(first + second):
        if n == 1:
            lse = parts[0][pl.ds(place, 1), :]
        else:
            lse = merge([parts[k][pl.ds(place ^ k, 1), :] for k in range(n)])
        if plan["n_parts"] > 1 and place == 0:
            norm_ref[...] = lse.reshape(nv)
        vectors = early[pl.ds(place * nv, nv), :] if place < first else late[pl.ds((place - first) * nv, nv), :]
        factor = jnp.exp(peak_ref[pl.ds(place, 1), :] - lse)
        term, weight = weigh((expo_ref[place] * factor).astype(jnp.bfloat16), vectors)
        total[...] = term if place == 0 else total[...] + term
        mass[...] = weight if place == 0 else mass[...] + weight
    if n == 1:
        norm_ref[...] = parts[0][pl.ds(lax.axis_index("item"), 1), :].reshape(nv)
    new_ref[...] = updated(total[...], mass[...], old_ref[...])


def send(value, items, cents, item_mask, cent_mask):
    pairs = [
        (i * cents + c, (i ^ item_mask) * cents + (c ^ cent_mask)) for i in range(items) for c in range(cents)
    ]
    return lax.ppermute(value, BOTH, pairs)


def shards(vectors, centroids):
    items, cents = lax.axis_size("item"), lax.axis_size("cent")
    nv, dim = vectors.shape
    rows = centroids.shape[0] // items
    scale = BETA / math.sqrt(dim)
    go = functools.partial(send, items=items, cents=cents)
    small = items == 4 and cents == 8
    if small:
        quarter = nv // 4
        core = lax.rem(lax.axis_index("cent"), 2)
        q = [lax.dynamic_slice_in_dim(vectors, core * (nv // 2) + s * quarter, quarter, 0) for s in range(2)]
        x1, y0 = go(q[1], item_mask=1, cent_mask=0), go(q[0], item_mask=2, cent_mask=0)
        x0, y1 = go(q[0], item_mask=1, cent_mask=0), go(q[1], item_mask=2, cent_mask=0)
        part = partial(vectors, centroids, scale)
        x1, y0, part = lax.optimization_barrier((x1, y0, part))
        lse = merge([part] + [go(part, item_mask=0, cent_mask=k) for k in range(1, cents)])
        lses = [lse] + [go(lse, item_mask=k, cent_mask=0) for k in range(1, items)]
        d0, d1 = go(y0, item_mask=1, cent_mask=0), go(x1, item_mask=2, cent_mask=0)

        def pieces_of(pairs, at):
            pieces, blocks = [], []
            for pair in pairs:
                entries = []
                for s, value in enumerate(pair):
                    for mine in (True, False):
                        entries.append((at + len(pieces), None, mine, s * quarter, quarter))
                        pieces.append(value if mine else go(value, item_mask=0, cent_mask=1))
                blocks.append(entries)
            return pieces, blocks

        early, early_blocks = pieces_of(((x0, x1), (y0, y1)), 1)
        early = [vectors] + early
        early_blocks = [[(0, None, None, 0, nv)]] + early_blocks
        late, late_blocks = pieces_of(((d0, d1),), 0)
    else:
        early = [lax.all_gather(vectors, "item", axis=0, tiled=True)]
        early_blocks = [[(0, i * nv, None, 0, nv)] for i in range(items)]
        late, late_blocks = [], []
        part = partial(vectors, centroids, scale)
        parts = lax.all_gather(part, "cent", axis=0, tiled=False)
        lse = lax.all_gather(merge([parts[i] for i in range(cents)]), "item", axis=0, tiled=False)
        lses = [lse[i] for i in range(items)]
    plan = dict(nv=nv, early=early_blocks, late=late_blocks, n_early=len(early), n_late=len(late))

    any_spec = pl.BlockSpec(memory_space=pl.ANY)
    vmem = pl.BlockSpec(memory_space=pltpu.VMEM)
    n_early, n_late = len(early_blocks), len(late_blocks)
    flops = 2 * nv * rows * dim
    params = pltpu.CompilerParams(vmem_limit_bytes=20 * MIB)
    table, own, total, mass = pl.pallas_call(
        functools.partial(open_kernel, plan, scale),
        in_specs=[any_spec] + [vmem] * n_early + [any_spec] * len(early),
        out_specs=[vmem] * 4,
        out_shape=[
            pltpu.VMEM((n_early * nv, dim), jnp.bfloat16),
            pltpu.VMEM((rows, dim), jnp.bfloat16),
            pltpu.VMEM((rows, dim), jnp.float32),
            pltpu.VMEM((rows, 1), jnp.float32),
        ],
        scratch_shapes=[
            pltpu.SemaphoreType.DMA((max(len(b) for b in early_blocks), n_early)),
            pltpu.SemaphoreType.DMA,
        ],
        compiler_params=params,
        cost_estimate=pl.CostEstimate(
            flops=2 * n_early * flops, bytes_accessed=2 * n_early * nv * dim, transcendentals=n_early * nv * rows
        ),
        name="early_blocks",
    )(centroids, *lses[:n_early], *early)

    late_out = [pltpu.VMEM((n_late * nv, dim), jnp.bfloat16)] if n_late else []
    late_sems = [pltpu.SemaphoreType.DMA((max(len(b) for b in late_blocks), n_late))] if n_late else []
    fresh, expo, peak, part, *tables = pl.pallas_call(
        functools.partial(close_kernel, plan, scale),
        in_specs=[vmem] * (4 + n_late) + [any_spec] * len(late),
        out_specs=[vmem] * (4 + len(late_out)),
        out_shape=[
            pltpu.VMEM((rows, dim), jnp.bfloat16),
            pltpu.VMEM((items, rows, nv), jnp.float32),
            pltpu.VMEM((items, nv), jnp.float32),
            pltpu.VMEM((items, nv), jnp.float32),
        ]
        + late_out,
        scratch_shapes=late_sems,
        compiler_params=params,
        cost_estimate=pl.CostEstimate(
            flops=(items + 2 * n_late) * flops,
            bytes_accessed=2 * n_late * nv * dim,
            transcendentals=(items + n_late) * nv * rows,
        ),
        name="late_blocks",
    )(in_vmem(table), in_vmem(own), in_vmem(total), in_vmem(mass), *lses[n_early:], *late)

    if small:
        lse = merge([part] + [go(part, item_mask=0, cent_mask=k) for k in range(1, cents)])
        parts = [lse] + [go(lse, item_mask=k, cent_mask=0) for k in range(1, items)]
    else:
        gathered = lax.all_gather(part, "cent", axis=0, tiled=False)
        lse = merge([gathered[i] for i in range(cents)])
        gathered = lax.all_gather(lse, "item", axis=0, tiled=False)
        parts = [merge([gathered[i] for i in range(items)])]
    plan["n_parts"] = len(parts)
    result, norm = pl.pallas_call(
        functools.partial(last_kernel, plan),
        in_specs=[vmem] * (4 + len(parts) + len(tables)),
        out_specs=[vmem] * 2,
        out_shape=[
            jax.ShapeDtypeStruct((rows, dim), jnp.bfloat16),
            jax.ShapeDtypeStruct((nv,), jnp.float32),
        ],
        scratch_shapes=[pltpu.VMEM((rows, dim), jnp.float32), pltpu.VMEM((rows, 1), jnp.float32)],
        compiler_params=params,
        cost_estimate=pl.CostEstimate(flops=items * flops, bytes_accessed=2 * rows * dim, transcendentals=0),
        name="last_iteration",
    )(in_vmem(fresh), in_vmem(expo), in_vmem(peak), *parts, in_vmem(table), *[in_vmem(t) for t in tables])
    return (result, norm)


def solution(mesh):
    in_specs = (P("item", None), P("cent", None))
    out_specs = (P(("cent", "item"), None), P("item"))
    return jax.shard_map(shards, mesh=mesh, in_specs=in_specs, out_specs=out_specs, check_vma=False)
```

time: 214 us -> 78.4 us (0.37)
  blocking collectives: 80.7 us -> 0 us
  waiting for transfers between devices: 81.9 us -> 26 us
  starting transfers between devices: 0.12 us -> 31.9 us
  other arithmetic: 20 us -> 0.11 us
  Pallas kernels: 0 us -> 18.2 us
  matrix products: 16.5 us -> 0 us
  between operations: 13.8 us -> 0.75 us
    psum x4 -> x0, blocking collectives: 46.3 us -> none  [the longest x2 27.2 us: normalize(): total = lax.psum(jnp.sum(expo, axis=1), 'cent')]
    reduce_scatter x2 -> x0, waiting for transfers between devices: 46.3 us -> none  [shards(): lax.psum_scatter(term_rows().astype(jnp.bfloat16), 'item', scatter_dimens...]
    all_gather x1 -> x0, waiting for transfers between devices: 35.6 us -> none  [shards(): lax.all_gather(fresh, 'item', axis=0, tiled=True)]
    pmax x2 -> x0, blocking collectives: 34.4 us -> none  [normalize(): peak = lax.pmax(local_peak, 'cent')]
    ppermute x0 -> x32, starting transfers between devices: none -> 31.9 us  [send(): return lax.ppermute(value, BOTH, pairs)]
    ppermute x0 -> x32, waiting for transfers between devices: none -> 26 us  [send(): return lax.ppermute(value, BOTH, pairs)]
    pallas_call x0 -> x4, Pallas kernels: none -> 18.2 us  [the longest x1 5.87 us: shards(): pl.pallas_call(functools.partial(open_kernel, plan, scale), in_specs=[any...]
    dot_general x4 -> x0, matrix products: 16.5 us -> none  [the longest x2 10.2 us: local_logits(): lax.dot_general(vectors, rows, (((1,), (1,)), ((), ())), preferred_elemen...]
  transfers between devices with their start and end apart: 3 -> 32, of which waited for: 3 -> 12; matrix products, arithmetic and copies ran while one was open for 0% -> 0% of each run, Pallas kernels for 0% -> 14%
where the time goes in v2:
time: 78.4 us; the launch traced here: 78.2 us
  starting transfers between devices  31.9 us (41%)
  waiting for transfers between devices  26 us (33%)
  Pallas kernels  18.2 us (23%)
  local copies, waits for them, and re-layouts  1.18 us (2%)
    ppermute x32, starting transfers between devices, send(): return lax.ppermute(value, BOTH, pairs)  31.9 us
    ppermute x32, waiting for transfers between devices, send(): return lax.ppermute(value, BOTH, pairs)  26 us
    pallas_call x1, Pallas kernels, shards(): pl.pallas_call(functools.partial(open_kernel, plan, scale), in_specs=[any...  5.87 us
    pallas_call x1, Pallas kernels, partial(): pl.pallas_call(functools.partial(partial_kernel, scale), grid=(k // rows,...  5.18 us
    pallas_call x1, Pallas kernels, shards(): pl.pallas_call(functools.partial(close_kernel, plan, scale), in_specs=[vm...  4.49 us
    pallas_call x1, Pallas kernels, shards(): pl.pallas_call(functools.partial(last_kernel, plan), in_specs=[vmem] * (4...  2.69 us
  transfers between devices with their start and end apart: 32, of which 12 were waited for; matrix products, arithmetic and copies ran while one was open for 0% of the time, Pallas kernels for 14%

profile of v2, /device:TPU:0, one launch (start us, length us, event | category | flops | bytes accessed | tf_op | source)
XLA Modules:
  0.0 78.2 jit_solution(16987320042891367838)
XLA Ops:
  1.8 3.0 %collective-permute-start.11 = (bf16[192,1024]{1,0:T(8,128)(2,1)S(1)}, bf16[192,1024]{1,0:T(8,128)(2,1)S(1)}, u32[]{:S(2)}, u32[]{:S(2)}) collective-permute-start(bf16[192,1024]{1,0:T(8,128)(2,1)S(1)} %get-tuple-element.26), channel_id=1, source_target_pairs={{0,8},{1,9},{2,10},{3,11},{4,12},{5,13},{6,14},{7,15},{8,0},{9,1},... | collective-permute-start | bytes 1179656 | tf_op jit(solution)/shard_map/ppermute | solution.py:190
  4.8 1.5 %collective-permute-start.1 = (bf16[192,1024]{1,0:T(8,128)(2,1)S(1)}, bf16[192,1024]{1,0:T(8,128)(2,1)S(1)}, u32[]{:S(2)}, u32[]{:S(2)}) collective-permute-start(bf16[192,1024]{1,0:T(8,128)(2,1)S(1)} %get-tuple-element.26), channel_id=1, source_target_pairs={{0,16},{1,17},{2,18},{3,19},{4,20},{5,21},{6,22},{7,23},{8,24},{9,... | collective-permute-start | bytes 1179656 | tf_op jit(solution)/shard_map/ppermute | solution.py:190
  6.9 7.8 %collective-permute-done.11.refs_4_ = bf16[192,1024]{1,0:T(8,128)(2,1)S(1)} collective-permute-done((bf16[192,1024]{1,0:T(8,128)(2,1)S(1)}, bf16[192,1024]{1,0:T(8,128)(2,1)S(1)}, u32[]{:S(2)}, u32[]{:S(2)}) %collective-permute-start.11) | collective-permute-done | bytes 393248 | tf_op jit(solution)/shard_map/ppermute | solution.py:190
  14.8 5.2 %partial_lse.1 = f32[1,768]{1,0:T(1,128)S(1)} custom-call(bf16[768,1024]{1,0:T(8,128)(2,1)} %refs_3_.1, bf16[1024,1024]{1,0:T(8,128)(2,1)} %c_ref.3), custom_call_target="tpu_custom_call" | custom-call | flops 1610612736 | bytes 3670016 | tf_op jit(solution)/shard_map/partial_lse/pallas_call | solution.py:64
  20.0 2.4 %collective-permute-done.refs_6_ = bf16[192,1024]{1,0:T(8,128)(2,1)S(1)} collective-permute-done((bf16[192,1024]{1,0:T(8,128)(2,1)S(1)}, bf16[192,1024]{1,0:T(8,128)(2,1)S(1)}, u32[]{:S(2)}, u32[]{:S(2)}) %collective-permute-start) | collective-permute-done | bytes 393248 | tf_op jit(solution)/shard_map/ppermute | solution.py:190
  22.4 2.4 %collective-permute-start.8 = (f32[1,768]{1,0:T(1,128)S(1)}, f32[1,768]{1,0:T(1,128)S(1)}, u32[]{:S(2)}, u32[]{:S(2)}) collective-permute-start(f32[1,768]{1,0:T(1,128)S(1)} %partial_lse.1), channel_id=1, source_target_pairs={{0,7},{1,6},{2,5},{3,4},{4,3},{5,2},{6,1},{7,0},{8,15},{9,14},{10,... | collective-permute-start | bytes 9224 | tf_op jit(solution)/shard_map/ppermute | solution.py:190
  24.8 1.5 %collective-permute-start.7 = (f32[1,768]{1,0:T(1,128)S(1)}, f32[1,768]{1,0:T(1,128)S(1)}, u32[]{:S(2)}, u32[]{:S(2)}) collective-permute-start(f32[1,768]{1,0:T(1,128)S(1)} %partial_lse.1), channel_id=1, source_target_pairs={{0,6},{1,7},{2,4},{3,5},{4,2},{5,3},{6,0},{7,1},{8,14},{9,15},{10,... | collective-permute-start | bytes 9224 | tf_op jit(solution)/shard_map/ppermute | solution.py:190
  27.2 1.7 %collective-permute-start.5 = (f32[1,768]{1,0:T(1,128)S(1)}, f32[1,768]{1,0:T(1,128)S(1)}, u32[]{:S(2)}, u32[]{:S(2)}) collective-permute-start(f32[1,768]{1,0:T(1,128)S(1)} %partial_lse.1), channel_id=1, source_target_pairs={{0,4},{1,5},{2,6},{3,7},{4,0},{5,1},{6,2},{7,3},{8,12},{9,13},{10,... | collective-permute-start | bytes 9224 | tf_op jit(solution)/shard_map/ppermute | solution.py:190
  28.9 1.3 %collective-permute-done.7 = f32[1,768]{1,0:T(1,128)S(1)} collective-permute-done((f32[1,768]{1,0:T(1,128)S(1)}, f32[1,768]{1,0:T(1,128)S(1)}, u32[]{:S(2)}, u32[]{:S(2)}) %collective-permute-start.7) | collective-permute-done | bytes 3104 | tf_op jit(solution)/shard_map/ppermute | solution.py:190
  30.2 2.0 %collective-permute-start.3 = (f32[1,768]{1,0:T(1,128)S(1)}, f32[1,768]{1,0:T(1,128)S(1)}, u32[]{:S(2)}, u32[]{:S(2)}) collective-permute-start(f32[1,768]{1,0:T(1,128)S(1)} %partial_lse.1), channel_id=1, source_target_pairs={{0,2},{1,3},{2,0},{3,1},{4,6},{5,7},{6,4},{7,5},{8,10},{9,11},{10,... | collective-permute-start | bytes 9224 | tf_op jit(solution)/shard_map/ppermute | solution.py:190
  33.2 1.5 %collective-permute-start.20 = (bf16[192,1024]{1,0:T(8,128)(2,1)S(1)}, bf16[192,1024]{1,0:T(8,128)(2,1)S(1)}, u32[]{:S(2)}, u32[]{:S(2)}) collective-permute-start(bf16[192,1024]{1,0:T(8,128)(2,1)S(1)} %collective-permute-done.refs_6_), channel_id=1, source_target_pairs={{0,16},{1,17},{2,18},{3,19},{4,20},{5,21},{6,22},{7,23},{8,24},{9,... | collective-permute-start | bytes 1179656 | tf_op jit(solution)/shard_map/ppermute | solution.py:190
  34.8 1.5 %collective-permute-start.18 = (bf16[192,1024]{1,0:T(8,128)(2,1)S(1)}, bf16[192,1024]{1,0:T(8,128)(2,1)S(1)}, u32[]{:S(2)}, u32[]{:S(2)}) collective-permute-start(bf16[192,1024]{1,0:T(8,128)(2,1)S(1)} %collective-permute-done.1.refs_8_), channel_id=1, source_target_pairs={{0,8},{1,9},{2,10},{3,11},{4,12},{5,13},{6,14},{7,15},{8,0},{9,1},... | collective-permute-start | bytes 1179656 | tf_op jit(solution)/shard_map/ppermute | solution.py:190
  37.5 7.2 %collective-permute-done.10.refs_2_ = f32[1,768]{1,0:T(1,128)S(1)} collective-permute-done((f32[1,768]{1,0:T(1,128)S(1)}, f32[1,768]{1,0:T(1,128)S(1)}, u32[]{:S(2)}, u32[]{:S(2)}) %collective-permute-start.10) | collective-permute-done | bytes 3104 | tf_op jit(solution)/shard_map/ppermute | solution.py:190
  44.7 1.2 %collective-permute-done.9.refs_1_ = f32[1,768]{1,0:T(1,128)S(1)} collective-permute-done((f32[1,768]{1,0:T(1,128)S(1)}, f32[1,768]{1,0:T(1,128)S(1)}, u32[]{:S(2)}, u32[]{:S(2)}) %collective-permute-start.9) | collective-permute-done | bytes 3104 | tf_op jit(solution)/shard_map/ppermute | solution.py:190
  47.0 1.9 %collective-permute-start.17 = (f32[1,768]{1,0:T(1,128)S(1)}, f32[1,768]{1,0:T(1,128)S(1)}, u32[]{:S(2)}, u32[]{:S(2)}) collective-permute-start(f32[1,768]{1,0:T(1,128)S(1)} %log_add_fusion.1.refs_0_), channel_id=1, source_target_pairs={{0,24},{1,25},{2,26},{3,27},{4,28},{5,29},{6,30},{7,31},{8,16},{9,... | collective-permute-start | bytes 9224 | tf_op jit(solution)/shard_map/ppermute | solution.py:190
  48.9 5.9 %early_blocks.1 = (bf16[2304,1024]{1,0:T(8,128)(2,1)S(1)}, bf16[256,1024]{1,0:T(8,128)(2,1)S(1)}, f32[256,1024]{1,0:T(8,128)S(1)}, f32[256,1]{1,0:T(8,128)S(1)}) custom-call(bf16[1024,1024]{1,0:T(8,128)(2,1)S(1)} %copy-done.1, f32[1,768]{1,0:T(1,128)S(1)} %log_add_fusion.1.refs_0_, f32[1,768]{1,0:T(1,128)S(1)} %collective-permute-done.9.refs_1_, ...), custom_call_target="tpu_custom_call" | custom-call | flops 2415919104 | bytes 4718592 | tf_op jit(solution)/shard_map/early_blocks/pallas_call | solution.py:242
  54.8 4.5 %late_blocks.1 = (bf16[256,1024]{1,0:T(8,128)(2,1)S(1)}, f32[4,256,768]{2,1,0:T(8,128)S(1)}, f32[4,768]{1,0:T(4,128)S(1)}, f32[4,768]{1,0:T(4,128)S(1)}, bf16[768,1024]{1,0:T(8,128)(2,1)S(1)}) custom-call(bf16[2304,1024]{1,0:T(8,128)(2,1)S(1)} %get-tuple-element.17.early.refs_4_, bf16[256,1024]{1,0:T(8,128)(2,1)S(1)} %get-tuple-element.18.own, ...), custom_call_target="tpu_custom_call" | custom-call | flops 2415919104 | bytes 1572864 | tf_op jit(solution)/shard_map/late_blocks/pallas_call | solution.py:265
  59.3 2.0 %collective-permute-start.28 = (f32[4,768]{1,0:T(4,128)S(1)}, f32[4,768]{1,0:T(4,128)S(1)}, u32[]{:S(2)}, u32[]{:S(2)}) collective-permute-start(f32[4,768]{1,0:T(4,128)S(1)} %get-tuple-element.24), channel_id=1, source_target_pairs={{0,7},{1,6},{2,5},{3,4},{4,3},{5,2},{6,1},{7,0},{8,15},{9,14},{10,... | collective-permute-start | bytes 36872 | tf_op jit(solution)/shard_map/ppermute | solution.py:190
  61.3 1.4 %collective-permute-start.27 = (f32[4,768]{1,0:T(4,128)S(1)}, f32[4,768]{1,0:T(4,128)S(1)}, u32[]{:S(2)}, u32[]{:S(2)}) collective-permute-start(f32[4,768]{1,0:T(4,128)S(1)} %get-tuple-element.24), channel_id=1, source_target_pairs={{0,6},{1,7},{2,4},{3,5},{4,2},{5,3},{6,0},{7,1},{8,14},{9,15},{10,... | collective-permute-start | bytes 36872 | tf_op jit(solution)/shard_map/ppermute | solution.py:190
  62.6 2.9 %collective-permute-start.25 = (f32[4,768]{1,0:T(4,128)S(1)}, f32[4,768]{1,0:T(4,128)S(1)}, u32[]{:S(2)}, u32[]{:S(2)}) collective-permute-start(f32[4,768]{1,0:T(4,128)S(1)} %get-tuple-element.24), channel_id=1, source_target_pairs={{0,4},{1,5},{2,6},{3,7},{4,0},{5,1},{6,2},{7,3},{8,12},{9,13},{10,... | collective-permute-start | bytes 36872 | tf_op jit(solution)/shard_map/ppermute | solution.py:190
  65.6 1.5 %collective-permute-start.23 = (f32[4,768]{1,0:T(4,128)S(1)}, f32[4,768]{1,0:T(4,128)S(1)}, u32[]{:S(2)}, u32[]{:S(2)}) collective-permute-start(f32[4,768]{1,0:T(4,128)S(1)} %get-tuple-element.24), channel_id=1, source_target_pairs={{0,2},{1,3},{2,0},{3,1},{4,6},{5,7},{6,4},{7,5},{8,10},{9,11},{10,... | collective-permute-start | bytes 36872 | tf_op jit(solution)/shard_map/ppermute | solution.py:190
  67.4 1.3 %collective-permute-done.24 = f32[4,768]{1,0:T(4,128)S(1)} collective-permute-done((f32[4,768]{1,0:T(4,128)S(1)}, f32[4,768]{1,0:T(4,128)S(1)}, u32[]{:S(2)}, u32[]{:S(2)}) %collective-permute-start.24) | collective-permute-done | bytes 12320 | tf_op jit(solution)/shard_map/ppermute | solution.py:190
  69.3 1.2 %collective-permute-start.31 = (f32[4,768]{1,0:T(4,128)S(1)}, f32[4,768]{1,0:T(4,128)S(1)}, u32[]{:S(2)}, u32[]{:S(2)}) collective-permute-start(f32[4,768]{1,0:T(4,128)S(1)} %log_add_fusion.refs_0_), channel_id=1, source_target_pairs={{0,24},{1,25},{2,26},{3,27},{4,28},{5,29},{6,30},{7,31},{8,16},{9,... | collective-permute-start | bytes 36872 | tf_op jit(solution)/shard_map/ppermute | solution.py:190
  75.5 2.7 %last_iteration.1 = (bf16[256,1024]{1,0:T(8,128)(2,1)}, f32[768]{0:T(1024)}) custom-call(bf16[256,1024]{1,0:T(8,128)(2,1)S(1)} %get-tuple-element.21.old_ref, f32[4,256,768]{2,1,0:T(8,128)S(1)} %get-tuple-element.22.expo_ref, f32[4,768]{1,0:T(4,128)S(1)} %get-tuple-element.23.peak_ref, f32[4,768]{1,0:T(4,128)S(1)} %log_add_fusion.refs_0_, ...), custom_call_target="tpu_custom_call" | custom-call | flops 1610612736 | bytes 524288 | tf_op jit(solution)/shard_map/last_iteration/pallas_call | solution.py:295
  (51 shorter events, 11.9 us)
Async XLA Ops:
  1.8 12.9 %collective-permute-start.11 = (bf16[192,1024]{1,0:T(8,128)(2,1)S(1)}, bf16[192,1024]{1,0:T(8,128)(2,1)S(1)}, u32[]{:S(2)}, u32[]{:S(2)}) collective-permute-start(bf16[192,1024]{1,0:T(8,128)(2,1)S(1)} %get-tuple-element.26), channel_id=1, source_target_pairs={{0,8},{1,9},{2,10},{3,11},{4,12},{5,13},{6,14},{7,15},{8,0},{9,1},... | collective-permute-start | bytes 1179656 | tf_op jit(solution)/shard_map/ppermute | solution.py:190
  4.8 15.1 %collective-permute-start.1 = (bf16[192,1024]{1,0:T(8,128)(2,1)S(1)}, bf16[192,1024]{1,0:T(8,128)(2,1)S(1)}, u32[]{:S(2)}, u32[]{:S(2)}) collective-permute-start(bf16[192,1024]{1,0:T(8,128)(2,1)S(1)} %get-tuple-element.26), channel_id=1, source_target_pairs={{0,16},{1,17},{2,18},{3,19},{4,20},{5,21},{6,22},{7,23},{8,24},{9,... | collective-permute-start | bytes 1179656 | tf_op jit(solution)/shard_map/ppermute | solution.py:190
  6.3 16.0 %collective-permute-start = (bf16[192,1024]{1,0:T(8,128)(2,1)S(1)}, bf16[192,1024]{1,0:T(8,128)(2,1)S(1)}, u32[]{:S(2)}, u32[]{:S(2)}) collective-permute-start(bf16[192,1024]{1,0:T(8,128)(2,1)S(1)} %get-tuple-element.27), channel_id=1, source_target_pairs={{0,8},{1,9},{2,10},{3,11},{4,12},{5,13},{6,14},{7,15},{8,0},{9,1},... | collective-permute-start | bytes 1179656 | tf_op jit(solution)/shard_map/ppermute | solution.py:190
  6.9 30.1 %collective-permute-start.15 = (bf16[192,1024]{1,0:T(8,128)(2,1)S(1)}, bf16[192,1024]{1,0:T(8,128)(2,1)S(1)}, u32[]{:S(2)}, u32[]{:S(2)}) collective-permute-start(bf16[192,1024]{1,0:T(8,128)(2,1)S(1)} %get-tuple-element.27), channel_id=1, source_target_pairs={{0,16},{1,17},{2,18},{3,19},{4,20},{5,21},{6,22},{7,23},{8,24},{9,... | collective-permute-start | bytes 1179656 | tf_op jit(solution)/shard_map/ppermute | solution.py:190
  14.8 31.2 %collective-permute-start.12 = (bf16[192,1024]{1,0:T(8,128)(2,1)S(1)}, bf16[192,1024]{1,0:T(8,128)(2,1)S(1)}, u32[]{:S(2)}, u32[]{:S(2)}) collective-permute-start(bf16[192,1024]{1,0:T(8,128)(2,1)S(1)} %collective-permute-done.11.refs_4_), channel_id=1, source_target_pairs={{0,1},{1,0},{2,3},{3,2},{4,5},{5,4},{6,7},{7,6},{8,9},{9,8},{10,11... | collective-permute-start | bytes 1179656 | tf_op jit(solution)/shard_map/ppermute | solution.py:190
  22.4 4.8 %collective-permute-start.8 = (f32[1,768]{1,0:T(1,128)S(1)}, f32[1,768]{1,0:T(1,128)S(1)}, u32[]{:S(2)}, u32[]{:S(2)}) collective-permute-start(f32[1,768]{1,0:T(1,128)S(1)} %partial_lse.1), channel_id=1, source_target_pairs={{0,7},{1,6},{2,5},{3,4},{4,3},{5,2},{6,1},{7,0},{8,15},{9,14},{10,... | collective-permute-start | bytes 9224 | tf_op jit(solution)/shard_map/ppermute | solution.py:190
  24.8 5.4 %collective-permute-start.7 = (f32[1,768]{1,0:T(1,128)S(1)}, f32[1,768]{1,0:T(1,128)S(1)}, u32[]{:S(2)}, u32[]{:S(2)}) collective-permute-start(f32[1,768]{1,0:T(1,128)S(1)} %partial_lse.1), channel_id=1, source_target_pairs={{0,6},{1,7},{2,4},{3,5},{4,2},{5,3},{6,0},{7,1},{8,14},{9,15},{10,... | collective-permute-start | bytes 9224 | tf_op jit(solution)/shard_map/ppermute | solution.py:190
  26.2 4.0 %collective-permute-start.6 = (f32[1,768]{1,0:T(1,128)S(1)}, f32[1,768]{1,0:T(1,128)S(1)}, u32[]{:S(2)}, u32[]{:S(2)}) collective-permute-start(f32[1,768]{1,0:T(1,128)S(1)} %partial_lse.1), channel_id=1, source_target_pairs={{0,5},{1,4},{2,7},{3,6},{4,1},{5,0},{6,3},{7,2},{8,13},{9,12},{10,... | collective-permute-start | bytes 9224 | tf_op jit(solution)/shard_map/ppermute | solution.py:190
  27.2 5.0 %collective-permute-start.5 = (f32[1,768]{1,0:T(1,128)S(1)}, f32[1,768]{1,0:T(1,128)S(1)}, u32[]{:S(2)}, u32[]{:S(2)}) collective-permute-start(f32[1,768]{1,0:T(1,128)S(1)} %partial_lse.1), channel_id=1, source_target_pairs={{0,4},{1,5},{2,6},{3,7},{4,0},{5,1},{6,2},{7,3},{8,12},{9,13},{10,... | collective-permute-start | bytes 9224 | tf_op jit(solution)/shard_map/ppermute | solution.py:190
  30.2 4.6 %collective-permute-start.3 = (f32[1,768]{1,0:T(1,128)S(1)}, f32[1,768]{1,0:T(1,128)S(1)}, u32[]{:S(2)}, u32[]{:S(2)}) collective-permute-start(f32[1,768]{1,0:T(1,128)S(1)} %partial_lse.1), channel_id=1, source_target_pairs={{0,2},{1,3},{2,0},{3,1},{4,6},{5,7},{6,4},{7,5},{8,10},{9,11},{10,... | collective-permute-start | bytes 9224 | tf_op jit(solution)/shard_map/ppermute | solution.py:190
  32.2 4.1 %collective-permute-start.2 = (f32[1,768]{1,0:T(1,128)S(1)}, f32[1,768]{1,0:T(1,128)S(1)}, u32[]{:S(2)}, u32[]{:S(2)}) collective-permute-start(f32[1,768]{1,0:T(1,128)S(1)} %partial_lse.1), channel_id=1, source_target_pairs={{0,1},{1,0},{2,3},{3,2},{4,5},{5,4},{6,7},{7,6},{8,9},{9,8},{10,11... | collective-permute-start | bytes 9224 | tf_op jit(solution)/shard_map/ppermute | solution.py:190
  33.2 13.2 %collective-permute-start.20 = (bf16[192,1024]{1,0:T(8,128)(2,1)S(1)}, bf16[192,1024]{1,0:T(8,128)(2,1)S(1)}, u32[]{:S(2)}, u32[]{:S(2)}) collective-permute-start(bf16[192,1024]{1,0:T(8,128)(2,1)S(1)} %collective-permute-done.refs_6_), channel_id=1, source_target_pairs={{0,16},{1,17},{2,18},{3,19},{4,20},{5,21},{6,22},{7,23},{8,24},{9,... | collective-permute-start | bytes 1179656 | tf_op jit(solution)/shard_map/ppermute | solution.py:190
  34.8 11.7 %collective-permute-start.18 = (bf16[192,1024]{1,0:T(8,128)(2,1)S(1)}, bf16[192,1024]{1,0:T(8,128)(2,1)S(1)}, u32[]{:S(2)}, u32[]{:S(2)}) collective-permute-start(bf16[192,1024]{1,0:T(8,128)(2,1)S(1)} %collective-permute-done.1.refs_8_), channel_id=1, source_target_pairs={{0,8},{1,9},{2,10},{3,11},{4,12},{5,13},{6,14},{7,15},{8,0},{9,1},... | collective-permute-start | bytes 1179656 | tf_op jit(solution)/shard_map/ppermute | solution.py:190
  36.3 8.4 %collective-permute-start.10 = (f32[1,768]{1,0:T(1,128)S(1)}, f32[1,768]{1,0:T(1,128)S(1)}, u32[]{:S(2)}, u32[]{:S(2)}) collective-permute-start(f32[1,768]{1,0:T(1,128)S(1)} %log_add_fusion.1.refs_0_), channel_id=1, source_target_pairs={{0,16},{1,17},{2,18},{3,19},{4,20},{5,21},{6,22},{7,23},{8,24},{9,... | collective-permute-start | bytes 9224 | tf_op jit(solution)/shard_map/ppermute | solution.py:190
  37.0 9.0 %collective-permute-start.9 = (f32[1,768]{1,0:T(1,128)S(1)}, f32[1,768]{1,0:T(1,128)S(1)}, u32[]{:S(2)}, u32[]{:S(2)}) collective-permute-start(f32[1,768]{1,0:T(1,128)S(1)} %log_add_fusion.1.refs_0_), channel_id=1, source_target_pairs={{0,8},{1,9},{2,10},{3,11},{4,12},{5,13},{6,14},{7,15},{8,0},{9,1},... | collective-permute-start | bytes 9224 | tf_op jit(solution)/shard_map/ppermute | solution.py:190
  46.4 8.3 %collective-permute-start.21 = (bf16[192,1024]{1,0:T(8,128)(2,1)S(1)}, bf16[192,1024]{1,0:T(8,128)(2,1)S(1)}, u32[]{:S(2)}, u32[]{:S(2)}) collective-permute-start(bf16[192,1024]{1,0:T(8,128)(2,1)S(1)} %collective-permute-done.20.refs_3_), channel_id=1, source_target_pairs={{0,1},{1,0},{2,3},{3,2},{4,5},{5,4},{6,7},{7,6},{8,9},{9,8},{10,11... | collective-permute-start | bytes 1179656 | tf_op jit(solution)/shard_map/ppermute | solution.py:190
  46.5 8.3 %collective-permute-start.19 = (bf16[192,1024]{1,0:T(8,128)(2,1)S(1)}, bf16[192,1024]{1,0:T(8,128)(2,1)S(1)}, u32[]{:S(2)}, u32[]{:S(2)}) collective-permute-start(bf16[192,1024]{1,0:T(8,128)(2,1)S(1)} %collective-permute-done.18.refs_1_), channel_id=1, source_target_pairs={{0,1},{1,0},{2,3},{3,2},{4,5},{5,4},{6,7},{7,6},{8,9},{9,8},{10,11... | collective-permute-start | bytes 1179656 | tf_op jit(solution)/shard_map/ppermute | solution.py:190
  47.0 7.8 %collective-permute-start.17 = (f32[1,768]{1,0:T(1,128)S(1)}, f32[1,768]{1,0:T(1,128)S(1)}, u32[]{:S(2)}, u32[]{:S(2)}) collective-permute-start(f32[1,768]{1,0:T(1,128)S(1)} %log_add_fusion.1.refs_0_), channel_id=1, source_target_pairs={{0,24},{1,25},{2,26},{3,27},{4,28},{5,29},{6,30},{7,31},{8,16},{9,... | collective-permute-start | bytes 9224 | tf_op jit(solution)/shard_map/ppermute | solution.py:190
  59.3 6.3 %collective-permute-start.28 = (f32[4,768]{1,0:T(4,128)S(1)}, f32[4,768]{1,0:T(4,128)S(1)}, u32[]{:S(2)}, u32[]{:S(2)}) collective-permute-start(f32[4,768]{1,0:T(4,128)S(1)} %get-tuple-element.24), channel_id=1, source_target_pairs={{0,7},{1,6},{2,5},{3,4},{4,3},{5,2},{6,1},{7,0},{8,15},{9,14},{10,... | collective-permute-start | bytes 36872 | tf_op jit(solution)/shard_map/ppermute | solution.py:190
  61.3 5.8 %collective-permute-start.27 = (f32[4,768]{1,0:T(4,128)S(1)}, f32[4,768]{1,0:T(4,128)S(1)}, u32[]{:S(2)}, u32[]{:S(2)}) collective-permute-start(f32[4,768]{1,0:T(4,128)S(1)} %get-tuple-element.24), channel_id=1, source_target_pairs={{0,6},{1,7},{2,4},{3,5},{4,2},{5,3},{6,0},{7,1},{8,14},{9,15},{10,... | collective-permute-start | bytes 36872 | tf_op jit(solution)/shard_map/ppermute | solution.py:190
  62.6 4.8 %collective-permute-start.26 = (f32[4,768]{1,0:T(4,128)S(1)}, f32[4,768]{1,0:T(4,128)S(1)}, u32[]{:S(2)}, u32[]{:S(2)}) collective-permute-start(f32[4,768]{1,0:T(4,128)S(1)} %get-tuple-element.24), channel_id=1, source_target_pairs={{0,5},{1,4},{2,7},{3,6},{4,1},{5,0},{6,3},{7,2},{8,13},{9,12},{10,... | collective-permute-start | bytes 36872 | tf_op jit(solution)/shard_map/ppermute | solution.py:190
  62.6 4.8 %collective-permute-start.25 = (f32[4,768]{1,0:T(4,128)S(1)}, f32[4,768]{1,0:T(4,128)S(1)}, u32[]{:S(2)}, u32[]{:S(2)}) collective-permute-start(f32[4,768]{1,0:T(4,128)S(1)} %get-tuple-element.24), channel_id=1, source_target_pairs={{0,4},{1,5},{2,6},{3,7},{4,0},{5,1},{6,2},{7,3},{8,12},{9,13},{10,... | collective-permute-start | bytes 36872 | tf_op jit(solution)/shard_map/ppermute | solution.py:190
  65.6 3.7 %collective-permute-start.23 = (f32[4,768]{1,0:T(4,128)S(1)}, f32[4,768]{1,0:T(4,128)S(1)}, u32[]{:S(2)}, u32[]{:S(2)}) collective-permute-start(f32[4,768]{1,0:T(4,128)S(1)} %get-tuple-element.24), channel_id=1, source_target_pairs={{0,2},{1,3},{2,0},{3,1},{4,6},{5,7},{6,4},{7,5},{8,10},{9,11},{10,... | collective-permute-start | bytes 36872 | tf_op jit(solution)/shard_map/ppermute | solution.py:190
  69.3 4.7 %collective-permute-start.31 = (f32[4,768]{1,0:T(4,128)S(1)}, f32[4,768]{1,0:T(4,128)S(1)}, u32[]{:S(2)}, u32[]{:S(2)}) collective-permute-start(f32[4,768]{1,0:T(4,128)S(1)} %log_add_fusion.refs_0_), channel_id=1, source_target_pairs={{0,24},{1,25},{2,26},{3,27},{4,28},{5,29},{6,30},{7,31},{8,16},{9,... | collective-permute-start | bytes 36872 | tf_op jit(solution)/shard_map/ppermute | solution.py:190
  (10 other events, 109.0 us)

commit v3 on v2

--- a/solution.py
+++ b/solution.py
@@ -102,9 +102,19 @@
     return ((total + old.astype(jnp.float32)) / (mass + 1.0)).astype(jnp.bfloat16)
 
 
-def open_kernel(plan, scale, c_ref, *refs):
+def index_of(plan, place):
+    return lax.axis_index("item") ^ place if plan["exchange"] else place
+
+
+def row_lse(plan, parts, place):
+    cents = plan["cents"]
+    rows = parts[pl.ds(pl.multiple_of(index_of(plan, place) * cents, cents), cents), :]
+    peak = jnp.max(rows, axis=0, keepdims=True)
+    return peak + jnp.log(jnp.sum(jnp.exp(rows - peak), axis=0, keepdims=True))
+
+
+def open_kernel(plan, scale, c_ref, parts, *refs):
     nv, blocks = plan["nv"], plan["early"]
-    lse, refs = refs[: len(blocks)], refs[len(blocks) :]
     pieces, refs = refs[: plan["n_early"]], refs[plan["n_early"] :]
     table, own, total, mass, sems, own_sem = refs
     rows = own.shape[0]
@@ -120,15 +130,14 @@
         for copy in block:
             copy.wait()
         vectors = table[pl.ds(place * nv, nv), :]
-        resp = jnp.exp(scores(own[...], vectors, scale) - lse[place][...]).astype(jnp.bfloat16)
+        resp = jnp.exp(scores(own[...], vectors, scale) - row_lse(plan, parts, place)).astype(jnp.bfloat16)
         term, weight = weigh(resp, vectors)
         total[...] = term if place == 0 else total[...] + term
         mass[...] = weight if place == 0 else mass[...] + weight
 
 
-def close_kernel(plan, scale, early, own, total, mass, *refs):
+def close_kernel(plan, scale, early, own, total, mass, parts, *refs):
     nv, blocks, first = plan["nv"], plan["late"], len(plan["early"])
-    lse, refs = refs[: len(blocks)], refs[len(blocks) :]
     pieces, refs = refs[: plan["n_late"]], refs[plan["n_late"] :]
     new_ref, expo_ref, peak_ref, part_ref = refs[:4]
     late = sems = None
@@ -143,7 +152,7 @@
             for copy in block:
                 copy.wait()
             vectors = late[pl.ds(place * nv, nv), :]
-            resp = jnp.exp(scores(own[...], vectors, scale) - lse[place][...]).astype(jnp.bfloat16)
+            resp = jnp.exp(scores(own[...], vectors, scale) - row_lse(plan, parts, first + place)).astype(jnp.bfloat16)
             term, weight = weigh(resp, vectors)
             sums, weights = sums + term, weights + weight
         new_ref[...] = updated(sums, weights, own[...])
@@ -156,30 +165,24 @@
         expo = jnp.exp(logits - peak)
         expo_ref[place] = expo
         peak_ref[pl.ds(place, 1), :] = peak
-        part_ref[pl.ds(place, 1), :] = peak + jnp.log(jnp.sum(expo, axis=0, keepdims=True))
-
-
-def last_kernel(plan, old_ref, expo_ref, peak_ref, *refs):
-    nv, n = plan["nv"], plan["n_parts"]
+        part_ref[pl.ds(index_of(plan, place), 1), :] = peak + jnp.log(jnp.sum(expo, axis=0, keepdims=True))
+
+
+def last_kernel(plan, old_ref, expo_ref, peak_ref, parts, *refs):
+    nv = plan["nv"]
     first, second = len(plan["early"]), len(plan["late"])
-    parts, refs = refs[:n], refs[n:]
     early, refs = refs[0], refs[1:]
     late = refs[0] if second else None
-    new_ref, norm_ref, total, mass = refs[1:] if second else refs
+    new_ref, norm_ref, lse_ref, total, mass = refs[1:] if second else refs
+    lse_ref[...] = merge([parts[i] for i in range(parts.shape[0])])
+    norm_ref[...] = lse_ref[pl.ds(lax.axis_index("item"), 1), :].reshape(nv)
     for place in range(first + second):
-        if n == 1:
-            lse = parts[0][pl.ds(place, 1), :]
-        else:
-            lse = merge([parts[k][pl.ds(place ^ k, 1), :] for k in range(n)])
-        if plan["n_parts"] > 1 and place == 0:
-            norm_ref[...] = lse.reshape(nv)
+        lse = lse_ref[pl.ds(index_of(plan, place), 1), :]
         vectors = early[pl.ds(place * nv, nv), :] if place < first else late[pl.ds((place - first) * nv, nv), :]
         factor = jnp.exp(peak_ref[pl.ds(place, 1), :] - lse)
         term, weight = weigh((expo_ref[place] * factor).astype(jnp.bfloat16), vectors)
         total[...] = term if place == 0 else total[...] + term
         mass[...] = weight if place == 0 else mass[...] + weight
-    if n == 1:
-        norm_ref[...] = parts[0][pl.ds(lax.axis_index("item"), 1), :].reshape(nv)
     new_ref[...] = updated(total[...], mass[...], old_ref[...])
 
 
@@ -188,6 +191,11 @@
         (i * cents + c, (i ^ item_mask) * cents + (c ^ cent_mask)) for i in range(items) for c in range(cents)
     ]
     return lax.ppermute(value, BOTH, pairs)
+
+
+def everyone(value, axes):
+    n = lax.axis_size(axes)
+    return lax.all_to_all(jnp.broadcast_to(value, (n,) + value.shape), axes, 0, 0, tiled=True)
 
 
 def shards(vectors, centroids):
@@ -204,9 +212,8 @@
         x1, y0 = go(q[1], item_mask=1, cent_mask=0), go(q[0], item_mask=2, cent_mask=0)
         x0, y1 = go(q[0], item_mask=1, cent_mask=0), go(q[1], item_mask=2, cent_mask=0)
         part = partial(vectors, centroids, scale)
-        x1, y0, part = lax.optimization_barrier((x1, y0, part))
-        lse = merge([part] + [go(part, item_mask=0, cent_mask=k) for k in range(1, cents)])
-        lses = [lse] + [go(lse, item_mask=k, cent_mask=0) for k in range(1, items)]
+        parts = everyone(part, BOTH).reshape(items * cents, nv)
+        x0, x1, y0, y1 = [lax.optimization_barrier((piece, parts))[0] for piece in (x0, x1, y0, y1)]
         d0, d1 = go(y0, item_mask=1, cent_mask=0), go(x1, item_mask=2, cent_mask=0)
 
         def pieces_of(pairs, at):
@@ -229,10 +236,8 @@
         early_blocks = [[(0, i * nv, None, 0, nv)] for i in range(items)]
         late, late_blocks = [], []
         part = partial(vectors, centroids, scale)
-        parts = lax.all_gather(part, "cent", axis=0, tiled=False)
-        lse = lax.all_gather(merge([parts[i] for i in range(cents)]), "item", axis=0, tiled=False)
-        lses = [lse[i] for i in range(items)]
-    plan = dict(nv=nv, early=early_blocks, late=late_blocks, n_early=len(early), n_late=len(late))
+        parts = lax.all_gather(part, BOTH, axis=0, tiled=True)
+    plan = dict(nv=nv, cents=cents, exchange=small, early=early_blocks, late=late_blocks, n_early=len(early), n_late=len(late))
 
     any_spec = pl.BlockSpec(memory_space=pl.ANY)
     vmem = pl.BlockSpec(memory_space=pltpu.VMEM)
@@ -241,7 +246,7 @@
     params = pltpu.CompilerParams(vmem_limit_bytes=20 * MIB)
     table, own, total, mass = pl.pallas_call(
         functools.partial(open_kernel, plan, scale),
-        in_specs=[any_spec] + [vmem] * n_early + [any_spec] * len(early),
+        in_specs=[any_spec, vmem] + [any_spec] * len(early),
         out_specs=[vmem] * 4,
         out_shape=[
             pltpu.VMEM((n_early * nv, dim), jnp.bfloat16),
@@ -258,13 +263,13 @@
             flops=2 * n_early * flops, bytes_accessed=2 * n_early * nv * dim, transcendentals=n_early * nv * rows
         ),
         name="early_blocks",
-    )(centroids, *lses[:n_early], *early)
+    )(centroids, parts, *early)
 
     late_out = [pltpu.VMEM((n_late * nv, dim), jnp.bfloat16)] if n_late else []
     late_sems = [pltpu.SemaphoreType.DMA((max(len(b) for b in late_blocks), n_late))] if n_late else []
     fresh, expo, peak, part, *tables = pl.pallas_call(
         functools.partial(close_kernel, plan, scale),
-        in_specs=[vmem] * (4 + n_late) + [any_spec] * len(late),
+        in_specs=[vmem] * 5 + [any_spec] * len(late),
         out_specs=[vmem] * (4 + len(late_out)),
         out_shape=[
             pltpu.VMEM((rows, dim), jnp.bfloat16),
@@ -281,30 +286,31 @@
             transcendentals=(items + n_late) * nv * rows,
         ),
         name="late_blocks",
-    )(in_vmem(table), in_vmem(own), in_vmem(total), in_vmem(mass), *lses[n_early:], *late)
+    )(in_vmem(table), in_vmem(own), in_vmem(total), in_vmem(mass), parts, *late)
 
     if small:
-        lse = merge([part] + [go(part, item_mask=0, cent_mask=k) for k in range(1, cents)])
-        parts = [lse] + [go(lse, item_mask=k, cent_mask=0) for k in range(1, items)]
+        gathered = everyone(part, "cent")
+        parts = everyone(merge([gathered[i] for i in range(cents)]), "item")
     else:
         gathered = lax.all_gather(part, "cent", axis=0, tiled=False)
-        lse = merge([gathered[i] for i in range(cents)])
-        gathered = lax.all_gather(lse, "item", axis=0, tiled=False)
-        parts = [merge([gathered[i] for i in range(items)])]
-    plan["n_parts"] = len(parts)
+        parts = lax.all_gather(merge([gathered[i] for i in range(cents)]), "item", axis=0, tiled=False)
     result, norm = pl.pallas_call(
         functools.partial(last_kernel, plan),
-        in_specs=[vmem] * (4 + len(parts) + len(tables)),
+        in_specs=[vmem] * (5 + len(tables)),
         out_specs=[vmem] * 2,
         out_shape=[
             jax.ShapeDtypeStruct((rows, dim), jnp.bfloat16),
             jax.ShapeDtypeStruct((nv,), jnp.float32),
         ],
-        scratch_shapes=[pltpu.VMEM((rows, dim), jnp.float32), pltpu.VMEM((rows, 1), jnp.float32)],
+        scratch_shapes=[
+            pltpu.VMEM((items, nv), jnp.float32),
+            pltpu.VMEM((rows, dim), jnp.float32),
+            pltpu.VMEM((rows, 1), jnp.float32),
+        ],
         compiler_params=params,
         cost_estimate=pl.CostEstimate(flops=items * flops, bytes_accessed=2 * rows * dim, transcendentals=0),
         name="last_iteration",
-    )(in_vmem(fresh), in_vmem(expo), in_vmem(peak), *parts, in_vmem(table), *[in_vmem(t) for t in tables])
+    )(in_vmem(fresh), in_vmem(expo), in_vmem(peak), parts, in_vmem(table), *[in_vmem(t) for t in tables])
     return (result, norm)
 
 

time: 78.4 us -> 79.4 us (1.013)
  blocking collectives: 0 us -> 18.5 us
  starting transfers between devices: 31.9 us -> 15.3 us
  waiting for transfers between devices: 26 us -> 21.9 us
  local copies, waits for them, and re-layouts: 1.18 us -> 4.37 us
    ppermute x32 -> x12, starting transfers between devices: 31.9 us -> 10.4 us  [send(): return lax.ppermute(value, BOTH, pairs)]
    all_to_all x0 -> x2, blocking collectives: none -> 18.5 us  [everyone(): lax.all_to_all(jnp.broadcast_to(value, (n,) + value.shape), axes, 0, 0, t...]
    ppermute x32 -> x12, waiting for transfers between devices: 26 us -> 17.9 us  [send(): return lax.ppermute(value, BOTH, pairs)]
    all_to_all x0 -> x1, starting transfers between devices: none -> 4.89 us  [everyone(): lax.all_to_all(jnp.broadcast_to(value, (n,) + value.shape), axes, 0, 0, t...]
    all_to_all x0 -> x1, waiting for transfers between devices: none -> 4.02 us  [everyone(): lax.all_to_all(jnp.broadcast_to(value, (n,) + value.shape), axes, 0, 0, t...]
    unnamed x4 -> x5, local copies, waits for them, and re-layouts: 0.01 us -> 1.6 us
    dynamic_slice x1, local copies, waits for them, and re-layouts: 1.17 us -> 2.06 us  [shards(): lax.dynamic_slice_in_dim(vectors, core * (nv // 2) + s * quarter, quarter...]
  transfers between devices with their start and end apart: 32 -> 13, of which waited for: 12 -> 5; matrix products, arithmetic and copies ran while one was open for 0% -> 1% of each run, Pallas kernels for 14% -> 14%
where the time goes in v3:
time: 79.4 us; the launch traced here: 79.1 us
  waiting for transfers between devices  21.9 us (28%)
  blocking collectives  18.5 us (23%)
  Pallas kernels  18.2 us (23%)
  starting transfers between devices  15.3 us (19%)
  local copies, waits for them, and re-layouts  4.37 us (6%)
    all_to_all x2, blocking collectives, everyone(): lax.all_to_all(jnp.broadcast_to(value, (n,) + value.shape), axes, 0, 0, t...  18.5 us
    ppermute x12, waiting for transfers between devices, send(): return lax.ppermute(value, BOTH, pairs)  17.9 us
    ppermute x12, starting transfers between devices, send(): return lax.ppermute(value, BOTH, pairs)  10.4 us
    pallas_call x1, Pallas kernels, shards(): pl.pallas_call(functools.partial(open_kernel, plan, scale), in_specs=[any...  5.81 us
    pallas_call x1, Pallas kernels, partial(): pl.pallas_call(functools.partial(partial_kernel, scale), grid=(k // rows,...  5.18 us
    all_to_all x1, starting transfers between devices, everyone(): lax.all_to_all(jnp.broadcast_to(value, (n,) + value.shape), axes, 0, 0, t...  4.89 us
    pallas_call x1, Pallas kernels, shards(): pl.pallas_call(functools.partial(close_kernel, plan, scale), in_specs=[vm...  4.43 us
    all_to_all x1, waiting for transfers between devices, everyone(): lax.all_to_all(jnp.broadcast_to(value, (n,) + value.shape), axes, 0, 0, t...  4.02 us
  transfers between devices with their start and end apart: 13, of which 5 were waited for; matrix products, arithmetic and copies ran while one was open for 1% of the time, Pallas kernels for 14%

profile of v3, /device:TPU:0, one launch (start us, length us, event | category | flops | bytes accessed | tf_op | source)
XLA Modules:
  0.0 79.1 jit_solution(15831727737827968098)
XLA Ops:
  0.6 2.1 %constant_dynamic-slice_fusion = (bf16[192,1024]{1,0:T(8,128)(2,1)}, bf16[192,1024]{1,0:T(8,128)(2,1)}) fusion(bf16[768,1024]{1,0:T(8,128)(2,1)} %refs_0_.1, s32[]{:T(128)S(6)} %select_n.7, s32[]{:T(128)S(6)} %select_n.6), kind=kLoop, calls=%fused_computation.10 | loop fusion | bytes 1572872 | tf_op jit(solution)/shard_map/dynamic_slice | solution.py:211
  2.7 3.0 %collective-permute-start.6 = (bf16[192,1024]{1,0:T(8,128)(2,1)}, bf16[192,1024]{1,0:T(8,128)(2,1)S(1)}, u32[]{:S(2)}, u32[]{:S(2)}) collective-permute-start(bf16[192,1024]{1,0:T(8,128)(2,1)} %get-tuple-element.28), channel_id=1, source_target_pairs={{0,16},{1,17},{2,18},{3,19},{4,20},{5,21},{6,22},{7,23},{8,24},{9,... | collective-permute-start | bytes 1179656 | tf_op jit(solution)/shard_map/ppermute | solution.py:193
  5.7 5.2 %partial_lse.1 = f32[1,768]{1,0:T(1,128)S(1)} custom-call(bf16[768,1024]{1,0:T(8,128)(2,1)} %refs_0_.1, bf16[1024,1024]{1,0:T(8,128)(2,1)} %c_ref.3), custom_call_target="tpu_custom_call" | custom-call | flops 1610612736 | bytes 3670016 | tf_op jit(solution)/shard_map/partial_lse/pallas_call | solution.py:64
  10.9 0.7 broadcast_in_dim.9
  11.6 4.9 %all-to-all-start = ((f32[32,1,768]{2,1,0:T(1,128)}), f32[32,1,768]{2,1,0:T(1,128)S(1)}, u32[]{:S(2)}, u32[]{:S(2)}) async-start(f32[32,1,768]{2,1,0:T(1,128)} %broadcast_in_dim.9), calls=%async_computation | async-start | bytes 196608 | tf_op jit(solution)/shard_map/all_to_all | solution.py:198
  16.5 1.8 %collective-permute-start.2 = (bf16[192,1024]{1,0:T(8,128)(2,1)}, bf16[192,1024]{1,0:T(8,128)(2,1)S(1)}, u32[]{:S(2)}, u32[]{:S(2)}) collective-permute-start(bf16[192,1024]{1,0:T(8,128)(2,1)} %get-tuple-element.28), channel_id=1, source_target_pairs={{0,8},{1,9},{2,10},{3,11},{4,12},{5,13},{6,14},{7,15},{8,0},{9,1},... | collective-permute-start | bytes 1179656 | tf_op jit(solution)/shard_map/ppermute | solution.py:193
  18.3 1.5 %collective-permute-start.4 = (bf16[192,1024]{1,0:T(8,128)(2,1)}, bf16[192,1024]{1,0:T(8,128)(2,1)S(1)}, u32[]{:S(2)}, u32[]{:S(2)}) collective-permute-start(bf16[192,1024]{1,0:T(8,128)(2,1)} %get-tuple-element.29), channel_id=1, source_target_pairs={{0,16},{1,17},{2,18},{3,19},{4,20},{5,21},{6,22},{7,23},{8,24},{9,... | collective-permute-start | bytes 1179656 | tf_op jit(solution)/shard_map/ppermute | solution.py:193
  19.8 0.6 collective-permute-start
  20.3 4.0 %all-to-all-done = f32[32,1,768]{2,1,0:T(1,128)S(1)} async-done(((f32[32,1,768]{2,1,0:T(1,128)}), f32[32,1,768]{2,1,0:T(1,128)S(1)}, u32[]{:S(2)}, u32[]{:S(2)}) %all-to-all-start) | async-done | bytes 98336 | tf_op jit(solution)/shard_map/all_to_all | solution.py:198
  24.4 0.1 collective-permute-start.7
  24.5 4.9 %collective-permute-done.2.refs_3_ = bf16[192,1024]{1,0:T(8,128)(2,1)S(1)} collective-permute-done((bf16[192,1024]{1,0:T(8,128)(2,1)}, bf16[192,1024]{1,0:T(8,128)(2,1)S(1)}, u32[]{:S(2)}, u32[]{:S(2)}) %collective-permute-start.2) | collective-permute-done | bytes 393248 | tf_op jit(solution)/shard_map/ppermute | solution.py:193
  29.5 1.7 %collective-permute-start.10 = (bf16[192,1024]{1,0:T(8,128)(2,1)S(1)}, bf16[192,1024]{1,0:T(8,128)(2,1)S(1)}, u32[]{:S(2)}, u32[]{:S(2)}) collective-permute-start(bf16[192,1024]{1,0:T(8,128)(2,1)S(1)} %collective-permute-done.2.refs_3_), channel_id=1, source_target_pairs={{0,16},{1,17},{2,18},{3,19},{4,20},{5,21},{6,22},{7,23},{8,24},{9,... | collective-permute-start | bytes 1179656 | tf_op jit(solution)/shard_map/ppermute | solution.py:193
  31.1 1.2 %collective-permute-start.8 = (bf16[192,1024]{1,0:T(8,128)(2,1)S(1)}, bf16[192,1024]{1,0:T(8,128)(2,1)S(1)}, u32[]{:S(2)}, u32[]{:S(2)}) collective-permute-start(bf16[192,1024]{1,0:T(8,128)(2,1)S(1)} %collective-permute-done.4.refs_5_), channel_id=1, source_target_pairs={{0,8},{1,9},{2,10},{3,11},{4,12},{5,13},{6,14},{7,15},{8,0},{9,1},... | collective-permute-start | bytes 1179656 | tf_op jit(solution)/shard_map/ppermute | solution.py:193
  32.4 5.5 %collective-permute-done.refs_1_ = bf16[192,1024]{1,0:T(8,128)(2,1)S(1)} collective-permute-done((bf16[192,1024]{1,0:T(8,128)(2,1)}, bf16[192,1024]{1,0:T(8,128)(2,1)S(1)}, u32[]{:S(2)}, u32[]{:S(2)}) %collective-permute-start) | collective-permute-done | bytes 393248 | tf_op jit(solution)/shard_map/ppermute | solution.py:193
  37.9 0.5 collective-permute-start.1
  38.4 1.1 %collective-permute-done.10.refs_2_ = bf16[192,1024]{1,0:T(8,128)(2,1)S(1)} collective-permute-done((bf16[192,1024]{1,0:T(8,128)(2,1)S(1)}, bf16[192,1024]{1,0:T(8,128)(2,1)S(1)}, u32[]{:S(2)}, u32[]{:S(2)}) %collective-permute-start.10) | collective-permute-done | bytes 393248 | tf_op jit(solution)/shard_map/ppermute | solution.py:193
  39.5 6.3 %collective-permute-done.8.refs_0_ = bf16[192,1024]{1,0:T(8,128)(2,1)S(1)} collective-permute-done((bf16[192,1024]{1,0:T(8,128)(2,1)S(1)}, bf16[192,1024]{1,0:T(8,128)(2,1)S(1)}, u32[]{:S(2)}, u32[]{:S(2)}) %collective-permute-start.8) | collective-permute-done | bytes 393248 | tf_op jit(solution)/shard_map/ppermute | solution.py:193
  45.8 1.6 %copy-done.1 = bf16[1024,1024]{1,0:T(8,128)(2,1)S(1)} copy-done((bf16[1024,1024]{1,0:T(8,128)(2,1)S(1)}, bf16[1024,1024]{1,0:T(8,128)(2,1)}, u32[]{:S(2)}) %copy-start.1) | copy-done | bytes 2097176
  47.4 5.8 %early_blocks.1 = (bf16[2304,1024]{1,0:T(8,128)(2,1)S(1)}, bf16[256,1024]{1,0:T(8,128)(2,1)S(1)}, f32[256,1024]{1,0:T(8,128)S(1)}, f32[256,1]{1,0:T(8,128)S(1)}) custom-call(bf16[1024,1024]{1,0:T(8,128)(2,1)S(1)} %copy-done.1, f32[32,768]{1,0:T(8,128)S(1)} %bitcast.35, bf16[768,1024]{1,0:T(8,128)(2,1)S(1)} %copy-done, ...), custom_call_target="tpu_custom_call" | custom-call | flops 2415919104 | bytes 4718592 | tf_op jit(solution)/shard_map/early_blocks/pallas_call | solution.py:247
  53.3 4.4 %late_blocks.1 = (bf16[256,1024]{1,0:T(8,128)(2,1)S(1)}, f32[4,256,768]{2,1,0:T(8,128)S(1)}, f32[4,768]{1,0:T(4,128)S(1)}, f32[4,768]{1,0:T(4,128)S(1)}, bf16[768,1024]{1,0:T(8,128)(2,1)S(1)}) custom-call(bf16[2304,1024]{1,0:T(8,128)(2,1)S(1)} %get-tuple-element.19.early.refs_0_, bf16[256,1024]{1,0:T(8,128)(2,1)S(1)} %get-tuple-element.20.own, ...), custom_call_target="tpu_custom_call" | custom-call | flops 2415919104 | bytes 1572864 | tf_op jit(solution)/shard_map/late_blocks/pallas_call | solution.py:270
  57.7 10.7 %all_to_all.15 = f32[8,4,768]{2,1,0:T(4,128)S(1)} all-to-all(f32[8,4,768]{2,1,0:T(4,128)S(1)} %broadcast_in_dim.10), channel_id=1, replica_groups=mesh['item'=4,'cent'=8] {'cent'}, dimensions={0} | all-to-all | bytes 196608 | tf_op jit(solution)/shard_map/all_to_all | solution.py:198
  68.5 0.1 log_add_fusion
  68.5 7.8 %all_to_all.16.parts = f32[4,4,768]{2,1,0:T(4,128)S(1)} all-to-all(f32[4,4,768]{2,1,0:T(4,128)S(1)} %broadcast_in_dim.11), channel_id=1, replica_groups=mesh['item'=4,'cent'=8] {'item'}, dimensions={0} | all-to-all | bytes 98304 | tf_op jit(solution)/shard_map/all_to_all | solution.py:198
  76.3 2.7 %last_iteration.1 = (bf16[256,1024]{1,0:T(8,128)(2,1)}, f32[768]{0:T(1024)}) custom-call(bf16[256,1024]{1,0:T(8,128)(2,1)S(1)} %get-tuple-element.23.old_ref, f32[4,256,768]{2,1,0:T(8,128)S(1)} %get-tuple-element.24.expo_ref, f32[4,768]{1,0:T(4,128)S(1)} %get-tuple-element.25.peak_ref, f32[4,4,768]{2,1,0:T(4,128)S(1)} %all_to_all.16.parts, ...), custom_call_target="tpu_custom_call" | custom-call | flops 1610612736 | bytes 524288 | tf_op jit(solution)/shard_map/last_iteration/pallas_call | solution.py:297
  (19 shorter events, 0.1 us)
Async XLA Ops:
  2.7 43.1 %copy-start = (bf16[768,1024]{1,0:T(8,128)(2,1)S(1)}, bf16[768,1024]{1,0:T(8,128)(2,1)}, u32[]{:S(2)}) copy-start(bf16[768,1024]{1,0:T(8,128)(2,1)} %refs_0_.1) | copy-start | bytes 4718596
  2.7 21.7 %collective-permute-start.6 = (bf16[192,1024]{1,0:T(8,128)(2,1)}, bf16[192,1024]{1,0:T(8,128)(2,1)S(1)}, u32[]{:S(2)}, u32[]{:S(2)}) collective-permute-start(bf16[192,1024]{1,0:T(8,128)(2,1)} %get-tuple-element.28), channel_id=1, source_target_pairs={{0,16},{1,17},{2,18},{3,19},{4,20},{5,21},{6,22},{7,23},{8,24},{9,... | collective-permute-start | bytes 1179656 | tf_op jit(solution)/shard_map/ppermute | solution.py:193
  11.6 12.8 %all-to-all-start = ((f32[32,1,768]{2,1,0:T(1,128)}), f32[32,1,768]{2,1,0:T(1,128)S(1)}, u32[]{:S(2)}, u32[]{:S(2)}) async-start(f32[32,1,768]{2,1,0:T(1,128)} %broadcast_in_dim.9), calls=%async_computation | async-start | bytes 196608 | tf_op jit(solution)/shard_map/all_to_all | solution.py:198
  16.5 13.0 %collective-permute-start.2 = (bf16[192,1024]{1,0:T(8,128)(2,1)}, bf16[192,1024]{1,0:T(8,128)(2,1)S(1)}, u32[]{:S(2)}, u32[]{:S(2)}) collective-permute-start(bf16[192,1024]{1,0:T(8,128)(2,1)} %get-tuple-element.28), channel_id=1, source_target_pairs={{0,8},{1,9},{2,10},{3,11},{4,12},{5,13},{6,14},{7,15},{8,0},{9,1},... | collective-permute-start | bytes 1179656 | tf_op jit(solution)/shard_map/ppermute | solution.py:193
  18.3 12.8 %collective-permute-start.4 = (bf16[192,1024]{1,0:T(8,128)(2,1)}, bf16[192,1024]{1,0:T(8,128)(2,1)S(1)}, u32[]{:S(2)}, u32[]{:S(2)}) collective-permute-start(bf16[192,1024]{1,0:T(8,128)(2,1)} %get-tuple-element.29), channel_id=1, source_target_pairs={{0,16},{1,17},{2,18},{3,19},{4,20},{5,21},{6,22},{7,23},{8,24},{9,... | collective-permute-start | bytes 1179656 | tf_op jit(solution)/shard_map/ppermute | solution.py:193
  19.8 18.1 %collective-permute-start = (bf16[192,1024]{1,0:T(8,128)(2,1)}, bf16[192,1024]{1,0:T(8,128)(2,1)S(1)}, u32[]{:S(2)}, u32[]{:S(2)}) collective-permute-start(bf16[192,1024]{1,0:T(8,128)(2,1)} %get-tuple-element.29), channel_id=1, source_target_pairs={{0,8},{1,9},{2,10},{3,11},{4,12},{5,13},{6,14},{7,15},{8,0},{9,1},... | collective-permute-start | bytes 1179656 | tf_op jit(solution)/shard_map/ppermute | solution.py:193
  24.4 13.5 %collective-permute-start.7 = (bf16[192,1024]{1,0:T(8,128)(2,1)S(1)}, bf16[192,1024]{1,0:T(8,128)(2,1)S(1)}, u32[]{:S(2)}, u32[]{:S(2)}) collective-permute-start(bf16[192,1024]{1,0:T(8,128)(2,1)S(1)} %collective-permute-done.6.refs_7_), channel_id=1, source_target_pairs={{0,1},{1,0},{2,3},{3,2},{4,5},{5,4},{6,7},{7,6},{8,9},{9,8},{10,11... | collective-permute-start | bytes 1179656 | tf_op jit(solution)/shard_map/ppermute | solution.py:193
  29.5 10.1 %collective-permute-start.10 = (bf16[192,1024]{1,0:T(8,128)(2,1)S(1)}, bf16[192,1024]{1,0:T(8,128)(2,1)S(1)}, u32[]{:S(2)}, u32[]{:S(2)}) collective-permute-start(bf16[192,1024]{1,0:T(8,128)(2,1)S(1)} %collective-permute-done.2.refs_3_), channel_id=1, source_target_pairs={{0,16},{1,17},{2,18},{3,19},{4,20},{5,21},{6,22},{7,23},{8,24},{9,... | collective-permute-start | bytes 1179656 | tf_op jit(solution)/shard_map/ppermute | solution.py:193
  31.1 14.7 %collective-permute-start.8 = (bf16[192,1024]{1,0:T(8,128)(2,1)S(1)}, bf16[192,1024]{1,0:T(8,128)(2,1)S(1)}, u32[]{:S(2)}, u32[]{:S(2)}) collective-permute-start(bf16[192,1024]{1,0:T(8,128)(2,1)S(1)} %collective-permute-done.4.refs_5_), channel_id=1, source_target_pairs={{0,8},{1,9},{2,10},{3,11},{4,12},{5,13},{6,14},{7,15},{8,0},{9,1},... | collective-permute-start | bytes 1179656 | tf_op jit(solution)/shard_map/ppermute | solution.py:193
  32.4 13.4 %collective-permute-start.3 = (bf16[192,1024]{1,0:T(8,128)(2,1)S(1)}, bf16[192,1024]{1,0:T(8,128)(2,1)S(1)}, u32[]{:S(2)}, u32[]{:S(2)}) collective-permute-start(bf16[192,1024]{1,0:T(8,128)(2,1)S(1)} %collective-permute-done.2.refs_3_), channel_id=1, source_target_pairs={{0,1},{1,0},{2,3},{3,2},{4,5},{5,4},{6,7},{7,6},{8,9},{9,8},{10,11... | collective-permute-start | bytes 1179656 | tf_op jit(solution)/shard_map/ppermute | solution.py:193
  37.9 7.9 %collective-permute-start.5 = (bf16[192,1024]{1,0:T(8,128)(2,1)S(1)}, bf16[192,1024]{1,0:T(8,128)(2,1)S(1)}, u32[]{:S(2)}, u32[]{:S(2)}) collective-permute-start(bf16[192,1024]{1,0:T(8,128)(2,1)S(1)} %collective-permute-done.4.refs_5_), channel_id=1, source_target_pairs={{0,1},{1,0},{2,3},{3,2},{4,5},{5,4},{6,7},{7,6},{8,9},{9,8},{10,11... | collective-permute-start | bytes 1179656 | tf_op jit(solution)/shard_map/ppermute | solution.py:193
  37.9 7.9 %collective-permute-start.1 = (bf16[192,1024]{1,0:T(8,128)(2,1)S(1)}, bf16[192,1024]{1,0:T(8,128)(2,1)S(1)}, u32[]{:S(2)}, u32[]{:S(2)}) collective-permute-start(bf16[192,1024]{1,0:T(8,128)(2,1)S(1)} %collective-permute-done.refs_1_), channel_id=1, source_target_pairs={{0,1},{1,0},{2,3},{3,2},{4,5},{5,4},{6,7},{7,6},{8,9},{9,8},{10,11... | collective-permute-start | bytes 1179656 | tf_op jit(solution)/shard_map/ppermute | solution.py:193
  39.5 13.7 %collective-permute-start.11 = (bf16[192,1024]{1,0:T(8,128)(2,1)S(1)}, bf16[192,1024]{1,0:T(8,128)(2,1)S(1)}, u32[]{:S(2)}, u32[]{:S(2)}) collective-permute-start(bf16[192,1024]{1,0:T(8,128)(2,1)S(1)} %collective-permute-done.10.refs_2_), channel_id=1, source_target_pairs={{0,1},{1,0},{2,3},{3,2},{4,5},{5,4},{6,7},{7,6},{8,9},{9,8},{10,11... | collective-permute-start | bytes 1179656 | tf_op jit(solution)/shard_map/ppermute | solution.py:193
  45.8 7.5 %collective-permute-start.9 = (bf16[192,1024]{1,0:T(8,128)(2,1)S(1)}, bf16[192,1024]{1,0:T(8,128)(2,1)S(1)}, u32[]{:S(2)}, u32[]{:S(2)}) collective-permute-start(bf16[192,1024]{1,0:T(8,128)(2,1)S(1)} %collective-permute-done.8.refs_0_), channel_id=1, source_target_pairs={{0,1},{1,0},{2,3},{3,2},{4,5},{5,4},{6,7},{7,6},{8,9},{9,8},{10,11... | collective-permute-start | bytes 1179656 | tf_op jit(solution)/shard_map/ppermute | solution.py:193
  45.8 1.6 %copy-start.1 = (bf16[1024,1024]{1,0:T(8,128)(2,1)S(1)}, bf16[1024,1024]{1,0:T(8,128)(2,1)}, u32[]{:S(2)}) copy-start(bf16[1024,1024]{1,0:T(8,128)(2,1)} %c_ref.3) | copy-start | bytes 6291460

commit v4 on v3

--- a/solution.py
+++ b/solution.py
@@ -106,17 +106,11 @@
     return lax.axis_index("item") ^ place if plan["exchange"] else place
 
 
-def row_lse(plan, parts, place):
-    cents = plan["cents"]
-    rows = parts[pl.ds(pl.multiple_of(index_of(plan, place) * cents, cents), cents), :]
-    peak = jnp.max(rows, axis=0, keepdims=True)
-    return peak + jnp.log(jnp.sum(jnp.exp(rows - peak), axis=0, keepdims=True))
-
-
 def open_kernel(plan, scale, c_ref, parts, *refs):
     nv, blocks = plan["nv"], plan["early"]
     pieces, refs = refs[: plan["n_early"]], refs[plan["n_early"] :]
-    table, own, total, mass, sems, own_sem = refs
+    table, own, total, mass, done, sems, own_sem = refs
+    done[...] = jnp.zeros_like(done)
     rows = own.shape[0]
     start = pl.multiple_of(lax.axis_index("item") * rows, rows)
     own_copy = pltpu.make_async_copy(c_ref.at[pl.ds(start, rows), :], own, own_sem)
@@ -130,7 +124,7 @@
         for copy in block:
             copy.wait()
         vectors = table[pl.ds(place * nv, nv), :]
-        resp = jnp.exp(scores(own[...], vectors, scale) - row_lse(plan, parts, place)).astype(jnp.bfloat16)
+        resp = jnp.exp(scores(own[...], vectors, scale) - parts[pl.ds(place, 1), :]).astype(jnp.bfloat16)
         term, weight = weigh(resp, vectors)
         total[...] = term if place == 0 else total[...] + term
         mass[...] = weight if place == 0 else mass[...] + weight
@@ -152,7 +146,7 @@
             for copy in block:
                 copy.wait()
             vectors = late[pl.ds(place * nv, nv), :]
-            resp = jnp.exp(scores(own[...], vectors, scale) - row_lse(plan, parts, first + place)).astype(jnp.bfloat16)
+            resp = jnp.exp(scores(own[...], vectors, scale) - parts[pl.ds(first + place, 1), :]).astype(jnp.bfloat16)
             term, weight = weigh(resp, vectors)
             sums, weights = sums + term, weights + weight
         new_ref[...] = updated(sums, weights, own[...])
@@ -193,9 +187,16 @@
     return lax.ppermute(value, BOTH, pairs)
 
 
-def everyone(value, axes):
-    n = lax.axis_size(axes)
-    return lax.all_to_all(jnp.broadcast_to(value, (n,) + value.shape), axes, 0, 0, tiled=True)
+def butterfly(part, go, cents):
+    mask = 1
+    while mask < cents:
+        part = merge([part, go(part, item_mask=0, cent_mask=mask)])
+        mask *= 2
+    return part
+
+
+def after(value, *others):
+    return lax.optimization_barrier((value, *others))[0]
 
 
 def shards(vectors, centroids):
@@ -206,53 +207,54 @@
     go = functools.partial(send, items=items, cents=cents)
     small = items == 4 and cents == 8
     if small:
-        quarter = nv // 4
+        half, quarter = nv // 2, nv // 4
         core = lax.rem(lax.axis_index("cent"), 2)
-        q = [lax.dynamic_slice_in_dim(vectors, core * (nv // 2) + s * quarter, quarter, 0) for s in range(2)]
-        x1, y0 = go(q[1], item_mask=1, cent_mask=0), go(q[0], item_mask=2, cent_mask=0)
-        x0, y1 = go(q[0], item_mask=1, cent_mask=0), go(q[1], item_mask=2, cent_mask=0)
-        part = partial(vectors, centroids, scale)
-        parts = everyone(part, BOTH).reshape(items * cents, nv)
-        x0, x1, y0, y1 = [lax.optimization_barrier((piece, parts))[0] for piece in (x0, x1, y0, y1)]
-        d0, d1 = go(y0, item_mask=1, cent_mask=0), go(x1, item_mask=2, cent_mask=0)
-
-        def pieces_of(pairs, at):
+        own_half = lax.dynamic_slice_in_dim(vectors, core * half, half, 0)
+        over_x, over_y = go(own_half, item_mask=1, cent_mask=0), go(own_half, item_mask=2, cent_mask=0)
+        lse = butterfly(partial(vectors, centroids, scale), go, cents)
+        over_x, over_y = after(over_x, lse), after(over_y, lse)
+        d0 = go(over_y[:quarter], item_mask=1, cent_mask=0)
+        d1 = go(over_x[quarter:], item_mask=2, cent_mask=0)
+        parts = jnp.concatenate([lse, go(lse, item_mask=1, cent_mask=0)], axis=0)
+        parts = jnp.concatenate([parts, go(parts, item_mask=2, cent_mask=0)], axis=0)
+
+        def pieces_of(values, at):
             pieces, blocks = [], []
-            for pair in pairs:
+            for block in values:
                 entries = []
-                for s, value in enumerate(pair):
+                for s, value in enumerate(block):
                     for mine in (True, False):
-                        entries.append((at + len(pieces), None, mine, s * quarter, quarter))
+                        entries.append((at + len(pieces), None, mine, s * quarter, value.shape[0]))
                         pieces.append(value if mine else go(value, item_mask=0, cent_mask=1))
                 blocks.append(entries)
             return pieces, blocks
 
-        early, early_blocks = pieces_of(((x0, x1), (y0, y1)), 1)
+        early, early_blocks = pieces_of([[after(over_x, parts)], [after(over_y, parts)]], 1)
         early = [vectors] + early
         early_blocks = [[(0, None, None, 0, nv)]] + early_blocks
-        late, late_blocks = pieces_of(((d0, d1),), 0)
     else:
         early = [lax.all_gather(vectors, "item", axis=0, tiled=True)]
         early_blocks = [[(0, i * nv, None, 0, nv)] for i in range(items)]
-        late, late_blocks = [], []
         part = partial(vectors, centroids, scale)
-        parts = lax.all_gather(part, BOTH, axis=0, tiled=True)
-    plan = dict(nv=nv, cents=cents, exchange=small, early=early_blocks, late=late_blocks, n_early=len(early), n_late=len(late))
+        parts = lax.all_gather(part, "cent", axis=0, tiled=False)
+        parts = lax.all_gather(merge([parts[i] for i in range(cents)]), "item", axis=0, tiled=True)
+    plan = dict(nv=nv, exchange=small, early=early_blocks, n_early=len(early))
 
     any_spec = pl.BlockSpec(memory_space=pl.ANY)
     vmem = pl.BlockSpec(memory_space=pltpu.VMEM)
-    n_early, n_late = len(early_blocks), len(late_blocks)
+    n_early = len(early_blocks)
     flops = 2 * nv * rows * dim
     params = pltpu.CompilerParams(vmem_limit_bytes=20 * MIB)
-    table, own, total, mass = pl.pallas_call(
+    table, own, total, mass, done = pl.pallas_call(
         functools.partial(open_kernel, plan, scale),
         in_specs=[any_spec, vmem] + [any_spec] * len(early),
-        out_specs=[vmem] * 4,
+        out_specs=[vmem] * 5,
         out_shape=[
             pltpu.VMEM((n_early * nv, dim), jnp.bfloat16),
             pltpu.VMEM((rows, dim), jnp.bfloat16),
             pltpu.VMEM((rows, dim), jnp.float32),
             pltpu.VMEM((rows, 1), jnp.float32),
+            jax.ShapeDtypeStruct((8, 128), jnp.float32),
         ],
         scratch_shapes=[
             pltpu.SemaphoreType.DMA((max(len(b) for b in early_blocks), n_early)),
@@ -265,6 +267,9 @@
         name="early_blocks",
     )(centroids, parts, *early)
 
+    late, late_blocks = pieces_of([[after(d0, done), after(d1, done)]], 0) if small else ([], [])
+    n_late = len(late_blocks)
+    plan = dict(plan, late=late_blocks, n_late=len(late))
     late_out = [pltpu.VMEM((n_late * nv, dim), jnp.bfloat16)] if n_late else []
     late_sems = [pltpu.SemaphoreType.DMA((max(len(b) for b in late_blocks), n_late))] if n_late else []
     fresh, expo, peak, part, *tables = pl.pallas_call(
@@ -289,8 +294,10 @@
     )(in_vmem(table), in_vmem(own), in_vmem(total), in_vmem(mass), parts, *late)
 
     if small:
-        gathered = everyone(part, "cent")
-        parts = everyone(merge([gathered[i] for i in range(cents)]), "item")
+        parts = butterfly(part, go, cents)
+        for mask in (1, 2):
+            parts = merge([parts, go(parts, item_mask=mask, cent_mask=0)])
+        parts = parts[None]
     else:
         gathered = lax.all_gather(part, "cent", axis=0, tiled=False)
         parts = lax.all_gather(merge([gathered[i] for i in range(cents)]), "item", axis=0, tiled=False)

time: 79.4 us -> 71.5 us (0.901)
  blocking collectives: 18.5 us -> 0 us
  waiting for transfers between devices: 21.9 us -> 31.9 us
  starting transfers between devices: 15.3 us -> 21.4 us
  local copies, waits for them, and re-layouts: 4.37 us -> 0.11 us
  Pallas kernels: 18.2 us -> 17 us
    all_to_all x2 -> x0, blocking collectives: 18.5 us -> none  [everyone(): lax.all_to_all(jnp.broadcast_to(value, (n,) + value.shape), axes, 0, 0, t...]
    ppermute x12 -> x18, waiting for transfers between devices: 17.9 us -> 31.9 us  [send(): return lax.ppermute(value, BOTH, pairs)]
    ppermute x12 -> x18, starting transfers between devices: 10.4 us -> 21.4 us  [send(): return lax.ppermute(value, BOTH, pairs)]
    all_to_all x1 -> x0, starting transfers between devices: 4.89 us -> none  [everyone(): lax.all_to_all(jnp.broadcast_to(value, (n,) + value.shape), axes, 0, 0, t...]
    all_to_all x1 -> x0, waiting for transfers between devices: 4.02 us -> none  [everyone(): lax.all_to_all(jnp.broadcast_to(value, (n,) + value.shape), axes, 0, 0, t...]
    dynamic_slice x1, local copies, waits for them, and re-layouts: 2.06 us -> 0.05 us  [shards(): own_half = lax.dynamic_slice_in_dim(vectors, core * half, half, 0)]
    unnamed x5 -> x4, local copies, waits for them, and re-layouts: 1.6 us -> 0.01 us
    pallas_call x1, Pallas kernels: 5.81 us -> 4.48 us  [shards(): pl.pallas_call(functools.partial(open_kernel, plan, scale), in_specs=[any...]
  transfers between devices with their start and end apart: 13 -> 18, of which waited for: 5 -> 14; matrix products, arithmetic and copies ran while one was open for 1% -> 0% of each run, Pallas kernels for 14% -> 6%
where the time goes in v4:
time: 71.5 us; the launch traced here: 71.3 us
  waiting for transfers between devices  31.9 us (45%)
  starting transfers between devices  21.4 us (30%)
  Pallas kernels  17 us (24%)
  between operations  0.74 us (1%)
    ppermute x18, waiting for transfers between devices, send(): return lax.ppermute(value, BOTH, pairs)  31.9 us
    ppermute x18, starting transfers between devices, send(): return lax.ppermute(value, BOTH, pairs)  21.4 us
    pallas_call x1, Pallas kernels, partial(): pl.pallas_call(functools.partial(partial_kernel, scale), grid=(k // rows,...  5.29 us
    pallas_call x1, Pallas kernels, shards(): pl.pallas_call(functools.partial(open_kernel, plan, scale), in_specs=[any...  4.48 us
    pallas_call x1, Pallas kernels, shards(): pl.pallas_call(functools.partial(close_kernel, plan, scale), in_specs=[vm...  4.45 us
    pallas_call x1, Pallas kernels, shards(): pl.pallas_call(functools.partial(last_kernel, plan), in_specs=[vmem] * (5...  2.74 us
  transfers between devices with their start and end apart: 18, of which 14 were waited for; matrix products, arithmetic and copies ran while one was open for 0% of the time, Pallas kernels for 6%

profile of v4, /device:TPU:0, one launch (start us, length us, event | category | flops | bytes accessed | tf_op | source)
XLA Modules:
  0.0 71.3 jit_solution(7407983792606515031)
XLA Ops:
  0.6 5.3 %partial_lse.1 = f32[1,768]{1,0:T(1,128)S(1)} custom-call(bf16[768,1024]{1,0:T(8,128)(2,1)} %refs_0_.1, bf16[1024,1024]{1,0:T(8,128)(2,1)} %c_ref.3), custom_call_target="tpu_custom_call" | custom-call | flops 1610612736 | bytes 3670016 | tf_op jit(solution)/shard_map/partial_lse/pallas_call | solution.py:64
  6.5 2.6 %collective-permute-start.7 = (bf16[384,1024]{1,0:T(8,128)(2,1)S(1)}, bf16[384,1024]{1,0:T(8,128)(2,1)S(1)}, u32[]{:S(2)}, u32[]{:S(2)}) collective-permute-start(bf16[384,1024]{1,0:T(8,128)(2,1)S(1)} %constant_dynamic-slice_fusion), channel_id=1, source_target_pairs={{0,16},{1,17},{2,18},{3,19},{4,20},{5,21},{6,22},{7,23},{8,24},{9,... | collective-permute-start | bytes 2359304 | tf_op jit(solution)/shard_map/ppermute | solution.py:187
  9.2 1.5 %collective-permute-start.5 = (bf16[384,1024]{1,0:T(8,128)(2,1)S(1)}, bf16[384,1024]{1,0:T(8,128)(2,1)S(1)}, u32[]{:S(2)}, u32[]{:S(2)}) collective-permute-start(bf16[384,1024]{1,0:T(8,128)(2,1)S(1)} %constant_dynamic-slice_fusion), channel_id=1, source_target_pairs={{0,8},{1,9},{2,10},{3,11},{4,12},{5,13},{6,14},{7,15},{8,0},{9,1},... | collective-permute-start | bytes 2359304 | tf_op jit(solution)/shard_map/ppermute | solution.py:187
  10.7 1.6 %collective-permute-start.1 = (f32[1,768]{1,0:T(1,128)S(1)}, f32[1,768]{1,0:T(1,128)S(1)}, u32[]{:S(2)}, u32[]{:S(2)}) collective-permute-start(f32[1,768]{1,0:T(1,128)S(1)} %log_add_fusion.6), channel_id=1, source_target_pairs={{0,2},{1,3},{2,0},{3,1},{4,6},{5,7},{6,4},{7,5},{8,10},{9,11},{10,... | collective-permute-start | bytes 9224 | tf_op jit(solution)/shard_map/ppermute | solution.py:187
  12.3 2.0 %collective-permute-done.1 = f32[1,768]{1,0:T(1,128)S(1)} collective-permute-done((f32[1,768]{1,0:T(1,128)S(1)}, f32[1,768]{1,0:T(1,128)S(1)}, u32[]{:S(2)}, u32[]{:S(2)}) %collective-permute-start.1) | collective-permute-done | bytes 3104 | tf_op jit(solution)/shard_map/ppermute | solution.py:187
  14.4 2.7 %collective-permute-start.2 = (f32[1,768]{1,0:T(1,128)S(1)}, f32[1,768]{1,0:T(1,128)S(1)}, u32[]{:S(2)}, u32[]{:S(2)}) collective-permute-start(f32[1,768]{1,0:T(1,128)S(1)} %log_add_fusion.5), channel_id=1, source_target_pairs={{0,4},{1,5},{2,6},{3,7},{4,0},{5,1},{6,2},{7,3},{8,12},{9,13},{10,... | collective-permute-start | bytes 9224 | tf_op jit(solution)/shard_map/ppermute | solution.py:187
  17.0 1.9 %collective-permute-done.2 = f32[1,768]{1,0:T(1,128)S(1)} collective-permute-done((f32[1,768]{1,0:T(1,128)S(1)}, f32[1,768]{1,0:T(1,128)S(1)}, u32[]{:S(2)}, u32[]{:S(2)}) %collective-permute-start.2) | collective-permute-done | bytes 3104 | tf_op jit(solution)/shard_map/ppermute | solution.py:187
  19.6 9.3 %collective-permute-done.3 = f32[1,768]{1,0:T(1,128)S(1)} collective-permute-done((f32[1,768]{1,0:T(1,128)S(1)}, f32[1,768]{1,0:T(1,128)S(1)}, u32[]{:S(2)}, u32[]{:S(2)}) %collective-permute-start.3) | collective-permute-done | bytes 3104 | tf_op jit(solution)/shard_map/ppermute | solution.py:187
  29.3 3.3 %collective-permute-done.4 = f32[2,768]{1,0:T(2,128)S(1)} collective-permute-done((f32[2,768]{1,0:T(2,128)S(1)}, f32[2,768]{1,0:T(2,128)S(1)}, u32[]{:S(2)}, u32[]{:S(2)}) %collective-permute-start.4) | collective-permute-done | bytes 6176 | tf_op jit(solution)/shard_map/ppermute | solution.py:187
  33.6 1.7 %collective-permute-start.9 = (bf16[192,1024]{1,0:T(8,128)(2,1)S(1)}, bf16[192,1024]{1,0:T(8,128)(2,1)S(1)}, u32[]{:S(2)}, u32[]{:S(2)}) collective-permute-start(bf16[192,1024]{1,0:T(8,128)(2,1)S(1)} %slice.6), channel_id=1, source_target_pairs={{0,8},{1,9},{2,10},{3,11},{4,12},{5,13},{6,14},{7,15},{8,0},{9,1},... | collective-permute-start | bytes 1179656 | tf_op jit(solution)/shard_map/ppermute | solution.py:187
  36.1 4.5 %early_blocks.1 = (bf16[2304,1024]{1,0:T(8,128)(2,1)S(1)}, bf16[256,1024]{1,0:T(8,128)(2,1)S(1)}, f32[256,1024]{1,0:T(8,128)S(1)}, f32[256,1]{1,0:T(8,128)S(1)}, f32[8,128]{1,0:T(8,128)}) custom-call(bf16[1024,1024]{1,0:T(8,128)(2,1)S(1)} %copy-done.1, f32[4,768]{1,0:T(4,128)S(1)} %pad_maximum_fusion.parts, bf16[768,1024]{1,0:T(8,128)(2,1)S(1)} %copy-done, ...), custom_call_target="tpu_custom_call" | custom-call | flops 2415919104 | bytes 4718592 | tf_op jit(solution)/shard_map/early_blocks/pallas_call | solution.py:248
  40.5 3.8 %collective-permute-done.11.refs_2_ = bf16[192,1024]{1,0:T(8,128)(2,1)S(1)} collective-permute-done((bf16[192,1024]{1,0:T(8,128)(2,1)S(1)}, bf16[192,1024]{1,0:T(8,128)(2,1)S(1)}, u32[]{:S(2)}, u32[]{:S(2)}) %collective-permute-start.11) | collective-permute-done | bytes 393248 | tf_op jit(solution)/shard_map/ppermute | solution.py:187
  45.0 1.2 %collective-permute-done.10.refs_1_ = bf16[192,1024]{1,0:T(8,128)(2,1)S(1)} collective-permute-done((bf16[192,1024]{1,0:T(8,128)(2,1)S(1)}, bf16[192,1024]{1,0:T(8,128)(2,1)S(1)}, u32[]{:S(2)}, u32[]{:S(2)}) %collective-permute-start.10) | collective-permute-done | bytes 393248 | tf_op jit(solution)/shard_map/ppermute | solution.py:187
  46.8 4.5 %late_blocks.1 = (bf16[256,1024]{1,0:T(8,128)(2,1)S(1)}, f32[4,256,768]{2,1,0:T(8,128)S(1)}, f32[4,768]{1,0:T(4,128)S(1)}, f32[4,768]{1,0:T(4,128)S(1)}, bf16[768,1024]{1,0:T(8,128)(2,1)S(1)}) custom-call(bf16[2304,1024]{1,0:T(8,128)(2,1)S(1)} %get-tuple-element.22.early.refs_0_, bf16[256,1024]{1,0:T(8,128)(2,1)S(1)} %get-tuple-element.23.own, ...), custom_call_target="tpu_custom_call" | custom-call | flops 2415919104 | bytes 1572864 | tf_op jit(solution)/shard_map/late_blocks/pallas_call | solution.py:275
  51.5 1.0 %collective-permute-done.13 = f32[4,768]{1,0:T(4,128)S(1)} collective-permute-done((f32[4,768]{1,0:T(4,128)S(1)}, f32[4,768]{1,0:T(4,128)S(1)}, u32[]{:S(2)}, u32[]{:S(2)}) %collective-permute-start.13) | collective-permute-done | bytes 12320 | tf_op jit(solution)/shard_map/ppermute | solution.py:187
  52.5 1.8 %collective-permute-start.14 = (f32[4,768]{1,0:T(4,128)S(1)}, f32[4,768]{1,0:T(4,128)S(1)}, u32[]{:S(2)}, u32[]{:S(2)}) collective-permute-start(f32[4,768]{1,0:T(4,128)S(1)} %log_add_fusion.3), channel_id=1, source_target_pairs={{0,2},{1,3},{2,0},{3,1},{4,6},{5,7},{6,4},{7,5},{8,10},{9,11},{10,... | collective-permute-start | bytes 36872 | tf_op jit(solution)/shard_map/ppermute | solution.py:187
  54.3 2.0 %collective-permute-done.14 = f32[4,768]{1,0:T(4,128)S(1)} collective-permute-done((f32[4,768]{1,0:T(4,128)S(1)}, f32[4,768]{1,0:T(4,128)S(1)}, u32[]{:S(2)}, u32[]{:S(2)}) %collective-permute-start.14) | collective-permute-done | bytes 12320 | tf_op jit(solution)/shard_map/ppermute | solution.py:187
  56.3 2.8 %collective-permute-start.15 = (f32[4,768]{1,0:T(4,128)S(1)}, f32[4,768]{1,0:T(4,128)S(1)}, u32[]{:S(2)}, u32[]{:S(2)}) collective-permute-start(f32[4,768]{1,0:T(4,128)S(1)} %log_add_fusion.2), channel_id=1, source_target_pairs={{0,4},{1,5},{2,6},{3,7},{4,0},{5,1},{6,2},{7,3},{8,12},{9,13},{10,... | collective-permute-start | bytes 36872 | tf_op jit(solution)/shard_map/ppermute | solution.py:187
  59.1 1.9 %collective-permute-done.15 = f32[4,768]{1,0:T(4,128)S(1)} collective-permute-done((f32[4,768]{1,0:T(4,128)S(1)}, f32[4,768]{1,0:T(4,128)S(1)}, u32[]{:S(2)}, u32[]{:S(2)}) %collective-permute-start.15) | collective-permute-done | bytes 12320 | tf_op jit(solution)/shard_map/ppermute | solution.py:187
  61.0 1.7 %collective-permute-start.16 = (f32[4,768]{1,0:T(4,128)S(1)}, f32[4,768]{1,0:T(4,128)S(1)}, u32[]{:S(2)}, u32[]{:S(2)}) collective-permute-start(f32[4,768]{1,0:T(4,128)S(1)} %log_add_fusion.1), channel_id=1, source_target_pairs={{0,8},{1,9},{2,10},{3,11},{4,12},{5,13},{6,14},{7,15},{8,0},{9,1},... | collective-permute-start | bytes 36872 | tf_op jit(solution)/shard_map/ppermute | solution.py:187
  62.7 2.0 %collective-permute-done.16 = f32[4,768]{1,0:T(4,128)S(1)} collective-permute-done((f32[4,768]{1,0:T(4,128)S(1)}, f32[4,768]{1,0:T(4,128)S(1)}, u32[]{:S(2)}, u32[]{:S(2)}) %collective-permute-start.16) | collective-permute-done | bytes 12320 | tf_op jit(solution)/shard_map/ppermute | solution.py:187
  64.8 1.7 %collective-permute-start.17 = (f32[4,768]{1,0:T(4,128)S(1)}, f32[4,768]{1,0:T(4,128)S(1)}, u32[]{:S(2)}, u32[]{:S(2)}) collective-permute-start(f32[4,768]{1,0:T(4,128)S(1)} %log_add_fusion), channel_id=1, source_target_pairs={{0,16},{1,17},{2,18},{3,19},{4,20},{5,21},{6,22},{7,23},{8,24},{9,... | collective-permute-start | bytes 36872 | tf_op jit(solution)/shard_map/ppermute | solution.py:187
  66.6 2.0 %collective-permute-done.17 = f32[4,768]{1,0:T(4,128)S(1)} collective-permute-done((f32[4,768]{1,0:T(4,128)S(1)}, f32[4,768]{1,0:T(4,128)S(1)}, u32[]{:S(2)}, u32[]{:S(2)}) %collective-permute-start.17) | collective-permute-done | bytes 12320 | tf_op jit(solution)/shard_map/ppermute | solution.py:187
  68.6 2.7 %last_iteration.1 = (bf16[256,1024]{1,0:T(8,128)(2,1)}, f32[768]{0:T(1024)}) custom-call(bf16[256,1024]{1,0:T(8,128)(2,1)S(1)} %get-tuple-element.29.old_ref, f32[4,256,768]{2,1,0:T(8,128)S(1)} %get-tuple-element.30.expo_ref, f32[4,768]{1,0:T(4,128)S(1)} %get-tuple-element.31.peak_ref, f32[1,4,768]{2,1,0:T(4,128)S(1)} %add_bitcast_fusion.parts, ...), custom_call_target="tpu_custom_call" | custom-call | flops 1610612736 | bytes 524288 | tf_op jit(solution)/shard_map/last_iteration/pallas_call | solution.py:304
  (33 shorter events, 5.0 us)
Async XLA Ops:
  0.6 5.8 %copy-start = (bf16[768,1024]{1,0:T(8,128)(2,1)S(1)}, bf16[768,1024]{1,0:T(8,128)(2,1)}, u32[]{:S(2)}) copy-start(bf16[768,1024]{1,0:T(8,128)(2,1)} %refs_0_.1) | copy-start | bytes 4718596
  5.9 4.7 %collective-permute-start = (f32[1,768]{1,0:T(1,128)S(1)}, f32[1,768]{1,0:T(1,128)S(1)}, u32[]{:S(2)}, u32[]{:S(2)}) collective-permute-start(f32[1,768]{1,0:T(1,128)S(1)} %partial_lse.1), channel_id=1, source_target_pairs={{0,1},{1,0},{2,3},{3,2},{4,5},{5,4},{6,7},{7,6},{8,9},{9,8},{10,11... | collective-permute-start | bytes 9224 | tf_op jit(solution)/shard_map/ppermute | solution.py:187
  6.5 29.6 %copy-start.1 = (bf16[1024,1024]{1,0:T(8,128)(2,1)S(1)}, bf16[1024,1024]{1,0:T(8,128)(2,1)}, u32[]{:S(2)}) copy-start(bf16[1024,1024]{1,0:T(8,128)(2,1)} %c_ref.3) | copy-start | bytes 6291460
  6.5 26.1 %collective-permute-start.7 = (bf16[384,1024]{1,0:T(8,128)(2,1)S(1)}, bf16[384,1024]{1,0:T(8,128)(2,1)S(1)}, u32[]{:S(2)}, u32[]{:S(2)}) collective-permute-start(bf16[384,1024]{1,0:T(8,128)(2,1)S(1)} %constant_dynamic-slice_fusion), channel_id=1, source_target_pairs={{0,16},{1,17},{2,18},{3,19},{4,20},{5,21},{6,22},{7,23},{8,24},{9,... | collective-permute-start | bytes 2359304 | tf_op jit(solution)/shard_map/ppermute | solution.py:187
  9.2 23.5 %collective-permute-start.5 = (bf16[384,1024]{1,0:T(8,128)(2,1)S(1)}, bf16[384,1024]{1,0:T(8,128)(2,1)S(1)}, u32[]{:S(2)}, u32[]{:S(2)}) collective-permute-start(bf16[384,1024]{1,0:T(8,128)(2,1)S(1)} %constant_dynamic-slice_fusion), channel_id=1, source_target_pairs={{0,8},{1,9},{2,10},{3,11},{4,12},{5,13},{6,14},{7,15},{8,0},{9,1},... | collective-permute-start | bytes 2359304 | tf_op jit(solution)/shard_map/ppermute | solution.py:187
  10.7 3.7 %collective-permute-start.1 = (f32[1,768]{1,0:T(1,128)S(1)}, f32[1,768]{1,0:T(1,128)S(1)}, u32[]{:S(2)}, u32[]{:S(2)}) collective-permute-start(f32[1,768]{1,0:T(1,128)S(1)} %log_add_fusion.6), channel_id=1, source_target_pairs={{0,2},{1,3},{2,0},{3,1},{4,6},{5,7},{6,4},{7,5},{8,10},{9,11},{10,... | collective-permute-start | bytes 9224 | tf_op jit(solution)/shard_map/ppermute | solution.py:187
  14.4 4.6 %collective-permute-start.2 = (f32[1,768]{1,0:T(1,128)S(1)}, f32[1,768]{1,0:T(1,128)S(1)}, u32[]{:S(2)}, u32[]{:S(2)}) collective-permute-start(f32[1,768]{1,0:T(1,128)S(1)} %log_add_fusion.5), channel_id=1, source_target_pairs={{0,4},{1,5},{2,6},{3,7},{4,0},{5,1},{6,2},{7,3},{8,12},{9,13},{10,... | collective-permute-start | bytes 9224 | tf_op jit(solution)/shard_map/ppermute | solution.py:187
  18.9 9.9 %collective-permute-start.3 = (f32[1,768]{1,0:T(1,128)S(1)}, f32[1,768]{1,0:T(1,128)S(1)}, u32[]{:S(2)}, u32[]{:S(2)}) collective-permute-start(f32[1,768]{1,0:T(1,128)S(1)} %log_add_fusion.4), channel_id=1, source_target_pairs={{0,8},{1,9},{2,10},{3,11},{4,12},{5,13},{6,14},{7,15},{8,0},{9,1},... | collective-permute-start | bytes 9224 | tf_op jit(solution)/shard_map/ppermute | solution.py:187
  28.9 3.7 %collective-permute-start.4 = (f32[2,768]{1,0:T(2,128)S(1)}, f32[2,768]{1,0:T(2,128)S(1)}, u32[]{:S(2)}, u32[]{:S(2)}) collective-permute-start(f32[2,768]{1,0:T(2,128)S(1)} %pad_maximum_fusion.1), channel_id=1, source_target_pairs={{0,16},{1,17},{2,18},{3,19},{4,20},{5,21},{6,22},{7,23},{8,24},{9,... | collective-permute-start | bytes 18440 | tf_op jit(solution)/shard_map/ppermute | solution.py:187
  32.6 2.8 %collective-permute-start.8 = (bf16[384,1024]{1,0:T(8,128)(2,1)S(1)}, bf16[384,1024]{1,0:T(8,128)(2,1)S(1)}, u32[]{:S(2)}, u32[]{:S(2)}) collective-permute-start(bf16[384,1024]{1,0:T(8,128)(2,1)S(1)} %collective-permute-done.7.refs_3_), channel_id=1, source_target_pairs={{0,1},{1,0},{2,3},{3,2},{4,5},{5,4},{6,7},{7,6},{8,9},{9,8},{10,11... | collective-permute-start | bytes 2359304 | tf_op jit(solution)/shard_map/ppermute | solution.py:187
  32.7 3.4 %collective-permute-start.6 = (bf16[384,1024]{1,0:T(8,128)(2,1)S(1)}, bf16[384,1024]{1,0:T(8,128)(2,1)S(1)}, u32[]{:S(2)}, u32[]{:S(2)}) collective-permute-start(bf16[384,1024]{1,0:T(8,128)(2,1)S(1)} %collective-permute-done.5.refs_1_), channel_id=1, source_target_pairs={{0,1},{1,0},{2,3},{3,2},{4,5},{5,4},{6,7},{7,6},{8,9},{9,8},{10,11... | collective-permute-start | bytes 2359304 | tf_op jit(solution)/shard_map/ppermute | solution.py:187
  33.2 11.2 %collective-permute-start.11 = (bf16[192,1024]{1,0:T(8,128)(2,1)S(1)}, bf16[192,1024]{1,0:T(8,128)(2,1)S(1)}, u32[]{:S(2)}, u32[]{:S(2)}) collective-permute-start(bf16[192,1024]{1,0:T(8,128)(2,1)S(1)} %slice.7), channel_id=1, source_target_pairs={{0,16},{1,17},{2,18},{3,19},{4,20},{5,21},{6,22},{7,23},{8,24},{9,... | collective-permute-start | bytes 1179656 | tf_op jit(solution)/shard_map/ppermute | solution.py:187
  33.6 10.9 %collective-permute-start.9 = (bf16[192,1024]{1,0:T(8,128)(2,1)S(1)}, bf16[192,1024]{1,0:T(8,128)(2,1)S(1)}, u32[]{:S(2)}, u32[]{:S(2)}) collective-permute-start(bf16[192,1024]{1,0:T(8,128)(2,1)S(1)} %slice.6), channel_id=1, source_target_pairs={{0,8},{1,9},{2,10},{3,11},{4,12},{5,13},{6,14},{7,15},{8,0},{9,1},... | collective-permute-start | bytes 1179656 | tf_op jit(solution)/shard_map/ppermute | solution.py:187
  44.5 1.7 %collective-permute-start.10 = (bf16[192,1024]{1,0:T(8,128)(2,1)S(1)}, bf16[192,1024]{1,0:T(8,128)(2,1)S(1)}, u32[]{:S(2)}, u32[]{:S(2)}) collective-permute-start(bf16[192,1024]{1,0:T(8,128)(2,1)S(1)} %collective-permute-done.9.refs_0_), channel_id=1, source_target_pairs={{0,1},{1,0},{2,3},{3,2},{4,5},{5,4},{6,7},{7,6},{8,9},{9,8},{10,11... | collective-permute-start | bytes 1179656 | tf_op jit(solution)/shard_map/ppermute | solution.py:187
  44.5 2.3 %collective-permute-start.12 = (bf16[192,1024]{1,0:T(8,128)(2,1)S(1)}, bf16[192,1024]{1,0:T(8,128)(2,1)S(1)}, u32[]{:S(2)}, u32[]{:S(2)}) collective-permute-start(bf16[192,1024]{1,0:T(8,128)(2,1)S(1)} %collective-permute-done.11.refs_2_), channel_id=1, source_target_pairs={{0,1},{1,0},{2,3},{3,2},{4,5},{5,4},{6,7},{7,6},{8,9},{9,8},{10,11... | collective-permute-start | bytes 1179656 | tf_op jit(solution)/shard_map/ppermute | solution.py:187
  51.3 1.2 %collective-permute-start.13 = (f32[4,768]{1,0:T(4,128)S(1)}, f32[4,768]{1,0:T(4,128)S(1)}, u32[]{:S(2)}, u32[]{:S(2)}) collective-permute-start(f32[4,768]{1,0:T(4,128)S(1)} %get-tuple-element.32), channel_id=1, source_target_pairs={{0,1},{1,0},{2,3},{3,2},{4,5},{5,4},{6,7},{7,6},{8,9},{9,8},{10,11... | collective-permute-start | bytes 36872 | tf_op jit(solution)/shard_map/ppermute | solution.py:187
  52.5 3.8 %collective-permute-start.14 = (f32[4,768]{1,0:T(4,128)S(1)}, f32[4,768]{1,0:T(4,128)S(1)}, u32[]{:S(2)}, u32[]{:S(2)}) collective-permute-start(f32[4,768]{1,0:T(4,128)S(1)} %log_add_fusion.3), channel_id=1, source_target_pairs={{0,2},{1,3},{2,0},{3,1},{4,6},{5,7},{6,4},{7,5},{8,10},{9,11},{10,... | collective-permute-start | bytes 36872 | tf_op jit(solution)/shard_map/ppermute | solution.py:187
  56.3 4.7 %collective-permute-start.15 = (f32[4,768]{1,0:T(4,128)S(1)}, f32[4,768]{1,0:T(4,128)S(1)}, u32[]{:S(2)}, u32[]{:S(2)}) collective-permute-start(f32[4,768]{1,0:T(4,128)S(1)} %log_add_fusion.2), channel_id=1, source_target_pairs={{0,4},{1,5},{2,6},{3,7},{4,0},{5,1},{6,2},{7,3},{8,12},{9,13},{10,... | collective-permute-start | bytes 36872 | tf_op jit(solution)/shard_map/ppermute | solution.py:187
  61.0 3.8 %collective-permute-start.16 = (f32[4,768]{1,0:T(4,128)S(1)}, f32[4,768]{1,0:T(4,128)S(1)}, u32[]{:S(2)}, u32[]{:S(2)}) collective-permute-start(f32[4,768]{1,0:T(4,128)S(1)} %log_add_fusion.1), channel_id=1, source_target_pairs={{0,8},{1,9},{2,10},{3,11},{4,12},{5,13},{6,14},{7,15},{8,0},{9,1},... | collective-permute-start | bytes 36872 | tf_op jit(solution)/shard_map/ppermute | solution.py:187
  64.8 3.8 %collective-permute-start.17 = (f32[4,768]{1,0:T(4,128)S(1)}, f32[4,768]{1,0:T(4,128)S(1)}, u32[]{:S(2)}, u32[]{:S(2)}) collective-permute-start(f32[4,768]{1,0:T(4,128)S(1)} %log_add_fusion), channel_id=1, source_target_pairs={{0,16},{1,17},{2,18},{3,19},{4,20},{5,21},{6,22},{7,23},{8,24},{9,... | collective-permute-start | bytes 36872 | tf_op jit(solution)/shard_map/ppermute | solution.py:187

commit v5 on v0

v5 whole, which is shorter than its diff:
```python
import functools
import math

import jax
import jax.numpy as jnp
from jax import lax
from jax.experimental import pallas as pl
from jax.experimental.pallas import tpu as pltpu
from jax.sharding import PartitionSpec as P

BETA = 3.0
BOTH = ("item", "cent")
MIB = 1024 * 1024
NT = (((1,), (1,)), ((), ()))
NN = (((1,), (0,)), ((), ()))


def scores(rows, vectors, scale):
    raw = lax.dot_general(rows, vectors, NT, preferred_element_type=jnp.float32)
    sqnorm = jnp.sum(jnp.square(rows.astype(jnp.float32)), axis=1, keepdims=True)
    return scale * (raw - 0.5 * sqnorm)


def merge(parts):
    peak = functools.reduce(jnp.maximum, parts)
    terms = [jnp.exp(p - peak) for p in parts]
    while len(terms) > 1:
        terms = [sum(terms[i : i + 2]) for i in range(0, len(terms), 2)]
    return peak + jnp.log(terms[0])


def in_vmem(value):
    return pltpu.with_memory_space_constraint(value, pltpu.VMEM)


def partial_kernel(scale, rows, v_ref, c_ref, out_ref):
    parts = []
    for start in range(0, c_ref.shape[0], rows):
        logits = scores(c_ref[start : start + rows, :], v_ref[...], scale)
        peak = jnp.max(logits, axis=0, keepdims=True)
        parts.append(peak + jnp.log(jnp.sum(jnp.exp(logits - peak), axis=0, keepdims=True)))
    out_ref[...] = merge(parts)


def partial(vectors, centroids, scale):
    nv, dim = vectors.shape
    k = centroids.shape[0]
    vmem = pl.BlockSpec(memory_space=pltpu.VMEM)
    return pl.pallas_call(
        functools.partial(partial_kernel, scale, min(256, k)),
        in_specs=[vmem, vmem],
        out_specs=vmem,
        out_shape=jax.ShapeDtypeStruct((1, nv), jnp.float32),
        compiler_params=pltpu.CompilerParams(vmem_limit_bytes=16 * MIB),
        cost_estimate=pl.CostEstimate(
            flops=2 * nv * k * dim, bytes_accessed=2 * (nv + k) * dim, transcendentals=nv * k
        ),
        name="partial_lse",
    )(in_vmem(vectors), in_vmem(centroids))


def core_index():
    return lax.rem(lax.axis_index("cent"), 2)


def index_of(plan, place):
    if not plan["exchange"]:
        return place
    mask = (0, 1 + core_index(), 2 - core_index(), 3)[place]
    return lax.axis_index("item") ^ mask


def local(plan, place, row):
    if not plan["exchange"] or place != 3:
        return row
    half = row.shape[1] // 2
    swapped = jnp.concatenate([row[:, half:], row[:, :half]], axis=1)
    return jnp.where(core_index() == 1, swapped, row)


def segments(block):
    offset = 0
    for operand, start, rows in block:
        yield operand, start, rows, offset
        offset += rows


def weigh(resp, vectors):
    term = lax.dot_general(resp, vectors, NN, preferred_element_type=jnp.float32)
    return term, jnp.sum(resp.astype(jnp.float32), axis=1, keepdims=True)


def updated(total, mass, old):
    return ((total + old.astype(jnp.float32)) / (mass + 1.0)).astype(jnp.bfloat16)


def absorb(blocks, first, plan, scale, own, parts, pieces, total, mass):
    for place, block in enumerate(blocks, first):
        lse = local(plan, place, parts[pl.ds(place, 1), :])
        for operand, start, rows, offset in segments(block):
            vectors = pieces[operand][pl.ds(start, rows), :]
            logits = scores(own, vectors, scale)
            resp = jnp.exp(logits - lse[:, offset : offset + rows]).astype(jnp.bfloat16)
            term, weight = weigh(resp, vectors)
            total = term if total is None else total + term
            mass = weight if mass is None else mass + weight
    return total, mass


def early_kernel(plan, scale, c_ref, parts, *refs):
    pieces, (total, mass, done) = refs[:-3], refs[-3:]
    done[...] = jnp.zeros_like(done)
    rows = total.shape[0]
    start = pl.multiple_of(lax.axis_index("item") * rows, rows)
    own = c_ref[pl.ds(start, rows), :]
    total[...], mass[...] = absorb(plan["early"], 0, plan, scale, own, parts, pieces, None, None)


def late_kernel(plan, scale, c_ref, parts, total, mass, *refs):
    pieces, (new_ref, expo_ref, peak_ref, part_ref) = refs[:-4], refs[-4:]
    rows = new_ref.shape[0]
    start = pl.multiple_of(lax.axis_index("item") * rows, rows)
    own = c_ref[pl.ds(start, rows), :]
    first = len(plan["early"])
    sums, weights = absorb(plan["late"], first, plan, scale, own, parts, pieces, total[...], mass[...])
    new_ref[...] = updated(sums, weights, own)
    for place, block in enumerate(plan["early"] + plan["late"]):
        peaks, sums = [], []
        for operand, start, count, offset in segments(block):
            logits = scores(new_ref[...], pieces[operand][pl.ds(start, count), :], scale)
            peak = jnp.max(logits, axis=0, keepdims=True)
            expo = jnp.exp(logits - peak)
            expo_ref[place, :, offset : offset + count] = expo
            peaks.append(peak)
            sums.append(jnp.sum(expo, axis=0, keepdims=True))
        peak, total_expo = jnp.concatenate(peaks, axis=1), jnp.concatenate(sums, axis=1)
        peak_ref[pl.ds(place, 1), :] = peak
        part_ref[pl.ds(index_of(plan, place), 1), :] = local(plan, place, peak + jnp.log(total_expo))


def last_kernel(plan, old_ref, expo_ref, peak_ref, parts, *refs):
    pieces, (new_ref, norm_ref, lse_ref) = refs[:-3], refs[-3:]
    lse_ref[...] = merge([parts[i] for i in range(parts.shape[0])])
    norm_ref[...] = lse_ref[pl.ds(lax.axis_index("item"), 1), :].reshape(norm_ref.shape)
    total = mass = None
    for place, block in enumerate(plan["early"] + plan["late"]):
        lse = local(plan, place, lse_ref[pl.ds(index_of(plan, place), 1), :])
        factor = jnp.exp(peak_ref[pl.ds(place, 1), :] - lse)
        resp = (expo_ref[place] * factor).astype(jnp.bfloat16)
        for operand, start, count, offset in segments(block):
            term, weight = weigh(resp[:, offset : offset + count], pieces[operand][pl.ds(start, count), :])
            total = term if total is None else total + term
            mass = weight if mass is None else mass + weight
    new_ref[...] = updated(total, mass, old_ref[...])


def send(value, items, cents, item_mask, cent_mask=0):
    masks = item_mask if isinstance(item_mask, tuple) else (item_mask, item_mask)
    pairs = [
        (i * cents + c, (i ^ masks[c % 2]) * cents + (c ^ cent_mask)) for i in range(items) for c in range(cents)
    ]
    return lax.ppermute(value, BOTH, pairs)


def merge_cent(part, go):
    part = merge([part, go(part, 0, 1)])
    return merge([part] + [go(part, 0, mask) for mask in (2, 4, 6)])


def after(value, *others):
    anywhere = pl.BlockSpec(memory_space=pl.ANY)
    return pl.pallas_call(
        lambda *refs: None,
        in_specs=[anywhere] * (1 + len(others)),
        out_specs=anywhere,
        out_shape=jax.ShapeDtypeStruct(value.shape, value.dtype),
        input_output_aliases={0: 0},
        name="after",
    )(value, *others)


def shards(vectors, centroids):
    items, cents = lax.axis_size("item"), lax.axis_size("cent")
    nv, dim = vectors.shape
    rows = centroids.shape[0] // items
    scale = BETA / math.sqrt(dim)

    def go(value, item_mask, cent_mask=0):
        return send(value, items, cents, item_mask, cent_mask)

    small = items == 4 and cents == 8
    part = partial(vectors, centroids, scale)
    if small:
        half = nv // 2
        near = go(vectors, (1, 2))
        lse = merge_cent(part, go)
        near = after(near, lse)
        give = lax.dynamic_slice_in_dim(near, core_index() * half, half, 0)
        far = go(give, (2, 1))
        parts = jnp.concatenate([lse, go(lse, (1, 2)), go(lse, (2, 1)), go(lse, 3)], axis=0)
        cross = go(near, 0, 1)
        early = [vectors, near, cross]
        early_blocks = [[(i, 0, nv)] for i in range(3)]
    else:
        early = [lax.all_gather(vectors, "item", axis=0, tiled=True)]
        early_blocks = [[(0, i * nv, nv)] for i in range(items)]
        parts = lax.all_gather(part, "cent", axis=0, tiled=False)
        parts = lax.all_gather(merge([parts[i] for i in range(cents)]), "item", axis=0, tiled=True)
    early = [in_vmem(piece) for piece in early]
    centroids = in_vmem(centroids)
    plan = dict(exchange=small, early=early_blocks)

    vmem = pl.BlockSpec(memory_space=pltpu.VMEM)
    n_early = len(early_blocks)
    flops = 2 * nv * rows * dim
    params = pltpu.CompilerParams(vmem_limit_bytes=20 * MIB)
    total, mass, done = pl.pallas_call(
        functools.partial(early_kernel, plan, scale),
        in_specs=[vmem] * (2 + len(early)),
        out_specs=[vmem] * 3,
        out_shape=[
            pltpu.VMEM((rows, dim), jnp.float32),
            pltpu.VMEM((rows, 1), jnp.float32),
            jax.ShapeDtypeStruct((8, 128), jnp.float32),
        ],
        compiler_params=params,
        cost_estimate=pl.CostEstimate(
            flops=2 * n_early * flops, bytes_accessed=2 * n_early * nv * dim, transcendentals=n_early * nv * rows
        ),
        name="early_blocks",
    )(centroids, parts, *early)

    late, late_blocks = [], []
    if small:
        far = after(far, done)
        late = [in_vmem(far), in_vmem(go(far, 0, 1))]
        late_blocks = [[(3, 0, half), (4, 0, half)]]
    plan["late"] = late_blocks
    n_late = len(late_blocks)
    pieces = early + late
    fresh, expo, peak, part = pl.pallas_call(
        functools.partial(late_kernel, plan, scale),
        in_specs=[vmem] * (4 + len(pieces)),
        out_specs=[vmem] * 4,
        out_shape=[
            pltpu.VMEM((rows, dim), jnp.bfloat16),
            pltpu.VMEM((items, rows, nv), jnp.float32),
            pltpu.VMEM((items, nv), jnp.float32),
            pltpu.VMEM((items, nv), jnp.float32),
        ],
        compiler_params=params,
        cost_estimate=pl.CostEstimate(
            flops=(items + 2 * n_late) * flops,
            bytes_accessed=2 * n_late * nv * dim,
            transcendentals=(items + n_late) * nv * rows,
        ),
        name="late_blocks",
    )(centroids, parts, in_vmem(total), in_vmem(mass), *pieces)

    if small:
        lse = merge_cent(part, go)
        parts = merge([lse] + [go(lse, mask) for mask in (1, 2, 3)])[None]
    else:
        gathered = lax.all_gather(part, "cent", axis=0, tiled=False)
        parts = lax.all_gather(merge([gathered[i] for i in range(cents)]), "item", axis=0, tiled=False)
    result, norm = pl.pallas_call(
        functools.partial(last_kernel, plan),
        in_specs=[vmem] * (4 + len(pieces)),
        out_specs=[vmem] * 2,
        out_shape=[
            jax.ShapeDtypeStruct((rows, dim), jnp.bfloat16),
            jax.ShapeDtypeStruct((nv,), jnp.float32),
        ],
        scratch_shapes=[pltpu.VMEM((items, nv), jnp.float32)],
        compiler_params=params,
        cost_estimate=pl.CostEstimate(flops=items * flops, bytes_accessed=2 * rows * dim, transcendentals=0),
        name="last_iteration",
    )(in_vmem(fresh), in_vmem(expo), in_vmem(peak), parts, *pieces)
    return (result, norm)


def solution(mesh):
    in_specs = (P("item", None), P("cent", None))
    out_specs = (P(("cent", "item"), None), P("item"))
    return jax.shard_map(shards, mesh=mesh, in_specs=in_specs, out_specs=out_specs, check_vma=False)
```

time: 214 us -> 79.7 us (0.37)
  blocking collectives: 80.7 us -> 0 us
  waiting for transfers between devices: 81.9 us -> 24.6 us
  starting transfers between devices: 0.12 us -> 22.3 us
  other arithmetic: 20 us -> 0.76 us
  Pallas kernels: 0 us -> 16.7 us
  matrix products: 16.5 us -> 0 us
  local copies, waits for them, and re-layouts: 0.02 us -> 14.1 us
  between operations: 13.8 us -> 0.75 us
    psum x4 -> x0, blocking collectives: 46.3 us -> none  [the longest x2 27.2 us: normalize(): total = lax.psum(jnp.sum(expo, axis=1), 'cent')]
    reduce_scatter x2 -> x0, waiting for transfers between devices: 46.3 us -> none  [shards(): lax.psum_scatter(term_rows().astype(jnp.bfloat16), 'item', scatter_dimens...]
    all_gather x1 -> x0, waiting for transfers between devices: 35.6 us -> none  [shards(): lax.all_gather(fresh, 'item', axis=0, tiled=True)]
    pmax x2 -> x0, blocking collectives: 34.4 us -> none  [normalize(): peak = lax.pmax(local_peak, 'cent')]
    ppermute x0 -> x18, waiting for transfers between devices: none -> 24.6 us  [send(): return lax.ppermute(value, BOTH, pairs)]
    ppermute x0 -> x18, starting transfers between devices: none -> 22.3 us  [send(): return lax.ppermute(value, BOTH, pairs)]
    pallas_call x0 -> x6, Pallas kernels: none -> 16.7 us  [the longest x1 5.67 us: shards(): pl.pallas_call(functools.partial(late_kernel, plan, scale), in_specs=[vme...]
    dot_general x4 -> x0, matrix products: 16.5 us -> none  [the longest x2 10.2 us: local_logits(): lax.dot_general(vectors, rows, (((1,), (1,)), ((), ())), preferred_elemen...]
  transfers between devices with their start and end apart: 3 -> 18, of which waited for: 3 -> 13; matrix products, arithmetic and copies ran while one was open for 0% -> 2% of each run, Pallas kernels for 0% -> 9%
where the time goes in v5:
time: 79.7 us; the launch traced here: 79.2 us
  waiting for transfers between devices  24.6 us (31%)
  starting transfers between devices  22.3 us (28%)
  Pallas kernels  16.7 us (21%)
  local copies, waits for them, and re-layouts  14.1 us (18%)
    ppermute x18, waiting for transfers between devices, send(): return lax.ppermute(value, BOTH, pairs)  24.6 us
    ppermute x18, starting transfers between devices, send(): return lax.ppermute(value, BOTH, pairs)  22.3 us
    unnamed x26, local copies, waits for them, and re-layouts  12.8 us
    pallas_call x1, Pallas kernels, shards(): pl.pallas_call(functools.partial(late_kernel, plan, scale), in_specs=[vme...  5.67 us
    pallas_call x1, Pallas kernels, shards(): pl.pallas_call(functools.partial(early_kernel, plan, scale), in_specs=[vm...  4.44 us
    pallas_call x1, Pallas kernels, shards(): pl.pallas_call(functools.partial(last_kernel, plan), in_specs=[vmem] * (4...  4.18 us
    pallas_call x1, Pallas kernels, partial(): pl.pallas_call(functools.partial(partial_kernel, scale, min(256, k)), in_...  2.42 us
  transfers between devices with their start and end apart: 18, of which 13 were waited for; matrix products, arithmetic and copies ran while one was open for 2% of the time, Pallas kernels for 9%

profile of v5, /device:TPU:0, one launch (start us, length us, event | category | flops | bytes accessed | tf_op | source)
XLA Modules:
  0.0 79.2 jit_solution(9175904784660856106)
XLA Ops:
  0.6 3.0 %collective-permute-start.7 = (bf16[768,1024]{1,0:T(8,128)(2,1)}, bf16[768,1024]{1,0:T(8,128)(2,1)S(1)}, u32[]{:S(2)}, u32[]{:S(2)}) collective-permute-start(bf16[768,1024]{1,0:T(8,128)(2,1)} %refs_0_.5), channel_id=1, source_target_pairs={{0,8},{1,17},{2,10},{3,19},{4,12},{5,21},{6,14},{7,23},{8,0},{9,25... | collective-permute-start | bytes 4718600 | tf_op jit(solution)/shard_map/ppermute | solution.py:162
  3.6 1.4 %copy-done.4 = bf16[768,1024]{1,0:T(8,128)(2,1)S(1)} copy-done((bf16[768,1024]{1,0:T(8,128)(2,1)S(1)}, bf16[768,1024]{1,0:T(8,128)(2,1)}, u32[]{:S(2)}) %copy-start.4) | copy-done | bytes 1572888
  5.1 1.6 %copy-done.8 = bf16[1024,1024]{1,0:T(8,128)(2,1)S(1)} copy-done((bf16[1024,1024]{1,0:T(8,128)(2,1)S(1)}, bf16[1024,1024]{1,0:T(8,128)(2,1)}, u32[]{:S(2)}) %copy-start.8) | copy-done | bytes 2097176
  6.7 2.4 %partial_lse.1 = f32[1,768]{1,0:T(1,128)S(1)} custom-call(bf16[768,1024]{1,0:T(8,128)(2,1)S(1)} %copy-done.4, bf16[1024,1024]{1,0:T(8,128)(2,1)S(1)} %copy-done.8), custom_call_target="tpu_custom_call" | custom-call | flops 1610612736 | bytes 3670016 | tf_op jit(solution)/shard_map/partial_lse/pallas_call | solution.py:49
  10.3 3.7 %collective-permute-start.3 = (f32[1,768]{1,0:T(1,128)S(1)}, f32[1,768]{1,0:T(1,128)S(1)}, u32[]{:S(2)}, u32[]{:S(2)}) collective-permute-start(f32[1,768]{1,0:T(1,128)S(1)} %log_add_fusion.3), channel_id=1, source_target_pairs={{0,6},{1,7},{2,4},{3,5},{4,2},{5,3},{6,0},{7,1},{8,14},{9,15},{10,... | collective-permute-start | bytes 9224 | tf_op jit(solution)/shard_map/ppermute | solution.py:162
  15.8 2.7 %collective-permute-done.2 = f32[1,768]{1,0:T(1,128)S(1)} collective-permute-done((f32[1,768]{1,0:T(1,128)S(1)}, f32[1,768]{1,0:T(1,128)S(1)}, u32[]{:S(2)}, u32[]{:S(2)}) %collective-permute-start.2) | collective-permute-done | bytes 3104 | tf_op jit(solution)/shard_map/ppermute | solution.py:162
  19.1 3.1 %collective-permute-done.7.refs_0_ = bf16[768,1024]{1,0:T(8,128)(2,1)S(1)} collective-permute-done((bf16[768,1024]{1,0:T(8,128)(2,1)}, bf16[768,1024]{1,0:T(8,128)(2,1)S(1)}, u32[]{:S(2)}, u32[]{:S(2)}) %collective-permute-start.7) | collective-permute-done | bytes 1572896 | tf_op jit(solution)/shard_map/ppermute | solution.py:162
  23.4 1.3 %constant_dynamic-slice_fusion = bf16[384,1024]{1,0:T(8,128)(2,1)S(1)} fusion(bf16[768,1024]{1,0:T(8,128)(2,1)} %after.2.refs_1_, s32[]{:T(128)S(6)} %select_n.3), kind=kLoop, calls=%fused_computation.10 | loop fusion | bytes 1572868 | tf_op jit(solution)/shard_map/dynamic_slice | solution.py:198
  24.7 2.1 %collective-permute-start.9 = (bf16[384,1024]{1,0:T(8,128)(2,1)S(1)}, bf16[384,1024]{1,0:T(8,128)(2,1)S(1)}, u32[]{:S(2)}, u32[]{:S(2)}) collective-permute-start(bf16[384,1024]{1,0:T(8,128)(2,1)S(1)} %constant_dynamic-slice_fusion), channel_id=1, source_target_pairs={{0,16},{1,9},{2,18},{3,11},{4,20},{5,13},{6,22},{7,15},{8,24},{9,1... | collective-permute-start | bytes 2359304 | tf_op jit(solution)/shard_map/ppermute | solution.py:162
  26.8 1.4 %collective-permute-start.6 = (f32[1,768]{1,0:T(1,128)S(1)}, f32[1,768]{1,0:T(1,128)S(1)}, u32[]{:S(2)}, u32[]{:S(2)}) collective-permute-start(f32[1,768]{1,0:T(1,128)S(1)} %copy-done.12), channel_id=1, source_target_pairs={{0,24},{1,25},{2,26},{3,27},{4,28},{5,29},{6,30},{7,31},{8,16},{9,... | collective-permute-start | bytes 9224 | tf_op jit(solution)/shard_map/ppermute | solution.py:162
  28.3 1.5 %collective-permute-start.5 = (f32[1,768]{1,0:T(1,128)S(1)}, f32[1,768]{1,0:T(1,128)S(1)}, u32[]{:S(2)}, u32[]{:S(2)}) collective-permute-start(f32[1,768]{1,0:T(1,128)S(1)} %copy-done.12), channel_id=1, source_target_pairs={{0,16},{1,9},{2,18},{3,11},{4,20},{5,13},{6,22},{7,15},{8,24},{9,1... | collective-permute-start | bytes 9224 | tf_op jit(solution)/shard_map/ppermute | solution.py:162
  31.4 5.5 %collective-permute-done.5 = f32[1,768]{1,0:T(1,128)S(1)} collective-permute-done((f32[1,768]{1,0:T(1,128)S(1)}, f32[1,768]{1,0:T(1,128)S(1)}, u32[]{:S(2)}, u32[]{:S(2)}) %collective-permute-start.5) | collective-permute-done | bytes 3104 | tf_op jit(solution)/shard_map/ppermute | solution.py:162
  37.0 1.4 %copy-done.5 = bf16[768,1024]{1,0:T(8,128)(2,1)S(1)} copy-done((bf16[768,1024]{1,0:T(8,128)(2,1)S(1)}, bf16[768,1024]{1,0:T(8,128)(2,1)}, u32[]{:S(2)}) %copy-start.5) | copy-done | bytes 1572888
  38.4 1.6 %copy-done.9 = bf16[1024,1024]{1,0:T(8,128)(2,1)S(1)} copy-done((bf16[1024,1024]{1,0:T(8,128)(2,1)S(1)}, bf16[1024,1024]{1,0:T(8,128)(2,1)}, u32[]{:S(2)}) %copy-start.9) | copy-done | bytes 2097176
  39.9 4.4 %early_blocks.1 = (f32[256,1024]{1,0:T(8,128)S(1)}, f32[256,1]{1,0:T(8,128)S(1)}, f32[8,128]{1,0:T(8,128)S(1)}) custom-call(bf16[1024,1024]{1,0:T(8,128)(2,1)S(1)} %copy-done.9, f32[4,768]{1,0:T(4,128)S(1)} %pad_maximum_fusion.parts, bf16[768,1024]{1,0:T(8,128)(2,1)S(1)} %copy-done.5, bf16[768,1024]{1,0:T(8,128)(2,1)S(1)} %copy-done.1, ...), custom_call_target="tpu_custom_call" | custom-call | flops 2415919104 | bytes 4718592 | tf_op jit(solution)/shard_map/early_blocks/pallas_call | solution.py:217
  46.6 2.1 %collective-permute-done.10.refs_4_ = bf16[384,1024]{1,0:T(8,128)(2,1)S(1)} collective-permute-done((bf16[384,1024]{1,0:T(8,128)(2,1)}, bf16[384,1024]{1,0:T(8,128)(2,1)S(1)}, u32[]{:S(2)}, u32[]{:S(2)}) %collective-permute-start.10) | collective-permute-done | bytes 786464 | tf_op jit(solution)/shard_map/ppermute | solution.py:162
  49.9 1.4 %copy-done.6 = bf16[768,1024]{1,0:T(8,128)(2,1)S(1)} copy-done((bf16[768,1024]{1,0:T(8,128)(2,1)S(1)}, bf16[768,1024]{1,0:T(8,128)(2,1)}, u32[]{:S(2)}) %copy-start.6) | copy-done | bytes 1572888
  51.3 1.6 %copy-done.10 = bf16[1024,1024]{1,0:T(8,128)(2,1)S(1)} copy-done((bf16[1024,1024]{1,0:T(8,128)(2,1)S(1)}, bf16[1024,1024]{1,0:T(8,128)(2,1)}, u32[]{:S(2)}) %copy-start.10) | copy-done | bytes 2097176
  52.9 5.7 %late_blocks.1 = (bf16[256,1024]{1,0:T(8,128)(2,1)S(1)}, f32[4,256,768]{2,1,0:T(8,128)S(1)}, f32[4,768]{1,0:T(4,128)S(1)}, f32[4,768]{1,0:T(4,128)S(1)}) custom-call(bf16[1024,1024]{1,0:T(8,128)(2,1)S(1)} %copy-done.10, f32[4,768]{1,0:T(4,128)S(1)} %pad_maximum_fusion.parts, f32[256,1024]{1,0:T(8,128)S(1)} %get-tuple-element.9.total, ...), custom_call_target="tpu_custom_call" | custom-call | flops 2415919104 | bytes 1572864 | tf_op jit(solution)/shard_map/late_blocks/pallas_call | solution.py:241
  59.8 3.8 %collective-permute-start.14 = (f32[4,768]{1,0:T(4,128)S(1)}, f32[4,768]{1,0:T(4,128)S(1)}, u32[]{:S(2)}, u32[]{:S(2)}) collective-permute-start(f32[4,768]{1,0:T(4,128)S(1)} %log_add_fusion.1), channel_id=1, source_target_pairs={{0,6},{1,7},{2,4},{3,5},{4,2},{5,3},{6,0},{7,1},{8,14},{9,15},{10,... | collective-permute-start | bytes 36872 | tf_op jit(solution)/shard_map/ppermute | solution.py:162
  65.4 2.9 %collective-permute-done.13 = f32[4,768]{1,0:T(4,128)S(1)} collective-permute-done((f32[4,768]{1,0:T(4,128)S(1)}, f32[4,768]{1,0:T(4,128)S(1)}, u32[]{:S(2)}, u32[]{:S(2)}) %collective-permute-start.13) | collective-permute-done | bytes 12320 | tf_op jit(solution)/shard_map/ppermute | solution.py:162
  68.3 2.5 %collective-permute-start.17 = (f32[4,768]{1,0:T(4,128)S(1)}, f32[4,768]{1,0:T(4,128)S(1)}, u32[]{:S(2)}, u32[]{:S(2)}) collective-permute-start(f32[4,768]{1,0:T(4,128)S(1)} %log_add_fusion), channel_id=1, source_target_pairs={{0,24},{1,25},{2,26},{3,27},{4,28},{5,29},{6,30},{7,31},{8,16},{9,... | collective-permute-start | bytes 36872 | tf_op jit(solution)/shard_map/ppermute | solution.py:162
  73.0 1.6 %collective-permute-done.16 = f32[4,768]{1,0:T(4,128)S(1)} collective-permute-done((f32[4,768]{1,0:T(4,128)S(1)}, f32[4,768]{1,0:T(4,128)S(1)}, u32[]{:S(2)}, u32[]{:S(2)}) %collective-permute-start.16) | collective-permute-done | bytes 12320 | tf_op jit(solution)/shard_map/ppermute | solution.py:162
  75.1 4.2 %last_iteration.1 = (bf16[256,1024]{1,0:T(8,128)(2,1)}, f32[768]{0:T(1024)}) custom-call(bf16[256,1024]{1,0:T(8,128)(2,1)S(1)} %get-tuple-element.12.old_ref, f32[4,256,768]{2,1,0:T(8,128)S(1)} %get-tuple-element.13.expo_ref, f32[4,768]{1,0:T(4,128)S(1)} %get-tuple-element.14.peak_ref, f32[1,4,768]{2,1,0:T(4,128)S(1)} %add_bitcast_fusion.parts, ...), custom_call_target="tpu_custom_call" | custom-call | flops 1610612736 | bytes 524288 | tf_op jit(solution)/shard_map/last_iteration/pallas_call | solution.py:266
  (51 shorter events, 15.5 us)
Async XLA Ops:
  0.6 21.6 %collective-permute-start.7 = (bf16[768,1024]{1,0:T(8,128)(2,1)}, bf16[768,1024]{1,0:T(8,128)(2,1)S(1)}, u32[]{:S(2)}, u32[]{:S(2)}) collective-permute-start(bf16[768,1024]{1,0:T(8,128)(2,1)} %refs_0_.5), channel_id=1, source_target_pairs={{0,8},{1,17},{2,10},{3,19},{4,12},{5,21},{6,14},{7,23},{8,0},{9,25... | collective-permute-start | bytes 4718600 | tf_op jit(solution)/shard_map/ppermute | solution.py:162
  5.1 1.6 %copy-start.8 = (bf16[1024,1024]{1,0:T(8,128)(2,1)S(1)}, bf16[1024,1024]{1,0:T(8,128)(2,1)}, u32[]{:S(2)}) copy-start(bf16[1024,1024]{1,0:T(8,128)(2,1)} %c_ref.5) | copy-start | bytes 6291460
  9.1 1.2 %collective-permute-start = (f32[1,768]{1,0:T(1,128)S(1)}, f32[1,768]{1,0:T(1,128)S(1)}, u32[]{:S(2)}, u32[]{:S(2)}) collective-permute-start(f32[1,768]{1,0:T(1,128)S(1)} %partial_lse.1), channel_id=1, source_target_pairs={{0,1},{1,0},{2,3},{3,2},{4,5},{5,4},{6,7},{7,6},{8,9},{9,8},{10,11... | collective-permute-start | bytes 9224 | tf_op jit(solution)/shard_map/ppermute | solution.py:162
  10.3 5.5 %collective-permute-start.3 = (f32[1,768]{1,0:T(1,128)S(1)}, f32[1,768]{1,0:T(1,128)S(1)}, u32[]{:S(2)}, u32[]{:S(2)}) collective-permute-start(f32[1,768]{1,0:T(1,128)S(1)} %log_add_fusion.3), channel_id=1, source_target_pairs={{0,6},{1,7},{2,4},{3,5},{4,2},{5,3},{6,0},{7,1},{8,14},{9,15},{10,... | collective-permute-start | bytes 9224 | tf_op jit(solution)/shard_map/ppermute | solution.py:162
  14.0 4.5 %collective-permute-start.2 = (f32[1,768]{1,0:T(1,128)S(1)}, f32[1,768]{1,0:T(1,128)S(1)}, u32[]{:S(2)}, u32[]{:S(2)}) collective-permute-start(f32[1,768]{1,0:T(1,128)S(1)} %log_add_fusion.3), channel_id=1, source_target_pairs={{0,4},{1,5},{2,6},{3,7},{4,0},{5,1},{6,2},{7,3},{8,12},{9,13},{10,... | collective-permute-start | bytes 9224 | tf_op jit(solution)/shard_map/ppermute | solution.py:162
  14.0 4.5 %collective-permute-start.1 = (f32[1,768]{1,0:T(1,128)S(1)}, f32[1,768]{1,0:T(1,128)S(1)}, u32[]{:S(2)}, u32[]{:S(2)}) collective-permute-start(f32[1,768]{1,0:T(1,128)S(1)} %log_add_fusion.3), channel_id=1, source_target_pairs={{0,2},{1,3},{2,0},{3,1},{4,6},{5,7},{6,4},{7,5},{8,10},{9,11},{10,... | collective-permute-start | bytes 9224 | tf_op jit(solution)/shard_map/ppermute | solution.py:162
  23.4 3.4 %copy-start.12 = (f32[1,768]{1,0:T(1,128)S(1)}, f32[1,768]{1,0:T(1,128)}, u32[]{:S(2)}) copy-start(f32[1,768]{1,0:T(1,128)} %log_add_fusion.2.refs_1_) | copy-start | bytes 9220
  23.4 13.5 %copy-start.1 = (bf16[768,1024]{1,0:T(8,128)(2,1)S(1)}, bf16[768,1024]{1,0:T(8,128)(2,1)}, u32[]{:S(2)}) copy-start(bf16[768,1024]{1,0:T(8,128)(2,1)} %after.2.refs_1_) | copy-start | bytes 4718596
  23.4 13.5 %collective-permute-start.8 = (bf16[768,1024]{1,0:T(8,128)(2,1)}, bf16[768,1024]{1,0:T(8,128)(2,1)}, u32[]{:S(2)}, u32[]{:S(2)}) collective-permute-start(bf16[768,1024]{1,0:T(8,128)(2,1)} %after.2.refs_1_), channel_id=1, source_target_pairs={{0,1},{1,0},{2,3},{3,2},{4,5},{5,4},{6,7},{7,6},{8,9},{9,8},{10,11... | collective-permute-start | bytes 4718600 | tf_op jit(solution)/shard_map/ppermute | solution.py:162
  24.7 20.3 %collective-permute-start.9 = (bf16[384,1024]{1,0:T(8,128)(2,1)S(1)}, bf16[384,1024]{1,0:T(8,128)(2,1)S(1)}, u32[]{:S(2)}, u32[]{:S(2)}) collective-permute-start(bf16[384,1024]{1,0:T(8,128)(2,1)S(1)} %constant_dynamic-slice_fusion), channel_id=1, source_target_pairs={{0,16},{1,9},{2,18},{3,11},{4,20},{5,13},{6,22},{7,15},{8,24},{9,1... | collective-permute-start | bytes 2359304 | tf_op jit(solution)/shard_map/ppermute | solution.py:162
  26.8 4.6 %collective-permute-start.6 = (f32[1,768]{1,0:T(1,128)S(1)}, f32[1,768]{1,0:T(1,128)S(1)}, u32[]{:S(2)}, u32[]{:S(2)}) collective-permute-start(f32[1,768]{1,0:T(1,128)S(1)} %copy-done.12), channel_id=1, source_target_pairs={{0,24},{1,25},{2,26},{3,27},{4,28},{5,29},{6,30},{7,31},{8,16},{9,... | collective-permute-start | bytes 9224 | tf_op jit(solution)/shard_map/ppermute | solution.py:162
  28.3 8.6 %collective-permute-start.5 = (f32[1,768]{1,0:T(1,128)S(1)}, f32[1,768]{1,0:T(1,128)S(1)}, u32[]{:S(2)}, u32[]{:S(2)}) collective-permute-start(f32[1,768]{1,0:T(1,128)S(1)} %copy-done.12), channel_id=1, source_target_pairs={{0,16},{1,9},{2,18},{3,11},{4,20},{5,13},{6,22},{7,15},{8,24},{9,1... | collective-permute-start | bytes 9224 | tf_op jit(solution)/shard_map/ppermute | solution.py:162
  29.8 7.1 %collective-permute-start.4 = (f32[1,768]{1,0:T(1,128)S(1)}, f32[1,768]{1,0:T(1,128)S(1)}, u32[]{:S(2)}, u32[]{:S(2)}) collective-permute-start(f32[1,768]{1,0:T(1,128)S(1)} %copy-done.12), channel_id=1, source_target_pairs={{0,8},{1,17},{2,10},{3,19},{4,12},{5,21},{6,14},{7,23},{8,0},{9,25... | collective-permute-start | bytes 9224 | tf_op jit(solution)/shard_map/ppermute | solution.py:162
  38.4 1.6 %copy-start.9 = (bf16[1024,1024]{1,0:T(8,128)(2,1)S(1)}, bf16[1024,1024]{1,0:T(8,128)(2,1)}, u32[]{:S(2)}) copy-start(bf16[1024,1024]{1,0:T(8,128)(2,1)} %c_ref.5) | copy-start | bytes 6291460
  45.9 2.8 %collective-permute-start.10 = (bf16[384,1024]{1,0:T(8,128)(2,1)}, bf16[384,1024]{1,0:T(8,128)(2,1)S(1)}, u32[]{:S(2)}, u32[]{:S(2)}) collective-permute-start(bf16[384,1024]{1,0:T(8,128)(2,1)} %after.3.refs_3_), channel_id=1, source_target_pairs={{0,1},{1,0},{2,3},{3,2},{4,5},{5,4},{6,7},{7,6},{8,9},{9,8},{10,11... | collective-permute-start | bytes 2359304 | tf_op jit(solution)/shard_map/ppermute | solution.py:162
  51.3 1.6 %copy-start.10 = (bf16[1024,1024]{1,0:T(8,128)(2,1)S(1)}, bf16[1024,1024]{1,0:T(8,128)(2,1)}, u32[]{:S(2)}) copy-start(bf16[1024,1024]{1,0:T(8,128)(2,1)} %c_ref.5) | copy-start | bytes 6291460
  52.9 22.2 %copy-start.7 = (bf16[768,1024]{1,0:T(8,128)(2,1)S(1)}, bf16[768,1024]{1,0:T(8,128)(2,1)}, u32[]{:S(2)}) copy-start(bf16[768,1024]{1,0:T(8,128)(2,1)} %refs_0_.5) | copy-start | bytes 4718596
  58.5 1.3 %collective-permute-start.11 = (f32[4,768]{1,0:T(4,128)S(1)}, f32[4,768]{1,0:T(4,128)S(1)}, u32[]{:S(2)}, u32[]{:S(2)}) collective-permute-start(f32[4,768]{1,0:T(4,128)S(1)} %get-tuple-element.15), channel_id=1, source_target_pairs={{0,1},{1,0},{2,3},{3,2},{4,5},{5,4},{6,7},{7,6},{8,9},{9,8},{10,11... | collective-permute-start | bytes 36872 | tf_op jit(solution)/shard_map/ppermute | solution.py:162
  59.8 5.6 %collective-permute-start.14 = (f32[4,768]{1,0:T(4,128)S(1)}, f32[4,768]{1,0:T(4,128)S(1)}, u32[]{:S(2)}, u32[]{:S(2)}) collective-permute-start(f32[4,768]{1,0:T(4,128)S(1)} %log_add_fusion.1), channel_id=1, source_target_pairs={{0,6},{1,7},{2,4},{3,5},{4,2},{5,3},{6,0},{7,1},{8,14},{9,15},{10,... | collective-permute-start | bytes 36872 | tf_op jit(solution)/shard_map/ppermute | solution.py:162
  63.7 4.6 %collective-permute-start.13 = (f32[4,768]{1,0:T(4,128)S(1)}, f32[4,768]{1,0:T(4,128)S(1)}, u32[]{:S(2)}, u32[]{:S(2)}) collective-permute-start(f32[4,768]{1,0:T(4,128)S(1)} %log_add_fusion.1), channel_id=1, source_target_pairs={{0,4},{1,5},{2,6},{3,7},{4,0},{5,1},{6,2},{7,3},{8,12},{9,13},{10,... | collective-permute-start | bytes 36872 | tf_op jit(solution)/shard_map/ppermute | solution.py:162
  63.7 4.6 %collective-permute-start.12 = (f32[4,768]{1,0:T(4,128)S(1)}, f32[4,768]{1,0:T(4,128)S(1)}, u32[]{:S(2)}, u32[]{:S(2)}) collective-permute-start(f32[4,768]{1,0:T(4,128)S(1)} %log_add_fusion.1), channel_id=1, source_target_pairs={{0,2},{1,3},{2,0},{3,1},{4,6},{5,7},{6,4},{7,5},{8,10},{9,11},{10,... | collective-permute-start | bytes 36872 | tf_op jit(solution)/shard_map/ppermute | solution.py:162
  68.3 4.7 %collective-permute-start.17 = (f32[4,768]{1,0:T(4,128)S(1)}, f32[4,768]{1,0:T(4,128)S(1)}, u32[]{:S(2)}, u32[]{:S(2)}) collective-permute-start(f32[4,768]{1,0:T(4,128)S(1)} %log_add_fusion), channel_id=1, source_target_pairs={{0,24},{1,25},{2,26},{3,27},{4,28},{5,29},{6,30},{7,31},{8,16},{9,... | collective-permute-start | bytes 36872 | tf_op jit(solution)/shard_map/ppermute | solution.py:162
  70.8 3.7 %collective-permute-start.16 = (f32[4,768]{1,0:T(4,128)S(1)}, f32[4,768]{1,0:T(4,128)S(1)}, u32[]{:S(2)}, u32[]{:S(2)}) collective-permute-start(f32[4,768]{1,0:T(4,128)S(1)} %log_add_fusion), channel_id=1, source_target_pairs={{0,16},{1,17},{2,18},{3,19},{4,20},{5,21},{6,22},{7,23},{8,24},{9,... | collective-permute-start | bytes 36872 | tf_op jit(solution)/shard_map/ppermute | solution.py:162
  71.3 3.7 %collective-permute-start.15 = (f32[4,768]{1,0:T(4,128)S(1)}, f32[4,768]{1,0:T(4,128)S(1)}, u32[]{:S(2)}, u32[]{:S(2)}) collective-permute-start(f32[4,768]{1,0:T(4,128)S(1)} %log_add_fusion), channel_id=1, source_target_pairs={{0,8},{1,9},{2,10},{3,11},{4,12},{5,13},{6,14},{7,15},{8,0},{9,1},... | collective-permute-start | bytes 36872 | tf_op jit(solution)/shard_map/ppermute | solution.py:162
  (7 other events, 8.1 us)

commit v6 on v5

v6 whole, which is shorter than its diff:
```python
import functools
import math

import jax
import jax.numpy as jnp
from jax import lax
from jax.experimental import pallas as pl
from jax.experimental.pallas import tpu as pltpu
from jax.sharding import PartitionSpec as P

BETA = 3.0
BOTH = ("item", "cent")
MIB = 1024 * 1024
NT = (((1,), (1,)), ((), ()))
NN = (((1,), (0,)), ((), ()))


def scores(rows, vectors, scale):
    raw = lax.dot_general(rows, vectors, NT, preferred_element_type=jnp.float32)
    sqnorm = jnp.sum(jnp.square(rows.astype(jnp.float32)), axis=1, keepdims=True)
    return scale * (raw - 0.5 * sqnorm)


def merge(parts):
    peak = functools.reduce(jnp.maximum, parts)
    terms = [jnp.exp(p - peak) for p in parts]
    while len(terms) > 1:
        terms = [sum(terms[i : i + 2]) for i in range(0, len(terms), 2)]
    return peak + jnp.log(terms[0])


def in_hbm(value):
    return pltpu.with_memory_space_constraint(value, pltpu.HBM)


def in_vmem(value):
    return pltpu.with_memory_space_constraint(value, pltpu.VMEM)


def partial_kernel(scale, rows, v_hbm, c_hbm, out_ref, v_ref, own_ref, c_ref, sems):
    nv, k, own = v_ref.shape[0], c_ref.shape[0], own_ref.shape[0]
    start = pl.multiple_of(lax.axis_index("item") * own, own)
    own_copy = pltpu.make_async_copy(c_hbm.at[pl.ds(start, own), :], own_ref, sems.at[0])
    third = nv // 3
    v_copies = [
        pltpu.make_async_copy(
            v_hbm.at[pl.ds(i * third, third), :], v_ref.at[pl.ds(i * third, third), :], sems.at[1 + i]
        )
        for i in range(3)
    ]
    c_copies = [
        pltpu.make_async_copy(c_hbm.at[pl.ds(i * rows, rows), :], c_ref.at[pl.ds(i * rows, rows), :], sems.at[4 + i])
        for i in range(k // rows)
    ]
    for copy in v_copies + c_copies + [own_copy]:
        copy.start()
    for copy in v_copies:
        copy.wait()
    parts = []
    for i, copy in enumerate(c_copies):
        copy.wait()
        logits = scores(c_ref[i * rows : (i + 1) * rows, :], v_ref[...], scale)
        peak = jnp.max(logits, axis=0, keepdims=True)
        parts.append(peak + jnp.log(jnp.sum(jnp.exp(logits - peak), axis=0, keepdims=True)))
    own_copy.wait()
    out_ref[...] = merge(parts)


def partial(vectors, centroids, own, scale):
    nv, dim = vectors.shape
    k = centroids.shape[0]
    rows = min(256, k)
    vmem = pl.BlockSpec(memory_space=pltpu.VMEM)
    hbm = pl.BlockSpec(memory_space=pl.ANY)
    return pl.pallas_call(
        functools.partial(partial_kernel, scale, rows),
        in_specs=[hbm, hbm],
        out_specs=[vmem] * 3,
        out_shape=[
            jax.ShapeDtypeStruct((1, nv), jnp.float32),
            pltpu.VMEM((nv, dim), jnp.bfloat16),
            pltpu.VMEM((own, dim), jnp.bfloat16),
        ],
        scratch_shapes=[pltpu.VMEM((k, dim), jnp.bfloat16), pltpu.SemaphoreType.DMA((4 + k // rows,))],
        compiler_params=pltpu.CompilerParams(vmem_limit_bytes=12 * MIB),
        cost_estimate=pl.CostEstimate(
            flops=2 * nv * k * dim, bytes_accessed=2 * (nv + k) * dim, transcendentals=nv * k
        ),
        name="partial_lse",
    )(in_hbm(vectors), in_hbm(centroids))


def core_index():
    return lax.rem(lax.axis_index("cent"), 2)


def index_of(plan, place):
    if not plan["exchange"]:
        return place
    mask = (0, 1 + core_index(), 2 - core_index(), 3)[place]
    return lax.axis_index("item") ^ mask


def fetches(nv, blocks, pieces, table, sems):
    result = []
    for place, entries in enumerate(blocks):
        copies = []
        for piece, start, mine, rows in entries:
            lead = 0 if mine is None else (core_index() if mine else 1 - core_index()) * (nv // 2)
            dst = pl.multiple_of(place * nv + lead, 64)
            src = pieces[piece].at[pl.ds(start, rows), :]
            copies.append(pltpu.make_async_copy(src, table.at[pl.ds(dst, rows), :], sems.at[len(copies), place]))
        result.append(copies)
    for copies in result:
        for copy in copies:
            copy.start()
    return result


def weigh(resp, vectors):
    term = lax.dot_general(resp, vectors, NN, preferred_element_type=jnp.float32)
    return term, jnp.sum(resp.astype(jnp.float32), axis=1, keepdims=True)


def updated(total, mass, old):
    return ((total + old.astype(jnp.float32)) / (mass + 1.0)).astype(jnp.bfloat16)


def absorb(own, vectors, lse, scale, total, mass):
    resp = jnp.exp(scores(own, vectors, scale) - lse).astype(jnp.bfloat16)
    term, weight = weigh(resp, vectors)
    return (term, weight) if total is None else (total + term, mass + weight)


def early_kernel(plan, scale, own_ref, parts, home, *refs):
    pieces, (table, total, mass, done, sems) = refs[:-5], refs[-5:]
    nv = home.shape[0]
    copies = fetches(nv, plan["early"], pieces, table, sems)
    done[...] = jnp.zeros_like(done)
    own = own_ref[...]
    sums = weights = None
    if plan["home"]:
        sums, weights = absorb(own, home[...], parts[pl.ds(0, 1), :], scale, sums, weights)
    for i, block in enumerate(copies):
        for copy in block:
            copy.wait()
        place = i + plan["home"]
        vectors = table[pl.ds(i * nv, nv), :]
        sums, weights = absorb(own, vectors, parts[pl.ds(place, 1), :], scale, sums, weights)
    total[...], mass[...] = sums, weights


def vectors_of(plan, place, home, tables):
    nv = home.shape[0]
    if place < plan["home"]:
        return home[...]
    place -= plan["home"]
    early = len(plan["early"])
    if place < early:
        return tables[0][pl.ds(place * nv, nv), :]
    return tables[1][pl.ds((place - early) * nv, nv), :]


def late_kernel(plan, scale, own_ref, parts, total, mass, home, table, *refs):
    n = plan["n_late"]
    pieces, refs = refs[:n], refs[n:]
    new_ref, expo_ref, peak_ref, part_ref = refs[:4]
    tables = [table]
    sums, weights = total[...], mass[...]
    own = own_ref[...]
    if n:
        late, sems = refs[4:]
        tables.append(late)
        copies = fetches(home.shape[0], plan["late"], pieces, late, sems)
        for i, block in enumerate(copies):
            for copy in block:
                copy.wait()
            place = plan["places"] - len(copies) + i
            vectors = vectors_of(plan, place, home, tables)
            sums, weights = absorb(own, vectors, parts[pl.ds(place, 1), :], scale, sums, weights)
    new_ref[...] = updated(sums, weights, own)
    for place in range(plan["places"]):
        logits = scores(new_ref[...], vectors_of(plan, place, home, tables), scale)
        peak = jnp.max(logits, axis=0, keepdims=True)
        expo = jnp.exp(logits - peak)
        expo_ref[place] = expo
        peak_ref[pl.ds(place, 1), :] = peak
        part_ref[pl.ds(index_of(plan, place), 1), :] = peak + jnp.log(jnp.sum(expo, axis=0, keepdims=True))


def last_kernel(plan, old_ref, expo_ref, peak_ref, parts, home, *refs):
    tables, (new_ref, norm_ref, lse_ref) = refs[:-3], refs[-3:]
    lse_ref[...] = merge([parts[i] for i in range(parts.shape[0])])
    norm_ref[...] = lse_ref[pl.ds(lax.axis_index("item"), 1), :].reshape(norm_ref.shape)
    total = mass = None
    for place in range(plan["places"]):
        factor = jnp.exp(peak_ref[pl.ds(place, 1), :] - lse_ref[pl.ds(index_of(plan, place), 1), :])
        resp = (expo_ref[place] * factor).astype(jnp.bfloat16)
        term, weight = weigh(resp, vectors_of(plan, place, home, tables))
        total = term if total is None else total + term
        mass = weight if mass is None else mass + weight
    new_ref[...] = updated(total, mass, old_ref[...])


def send(value, items, cents, item_mask, cent_mask=0):
    masks = item_mask if isinstance(item_mask, tuple) else (item_mask, item_mask)
    pairs = [
        (i * cents + c, (i ^ masks[c % 2]) * cents + (c ^ cent_mask)) for i in range(items) for c in range(cents)
    ]
    return lax.ppermute(value, BOTH, pairs)


def merge_cent(part, go):
    part = merge([part, go(part, 0, 1)])
    return merge([part] + [go(part, 0, mask) for mask in (2, 4, 6)])


def after(value, *others):
    vmem = pl.BlockSpec(memory_space=pltpu.VMEM)
    return pl.pallas_call(
        lambda *refs: None,
        in_specs=[vmem] + [pl.BlockSpec(memory_space=pl.ANY)] * len(others),
        out_specs=vmem,
        out_shape=pltpu.VMEM(value.shape, value.dtype),
        input_output_aliases={0: 0},
        name="after",
    )(in_vmem(value), *others)


def shards(vectors, centroids):
    items, cents = lax.axis_size("item"), lax.axis_size("cent")
    nv, dim = vectors.shape
    rows = centroids.shape[0] // items
    scale = BETA / math.sqrt(dim)

    def go(value, item_mask, cent_mask=0):
        return send(value, items, cents, item_mask, cent_mask)

    small = items == 4 and cents == 8
    if small:
        half = nv // 2
        core = core_index()
        first = go(lax.dynamic_slice_in_dim(vectors, core * half, half, 0), (1, 2))
        second = go(lax.dynamic_slice_in_dim(vectors, (1 - core) * half, half, 0), (1, 2))
        part, home, own = partial(vectors, centroids, rows, scale)
        lse = merge_cent(part, go)
        parts = jnp.concatenate([lse, go(lse, (1, 2)), go(lse, (2, 1)), go(lse, 3)], axis=0)
        first, second = after(first, parts), after(second, parts)
        far = go(first, (2, 1))
        early = [first, second, go(first, 0, 1), go(second, 0, 1)]
        early_blocks = [[(0, 0, True, half), (1, 0, False, half)], [(2, 0, False, half), (3, 0, True, half)]]
        plan = dict(exchange=True, home=1, places=4)
    else:
        part, home, own = partial(vectors, centroids, rows, scale)
        early = [lax.all_gather(vectors, "item", axis=0, tiled=True)]
        early_blocks = [[(0, i * nv, None, nv)] for i in range(items)]
        parts = lax.all_gather(part, "cent", axis=0, tiled=False)
        parts = lax.all_gather(merge([parts[i] for i in range(cents)]), "item", axis=0, tiled=True)
        plan = dict(exchange=False, home=0, places=items)
    plan["early"] = early_blocks

    vmem = pl.BlockSpec(memory_space=pltpu.VMEM)
    hbm = pl.BlockSpec(memory_space=pl.ANY)
    n_early = len(early_blocks)
    flops = 2 * nv * rows * dim
    params = pltpu.CompilerParams(vmem_limit_bytes=16 * MIB)
    table, total, mass, done = pl.pallas_call(
        functools.partial(early_kernel, plan, scale),
        in_specs=[vmem] * 3 + [hbm] * len(early),
        out_specs=[vmem] * 4,
        out_shape=[
            pltpu.VMEM((n_early * nv, dim), jnp.bfloat16),
            pltpu.VMEM((rows, dim), jnp.float32),
            pltpu.VMEM((rows, 1), jnp.float32),
            jax.ShapeDtypeStruct((8, 128), jnp.float32),
        ],
        scratch_shapes=[pltpu.SemaphoreType.DMA((max(len(b) for b in early_blocks), n_early))],
        compiler_params=params,
        cost_estimate=pl.CostEstimate(
            flops=2 * n_early * flops, bytes_accessed=2 * n_early * nv * dim, transcendentals=n_early * nv * rows
        ),
        name="early_blocks",
    )(in_vmem(own), parts, in_vmem(home), *early)

    late, late_blocks = [], []
    if small:
        far = after(far, done)
        late = [far, go(far, 0, 1)]
        late_blocks = [[(0, 0, True, half), (1, 0, False, half)]]
    plan["late"], plan["n_late"] = late_blocks, len(late)
    n_late = len(late_blocks)
    late_out = [pltpu.VMEM((n_late * nv, dim), jnp.bfloat16)] if n_late else []
    fresh, expo, peak, part, *tables = pl.pallas_call(
        functools.partial(late_kernel, plan, scale),
        in_specs=[vmem] * 6 + [hbm] * len(late),
        out_specs=[vmem] * (4 + len(late_out)),
        out_shape=[
            pltpu.VMEM((rows, dim), jnp.bfloat16),
            pltpu.VMEM((items, rows, nv), jnp.float32),
            pltpu.VMEM((items, nv), jnp.float32),
            pltpu.VMEM((items, nv), jnp.float32),
        ]
        + late_out,
        scratch_shapes=[pltpu.SemaphoreType.DMA((2, n_late))] if n_late else [],
        compiler_params=params,
        cost_estimate=pl.CostEstimate(
            flops=(items + 2 * n_late) * flops,
            bytes_accessed=2 * n_late * nv * dim,
            transcendentals=(items + n_late) * nv * rows,
        ),
        name="late_blocks",
    )(in_vmem(own), parts, in_vmem(total), in_vmem(mass), in_vmem(home), in_vmem(table), *late)

    if small:
        lse = merge_cent(part, go)
        parts = merge([lse] + [go(lse, mask) for mask in (1, 2, 3)])[None]
    else:
        gathered = lax.all_gather(part, "cent", axis=0, tiled=False)
        parts = lax.all_gather(merge([gathered[i] for i in range(cents)]), "item", axis=0, tiled=False)
    result, norm = pl.pallas_call(
        functools.partial(last_kernel, plan),
        in_specs=[vmem] * (6 + len(tables)),
        out_specs=[vmem] * 2,
        out_shape=[
            jax.ShapeDtypeStruct((rows, dim), jnp.bfloat16),
            jax.ShapeDtypeStruct((nv,), jnp.float32),
        ],
        scratch_shapes=[pltpu.VMEM((items, nv), jnp.float32)],
        compiler_params=params,
        cost_estimate=pl.CostEstimate(flops=items * flops, bytes_accessed=2 * rows * dim, transcendentals=0),
        name="last_iteration",
    )(in_vmem(fresh), in_vmem(expo), in_vmem(peak), parts, in_vmem(home), in_vmem(table), *[in_vmem(t) for t in tables])
    return (result, norm)


def solution(mesh):
    in_specs = (P("item", None), P("cent", None))
    out_specs = (P(("cent", "item"), None), P("item"))
    return jax.shard_map(shards, mesh=mesh, in_specs=in_specs, out_specs=out_specs, check_vma=False)
```

time: 79.7 us -> 72.9 us (0.915)
  waiting for transfers between devices: 24.6 us -> 18.4 us
  local copies, waits for them, and re-layouts: 14.1 us -> 15.6 us
  Pallas kernels: 16.7 us -> 15.4 us
    ppermute x18 -> x20, waiting for transfers between devices: 24.6 us -> 18.4 us  [send(): return lax.ppermute(value, BOTH, pairs)]
    pallas_call x1, Pallas kernels: 5.67 us -> 3.76 us  [shards(): pl.pallas_call(functools.partial(late_kernel, plan, scale), in_specs=[vme...]
    pallas_call x4 -> x5, Pallas kernels: 6.6 us -> 7.85 us  [the longest x1 5.18 us: partial(): pl.pallas_call(functools.partial(partial_kernel, scale, rows), in_specs=[...]
    dynamic_slice x1, local copies, waits for them, and re-layouts: 1.31 us -> 2.38 us  [shards(): lax.dynamic_slice_in_dim(vectors, (1 - core) * half, half, 0)]
    ppermute x18 -> x20, starting transfers between devices: 22.3 us -> 21.6 us  [send(): return lax.ppermute(value, BOTH, pairs)]
    unnamed x26 -> x28, local copies, waits for them, and re-layouts: 12.8 us -> 13.3 us
  transfers between devices with their start and end apart: 18 -> 20, of which waited for: 13 -> 17; matrix products, arithmetic and copies ran while one was open for 2% -> 1% of each run, Pallas kernels for 9% -> 12%
where the time goes in v6:
time: 72.9 us; the launch traced here: 72.5 us
  starting transfers between devices  21.6 us (30%)
  waiting for transfers between devices  18.4 us (25%)
  local copies, waits for them, and re-layouts  15.6 us (21%)
  Pallas kernels  15.4 us (21%)
  other arithmetic  0.77 us (1%)
  between operations  0.74 us (1%)
    ppermute x20, starting transfers between devices, send(): return lax.ppermute(value, BOTH, pairs)  21.6 us
    ppermute x20, waiting for transfers between devices, send(): return lax.ppermute(value, BOTH, pairs)  18.4 us
    unnamed x28, local copies, waits for them, and re-layouts  13.3 us
    pallas_call x1, Pallas kernels, partial(): pl.pallas_call(functools.partial(partial_kernel, scale, rows), in_specs=[...  5.18 us
    pallas_call x1, Pallas kernels, shards(): pl.pallas_call(functools.partial(early_kernel, plan, scale), in_specs=[vm...  3.77 us
    pallas_call x1, Pallas kernels, shards(): pl.pallas_call(functools.partial(late_kernel, plan, scale), in_specs=[vme...  3.76 us
    pallas_call x1, Pallas kernels, shards(): pl.pallas_call(functools.partial(last_kernel, plan), in_specs=[vmem] * (6...  2.67 us
    dynamic_slice x1, local copies, waits for them, and re-layouts, shards(): lax.dynamic_slice_in_dim(vectors, (1 - core) * half, half, 0)  2.38 us
  transfers between devices with their start and end apart: 20, of which 17 were waited for; matrix products, arithmetic and copies ran while one was open for 1% of the time, Pallas kernels for 12%

profile of v6, /device:TPU:0, one launch (start us, length us, event | category | flops | bytes accessed | tf_op | source)
XLA Modules:
  0.0 72.5 jit_solution(14373819347501567476)
XLA Ops:
  0.6 2.4 %constant_dynamic-slice_fusion = (bf16[384,1024]{1,0:T(8,128)(2,1)S(1)}, bf16[384,1024]{1,0:T(8,128)(2,1)}) fusion(bf16[768,1024]{1,0:T(8,128)(2,1)} %v_hbm.1, s32[]{:T(128)S(6)} %select_n.7, s32[]{:T(128)S(6)} %select_n.6), kind=kLoop, calls=%fused_computation.10 | loop fusion | bytes 3145736 | tf_op jit(solution)/shard_map/dynamic_slice | solution.py:244
  3.0 2.9 %collective-permute-start.8 = (bf16[384,1024]{1,0:T(8,128)(2,1)S(1)}, bf16[384,1024]{1,0:T(8,128)(2,1)S(1)}, u32[]{:S(2)}, u32[]{:S(2)}) collective-permute-start(bf16[384,1024]{1,0:T(8,128)(2,1)S(1)} %get-tuple-element.26), channel_id=1, source_target_pairs={{0,8},{1,17},{2,10},{3,19},{4,12},{5,21},{6,14},{7,23},{8,0},{9,25... | collective-permute-start | bytes 2359304 | tf_op jit(solution)/shard_map/ppermute | solution.py:210
  6.0 5.2 %partial_lse.1 = (f32[1,768]{1,0:T(1,128)S(1)}, bf16[768,1024]{1,0:T(8,128)(2,1)S(1)}, bf16[256,1024]{1,0:T(8,128)(2,1)S(1)}) custom-call(bf16[768,1024]{1,0:T(8,128)(2,1)} %v_hbm.1, bf16[1024,1024]{1,0:T(8,128)(2,1)} %c_hbm.1), custom_call_target="tpu_custom_call" | custom-call | flops 1610612736 | bytes 3670016 | tf_op jit(solution)/shard_map/partial_lse/pallas_call | solution.py:75
  12.0 1.2 %collective-permute-done = f32[1,768]{1,0:T(1,128)S(1)} collective-permute-done((f32[1,768]{1,0:T(1,128)S(1)}, f32[1,768]{1,0:T(1,128)S(1)}, u32[]{:S(2)}, u32[]{:S(2)}) %collective-permute-start) | collective-permute-done | bytes 3104 | tf_op jit(solution)/shard_map/ppermute | solution.py:210
  13.2 4.2 %collective-permute-start.3 = (f32[1,768]{1,0:T(1,128)S(1)}, f32[1,768]{1,0:T(1,128)S(1)}, u32[]{:S(2)}, u32[]{:S(2)}) collective-permute-start(f32[1,768]{1,0:T(1,128)S(1)} %log_add_fusion.3), channel_id=1, source_target_pairs={{0,6},{1,7},{2,4},{3,5},{4,2},{5,3},{6,0},{7,1},{8,14},{9,15},{10,... | collective-permute-start | bytes 9224 | tf_op jit(solution)/shard_map/ppermute | solution.py:210
  18.9 2.9 %collective-permute-done.2 = f32[1,768]{1,0:T(1,128)S(1)} collective-permute-done((f32[1,768]{1,0:T(1,128)S(1)}, f32[1,768]{1,0:T(1,128)S(1)}, u32[]{:S(2)}, u32[]{:S(2)}) %collective-permute-start.2) | collective-permute-done | bytes 3104 | tf_op jit(solution)/shard_map/ppermute | solution.py:210
  21.9 2.5 %collective-permute-start.6 = (f32[1,768]{1,0:T(1,128)S(1)}, f32[1,768]{1,0:T(1,128)S(1)}, u32[]{:S(2)}, u32[]{:S(2)}) collective-permute-start(f32[1,768]{1,0:T(1,128)S(1)} %log_add_fusion.2), channel_id=1, source_target_pairs={{0,24},{1,25},{2,26},{3,27},{4,28},{5,29},{6,30},{7,31},{8,16},{9,... | collective-permute-start | bytes 9224 | tf_op jit(solution)/shard_map/ppermute | solution.py:210
  26.4 1.5 %collective-permute-done.5 = f32[1,768]{1,0:T(1,128)S(1)} collective-permute-done((f32[1,768]{1,0:T(1,128)S(1)}, f32[1,768]{1,0:T(1,128)S(1)}, u32[]{:S(2)}, u32[]{:S(2)}) %collective-permute-start.5) | collective-permute-done | bytes 3104 | tf_op jit(solution)/shard_map/ppermute | solution.py:210
  30.0 1.1 %copy-done.4 = bf16[384,1024]{1,0:T(8,128)(2,1)S(1)} copy-done((bf16[384,1024]{1,0:T(8,128)(2,1)S(1)}, bf16[384,1024]{1,0:T(8,128)(2,1)}, u32[]{:S(2)}) %copy-start.4) | copy-done | bytes 786456
  31.7 1.5 %collective-permute-start.11 = (bf16[384,1024]{1,0:T(8,128)(2,1)S(1)}, bf16[384,1024]{1,0:T(8,128)(2,1)S(1)}, u32[]{:S(2)}, u32[]{:S(2)}) collective-permute-start(bf16[384,1024]{1,0:T(8,128)(2,1)S(1)} %after.3.refs_0_), channel_id=1, source_target_pairs={{0,16},{1,9},{2,18},{3,11},{4,20},{5,13},{6,22},{7,15},{8,24},{9,1... | collective-permute-start | bytes 2359304 | tf_op jit(solution)/shard_map/ppermute | solution.py:210
  35.6 3.8 %early_blocks.1 = (bf16[1536,1024]{1,0:T(8,128)(2,1)S(1)}, f32[256,1024]{1,0:T(8,128)S(1)}, f32[256,1]{1,0:T(8,128)S(1)}, f32[8,128]{1,0:T(8,128)S(1)}) custom-call(bf16[256,1024]{1,0:T(8,128)(2,1)S(1)} %copy-done.12, f32[4,768]{1,0:T(4,128)S(1)} %copy-done.7, bf16[768,1024]{1,0:T(8,128)(2,1)S(1)} %get-tuple-element.16.home, ...), custom_call_target="tpu_custom_call" | custom-call | flops 1610612736 | bytes 3145728 | tf_op jit(solution)/shard_map/early_blocks/pallas_call | solution.py:267
  39.4 1.6 %copy-done = bf16[1536,1024]{1,0:T(8,128)(2,1)} copy-done((bf16[1536,1024]{1,0:T(8,128)(2,1)}, bf16[1536,1024]{1,0:T(8,128)(2,1)S(1)}, u32[]{:S(2)}) %copy-start) | copy-done | bytes 3145752
  44.6 1.1 %copy-done.6 = bf16[384,1024]{1,0:T(8,128)(2,1)S(1)} copy-done((bf16[384,1024]{1,0:T(8,128)(2,1)S(1)}, bf16[384,1024]{1,0:T(8,128)(2,1)}, u32[]{:S(2)}) %copy-start.6) | copy-done | bytes 786456
  45.7 2.3 %collective-permute-done.12.refs_1_ = bf16[384,1024]{1,0:T(8,128)(2,1)S(1)} collective-permute-done((bf16[384,1024]{1,0:T(8,128)(2,1)S(1)}, bf16[384,1024]{1,0:T(8,128)(2,1)S(1)}, u32[]{:S(2)}, u32[]{:S(2)}) %collective-permute-start.12) | collective-permute-done | bytes 786464 | tf_op jit(solution)/shard_map/ppermute | solution.py:210
  48.0 1.9 %copy-done.1 = bf16[1536,1024]{1,0:T(8,128)(2,1)S(1)} copy-done((bf16[1536,1024]{1,0:T(8,128)(2,1)S(1)}, bf16[1536,1024]{1,0:T(8,128)(2,1)}, u32[]{:S(2)}) %copy-start.1) | copy-done | bytes 3145752
  49.9 1.2 %copy-done.10 = f32[256,1024]{1,0:T(8,128)S(1)} copy-done((f32[256,1024]{1,0:T(8,128)S(1)}, f32[256,1024]{1,0:T(8,128)}, u32[]{:S(2)}) %copy-start.10) | copy-done | bytes 1048600
  52.1 3.8 %late_blocks.1 = (bf16[256,1024]{1,0:T(8,128)(2,1)S(1)}, f32[4,256,768]{2,1,0:T(8,128)S(1)}, f32[4,768]{1,0:T(4,128)S(1)}, f32[4,768]{1,0:T(4,128)S(1)}, bf16[768,1024]{1,0:T(8,128)(2,1)S(1)}) custom-call(bf16[256,1024]{1,0:T(8,128)(2,1)S(1)} %copy-done.13, f32[4,768]{1,0:T(4,128)S(1)} %copy-done.7, f32[256,1024]{1,0:T(8,128)S(1)} %copy-done.10, ...), custom_call_target="tpu_custom_call" | custom-call | flops 2415919104 | bytes 1572864 | tf_op jit(solution)/shard_map/late_blocks/pallas_call | solution.py:293
  57.2 1.5 %collective-permute-start.16 = (f32[4,768]{1,0:T(4,128)S(1)}, f32[4,768]{1,0:T(4,128)S(1)}, u32[]{:S(2)}, u32[]{:S(2)}) collective-permute-start(f32[4,768]{1,0:T(4,128)S(1)} %log_add_fusion.1), channel_id=1, source_target_pairs={{0,6},{1,7},{2,4},{3,5},{4,2},{5,3},{6,0},{7,1},{8,14},{9,15},{10,... | collective-permute-start | bytes 36872 | tf_op jit(solution)/shard_map/ppermute | solution.py:210
  59.3 2.3 %collective-permute-start.14 = (f32[4,768]{1,0:T(4,128)S(1)}, f32[4,768]{1,0:T(4,128)S(1)}, u32[]{:S(2)}, u32[]{:S(2)}) collective-permute-start(f32[4,768]{1,0:T(4,128)S(1)} %log_add_fusion.1), channel_id=1, source_target_pairs={{0,2},{1,3},{2,0},{3,1},{4,6},{5,7},{6,4},{7,5},{8,10},{9,11},{10,... | collective-permute-start | bytes 36872 | tf_op jit(solution)/shard_map/ppermute | solution.py:210
  61.6 1.2 %collective-permute-done.16 = f32[4,768]{1,0:T(4,128)S(1)} collective-permute-done((f32[4,768]{1,0:T(4,128)S(1)}, f32[4,768]{1,0:T(4,128)S(1)}, u32[]{:S(2)}, u32[]{:S(2)}) %collective-permute-start.16) | collective-permute-done | bytes 12320 | tf_op jit(solution)/shard_map/ppermute | solution.py:210
  63.5 1.6 %collective-permute-start.19 = (f32[4,768]{1,0:T(4,128)S(1)}, f32[4,768]{1,0:T(4,128)S(1)}, u32[]{:S(2)}, u32[]{:S(2)}) collective-permute-start(f32[4,768]{1,0:T(4,128)S(1)} %log_add_fusion), channel_id=1, source_target_pairs={{0,24},{1,25},{2,26},{3,27},{4,28},{5,29},{6,30},{7,31},{8,16},{9,... | collective-permute-start | bytes 36872 | tf_op jit(solution)/shard_map/ppermute | solution.py:210
  65.0 1.1 %collective-permute-start.18 = (f32[4,768]{1,0:T(4,128)S(1)}, f32[4,768]{1,0:T(4,128)S(1)}, u32[]{:S(2)}, u32[]{:S(2)}) collective-permute-start(f32[4,768]{1,0:T(4,128)S(1)} %log_add_fusion), channel_id=1, source_target_pairs={{0,16},{1,17},{2,18},{3,19},{4,20},{5,21},{6,22},{7,23},{8,24},{9,... | collective-permute-start | bytes 36872 | tf_op jit(solution)/shard_map/ppermute | solution.py:210
  67.0 1.1 %collective-permute-done.19 = f32[4,768]{1,0:T(4,128)S(1)} collective-permute-done((f32[4,768]{1,0:T(4,128)S(1)}, f32[4,768]{1,0:T(4,128)S(1)}, u32[]{:S(2)}, u32[]{:S(2)}) %collective-permute-start.19) | collective-permute-done | bytes 12320 | tf_op jit(solution)/shard_map/ppermute | solution.py:210
  69.8 2.7 %last_iteration.1 = (bf16[256,1024]{1,0:T(8,128)(2,1)}, f32[768]{0:T(1024)}) custom-call(bf16[256,1024]{1,0:T(8,128)(2,1)S(1)} %get-tuple-element.21.old_ref, f32[4,256,768]{2,1,0:T(8,128)S(1)} %get-tuple-element.22.expo_ref, f32[4,768]{1,0:T(4,128)S(1)} %get-tuple-element.23.peak_ref, f32[1,4,768]{2,1,0:T(4,128)S(1)} %add_bitcast_fusion.parts, ...), custom_call_target="tpu_custom_call" | custom-call | flops 1610612736 | bytes 524288 | tf_op jit(solution)/shard_map/last_iteration/pallas_call | solution.py:320
  (58 shorter events, 19.2 us)
Async XLA Ops:
  3.0 26.1 %collective-permute-start.8 = (bf16[384,1024]{1,0:T(8,128)(2,1)S(1)}, bf16[384,1024]{1,0:T(8,128)(2,1)S(1)}, u32[]{:S(2)}, u32[]{:S(2)}) collective-permute-start(bf16[384,1024]{1,0:T(8,128)(2,1)S(1)} %get-tuple-element.26), channel_id=1, source_target_pairs={{0,8},{1,17},{2,10},{3,19},{4,12},{5,21},{6,14},{7,23},{8,0},{9,25... | collective-permute-start | bytes 2359304 | tf_op jit(solution)/shard_map/ppermute | solution.py:210
  6.0 25.2 %collective-permute-start.7 = (bf16[384,1024]{1,0:T(8,128)(2,1)}, bf16[384,1024]{1,0:T(8,128)(2,1)S(1)}, u32[]{:S(2)}, u32[]{:S(2)}) collective-permute-start(bf16[384,1024]{1,0:T(8,128)(2,1)} %get-tuple-element.27), channel_id=1, source_target_pairs={{0,8},{1,17},{2,10},{3,19},{4,12},{5,21},{6,14},{7,23},{8,0},{9,25... | collective-permute-start | bytes 2359304 | tf_op jit(solution)/shard_map/ppermute | solution.py:210
  12.0 1.2 %collective-permute-start = (f32[1,768]{1,0:T(1,128)S(1)}, f32[1,768]{1,0:T(1,128)S(1)}, u32[]{:S(2)}, u32[]{:S(2)}) collective-permute-start(f32[1,768]{1,0:T(1,128)S(1)} %get-tuple-element.15), channel_id=1, source_target_pairs={{0,1},{1,0},{2,3},{3,2},{4,5},{5,4},{6,7},{7,6},{8,9},{9,8},{10,11... | collective-permute-start | bytes 9224 | tf_op jit(solution)/shard_map/ppermute | solution.py:210
  13.2 5.8 %collective-permute-start.3 = (f32[1,768]{1,0:T(1,128)S(1)}, f32[1,768]{1,0:T(1,128)S(1)}, u32[]{:S(2)}, u32[]{:S(2)}) collective-permute-start(f32[1,768]{1,0:T(1,128)S(1)} %log_add_fusion.3), channel_id=1, source_target_pairs={{0,6},{1,7},{2,4},{3,5},{4,2},{5,3},{6,0},{7,1},{8,14},{9,15},{10,... | collective-permute-start | bytes 9224 | tf_op jit(solution)/shard_map/ppermute | solution.py:210
  17.3 4.5 %collective-permute-start.2 = (f32[1,768]{1,0:T(1,128)S(1)}, f32[1,768]{1,0:T(1,128)S(1)}, u32[]{:S(2)}, u32[]{:S(2)}) collective-permute-start(f32[1,768]{1,0:T(1,128)S(1)} %log_add_fusion.3), channel_id=1, source_target_pairs={{0,4},{1,5},{2,6},{3,7},{4,0},{5,1},{6,2},{7,3},{8,12},{9,13},{10,... | collective-permute-start | bytes 9224 | tf_op jit(solution)/shard_map/ppermute | solution.py:210
  17.3 4.5 %collective-permute-start.1 = (f32[1,768]{1,0:T(1,128)S(1)}, f32[1,768]{1,0:T(1,128)S(1)}, u32[]{:S(2)}, u32[]{:S(2)}) collective-permute-start(f32[1,768]{1,0:T(1,128)S(1)} %log_add_fusion.3), channel_id=1, source_target_pairs={{0,2},{1,3},{2,0},{3,1},{4,6},{5,7},{6,4},{7,5},{8,10},{9,11},{10,... | collective-permute-start | bytes 9224 | tf_op jit(solution)/shard_map/ppermute | solution.py:210
  21.9 4.6 %collective-permute-start.6 = (f32[1,768]{1,0:T(1,128)S(1)}, f32[1,768]{1,0:T(1,128)S(1)}, u32[]{:S(2)}, u32[]{:S(2)}) collective-permute-start(f32[1,768]{1,0:T(1,128)S(1)} %log_add_fusion.2), channel_id=1, source_target_pairs={{0,24},{1,25},{2,26},{3,27},{4,28},{5,29},{6,30},{7,31},{8,16},{9,... | collective-permute-start | bytes 9224 | tf_op jit(solution)/shard_map/ppermute | solution.py:210
  24.4 3.6 %collective-permute-start.5 = (f32[1,768]{1,0:T(1,128)S(1)}, f32[1,768]{1,0:T(1,128)S(1)}, u32[]{:S(2)}, u32[]{:S(2)}) collective-permute-start(f32[1,768]{1,0:T(1,128)S(1)} %log_add_fusion.2), channel_id=1, source_target_pairs={{0,16},{1,9},{2,18},{3,11},{4,20},{5,13},{6,22},{7,15},{8,24},{9,1... | collective-permute-start | bytes 9224 | tf_op jit(solution)/shard_map/ppermute | solution.py:210
  24.9 3.6 %collective-permute-start.4 = (f32[1,768]{1,0:T(1,128)S(1)}, f32[1,768]{1,0:T(1,128)S(1)}, u32[]{:S(2)}, u32[]{:S(2)}) collective-permute-start(f32[1,768]{1,0:T(1,128)S(1)} %log_add_fusion.2), channel_id=1, source_target_pairs={{0,8},{1,17},{2,10},{3,19},{4,12},{5,21},{6,14},{7,23},{8,0},{9,25... | collective-permute-start | bytes 9224 | tf_op jit(solution)/shard_map/ppermute | solution.py:210
  31.2 3.4 %copy-start.7 = (f32[4,768]{1,0:T(4,128)S(1)}, f32[4,768]{1,0:T(4,128)}, u32[]{:S(2)}) copy-start(f32[4,768]{1,0:T(4,128)} %pad_maximum_fusion.refs_1_.parts) | copy-start | bytes 36868
  31.2 2.7 %collective-permute-start.10 = (bf16[384,1024]{1,0:T(8,128)(2,1)S(1)}, bf16[384,1024]{1,0:T(8,128)(2,1)}, u32[]{:S(2)}, u32[]{:S(2)}) collective-permute-start(bf16[384,1024]{1,0:T(8,128)(2,1)S(1)} %after.4.refs_1_), channel_id=1, source_target_pairs={{0,1},{1,0},{2,3},{3,2},{4,5},{5,4},{6,7},{7,6},{8,9},{9,8},{10,11... | collective-permute-start | bytes 2359304 | tf_op jit(solution)/shard_map/ppermute | solution.py:210
  31.2 3.4 %collective-permute-start.9 = (bf16[384,1024]{1,0:T(8,128)(2,1)S(1)}, bf16[384,1024]{1,0:T(8,128)(2,1)S(1)}, u32[]{:S(2)}, u32[]{:S(2)}) collective-permute-start(bf16[384,1024]{1,0:T(8,128)(2,1)S(1)} %after.3.refs_0_), channel_id=1, source_target_pairs={{0,1},{1,0},{2,3},{3,2},{4,5},{5,4},{6,7},{7,6},{8,9},{9,8},{10,11... | collective-permute-start | bytes 2359304 | tf_op jit(solution)/shard_map/ppermute | solution.py:210
  31.7 12.0 %collective-permute-start.11 = (bf16[384,1024]{1,0:T(8,128)(2,1)S(1)}, bf16[384,1024]{1,0:T(8,128)(2,1)S(1)}, u32[]{:S(2)}, u32[]{:S(2)}) collective-permute-start(bf16[384,1024]{1,0:T(8,128)(2,1)S(1)} %after.3.refs_0_), channel_id=1, source_target_pairs={{0,16},{1,9},{2,18},{3,11},{4,20},{5,13},{6,22},{7,15},{8,24},{9,1... | collective-permute-start | bytes 2359304 | tf_op jit(solution)/shard_map/ppermute | solution.py:210
  39.4 1.6 %copy-start = (bf16[1536,1024]{1,0:T(8,128)(2,1)}, bf16[1536,1024]{1,0:T(8,128)(2,1)S(1)}, u32[]{:S(2)}) copy-start(bf16[1536,1024]{1,0:T(8,128)(2,1)S(1)} %get-tuple-element.19.table.refs_0_) | copy-start | bytes 9437188
  45.7 2.3 %collective-permute-start.12 = (bf16[384,1024]{1,0:T(8,128)(2,1)S(1)}, bf16[384,1024]{1,0:T(8,128)(2,1)S(1)}, u32[]{:S(2)}, u32[]{:S(2)}) collective-permute-start(bf16[384,1024]{1,0:T(8,128)(2,1)S(1)} %after.5.refs_0_), channel_id=1, source_target_pairs={{0,1},{1,0},{2,3},{3,2},{4,5},{5,4},{6,7},{7,6},{8,9},{9,8},{10,11... | collective-permute-start | bytes 2359304 | tf_op jit(solution)/shard_map/ppermute | solution.py:210
  48.0 1.9 %copy-start.1 = (bf16[1536,1024]{1,0:T(8,128)(2,1)S(1)}, bf16[1536,1024]{1,0:T(8,128)(2,1)}, u32[]{:S(2)}) copy-start(bf16[1536,1024]{1,0:T(8,128)(2,1)} %copy-done) | copy-start | bytes 9437188
  52.1 17.7 %copy-start.2 = (bf16[1536,1024]{1,0:T(8,128)(2,1)S(1)}, bf16[1536,1024]{1,0:T(8,128)(2,1)}, u32[]{:S(2)}) copy-start(bf16[1536,1024]{1,0:T(8,128)(2,1)} %copy-done) | copy-start | bytes 9437188
  55.9 1.2 %collective-permute-start.13 = (f32[4,768]{1,0:T(4,128)S(1)}, f32[4,768]{1,0:T(4,128)S(1)}, u32[]{:S(2)}, u32[]{:S(2)}) collective-permute-start(f32[4,768]{1,0:T(4,128)S(1)} %get-tuple-element.24), channel_id=1, source_target_pairs={{0,1},{1,0},{2,3},{3,2},{4,5},{5,4},{6,7},{7,6},{8,9},{9,8},{10,11... | collective-permute-start | bytes 36872 | tf_op jit(solution)/shard_map/ppermute | solution.py:210
  57.2 5.6 %collective-permute-start.16 = (f32[4,768]{1,0:T(4,128)S(1)}, f32[4,768]{1,0:T(4,128)S(1)}, u32[]{:S(2)}, u32[]{:S(2)}) collective-permute-start(f32[4,768]{1,0:T(4,128)S(1)} %log_add_fusion.1), channel_id=1, source_target_pairs={{0,6},{1,7},{2,4},{3,5},{4,2},{5,3},{6,0},{7,1},{8,14},{9,15},{10,... | collective-permute-start | bytes 36872 | tf_op jit(solution)/shard_map/ppermute | solution.py:210
  58.7 4.6 %collective-permute-start.15 = (f32[4,768]{1,0:T(4,128)S(1)}, f32[4,768]{1,0:T(4,128)S(1)}, u32[]{:S(2)}, u32[]{:S(2)}) collective-permute-start(f32[4,768]{1,0:T(4,128)S(1)} %log_add_fusion.1), channel_id=1, source_target_pairs={{0,4},{1,5},{2,6},{3,7},{4,0},{5,1},{6,2},{7,3},{8,12},{9,13},{10,... | collective-permute-start | bytes 36872 | tf_op jit(solution)/shard_map/ppermute | solution.py:210
  59.3 4.1 %collective-permute-start.14 = (f32[4,768]{1,0:T(4,128)S(1)}, f32[4,768]{1,0:T(4,128)S(1)}, u32[]{:S(2)}, u32[]{:S(2)}) collective-permute-start(f32[4,768]{1,0:T(4,128)S(1)} %log_add_fusion.1), channel_id=1, source_target_pairs={{0,2},{1,3},{2,0},{3,1},{4,6},{5,7},{6,4},{7,5},{8,10},{9,11},{10,... | collective-permute-start | bytes 36872 | tf_op jit(solution)/shard_map/ppermute | solution.py:210
  63.5 4.7 %collective-permute-start.19 = (f32[4,768]{1,0:T(4,128)S(1)}, f32[4,768]{1,0:T(4,128)S(1)}, u32[]{:S(2)}, u32[]{:S(2)}) collective-permute-start(f32[4,768]{1,0:T(4,128)S(1)} %log_add_fusion), channel_id=1, source_target_pairs={{0,24},{1,25},{2,26},{3,27},{4,28},{5,29},{6,30},{7,31},{8,16},{9,... | collective-permute-start | bytes 36872 | tf_op jit(solution)/shard_map/ppermute | solution.py:210
  65.0 3.7 %collective-permute-start.18 = (f32[4,768]{1,0:T(4,128)S(1)}, f32[4,768]{1,0:T(4,128)S(1)}, u32[]{:S(2)}, u32[]{:S(2)}) collective-permute-start(f32[4,768]{1,0:T(4,128)S(1)} %log_add_fusion), channel_id=1, source_target_pairs={{0,16},{1,17},{2,18},{3,19},{4,20},{5,21},{6,22},{7,23},{8,24},{9,... | collective-permute-start | bytes 36872 | tf_op jit(solution)/shard_map/ppermute | solution.py:210
  66.1 3.7 %collective-permute-start.17 = (f32[4,768]{1,0:T(4,128)S(1)}, f32[4,768]{1,0:T(4,128)S(1)}, u32[]{:S(2)}, u32[]{:S(2)}) collective-permute-start(f32[4,768]{1,0:T(4,128)S(1)} %log_add_fusion), channel_id=1, source_target_pairs={{0,8},{1,9},{2,10},{3,11},{4,12},{5,13},{6,14},{7,15},{8,0},{9,1},... | collective-permute-start | bytes 36872 | tf_op jit(solution)/shard_map/ppermute | solution.py:210
  (10 other events, 9.8 us)

commit v7 on v6

--- a/solution.py
+++ b/solution.py
@@ -37,57 +37,78 @@
     return pltpu.with_memory_space_constraint(value, pltpu.VMEM)
 
 
-def partial_kernel(scale, rows, v_hbm, c_hbm, out_ref, v_ref, own_ref, c_ref, sems):
-    nv, k, own = v_ref.shape[0], c_ref.shape[0], own_ref.shape[0]
-    start = pl.multiple_of(lax.axis_index("item") * own, own)
-    own_copy = pltpu.make_async_copy(c_hbm.at[pl.ds(start, own), :], own_ref, sems.at[0])
-    third = nv // 3
-    v_copies = [
+def load_kernel(v_hbm, c_hbm, v_ref, c_ref, mine_ref, other_ref, v_sems, c_sems):
+    half = mine_ref.shape[0]
+    v_count, c_count = v_sems.shape[0], c_sems.shape[0]
+    v_rows, c_rows = v_ref.shape[0] // v_count, c_ref.shape[0] // c_count
+    copies = [
         pltpu.make_async_copy(
-            v_hbm.at[pl.ds(i * third, third), :], v_ref.at[pl.ds(i * third, third), :], sems.at[1 + i]
+            v_hbm.at[pl.ds(i * v_rows, v_rows), :], v_ref.at[pl.ds(i * v_rows, v_rows), :], v_sems.at[i]
         )
-        for i in range(3)
+        for i in range(v_count)
+    ] + [
+        pltpu.make_async_copy(
+            c_hbm.at[pl.ds(i * c_rows, c_rows), :], c_ref.at[pl.ds(i * c_rows, c_rows), :], c_sems.at[i]
+        )
+        for i in range(c_count)
     ]
-    c_copies = [
-        pltpu.make_async_copy(c_hbm.at[pl.ds(i * rows, rows), :], c_ref.at[pl.ds(i * rows, rows), :], sems.at[4 + i])
-        for i in range(k // rows)
-    ]
-    for copy in v_copies + c_copies + [own_copy]:
+    for copy in copies:
         copy.start()
-    for copy in v_copies:
+    for copy in copies[:v_count]:
         copy.wait()
-    parts = []
-    for i, copy in enumerate(c_copies):
+    core = core_index()
+    mine_ref[...] = v_ref[pl.ds(pl.multiple_of(core * half, half), half), :]
+    other_ref[...] = v_ref[pl.ds(pl.multiple_of((1 - core) * half, half), half), :]
+    for copy in copies[v_count:]:
         copy.wait()
-        logits = scores(c_ref[i * rows : (i + 1) * rows, :], v_ref[...], scale)
-        peak = jnp.max(logits, axis=0, keepdims=True)
-        parts.append(peak + jnp.log(jnp.sum(jnp.exp(logits - peak), axis=0, keepdims=True)))
-    own_copy.wait()
-    out_ref[...] = merge(parts)
-
-
-def partial(vectors, centroids, own, scale):
+
+
+def load(vectors, centroids):
     nv, dim = vectors.shape
     k = centroids.shape[0]
-    rows = min(256, k)
     vmem = pl.BlockSpec(memory_space=pltpu.VMEM)
     hbm = pl.BlockSpec(memory_space=pl.ANY)
     return pl.pallas_call(
-        functools.partial(partial_kernel, scale, rows),
+        load_kernel,
         in_specs=[hbm, hbm],
-        out_specs=[vmem] * 3,
+        out_specs=[vmem] * 4,
         out_shape=[
-            jax.ShapeDtypeStruct((1, nv), jnp.float32),
             pltpu.VMEM((nv, dim), jnp.bfloat16),
-            pltpu.VMEM((own, dim), jnp.bfloat16),
+            pltpu.VMEM((k, dim), jnp.bfloat16),
+            pltpu.VMEM((nv // 2, dim), jnp.bfloat16),
+            pltpu.VMEM((nv // 2, dim), jnp.bfloat16),
         ],
-        scratch_shapes=[pltpu.VMEM((k, dim), jnp.bfloat16), pltpu.SemaphoreType.DMA((4 + k // rows,))],
+        scratch_shapes=[pltpu.SemaphoreType.DMA((6,)), pltpu.SemaphoreType.DMA((8,))],
+        compiler_params=pltpu.CompilerParams(vmem_limit_bytes=4 * MIB),
+        cost_estimate=pl.CostEstimate(flops=0, bytes_accessed=4 * (nv + k) * dim, transcendentals=0),
+        name="load",
+    )(in_hbm(vectors), in_hbm(centroids))
+
+
+def partial_kernel(scale, rows, v_ref, c_ref, out_ref):
+    parts = []
+    for start in range(0, c_ref.shape[0], rows):
+        logits = scores(c_ref[start : start + rows, :], v_ref[...], scale)
+        peak = jnp.max(logits, axis=0, keepdims=True)
+        parts.append(peak + jnp.log(jnp.sum(jnp.exp(logits - peak), axis=0, keepdims=True)))
+    out_ref[...] = merge(parts)
+
+
+def partial(vectors, centroids, scale):
+    nv, dim = vectors.shape
+    k = centroids.shape[0]
+    vmem = pl.BlockSpec(memory_space=pltpu.VMEM)
+    return pl.pallas_call(
+        functools.partial(partial_kernel, scale, min(256, k)),
+        in_specs=[vmem, vmem],
+        out_specs=vmem,
+        out_shape=jax.ShapeDtypeStruct((1, nv), jnp.float32),
         compiler_params=pltpu.CompilerParams(vmem_limit_bytes=12 * MIB),
         cost_estimate=pl.CostEstimate(
             flops=2 * nv * k * dim, bytes_accessed=2 * (nv + k) * dim, transcendentals=nv * k
         ),
         name="partial_lse",
-    )(in_hbm(vectors), in_hbm(centroids))
+    )(in_vmem(vectors), in_vmem(centroids))
 
 
 def core_index():
@@ -132,21 +153,26 @@
     return (term, weight) if total is None else (total + term, mass + weight)
 
 
-def early_kernel(plan, scale, own_ref, parts, home, *refs):
-    pieces, (table, total, mass, done, sems) = refs[:-5], refs[-5:]
+def own_rows(c_ref, rows):
+    return c_ref[pl.ds(pl.multiple_of(lax.axis_index("item") * rows, rows), rows), :]
+
+
+def early_kernel(plan, scale, c_ref, home, *refs):
+    n = plan["n_early"]
+    parts, pieces, (table, total, mass, done, sems) = refs[:n], refs[n:-5], refs[-5:]
     nv = home.shape[0]
     copies = fetches(nv, plan["early"], pieces, table, sems)
     done[...] = jnp.zeros_like(done)
-    own = own_ref[...]
+    own = own_rows(c_ref, total.shape[0])
     sums = weights = None
     if plan["home"]:
-        sums, weights = absorb(own, home[...], parts[pl.ds(0, 1), :], scale, sums, weights)
+        sums, weights = absorb(own, home[...], parts[0][...], scale, sums, weights)
     for i, block in enumerate(copies):
         for copy in block:
             copy.wait()
         place = i + plan["home"]
         vectors = table[pl.ds(i * nv, nv), :]
-        sums, weights = absorb(own, vectors, parts[pl.ds(place, 1), :], scale, sums, weights)
+        sums, weights = absorb(own, vectors, parts[place][...], scale, sums, weights)
     total[...], mass[...] = sums, weights
 
 
@@ -161,13 +187,14 @@
     return tables[1][pl.ds((place - early) * nv, nv), :]
 
 
-def late_kernel(plan, scale, own_ref, parts, total, mass, home, table, *refs):
-    n = plan["n_late"]
+def late_kernel(plan, scale, c_ref, total, mass, home, table, *refs):
+    n, late_places = plan["n_late"], len(plan["late"])
+    parts, refs = refs[:late_places], refs[late_places:]
     pieces, refs = refs[:n], refs[n:]
     new_ref, expo_ref, peak_ref, part_ref = refs[:4]
     tables = [table]
     sums, weights = total[...], mass[...]
-    own = own_ref[...]
+    own = own_rows(c_ref, new_ref.shape[0])
     if n:
         late, sems = refs[4:]
         tables.append(late)
@@ -177,7 +204,7 @@
                 copy.wait()
             place = plan["places"] - len(copies) + i
             vectors = vectors_of(plan, place, home, tables)
-            sums, weights = absorb(own, vectors, parts[pl.ds(place, 1), :], scale, sums, weights)
+            sums, weights = absorb(own, vectors, parts[i][...], scale, sums, weights)
     new_ref[...] = updated(sums, weights, own)
     for place in range(plan["places"]):
         logits = scores(new_ref[...], vectors_of(plan, place, home, tables), scale)
@@ -223,6 +250,7 @@
         out_specs=vmem,
         out_shape=pltpu.VMEM(value.shape, value.dtype),
         input_output_aliases={0: 0},
+        compiler_params=pltpu.CompilerParams(vmem_limit_bytes=2 * MIB),
         name="after",
     )(in_vmem(value), *others)
 
@@ -237,27 +265,27 @@
         return send(value, items, cents, item_mask, cent_mask)
 
     small = items == 4 and cents == 8
+    home, centroids, mine, other = load(vectors, centroids)
     if small:
         half = nv // 2
-        core = core_index()
-        first = go(lax.dynamic_slice_in_dim(vectors, core * half, half, 0), (1, 2))
-        second = go(lax.dynamic_slice_in_dim(vectors, (1 - core) * half, half, 0), (1, 2))
-        part, home, own = partial(vectors, centroids, rows, scale)
-        lse = merge_cent(part, go)
-        parts = jnp.concatenate([lse, go(lse, (1, 2)), go(lse, (2, 1)), go(lse, 3)], axis=0)
-        first, second = after(first, parts), after(second, parts)
+        first, second = go(mine, (1, 2)), go(other, (1, 2))
+        lse = merge_cent(partial(home, centroids, scale), go)
+        parts = [lse, go(lse, (1, 2)), go(lse, (2, 1)), go(lse, 3)]
+        first, second = after(first, *parts), after(second, *parts)
         far = go(first, (2, 1))
         early = [first, second, go(first, 0, 1), go(second, 0, 1)]
         early_blocks = [[(0, 0, True, half), (1, 0, False, half)], [(2, 0, False, half), (3, 0, True, half)]]
         plan = dict(exchange=True, home=1, places=4)
     else:
-        part, home, own = partial(vectors, centroids, rows, scale)
         early = [lax.all_gather(vectors, "item", axis=0, tiled=True)]
         early_blocks = [[(0, i * nv, None, nv)] for i in range(items)]
+        part = partial(home, centroids, scale)
         parts = lax.all_gather(part, "cent", axis=0, tiled=False)
-        parts = lax.all_gather(merge([parts[i] for i in range(cents)]), "item", axis=0, tiled=True)
+        parts = lax.all_gather(merge([parts[i] for i in range(cents)]), "item", axis=0, tiled=False)
+        parts = [parts[i] for i in range(items)]
         plan = dict(exchange=False, home=0, places=items)
     plan["early"] = early_blocks
+    plan["n_early"] = n_parts = plan["home"] + len(early_blocks)
 
     vmem = pl.BlockSpec(memory_space=pltpu.VMEM)
     hbm = pl.BlockSpec(memory_space=pl.ANY)
@@ -266,7 +294,7 @@
     params = pltpu.CompilerParams(vmem_limit_bytes=16 * MIB)
     table, total, mass, done = pl.pallas_call(
         functools.partial(early_kernel, plan, scale),
-        in_specs=[vmem] * 3 + [hbm] * len(early),
+        in_specs=[vmem] * (2 + n_parts) + [hbm] * len(early),
         out_specs=[vmem] * 4,
         out_shape=[
             pltpu.VMEM((n_early * nv, dim), jnp.bfloat16),
@@ -280,7 +308,7 @@
             flops=2 * n_early * flops, bytes_accessed=2 * n_early * nv * dim, transcendentals=n_early * nv * rows
         ),
         name="early_blocks",
-    )(in_vmem(own), parts, in_vmem(home), *early)
+    )(in_vmem(centroids), in_vmem(home), *parts[:n_parts], *early)
 
     late, late_blocks = [], []
     if small:
@@ -292,7 +320,7 @@
     late_out = [pltpu.VMEM((n_late * nv, dim), jnp.bfloat16)] if n_late else []
     fresh, expo, peak, part, *tables = pl.pallas_call(
         functools.partial(late_kernel, plan, scale),
-        in_specs=[vmem] * 6 + [hbm] * len(late),
+        in_specs=[vmem] * (5 + n_late) + [hbm] * len(late),
         out_specs=[vmem] * (4 + len(late_out)),
         out_shape=[
             pltpu.VMEM((rows, dim), jnp.bfloat16),
@@ -309,7 +337,7 @@
             transcendentals=(items + n_late) * nv * rows,
         ),
         name="late_blocks",
-    )(in_vmem(own), parts, in_vmem(total), in_vmem(mass), in_vmem(home), in_vmem(table), *late)
+    )(in_vmem(centroids), in_vmem(total), in_vmem(mass), in_vmem(home), in_vmem(table), *parts[n_parts:], *late)
 
     if small:
         lse = merge_cent(part, go)

time: 72.9 us -> 63.7 us (0.87)
  local copies, waits for them, and re-layouts: 15.6 us -> 0 us
  waiting for transfers between devices: 18.4 us -> 26.9 us
  starting transfers between devices: 21.6 us -> 20.8 us
    unnamed x28 -> x0, local copies, waits for them, and re-layouts: 13.3 us -> none
    ppermute x20, waiting for transfers between devices: 18.4 us -> 26.9 us  [send(): return lax.ppermute(value, BOTH, pairs)]
    dynamic_slice x1 -> x0, local copies, waits for them, and re-layouts: 2.38 us -> none  [shards(): lax.dynamic_slice_in_dim(vectors, (1 - core) * half, half, 0)]
    ppermute x20, starting transfers between devices: 21.6 us -> 20.8 us  [send(): return lax.ppermute(value, BOTH, pairs)]
    pallas_call x1 -> x2, Pallas kernels: 5.18 us -> 4.61 us  [the longest x1 2.46 us: partial(): pl.pallas_call(functools.partial(partial_kernel, scale, min(256, k)), in_...]
  transfers between devices with their start and end apart: 20 -> 20, of which waited for: 17 -> 14; matrix products, arithmetic and copies ran while one was open for 1% -> 0% of each run, Pallas kernels for 12% -> 10%
where the time goes in v7:
time: 63.7 us; the launch traced here: 63.5 us
  waiting for transfers between devices  26.9 us (42%)
  starting transfers between devices  20.8 us (33%)
  Pallas kernels  15 us (24%)
  between operations  0.73 us (1%)
    ppermute x20, waiting for transfers between devices, send(): return lax.ppermute(value, BOTH, pairs)  26.9 us
    ppermute x20, starting transfers between devices, send(): return lax.ppermute(value, BOTH, pairs)  20.8 us
    pallas_call x1, Pallas kernels, shards(): pl.pallas_call(functools.partial(early_kernel, plan, scale), in_specs=[vm...  3.82 us
    pallas_call x1, Pallas kernels, shards(): pl.pallas_call(functools.partial(late_kernel, plan, scale), in_specs=[vme...  3.8 us
    pallas_call x1, Pallas kernels, shards(): pl.pallas_call(functools.partial(last_kernel, plan), in_specs=[vmem] * (6...  2.71 us
    pallas_call x1, Pallas kernels, partial(): pl.pallas_call(functools.partial(partial_kernel, scale, min(256, k)), in_...  2.46 us
    pallas_call x1, Pallas kernels, load(): pl.pallas_call(load_kernel, in_specs=[hbm, hbm], out_specs=[vmem] * 4, ou...  2.15 us
  transfers between devices with their start and end apart: 20, of which 14 were waited for; matrix products, arithmetic and copies ran while one was open for 0% of the time, Pallas kernels for 10%

profile of v7, /device:TPU:0, one launch (start us, length us, event | category | flops | bytes accessed | tf_op | source)
XLA Modules:
  0.0 63.5 jit_solution(7595578649769977941)
XLA Ops:
  0.6 2.2 %load.1 = (bf16[768,1024]{1,0:T(8,128)(2,1)S(1)}, bf16[1024,1024]{1,0:T(8,128)(2,1)S(1)}, bf16[384,1024]{1,0:T(8,128)(2,1)S(1)}, bf16[384,1024]{1,0:T(8,128)(2,1)S(1)}) custom-call(bf16[768,1024]{1,0:T(8,128)(2,1)} %v_hbm.1, bf16[1024,1024]{1,0:T(8,128)(2,1)} %c_hbm.1), custom_call_target="tpu_custom_call" | custom-call | bytes 7340032 | tf_op jit(solution)/shard_map/load/pallas_call | solution.py:71
  2.8 3.0 %collective-permute-start.6 = (bf16[384,1024]{1,0:T(8,128)(2,1)S(1)}, bf16[384,1024]{1,0:T(8,128)(2,1)S(1)}, u32[]{:S(2)}, u32[]{:S(2)}) collective-permute-start(bf16[384,1024]{1,0:T(8,128)(2,1)S(1)} %get-tuple-element.17), channel_id=1, source_target_pairs={{0,8},{1,17},{2,10},{3,19},{4,12},{5,21},{6,14},{7,23},{8,0},{9,25... | collective-permute-start | bytes 2359304 | tf_op jit(solution)/shard_map/ppermute | solution.py:237
  5.9 2.5 %partial_lse.1 = f32[1,768]{1,0:T(1,128)S(1)} custom-call(bf16[768,1024]{1,0:T(8,128)(2,1)S(1)} %get-tuple-element.16.v_ref.home, bf16[1024,1024]{1,0:T(8,128)(2,1)S(1)} %get-tuple-element.15.c_ref), custom_call_target="tpu_custom_call" | custom-call | flops 1610612736 | bytes 3670016 | tf_op jit(solution)/shard_map/partial_lse/pallas_call | solution.py:101
  8.4 1.1 %collective-permute-done = f32[1,768]{1,0:T(1,128)S(1)} collective-permute-done((f32[1,768]{1,0:T(1,128)S(1)}, f32[1,768]{1,0:T(1,128)S(1)}, u32[]{:S(2)}, u32[]{:S(2)}) %collective-permute-start) | collective-permute-done | bytes 3104 | tf_op jit(solution)/shard_map/ppermute | solution.py:237
  9.6 4.1 %collective-permute-start.3 = (f32[1,768]{1,0:T(1,128)S(1)}, f32[1,768]{1,0:T(1,128)S(1)}, u32[]{:S(2)}, u32[]{:S(2)}) collective-permute-start(f32[1,768]{1,0:T(1,128)S(1)} %log_add_fusion.3), channel_id=1, source_target_pairs={{0,6},{1,7},{2,4},{3,5},{4,2},{5,3},{6,0},{7,1},{8,14},{9,15},{10,... | collective-permute-start | bytes 9224 | tf_op jit(solution)/shard_map/ppermute | solution.py:237
  14.4 0.9 %collective-permute-done.3 = f32[1,768]{1,0:T(1,128)S(1)} collective-permute-done((f32[1,768]{1,0:T(1,128)S(1)}, f32[1,768]{1,0:T(1,128)S(1)}, u32[]{:S(2)}, u32[]{:S(2)}) %collective-permute-start.3) | collective-permute-done | bytes 3104 | tf_op jit(solution)/shard_map/ppermute | solution.py:237
  15.3 2.9 %collective-permute-done.2 = f32[1,768]{1,0:T(1,128)S(1)} collective-permute-done((f32[1,768]{1,0:T(1,128)S(1)}, f32[1,768]{1,0:T(1,128)S(1)}, u32[]{:S(2)}, u32[]{:S(2)}) %collective-permute-start.2) | collective-permute-done | bytes 3104 | tf_op jit(solution)/shard_map/ppermute | solution.py:237
  18.3 2.5 %collective-permute-start.7 = (f32[1,768]{1,0:T(1,128)S(1)}, f32[1,768]{1,0:T(1,128)S(1)}, u32[]{:S(2)}, u32[]{:S(2)}) collective-permute-start(f32[1,768]{1,0:T(1,128)S(1)} %log_add_fusion.2.refs_1_.refs_0_), channel_id=1, source_target_pairs={{0,24},{1,25},{2,26},{3,27},{4,28},{5,29},{6,30},{7,31},{8,16},{9,... | collective-permute-start | bytes 9224 | tf_op jit(solution)/shard_map/ppermute | solution.py:237
  21.8 4.0 %collective-permute-done.7.refs_4_.refs_0_ = f32[1,768]{1,0:T(1,128)S(1)} collective-permute-done((f32[1,768]{1,0:T(1,128)S(1)}, f32[1,768]{1,0:T(1,128)S(1)}, u32[]{:S(2)}, u32[]{:S(2)}) %collective-permute-start.7) | collective-permute-done | bytes 3104 | tf_op jit(solution)/shard_map/ppermute | solution.py:237
  26.9 1.2 %collective-permute-done.9.refs_5_ = bf16[384,1024]{1,0:T(8,128)(2,1)S(1)} collective-permute-done((bf16[384,1024]{1,0:T(8,128)(2,1)S(1)}, bf16[384,1024]{1,0:T(8,128)(2,1)S(1)}, u32[]{:S(2)}, u32[]{:S(2)}) %collective-permute-start.9) | collective-permute-done | bytes 786464 | tf_op jit(solution)/shard_map/ppermute | solution.py:237
  28.1 1.1 %collective-permute-done.10.refs_6_ = bf16[384,1024]{1,0:T(8,128)(2,1)S(1)} collective-permute-done((bf16[384,1024]{1,0:T(8,128)(2,1)S(1)}, bf16[384,1024]{1,0:T(8,128)(2,1)S(1)}, u32[]{:S(2)}, u32[]{:S(2)}) %collective-permute-start.10) | collective-permute-done | bytes 786464 | tf_op jit(solution)/shard_map/ppermute | solution.py:237
  29.3 3.8 %early_blocks.1 = (bf16[1536,1024]{1,0:T(8,128)(2,1)S(1)}, f32[256,1024]{1,0:T(8,128)S(1)}, f32[256,1]{1,0:T(8,128)S(1)}, f32[8,128]{1,0:T(8,128)S(1)}) custom-call(bf16[1024,1024]{1,0:T(8,128)(2,1)S(1)} %get-tuple-element.15.c_ref, bf16[768,1024]{1,0:T(8,128)(2,1)S(1)} %get-tuple-element.16.v_ref.home, f32[1,768]{1,0:T(1,128)S(1)} %log_add_fusion.2.refs_1_.refs_0_, ...), custom_call_target="tpu_custom_call" | custom-call | flops 1610612736 | bytes 3145728 | tf_op jit(solution)/shard_map/early_blocks/pallas_call | solution.py:295
  33.1 5.3 %collective-permute-done.11.refs_0_ = bf16[384,1024]{1,0:T(8,128)(2,1)S(1)} collective-permute-done((bf16[384,1024]{1,0:T(8,128)(2,1)S(1)}, bf16[384,1024]{1,0:T(8,128)(2,1)S(1)}, u32[]{:S(2)}, u32[]{:S(2)}) %collective-permute-start.11) | collective-permute-done | bytes 786464 | tf_op jit(solution)/shard_map/ppermute | solution.py:237
  38.4 2.3 %collective-permute-done.12.refs_2_ = bf16[384,1024]{1,0:T(8,128)(2,1)S(1)} collective-permute-done((bf16[384,1024]{1,0:T(8,128)(2,1)S(1)}, bf16[384,1024]{1,0:T(8,128)(2,1)S(1)}, u32[]{:S(2)}, u32[]{:S(2)}) %collective-permute-start.12) | collective-permute-done | bytes 786464 | tf_op jit(solution)/shard_map/ppermute | solution.py:237
  40.7 3.8 %late_blocks.1 = (bf16[256,1024]{1,0:T(8,128)(2,1)S(1)}, f32[4,256,768]{2,1,0:T(8,128)S(1)}, f32[4,768]{1,0:T(4,128)S(1)}, f32[4,768]{1,0:T(4,128)S(1)}, bf16[768,1024]{1,0:T(8,128)(2,1)S(1)}) custom-call(bf16[1024,1024]{1,0:T(8,128)(2,1)S(1)} %get-tuple-element.15.c_ref, f32[256,1024]{1,0:T(8,128)S(1)} %get-tuple-element.19.total, ...), custom_call_target="tpu_custom_call" | custom-call | flops 2415919104 | bytes 1572864 | tf_op jit(solution)/shard_map/late_blocks/pallas_call | solution.py:321
  44.7 1.0 %collective-permute-done.13 = f32[4,768]{1,0:T(4,128)S(1)} collective-permute-done((f32[4,768]{1,0:T(4,128)S(1)}, f32[4,768]{1,0:T(4,128)S(1)}, u32[]{:S(2)}, u32[]{:S(2)}) %collective-permute-start.13) | collective-permute-done | bytes 12320 | tf_op jit(solution)/shard_map/ppermute | solution.py:237
  45.7 3.7 %collective-permute-start.16 = (f32[4,768]{1,0:T(4,128)S(1)}, f32[4,768]{1,0:T(4,128)S(1)}, u32[]{:S(2)}, u32[]{:S(2)}) collective-permute-start(f32[4,768]{1,0:T(4,128)S(1)} %log_add_fusion.1), channel_id=1, source_target_pairs={{0,6},{1,7},{2,4},{3,5},{4,2},{5,3},{6,0},{7,1},{8,14},{9,15},{10,... | collective-permute-start | bytes 36872 | tf_op jit(solution)/shard_map/ppermute | solution.py:237
  50.2 1.1 %collective-permute-done.16 = f32[4,768]{1,0:T(4,128)S(1)} collective-permute-done((f32[4,768]{1,0:T(4,128)S(1)}, f32[4,768]{1,0:T(4,128)S(1)}, u32[]{:S(2)}, u32[]{:S(2)}) %collective-permute-start.16) | collective-permute-done | bytes 12320 | tf_op jit(solution)/shard_map/ppermute | solution.py:237
  51.3 2.7 %collective-permute-done.15 = f32[4,768]{1,0:T(4,128)S(1)} collective-permute-done((f32[4,768]{1,0:T(4,128)S(1)}, f32[4,768]{1,0:T(4,128)S(1)}, u32[]{:S(2)}, u32[]{:S(2)}) %collective-permute-start.15) | collective-permute-done | bytes 12320 | tf_op jit(solution)/shard_map/ppermute | solution.py:237
  54.0 1.5 %collective-permute-start.19 = (f32[4,768]{1,0:T(4,128)S(1)}, f32[4,768]{1,0:T(4,128)S(1)}, u32[]{:S(2)}, u32[]{:S(2)}) collective-permute-start(f32[4,768]{1,0:T(4,128)S(1)} %log_add_fusion), channel_id=1, source_target_pairs={{0,24},{1,25},{2,26},{3,27},{4,28},{5,29},{6,30},{7,31},{8,16},{9,... | collective-permute-start | bytes 36872 | tf_op jit(solution)/shard_map/ppermute | solution.py:237
  55.5 1.5 %collective-permute-start.18 = (f32[4,768]{1,0:T(4,128)S(1)}, f32[4,768]{1,0:T(4,128)S(1)}, u32[]{:S(2)}, u32[]{:S(2)}) collective-permute-start(f32[4,768]{1,0:T(4,128)S(1)} %log_add_fusion), channel_id=1, source_target_pairs={{0,16},{1,17},{2,18},{3,19},{4,20},{5,21},{6,22},{7,23},{8,24},{9,... | collective-permute-start | bytes 36872 | tf_op jit(solution)/shard_map/ppermute | solution.py:237
  57.6 1.1 %collective-permute-done.19 = f32[4,768]{1,0:T(4,128)S(1)} collective-permute-done((f32[4,768]{1,0:T(4,128)S(1)}, f32[4,768]{1,0:T(4,128)S(1)}, u32[]{:S(2)}, u32[]{:S(2)}) %collective-permute-start.19) | collective-permute-done | bytes 12320 | tf_op jit(solution)/shard_map/ppermute | solution.py:237
  59.2 1.5 %collective-permute-done.17 = f32[4,768]{1,0:T(4,128)S(1)} collective-permute-done((f32[4,768]{1,0:T(4,128)S(1)}, f32[4,768]{1,0:T(4,128)S(1)}, u32[]{:S(2)}, u32[]{:S(2)}) %collective-permute-start.17) | collective-permute-done | bytes 12320 | tf_op jit(solution)/shard_map/ppermute | solution.py:237
  60.8 2.7 %last_iteration.1 = (bf16[256,1024]{1,0:T(8,128)(2,1)}, f32[768]{0:T(1024)}) custom-call(bf16[256,1024]{1,0:T(8,128)(2,1)S(1)} %get-tuple-element.23.old_ref, f32[4,256,768]{2,1,0:T(8,128)S(1)} %get-tuple-element.24.expo_ref, f32[4,768]{1,0:T(4,128)S(1)} %get-tuple-element.25.peak_ref, f32[1,4,768]{2,1,0:T(4,128)S(1)} %add_bitcast_fusion.parts, ...), custom_call_target="tpu_custom_call" | custom-call | flops 1610612736 | bytes 524288 | tf_op jit(solution)/shard_map/last_iteration/pallas_call | solution.py:348
  (29 shorter events, 5.2 us)
Async XLA Ops:
  2.8 23.0 %collective-permute-start.6 = (bf16[384,1024]{1,0:T(8,128)(2,1)S(1)}, bf16[384,1024]{1,0:T(8,128)(2,1)S(1)}, u32[]{:S(2)}, u32[]{:S(2)}) collective-permute-start(bf16[384,1024]{1,0:T(8,128)(2,1)S(1)} %get-tuple-element.17), channel_id=1, source_target_pairs={{0,8},{1,17},{2,10},{3,19},{4,12},{5,21},{6,14},{7,23},{8,0},{9,25... | collective-permute-start | bytes 2359304 | tf_op jit(solution)/shard_map/ppermute | solution.py:237
  5.8 20.1 %collective-permute-start.8 = (bf16[384,1024]{1,0:T(8,128)(2,1)S(1)}, bf16[384,1024]{1,0:T(8,128)(2,1)S(1)}, u32[]{:S(2)}, u32[]{:S(2)}) collective-permute-start(bf16[384,1024]{1,0:T(8,128)(2,1)S(1)} %get-tuple-element.18), channel_id=1, source_target_pairs={{0,8},{1,17},{2,10},{3,19},{4,12},{5,21},{6,14},{7,23},{8,0},{9,25... | collective-permute-start | bytes 2359304 | tf_op jit(solution)/shard_map/ppermute | solution.py:237
  8.3 1.2 %collective-permute-start = (f32[1,768]{1,0:T(1,128)S(1)}, f32[1,768]{1,0:T(1,128)S(1)}, u32[]{:S(2)}, u32[]{:S(2)}) collective-permute-start(f32[1,768]{1,0:T(1,128)S(1)} %partial_lse.1), channel_id=1, source_target_pairs={{0,1},{1,0},{2,3},{3,2},{4,5},{5,4},{6,7},{7,6},{8,9},{9,8},{10,11... | collective-permute-start | bytes 9224 | tf_op jit(solution)/shard_map/ppermute | solution.py:237
  9.6 5.7 %collective-permute-start.3 = (f32[1,768]{1,0:T(1,128)S(1)}, f32[1,768]{1,0:T(1,128)S(1)}, u32[]{:S(2)}, u32[]{:S(2)}) collective-permute-start(f32[1,768]{1,0:T(1,128)S(1)} %log_add_fusion.3), channel_id=1, source_target_pairs={{0,6},{1,7},{2,4},{3,5},{4,2},{5,3},{6,0},{7,1},{8,14},{9,15},{10,... | collective-permute-start | bytes 9224 | tf_op jit(solution)/shard_map/ppermute | solution.py:237
  13.7 4.5 %collective-permute-start.2 = (f32[1,768]{1,0:T(1,128)S(1)}, f32[1,768]{1,0:T(1,128)S(1)}, u32[]{:S(2)}, u32[]{:S(2)}) collective-permute-start(f32[1,768]{1,0:T(1,128)S(1)} %log_add_fusion.3), channel_id=1, source_target_pairs={{0,4},{1,5},{2,6},{3,7},{4,0},{5,1},{6,2},{7,3},{8,12},{9,13},{10,... | collective-permute-start | bytes 9224 | tf_op jit(solution)/shard_map/ppermute | solution.py:237
  13.7 4.5 %collective-permute-start.1 = (f32[1,768]{1,0:T(1,128)S(1)}, f32[1,768]{1,0:T(1,128)S(1)}, u32[]{:S(2)}, u32[]{:S(2)}) collective-permute-start(f32[1,768]{1,0:T(1,128)S(1)} %log_add_fusion.3), channel_id=1, source_target_pairs={{0,2},{1,3},{2,0},{3,1},{4,6},{5,7},{6,4},{7,5},{8,10},{9,11},{10,... | collective-permute-start | bytes 9224 | tf_op jit(solution)/shard_map/ppermute | solution.py:237
  18.3 7.5 %collective-permute-start.7 = (f32[1,768]{1,0:T(1,128)S(1)}, f32[1,768]{1,0:T(1,128)S(1)}, u32[]{:S(2)}, u32[]{:S(2)}) collective-permute-start(f32[1,768]{1,0:T(1,128)S(1)} %log_add_fusion.2.refs_1_.refs_0_), channel_id=1, source_target_pairs={{0,24},{1,25},{2,26},{3,27},{4,28},{5,29},{6,30},{7,31},{8,16},{9,... | collective-permute-start | bytes 9224 | tf_op jit(solution)/shard_map/ppermute | solution.py:237
  20.8 5.0 %collective-permute-start.5 = (f32[1,768]{1,0:T(1,128)S(1)}, f32[1,768]{1,0:T(1,128)S(1)}, u32[]{:S(2)}, u32[]{:S(2)}) collective-permute-start(f32[1,768]{1,0:T(1,128)S(1)} %log_add_fusion.2.refs_1_.refs_0_), channel_id=1, source_target_pairs={{0,16},{1,9},{2,18},{3,11},{4,20},{5,13},{6,22},{7,15},{8,24},{9,1... | collective-permute-start | bytes 9224 | tf_op jit(solution)/shard_map/ppermute | solution.py:237
  21.3 4.5 %collective-permute-start.4 = (f32[1,768]{1,0:T(1,128)S(1)}, f32[1,768]{1,0:T(1,128)S(1)}, u32[]{:S(2)}, u32[]{:S(2)}) collective-permute-start(f32[1,768]{1,0:T(1,128)S(1)} %log_add_fusion.2.refs_1_.refs_0_), channel_id=1, source_target_pairs={{0,8},{1,17},{2,10},{3,19},{4,12},{5,21},{6,14},{7,23},{8,0},{9,25... | collective-permute-start | bytes 9224 | tf_op jit(solution)/shard_map/ppermute | solution.py:237
  25.8 2.4 %collective-permute-start.9 = (bf16[384,1024]{1,0:T(8,128)(2,1)S(1)}, bf16[384,1024]{1,0:T(8,128)(2,1)S(1)}, u32[]{:S(2)}, u32[]{:S(2)}) collective-permute-start(bf16[384,1024]{1,0:T(8,128)(2,1)S(1)} %after.3.refs_3_), channel_id=1, source_target_pairs={{0,1},{1,0},{2,3},{3,2},{4,5},{5,4},{6,7},{7,6},{8,9},{9,8},{10,11... | collective-permute-start | bytes 2359304 | tf_op jit(solution)/shard_map/ppermute | solution.py:237
  25.9 3.4 %collective-permute-start.10 = (bf16[384,1024]{1,0:T(8,128)(2,1)S(1)}, bf16[384,1024]{1,0:T(8,128)(2,1)S(1)}, u32[]{:S(2)}, u32[]{:S(2)}) collective-permute-start(bf16[384,1024]{1,0:T(8,128)(2,1)S(1)} %after.4.refs_4_), channel_id=1, source_target_pairs={{0,1},{1,0},{2,3},{3,2},{4,5},{5,4},{6,7},{7,6},{8,9},{9,8},{10,11... | collective-permute-start | bytes 2359304 | tf_op jit(solution)/shard_map/ppermute | solution.py:237
  26.4 12.0 %collective-permute-start.11 = (bf16[384,1024]{1,0:T(8,128)(2,1)S(1)}, bf16[384,1024]{1,0:T(8,128)(2,1)S(1)}, u32[]{:S(2)}, u32[]{:S(2)}) collective-permute-start(bf16[384,1024]{1,0:T(8,128)(2,1)S(1)} %after.3.refs_3_), channel_id=1, source_target_pairs={{0,16},{1,9},{2,18},{3,11},{4,20},{5,13},{6,22},{7,15},{8,24},{9,1... | collective-permute-start | bytes 2359304 | tf_op jit(solution)/shard_map/ppermute | solution.py:237
  38.4 2.3 %collective-permute-start.12 = (bf16[384,1024]{1,0:T(8,128)(2,1)S(1)}, bf16[384,1024]{1,0:T(8,128)(2,1)S(1)}, u32[]{:S(2)}, u32[]{:S(2)}) collective-permute-start(bf16[384,1024]{1,0:T(8,128)(2,1)S(1)} %after.5.refs_1_), channel_id=1, source_target_pairs={{0,1},{1,0},{2,3},{3,2},{4,5},{5,4},{6,7},{7,6},{8,9},{9,8},{10,11... | collective-permute-start | bytes 2359304 | tf_op jit(solution)/shard_map/ppermute | solution.py:237
  44.5 1.2 %collective-permute-start.13 = (f32[4,768]{1,0:T(4,128)S(1)}, f32[4,768]{1,0:T(4,128)S(1)}, u32[]{:S(2)}, u32[]{:S(2)}) collective-permute-start(f32[4,768]{1,0:T(4,128)S(1)} %get-tuple-element.26), channel_id=1, source_target_pairs={{0,1},{1,0},{2,3},{3,2},{4,5},{5,4},{6,7},{7,6},{8,9},{9,8},{10,11... | collective-permute-start | bytes 36872 | tf_op jit(solution)/shard_map/ppermute | solution.py:237
  45.7 5.6 %collective-permute-start.16 = (f32[4,768]{1,0:T(4,128)S(1)}, f32[4,768]{1,0:T(4,128)S(1)}, u32[]{:S(2)}, u32[]{:S(2)}) collective-permute-start(f32[4,768]{1,0:T(4,128)S(1)} %log_add_fusion.1), channel_id=1, source_target_pairs={{0,6},{1,7},{2,4},{3,5},{4,2},{5,3},{6,0},{7,1},{8,14},{9,15},{10,... | collective-permute-start | bytes 36872 | tf_op jit(solution)/shard_map/ppermute | solution.py:237
  49.4 4.6 %collective-permute-start.15 = (f32[4,768]{1,0:T(4,128)S(1)}, f32[4,768]{1,0:T(4,128)S(1)}, u32[]{:S(2)}, u32[]{:S(2)}) collective-permute-start(f32[4,768]{1,0:T(4,128)S(1)} %log_add_fusion.1), channel_id=1, source_target_pairs={{0,4},{1,5},{2,6},{3,7},{4,0},{5,1},{6,2},{7,3},{8,12},{9,13},{10,... | collective-permute-start | bytes 36872 | tf_op jit(solution)/shard_map/ppermute | solution.py:237
  49.4 4.6 %collective-permute-start.14 = (f32[4,768]{1,0:T(4,128)S(1)}, f32[4,768]{1,0:T(4,128)S(1)}, u32[]{:S(2)}, u32[]{:S(2)}) collective-permute-start(f32[4,768]{1,0:T(4,128)S(1)} %log_add_fusion.1), channel_id=1, source_target_pairs={{0,2},{1,3},{2,0},{3,1},{4,6},{5,7},{6,4},{7,5},{8,10},{9,11},{10,... | collective-permute-start | bytes 36872 | tf_op jit(solution)/shard_map/ppermute | solution.py:237
  54.0 4.7 %collective-permute-start.19 = (f32[4,768]{1,0:T(4,128)S(1)}, f32[4,768]{1,0:T(4,128)S(1)}, u32[]{:S(2)}, u32[]{:S(2)}) collective-permute-start(f32[4,768]{1,0:T(4,128)S(1)} %log_add_fusion), channel_id=1, source_target_pairs={{0,24},{1,25},{2,26},{3,27},{4,28},{5,29},{6,30},{7,31},{8,16},{9,... | collective-permute-start | bytes 36872 | tf_op jit(solution)/shard_map/ppermute | solution.py:237
  55.5 3.7 %collective-permute-start.18 = (f32[4,768]{1,0:T(4,128)S(1)}, f32[4,768]{1,0:T(4,128)S(1)}, u32[]{:S(2)}, u32[]{:S(2)}) collective-permute-start(f32[4,768]{1,0:T(4,128)S(1)} %log_add_fusion), channel_id=1, source_target_pairs={{0,16},{1,17},{2,18},{3,19},{4,20},{5,21},{6,22},{7,23},{8,24},{9,... | collective-permute-start | bytes 36872 | tf_op jit(solution)/shard_map/ppermute | solution.py:237
  57.1 3.7 %collective-permute-start.17 = (f32[4,768]{1,0:T(4,128)S(1)}, f32[4,768]{1,0:T(4,128)S(1)}, u32[]{:S(2)}, u32[]{:S(2)}) collective-permute-start(f32[4,768]{1,0:T(4,128)S(1)} %log_add_fusion), channel_id=1, source_target_pairs={{0,8},{1,9},{2,10},{3,11},{4,12},{5,13},{6,14},{7,15},{8,0},{9,1},... | collective-permute-start | bytes 36872 | tf_op jit(solution)/shard_map/ppermute | solution.py:237

commit v8 on v5

v8 whole, which is shorter than its diff:
```python
import functools
import math

import jax
import jax.numpy as jnp
from jax import lax
from jax.experimental import pallas as pl
from jax.experimental.pallas import tpu as pltpu
from jax.sharding import PartitionSpec as P

BETA = 3.0
BOTH = ("item", "cent")
MIB = 1024 * 1024
NT = (((1,), (1,)), ((), ()))
NN = (((1,), (0,)), ((), ()))


def scores(rows, vectors, scale):
    raw = lax.dot_general(rows, vectors, NT, preferred_element_type=jnp.float32)
    sqnorm = jnp.sum(jnp.square(rows.astype(jnp.float32)), axis=1, keepdims=True)
    return scale * (raw - 0.5 * sqnorm)


def merge(parts):
    peak = functools.reduce(jnp.maximum, parts)
    terms = [jnp.exp(p - peak) for p in parts]
    while len(terms) > 1:
        terms = [sum(terms[i : i + 2]) for i in range(0, len(terms), 2)]
    return peak + jnp.log(terms[0])


def in_hbm(value):
    return pltpu.with_memory_space_constraint(value, pltpu.HBM)


def in_vmem(value):
    return pltpu.with_memory_space_constraint(value, pltpu.VMEM)


def copy_rows(pairs, sems):
    copies = [pltpu.make_async_copy(src, dst, sems.at[i]) for i, (src, dst) in enumerate(pairs)]
    for copy in copies:
        copy.start()
    for copy in copies:
        copy.wait()


def core_index():
    return lax.rem(lax.axis_index("cent"), 2)


def pair_index():
    return lax.rem(lax.axis_index("cent") // 2, 2)


def leads(nv, core):
    half, quarter = nv // 2, nv // 4
    rest = (1 - core) * half
    direct = rest + pair_index() * quarter
    swapped = rest + (1 - pair_index()) * quarter
    return [pl.multiple_of(lead, 64) for lead in (core * half, direct, swapped)]


def outgoing_kernel(v_hbm, half_ref, quarter_ref, sems):
    half_lead, direct, _ = leads(v_hbm.shape[0], core_index())
    rows = quarter_ref.shape[0]
    copy_rows(
        [
            (v_hbm.at[pl.ds(direct, rows), :], quarter_ref),
            (v_hbm.at[pl.ds(half_lead, rows), :], half_ref.at[pl.ds(0, rows), :]),
            (v_hbm.at[pl.ds(half_lead + rows, rows), :], half_ref.at[pl.ds(rows, rows), :]),
        ],
        sems,
    )


def outgoing(vectors):
    nv, dim = vectors.shape
    vmem = pl.BlockSpec(memory_space=pltpu.VMEM)
    return pl.pallas_call(
        outgoing_kernel,
        in_specs=[pl.BlockSpec(memory_space=pl.ANY)],
        out_specs=[vmem] * 2,
        out_shape=[pltpu.VMEM((nv // 2, dim), jnp.bfloat16), pltpu.VMEM((nv // 4, dim), jnp.bfloat16)],
        scratch_shapes=[pltpu.SemaphoreType.DMA((3,))],
        compiler_params=pltpu.CompilerParams(vmem_limit_bytes=2 * MIB),
        cost_estimate=pl.CostEstimate(flops=0, bytes_accessed=2 * nv * dim, transcendentals=0),
        name="outgoing",
    )(in_hbm(vectors))


def load_kernel(v_hbm, c_hbm, v_ref, c_ref, sems):
    pairs = []
    for src, dst, count in ((v_hbm, v_ref, 6), (c_hbm, c_ref, 8)):
        rows = dst.shape[0] // count
        pairs += [(src.at[pl.ds(i * rows, rows), :], dst.at[pl.ds(i * rows, rows), :]) for i in range(count)]
    copy_rows(pairs, sems)


def load(vectors, centroids):
    vmem = pl.BlockSpec(memory_space=pltpu.VMEM)
    hbm = pl.BlockSpec(memory_space=pl.ANY)
    return pl.pallas_call(
        load_kernel,
        in_specs=[hbm, hbm],
        out_specs=[vmem] * 2,
        out_shape=[pltpu.VMEM(vectors.shape, jnp.bfloat16), pltpu.VMEM(centroids.shape, jnp.bfloat16)],
        scratch_shapes=[pltpu.SemaphoreType.DMA((14,))],
        compiler_params=pltpu.CompilerParams(vmem_limit_bytes=2 * MIB),
        cost_estimate=pl.CostEstimate(
            flops=0, bytes_accessed=4 * (vectors.size + centroids.size), transcendentals=0
        ),
        name="load",
    )(in_hbm(vectors), in_hbm(centroids))


def partial_kernel(scale, rows, v_ref, c_ref, out_ref):
    parts = []
    for start in range(0, c_ref.shape[0], rows):
        logits = scores(c_ref[start : start + rows, :], v_ref[...], scale)
        peak = jnp.max(logits, axis=0, keepdims=True)
        parts.append(peak + jnp.log(jnp.sum(jnp.exp(logits - peak), axis=0, keepdims=True)))
    part = merge(parts)
    for i in range(out_ref.shape[0]):
        out_ref[i] = part


def partial(vectors, centroids, scale, copies):
    nv, dim = vectors.shape
    k = centroids.shape[0]
    vmem = pl.BlockSpec(memory_space=pltpu.VMEM)
    return pl.pallas_call(
        functools.partial(partial_kernel, scale, min(256, k)),
        in_specs=[vmem, vmem],
        out_specs=vmem,
        out_shape=jax.ShapeDtypeStruct((copies, 1, nv), jnp.float32),
        compiler_params=pltpu.CompilerParams(vmem_limit_bytes=12 * MIB),
        cost_estimate=pl.CostEstimate(
            flops=2 * nv * k * dim, bytes_accessed=2 * (nv + k) * dim, transcendentals=nv * k
        ),
        name="partial_lse",
    )(in_vmem(vectors), in_vmem(centroids))


def index_of(plan, place):
    if not plan["exchange"]:
        return place
    mask = (0, 1 + core_index(), 2 - core_index(), 3)[place]
    return lax.axis_index("item") ^ mask


def row_lse(plan, parts, place):
    n = plan["cents"]
    first = index_of(plan, place) * n
    return merge([parts[first + i] for i in range(n)])


def weigh(resp, vectors):
    term = lax.dot_general(resp, vectors, NN, preferred_element_type=jnp.float32)
    return term, jnp.sum(resp.astype(jnp.float32), axis=1, keepdims=True)


def updated(total, mass, old):
    return ((total + old.astype(jnp.float32)) / (mass + 1.0)).astype(jnp.bfloat16)


def own_rows(c_ref, rows):
    return c_ref[pl.ds(pl.multiple_of(lax.axis_index("item") * rows, rows), rows), :]


def absorb(own, vectors, lse, scale, total, mass):
    resp = jnp.exp(scores(own, vectors, scale) - lse).astype(jnp.bfloat16)
    term, weight = weigh(resp, vectors)
    return (term, weight) if total is None else (total + term, mass + weight)


def own_rows(c_ref, rows):
    return c_ref[pl.ds(pl.multiple_of(lax.axis_index("item") * rows, rows), rows), :]


def early_kernel(plan, scale, c_ref, parts, *refs):
    n = plan["pieces"]
    pieces, arrived, outs = refs[:n], refs[n : n + plan["arrived"]], refs[n + plan["arrived"] :]
    total, mass, done = outs[:3]
    done[...] = jnp.zeros_like(done)
    own = own_rows(c_ref, total.shape[0])
    if arrived:
        table, nv = outs[3], plan["nv"]
        core = core_index()
        half_lead, direct, swapped = leads(nv, core)
        places = [half_lead, direct, swapped]
        half_lead, direct, swapped = leads(nv, 1 - core)
        places += [nv + half_lead, nv + half_lead + nv // 4, nv + direct, nv + swapped]
        for lead, ref in zip(places, arrived):
            table[pl.ds(pl.multiple_of(lead, 64), ref.shape[0]), :] = ref[...]
        pieces += (table,)
    sums = weights = None
    for place in range(plan["early"]):
        vectors = vectors_of(plan, place, pieces)
        sums, weights = absorb(own, vectors, row_lse(plan, parts, place), scale, sums, weights)
    total[...], mass[...] = sums, weights


def vectors_of(plan, place, pieces):
    operand, start = plan["blocks"][place]
    return pieces[operand][pl.ds(start, plan["nv"]), :]


def late_kernel(plan, scale, c_ref, parts, total, mass, *refs):
    n, early = plan["pieces"], plan["early"]
    pieces, refs = refs[:n], refs[n:]
    sums, weights = total[...], mass[...]
    if early < plan["places"]:
        mine, other, new_ref, expo_ref, peak_ref, part_ref, block = refs
        pieces += (block,)
        half = mine.shape[0]
        block[pl.ds(pl.multiple_of(core_index() * half, half), half), :] = mine[...]
        block[pl.ds(pl.multiple_of((1 - core_index()) * half, half), half), :] = other[...]
    else:
        new_ref, expo_ref, peak_ref, part_ref = refs
    own = own_rows(c_ref, new_ref.shape[0])
    for place in range(early, plan["places"]):
        vectors = vectors_of(plan, place, pieces)
        sums, weights = absorb(own, vectors, row_lse(plan, parts, place), scale, sums, weights)
    new_ref[...] = updated(sums, weights, own)
    for place in range(plan["places"]):
        logits = scores(new_ref[...], vectors_of(plan, place, pieces), scale)
        peak = jnp.max(logits, axis=0, keepdims=True)
        expo = jnp.exp(logits - peak)
        expo_ref[place] = expo
        peak_ref[pl.ds(place, 1), :] = peak
        part_ref[pl.ds(index_of(plan, place), 1), :] = peak + jnp.log(jnp.sum(expo, axis=0, keepdims=True))


def last_kernel(plan, old_ref, expo_ref, peak_ref, parts, *refs):
    pieces, (new_ref, norm_ref, lse_ref) = refs[:-3], refs[-3:]
    lse_ref[...] = merge([parts[i] for i in range(parts.shape[0])])
    norm_ref[...] = lse_ref[pl.ds(lax.axis_index("item"), 1), :].reshape(norm_ref.shape)
    total = mass = None
    for place in range(plan["places"]):
        factor = jnp.exp(peak_ref[pl.ds(place, 1), :] - lse_ref[pl.ds(index_of(plan, place), 1), :])
        resp = (expo_ref[place] * factor).astype(jnp.bfloat16)
        term, weight = weigh(resp, vectors_of(plan, place, pieces))
        total = term if total is None else total + term
        mass = weight if mass is None else mass + weight
    new_ref[...] = updated(total, mass, old_ref[...])


def send(value, items, cents, item_mask, cent_mask=0):
    masks = item_mask if isinstance(item_mask, tuple) else (item_mask, item_mask)
    pairs = [
        (i * cents + c, (i ^ masks[c % 2]) * cents + (c ^ cent_mask)) for i in range(items) for c in range(cents)
    ]
    return lax.ppermute(value, BOTH, pairs)


def merge_cent(part, go):
    part = merge([part, go(part, 0, 1)])
    return merge([part] + [go(part, 0, mask) for mask in (2, 4, 6)])


def after(value, *others):
    vmem = pl.BlockSpec(memory_space=pltpu.VMEM)
    return pl.pallas_call(
        lambda *refs: None,
        in_specs=[vmem] + [pl.BlockSpec(memory_space=pl.ANY)] * len(others),
        out_specs=vmem,
        out_shape=pltpu.VMEM(value.shape, value.dtype),
        input_output_aliases={0: 0},
        compiler_params=pltpu.CompilerParams(vmem_limit_bytes=2 * MIB),
        name="after",
    )(in_vmem(value), *others)


def shards(vectors, centroids):
    items, cents = lax.axis_size("item"), lax.axis_size("cent")
    nv, dim = vectors.shape
    rows = centroids.shape[0] // items
    scale = BETA / math.sqrt(dim)

    def go(value, item_mask, cent_mask=0):
        return send(value, items, cents, item_mask, cent_mask)

    small = items == 4 and cents == 8
    if small:
        half, quarter = outgoing(vectors)
        near_quarter, near_half = go(quarter, (1, 2)), go(half, (1, 2))
        home, centroids = load(vectors, centroids)
        part = partial(home, centroids, scale, items * cents)
        parts = lax.all_to_all(part, BOTH, 0, 0, tiled=True)
        near_quarter, near_half = after(near_quarter, part), after(near_half, part)
        swapped = go(near_quarter, 0, 2)
        far = go(near_half, (2, 1))
        over = [near_half[: nv // 4], near_half[nv // 4 :], near_quarter, swapped]
        near = [near_half, near_quarter, swapped] + [go(piece, 0, 1) for piece in over]
        pieces = [home]
        plan = dict(exchange=True, cents=cents, early=3, blocks=[(0, 0), (1, 0), (1, nv), (2, 0)])
    else:
        home, centroids = load(vectors, centroids)
        parts = lax.all_gather(partial(home, centroids, scale, 1)[0], "cent", axis=0, tiled=False)
        parts = merge([parts[i] for i in range(cents)])
        parts = lax.all_gather(parts, "item", axis=0, tiled=False)
        pieces = [lax.all_gather(vectors, "item", axis=0, tiled=True)]
        near = []
        plan = dict(exchange=False, cents=1, early=items, blocks=[(0, i * nv) for i in range(items)])
    plan.update(nv=nv, places=items, pieces=len(pieces), arrived=len(near))
    pieces = [in_vmem(piece) for piece in pieces]
    centroids = in_vmem(centroids)

    vmem = pl.BlockSpec(memory_space=pltpu.VMEM)
    flops = 2 * nv * rows * dim
    early, late = plan["early"], items - plan["early"]
    params = pltpu.CompilerParams(vmem_limit_bytes=16 * MIB)
    tables = [pltpu.VMEM((2 * nv, dim), jnp.bfloat16)] if near else []
    total, mass, done, *table = pl.pallas_call(
        functools.partial(early_kernel, dict(plan), scale),
        in_specs=[vmem] * (2 + len(pieces) + len(near)),
        out_specs=[vmem] * (3 + len(tables)),
        out_shape=[
            pltpu.VMEM((rows, dim), jnp.float32),
            pltpu.VMEM((rows, 1), jnp.float32),
            jax.ShapeDtypeStruct((8, 128), jnp.float32),
        ]
        + tables,
        compiler_params=params,
        cost_estimate=pl.CostEstimate(flops=0, bytes_accessed=0, transcendentals=0),
        name="early_blocks",
    )(centroids, parts, *pieces, *[in_vmem(piece) for piece in near])
    pieces += [in_vmem(piece) for piece in table]
    plan["pieces"] = len(pieces)

    arrived = []
    if late:
        far = after(far, done)
        arrived = [in_vmem(far), in_vmem(go(far, 0, 1))]
    fresh, expo, peak, part, *block = pl.pallas_call(
        functools.partial(late_kernel, dict(plan), scale),
        in_specs=[vmem] * (4 + len(pieces) + len(arrived)),
        out_specs=[vmem] * (4 + late),
        out_shape=[
            pltpu.VMEM((rows, dim), jnp.bfloat16),
            pltpu.VMEM((items, rows, nv), jnp.float32),
            pltpu.VMEM((items, nv), jnp.float32),
            pltpu.VMEM((items, nv), jnp.float32),
        ]
        + [pltpu.VMEM((nv, dim), jnp.bfloat16)] * late,
        compiler_params=params,
        cost_estimate=pl.CostEstimate(
            flops=(items + 2 * late) * flops,
            bytes_accessed=2 * late * nv * dim,
            transcendentals=(items + late) * nv * rows,
        ),
        name="late_blocks",
    )(centroids, parts, in_vmem(total), in_vmem(mass), *pieces, *arrived)
    pieces += [in_vmem(piece) for piece in block]

    if small:
        lse = merge_cent(part, go)
        parts = merge([lse] + [go(lse, mask) for mask in (1, 2, 3)])[None]
    else:
        gathered = lax.all_gather(part, "cent", axis=0, tiled=False)
        parts = lax.all_gather(merge([gathered[i] for i in range(cents)]), "item", axis=0, tiled=False)
    result, norm = pl.pallas_call(
        functools.partial(last_kernel, dict(plan)),
        in_specs=[vmem] * (4 + len(pieces)),
        out_specs=[vmem] * 2,
        out_shape=[
            jax.ShapeDtypeStruct((rows, dim), jnp.bfloat16),
            jax.ShapeDtypeStruct((nv,), jnp.float32),
        ],
        scratch_shapes=[pltpu.VMEM((items, nv), jnp.float32)],
        compiler_params=params,
        cost_estimate=pl.CostEstimate(flops=items * flops, bytes_accessed=2 * rows * dim, transcendentals=0),
        name="last_iteration",
    )(in_vmem(fresh), in_vmem(expo), in_vmem(peak), parts, *pieces)
    return (result, norm)


def solution(mesh):
    in_specs = (P("item", None), P("cent", None))
    out_specs = (P(("cent", "item"), None), P("item"))
    return jax.shard_map(shards, mesh=mesh, in_specs=in_specs, out_specs=out_specs, check_vma=False)
```

time: 79.7 us -> 69.5 us (0.87)
  local copies, waits for them, and re-layouts: 14.1 us -> 0.05 us
  blocking collectives: 0 us -> 13.6 us
  starting transfers between devices: 22.3 us -> 16.3 us
  waiting for transfers between devices: 24.6 us -> 22.8 us
  Pallas kernels: 16.7 us -> 15.8 us
    all_to_all x0 -> x1, blocking collectives: none -> 13.6 us  [shards(): parts = lax.all_to_all(part, BOTH, 0, 0, tiled=True)]
    unnamed x26 -> x0, local copies, waits for them, and re-layouts: 12.8 us -> none
    ppermute x18 -> x16, starting transfers between devices: 22.3 us -> 16.3 us  [send(): return lax.ppermute(value, BOTH, pairs)]
    ppermute x18 -> x16, waiting for transfers between devices: 24.6 us -> 22.8 us  [send(): return lax.ppermute(value, BOTH, pairs)]
    dynamic_slice x1 -> x0, local copies, waits for them, and re-layouts: 1.31 us -> none  [shards(): give = lax.dynamic_slice_in_dim(near, core_index() * half, half, 0)]
    pallas_call x5 -> x8, Pallas kernels: 14.3 us -> 13.3 us  [the longest x1 3.75 us: shards(): pl.pallas_call(functools.partial(late_kernel, dict(plan), scale), in_spec...]
  transfers between devices with their start and end apart: 18 -> 16, of which waited for: 13 -> 8; matrix products, arithmetic and copies ran while one was open for 2% -> 0% of each run, Pallas kernels for 9% -> 12%
where the time goes in v8:
time: 69.5 us; the launch traced here: 69.3 us
  waiting for transfers between devices  22.8 us (33%)
  starting transfers between devices  16.3 us (23%)
  Pallas kernels  15.8 us (23%)
  blocking collectives  13.6 us (20%)
  between operations  0.71 us (1%)
    ppermute x16, waiting for transfers between devices, send(): return lax.ppermute(value, BOTH, pairs)  22.8 us
    ppermute x16, starting transfers between devices, send(): return lax.ppermute(value, BOTH, pairs)  16.3 us
    all_to_all x1, blocking collectives, shards(): parts = lax.all_to_all(part, BOTH, 0, 0, tiled=True)  13.6 us
    pallas_call x1, Pallas kernels, shards(): pl.pallas_call(functools.partial(late_kernel, dict(plan), scale), in_spec...  3.75 us
    pallas_call x1, Pallas kernels, shards(): pl.pallas_call(functools.partial(early_kernel, dict(plan), scale), in_spe...  3.46 us
    pallas_call x1, Pallas kernels, shards(): pl.pallas_call(functools.partial(last_kernel, dict(plan)), in_specs=[vmem...  2.71 us
    pallas_call x1, Pallas kernels, partial(): pl.pallas_call(functools.partial(partial_kernel, scale, min(256, k)), in_...  2.48 us
    pallas_call x1, Pallas kernels, load(): pl.pallas_call(load_kernel, in_specs=[hbm, hbm], out_specs=[vmem] * 2, ou...  2.09 us
  transfers between devices with their start and end apart: 16, of which 8 were waited for; matrix products, arithmetic and copies ran while one was open for 0% of the time, Pallas kernels for 12%

profile of v8, /device:TPU:0, one launch (start us, length us, event | category | flops | bytes accessed | tf_op | source)
XLA Modules:
  0.0 69.3 jit_solution(8258222853157383903)
XLA Ops:
  0.6 1.3 %outgoing.1 = (bf16[384,1024]{1,0:T(8,128)(2,1)S(1)}, bf16[192,1024]{1,0:T(8,128)(2,1)S(1)}) custom-call(bf16[768,1024]{1,0:T(8,128)(2,1)} %v_hbm.3), custom_call_target="tpu_custom_call" | custom-call | bytes 1572864 | tf_op jit(solution)/shard_map/outgoing/pallas_call | solution.py:80
  1.9 3.0 %collective-permute-start = (bf16[384,1024]{1,0:T(8,128)(2,1)S(1)}, bf16[384,1024]{1,0:T(8,128)(2,1)S(1)}, u32[]{:S(2)}, u32[]{:S(2)}) collective-permute-start(bf16[384,1024]{1,0:T(8,128)(2,1)S(1)} %get-tuple-element.17), channel_id=1, source_target_pairs={{0,8},{1,17},{2,10},{3,19},{4,12},{5,21},{6,14},{7,23},{8,0},{9,25... | collective-permute-start | bytes 2359304 | tf_op jit(solution)/shard_map/ppermute | solution.py:254
  5.0 2.1 %load.1 = (bf16[768,1024]{1,0:T(8,128)(2,1)S(1)}, bf16[1024,1024]{1,0:T(8,128)(2,1)S(1)}) custom-call(bf16[768,1024]{1,0:T(8,128)(2,1)} %v_hbm.3, bf16[1024,1024]{1,0:T(8,128)(2,1)} %c_hbm.1), custom_call_target="tpu_custom_call" | custom-call | bytes 7340032 | tf_op jit(solution)/shard_map/load/pallas_call | solution.py:103
  7.1 2.5 %partial_lse.1.refs_1_ = f32[32,1,768]{2,1,0:T(1,128)S(1)} custom-call(bf16[768,1024]{1,0:T(8,128)(2,1)S(1)} %get-tuple-element.16.v_ref.refs_0_, bf16[1024,1024]{1,0:T(8,128)(2,1)S(1)} %get-tuple-element.15.c_ref), custom_call_target="tpu_custom_call" | custom-call | flops 1610612736 | bytes 3670016 | tf_op jit(solution)/shard_map/partial_lse/pallas_call | solution.py:132
  9.6 9.5 %collective-permute-done.1.refs_0_ = bf16[192,1024]{1,0:T(8,128)(2,1)S(1)} collective-permute-done((bf16[192,1024]{1,0:T(8,128)(2,1)S(1)}, bf16[192,1024]{1,0:T(8,128)(2,1)S(1)}, u32[]{:S(2)}, u32[]{:S(2)}) %collective-permute-start.1) | collective-permute-done | bytes 393248 | tf_op jit(solution)/shard_map/ppermute | solution.py:254
  19.1 2.1 %collective-permute-start.2 = (bf16[192,1024]{1,0:T(8,128)(2,1)S(1)}, bf16[192,1024]{1,0:T(8,128)(2,1)S(1)}, u32[]{:S(2)}, u32[]{:S(2)}) collective-permute-start(bf16[192,1024]{1,0:T(8,128)(2,1)S(1)} %after.4.refs_2_), channel_id=1, source_target_pairs={{0,2},{1,3},{2,0},{3,1},{4,6},{5,7},{6,4},{7,5},{8,10},{9,11},{10,... | collective-permute-start | bytes 1179656 | tf_op jit(solution)/shard_map/ppermute | solution.py:254
  21.2 1.5 %collective-permute-start.7 = (bf16[384,1024]{1,0:T(8,128)(2,1)S(1)}, bf16[384,1024]{1,0:T(8,128)(2,1)S(1)}, u32[]{:S(2)}, u32[]{:S(2)}) collective-permute-start(bf16[384,1024]{1,0:T(8,128)(2,1)S(1)} %after.3.refs_1_), channel_id=1, source_target_pairs={{0,16},{1,9},{2,18},{3,11},{4,20},{5,13},{6,22},{7,15},{8,24},{9,1... | collective-permute-start | bytes 2359304 | tf_op jit(solution)/shard_map/ppermute | solution.py:254
  22.8 0.6 collective-permute-start.4
  23.4 6.1 %collective-permute-done.2.refs_3_ = bf16[192,1024]{1,0:T(8,128)(2,1)S(1)} collective-permute-done((bf16[192,1024]{1,0:T(8,128)(2,1)S(1)}, bf16[192,1024]{1,0:T(8,128)(2,1)S(1)}, u32[]{:S(2)}, u32[]{:S(2)}) %collective-permute-start.2) | collective-permute-done | bytes 393248 | tf_op jit(solution)/shard_map/ppermute | solution.py:254
  30.0 13.6 %all_to_all.5.parts = f32[32,1,768]{2,1,0:T(1,128)S(1)} all-to-all(f32[32,1,768]{2,1,0:T(1,128)S(1)} %partial_lse.1.refs_1_), channel_id=1, replica_groups=mesh['item'=4,'cent'=8] {'item','cent'}, dimensions={0} | all-to-all | bytes 196608 | tf_op jit(solution)/shard_map/all_to_all | solution.py:290
  43.6 3.5 %early_blocks.1 = (f32[256,1024]{1,0:T(8,128)S(1)}, f32[256,1]{1,0:T(8,128)S(1)}, f32[8,128]{1,0:T(8,128)S(1)}, bf16[1536,1024]{1,0:T(8,128)(2,1)S(1)}) custom-call(bf16[1024,1024]{1,0:T(8,128)(2,1)S(1)} %get-tuple-element.15.c_ref, f32[32,1,768]{2,1,0:T(1,128)S(1)} %all_to_all.5.parts, bf16[768,1024]{1,0:T(8,128)(2,1)S(1)} %get-tuple-element.16.v_ref.refs_0_, ...), custom_call_target="tpu_custom_call" | custom-call | tf_op jit(solution)/shard_map/early_blocks/pallas_call | solution.py:315
  47.3 2.1 %collective-permute-done.8.refs_3_ = bf16[384,1024]{1,0:T(8,128)(2,1)S(1)} collective-permute-done((bf16[384,1024]{1,0:T(8,128)(2,1)S(1)}, bf16[384,1024]{1,0:T(8,128)(2,1)S(1)}, u32[]{:S(2)}, u32[]{:S(2)}) %collective-permute-start.8) | collective-permute-done | bytes 786464 | tf_op jit(solution)/shard_map/ppermute | solution.py:254
  49.4 3.8 %late_blocks.1 = (bf16[256,1024]{1,0:T(8,128)(2,1)S(1)}, f32[4,256,768]{2,1,0:T(8,128)S(1)}, f32[4,768]{1,0:T(4,128)S(1)}, f32[4,768]{1,0:T(4,128)S(1)}, bf16[768,1024]{1,0:T(8,128)(2,1)S(1)}) custom-call(bf16[1024,1024]{1,0:T(8,128)(2,1)S(1)} %get-tuple-element.15.c_ref, f32[32,1,768]{2,1,0:T(1,128)S(1)} %all_to_all.5.parts, ...), custom_call_target="tpu_custom_call" | custom-call | flops 2415919104 | bytes 1572864 | tf_op jit(solution)/shard_map/late_blocks/pallas_call | solution.py:336
  53.5 1.0 %collective-permute-done.9 = f32[4,768]{1,0:T(4,128)S(1)} collective-permute-done((f32[4,768]{1,0:T(4,128)S(1)}, f32[4,768]{1,0:T(4,128)S(1)}, u32[]{:S(2)}, u32[]{:S(2)}) %collective-permute-start.9) | collective-permute-done | bytes 12320 | tf_op jit(solution)/shard_map/ppermute | solution.py:254
  54.5 0.9 %collective-permute-start.12 = (f32[4,768]{1,0:T(4,128)S(1)}, f32[4,768]{1,0:T(4,128)S(1)}, u32[]{:S(2)}, u32[]{:S(2)}) collective-permute-start(f32[4,768]{1,0:T(4,128)S(1)} %log_add_fusion.1), channel_id=1, source_target_pairs={{0,6},{1,7},{2,4},{3,5},{4,2},{5,3},{6,0},{7,1},{8,14},{9,15},{10,... | collective-permute-start | bytes 36872 | tf_op jit(solution)/shard_map/ppermute | solution.py:254
  55.4 1.1 %collective-permute-start.11 = (f32[4,768]{1,0:T(4,128)S(1)}, f32[4,768]{1,0:T(4,128)S(1)}, u32[]{:S(2)}, u32[]{:S(2)}) collective-permute-start(f32[4,768]{1,0:T(4,128)S(1)} %log_add_fusion.1), channel_id=1, source_target_pairs={{0,4},{1,5},{2,6},{3,7},{4,0},{5,1},{6,2},{7,3},{8,12},{9,13},{10,... | collective-permute-start | bytes 36872 | tf_op jit(solution)/shard_map/ppermute | solution.py:254
  56.4 2.5 %collective-permute-start.10 = (f32[4,768]{1,0:T(4,128)S(1)}, f32[4,768]{1,0:T(4,128)S(1)}, u32[]{:S(2)}, u32[]{:S(2)}) collective-permute-start(f32[4,768]{1,0:T(4,128)S(1)} %log_add_fusion.1), channel_id=1, source_target_pairs={{0,2},{1,3},{2,0},{3,1},{4,6},{5,7},{6,4},{7,5},{8,10},{9,11},{10,... | collective-permute-start | bytes 36872 | tf_op jit(solution)/shard_map/ppermute | solution.py:254
  58.9 1.2 %collective-permute-done.12 = f32[4,768]{1,0:T(4,128)S(1)} collective-permute-done((f32[4,768]{1,0:T(4,128)S(1)}, f32[4,768]{1,0:T(4,128)S(1)}, u32[]{:S(2)}, u32[]{:S(2)}) %collective-permute-start.12) | collective-permute-done | bytes 12320 | tf_op jit(solution)/shard_map/ppermute | solution.py:254
  60.6 0.9 %collective-permute-start.15 = (f32[4,768]{1,0:T(4,128)S(1)}, f32[4,768]{1,0:T(4,128)S(1)}, u32[]{:S(2)}, u32[]{:S(2)}) collective-permute-start(f32[4,768]{1,0:T(4,128)S(1)} %log_add_fusion), channel_id=1, source_target_pairs={{0,24},{1,25},{2,26},{3,27},{4,28},{5,29},{6,30},{7,31},{8,16},{9,... | collective-permute-start | bytes 36872 | tf_op jit(solution)/shard_map/ppermute | solution.py:254
  61.6 1.3 %collective-permute-start.14 = (f32[4,768]{1,0:T(4,128)S(1)}, f32[4,768]{1,0:T(4,128)S(1)}, u32[]{:S(2)}, u32[]{:S(2)}) collective-permute-start(f32[4,768]{1,0:T(4,128)S(1)} %log_add_fusion), channel_id=1, source_target_pairs={{0,16},{1,17},{2,18},{3,19},{4,20},{5,21},{6,22},{7,23},{8,24},{9,... | collective-permute-start | bytes 36872 | tf_op jit(solution)/shard_map/ppermute | solution.py:254
  62.9 1.3 %collective-permute-start.13 = (f32[4,768]{1,0:T(4,128)S(1)}, f32[4,768]{1,0:T(4,128)S(1)}, u32[]{:S(2)}, u32[]{:S(2)}) collective-permute-start(f32[4,768]{1,0:T(4,128)S(1)} %log_add_fusion), channel_id=1, source_target_pairs={{0,8},{1,9},{2,10},{3,11},{4,12},{5,13},{6,14},{7,15},{8,0},{9,1},... | collective-permute-start | bytes 36872 | tf_op jit(solution)/shard_map/ppermute | solution.py:254
  64.2 1.2 %collective-permute-done.15 = f32[4,768]{1,0:T(4,128)S(1)} collective-permute-done((f32[4,768]{1,0:T(4,128)S(1)}, f32[4,768]{1,0:T(4,128)S(1)}, u32[]{:S(2)}, u32[]{:S(2)}) %collective-permute-start.15) | collective-permute-done | bytes 12320 | tf_op jit(solution)/shard_map/ppermute | solution.py:254
  65.4 1.2 %collective-permute-done.13 = f32[4,768]{1,0:T(4,128)S(1)} collective-permute-done((f32[4,768]{1,0:T(4,128)S(1)}, f32[4,768]{1,0:T(4,128)S(1)}, u32[]{:S(2)}, u32[]{:S(2)}) %collective-permute-start.13) | collective-permute-done | bytes 12320 | tf_op jit(solution)/shard_map/ppermute | solution.py:254
  66.6 2.7 %last_iteration.1 = (bf16[256,1024]{1,0:T(8,128)(2,1)}, f32[768]{0:T(1024)}) custom-call(bf16[256,1024]{1,0:T(8,128)(2,1)S(1)} %get-tuple-element.23.old_ref, f32[4,256,768]{2,1,0:T(8,128)S(1)} %get-tuple-element.24.expo_ref, f32[4,768]{1,0:T(4,128)S(1)} %get-tuple-element.25.peak_ref, f32[1,4,768]{2,1,0:T(4,128)S(1)} %add_bitcast_fusion.parts, ...), custom_call_target="tpu_custom_call" | custom-call | flops 1610612736 | bytes 524288 | tf_op jit(solution)/shard_map/last_iteration/pallas_call | solution.py:363
  (22 shorter events, 1.8 us)
Async XLA Ops:
  1.9 19.3 %collective-permute-start = (bf16[384,1024]{1,0:T(8,128)(2,1)S(1)}, bf16[384,1024]{1,0:T(8,128)(2,1)S(1)}, u32[]{:S(2)}, u32[]{:S(2)}) collective-permute-start(bf16[384,1024]{1,0:T(8,128)(2,1)S(1)} %get-tuple-element.17), channel_id=1, source_target_pairs={{0,8},{1,17},{2,10},{3,19},{4,12},{5,21},{6,14},{7,23},{8,0},{9,25... | collective-permute-start | bytes 2359304 | tf_op jit(solution)/shard_map/ppermute | solution.py:254
  4.9 14.2 %collective-permute-start.1 = (bf16[192,1024]{1,0:T(8,128)(2,1)S(1)}, bf16[192,1024]{1,0:T(8,128)(2,1)S(1)}, u32[]{:S(2)}, u32[]{:S(2)}) collective-permute-start(bf16[192,1024]{1,0:T(8,128)(2,1)S(1)} %get-tuple-element.18), channel_id=1, source_target_pairs={{0,8},{1,17},{2,10},{3,19},{4,12},{5,21},{6,14},{7,23},{8,0},{9,25... | collective-permute-start | bytes 1179656 | tf_op jit(solution)/shard_map/ppermute | solution.py:254
  19.1 10.4 %collective-permute-start.2 = (bf16[192,1024]{1,0:T(8,128)(2,1)S(1)}, bf16[192,1024]{1,0:T(8,128)(2,1)S(1)}, u32[]{:S(2)}, u32[]{:S(2)}) collective-permute-start(bf16[192,1024]{1,0:T(8,128)(2,1)S(1)} %after.4.refs_2_), channel_id=1, source_target_pairs={{0,2},{1,3},{2,0},{3,1},{4,6},{5,7},{6,4},{7,5},{8,10},{9,11},{10,... | collective-permute-start | bytes 1179656 | tf_op jit(solution)/shard_map/ppermute | solution.py:254
  21.2 25.9 %collective-permute-start.7 = (bf16[384,1024]{1,0:T(8,128)(2,1)S(1)}, bf16[384,1024]{1,0:T(8,128)(2,1)S(1)}, u32[]{:S(2)}, u32[]{:S(2)}) collective-permute-start(bf16[384,1024]{1,0:T(8,128)(2,1)S(1)} %after.3.refs_1_), channel_id=1, source_target_pairs={{0,16},{1,9},{2,18},{3,11},{4,20},{5,13},{6,22},{7,15},{8,24},{9,1... | collective-permute-start | bytes 2359304 | tf_op jit(solution)/shard_map/ppermute | solution.py:254
  22.7 20.8 %collective-permute-start.5 = (bf16[192,1024]{1,0:T(8,128)(2,1)S(1)}, bf16[192,1024]{1,0:T(8,128)(2,1)S(1)}, u32[]{:S(2)}, u32[]{:S(2)}) collective-permute-start(bf16[192,1024]{1,0:T(8,128)(2,1)S(1)} %after.4.refs_2_), channel_id=1, source_target_pairs={{0,1},{1,0},{2,3},{3,2},{4,5},{5,4},{6,7},{7,6},{8,9},{9,8},{10,11... | collective-permute-start | bytes 1179656 | tf_op jit(solution)/shard_map/ppermute | solution.py:254
  22.8 20.8 %collective-permute-start.4 = (bf16[192,1024]{1,0:T(8,128)(2,1)S(1)}, bf16[192,1024]{1,0:T(8,128)(2,1)S(1)}, u32[]{:S(2)}, u32[]{:S(2)}) collective-permute-start(bf16[192,1024]{1,0:T(8,128)(2,1)S(1)} %get-tuple-element.28), channel_id=1, source_target_pairs={{0,1},{1,0},{2,3},{3,2},{4,5},{5,4},{6,7},{7,6},{8,9},{9,8},{10,11... | collective-permute-start | bytes 1179656 | tf_op jit(solution)/shard_map/ppermute | solution.py:254
  29.5 14.1 %collective-permute-start.6 = (bf16[192,1024]{1,0:T(8,128)(2,1)S(1)}, bf16[192,1024]{1,0:T(8,128)(2,1)S(1)}, u32[]{:S(2)}, u32[]{:S(2)}) collective-permute-start(bf16[192,1024]{1,0:T(8,128)(2,1)S(1)} %collective-permute-done.2.refs_3_), channel_id=1, source_target_pairs={{0,1},{1,0},{2,3},{3,2},{4,5},{5,4},{6,7},{7,6},{8,9},{9,8},{10,11... | collective-permute-start | bytes 1179656 | tf_op jit(solution)/shard_map/ppermute | solution.py:254
  29.5 14.1 %collective-permute-start.3 = (bf16[192,1024]{1,0:T(8,128)(2,1)S(1)}, bf16[192,1024]{1,0:T(8,128)(2,1)S(1)}, u32[]{:S(2)}, u32[]{:S(2)}) collective-permute-start(bf16[192,1024]{1,0:T(8,128)(2,1)S(1)} %get-tuple-element.29), channel_id=1, source_target_pairs={{0,1},{1,0},{2,3},{3,2},{4,5},{5,4},{6,7},{7,6},{8,9},{9,8},{10,11... | collective-permute-start | bytes 1179656 | tf_op jit(solution)/shard_map/ppermute | solution.py:254
  47.1 2.4 %collective-permute-start.8 = (bf16[384,1024]{1,0:T(8,128)(2,1)S(1)}, bf16[384,1024]{1,0:T(8,128)(2,1)S(1)}, u32[]{:S(2)}, u32[]{:S(2)}) collective-permute-start(bf16[384,1024]{1,0:T(8,128)(2,1)S(1)} %after.5.refs_2_), channel_id=1, source_target_pairs={{0,1},{1,0},{2,3},{3,2},{4,5},{5,4},{6,7},{7,6},{8,9},{9,8},{10,11... | collective-permute-start | bytes 2359304 | tf_op jit(solution)/shard_map/ppermute | solution.py:254
  53.2 1.2 %collective-permute-start.9 = (f32[4,768]{1,0:T(4,128)S(1)}, f32[4,768]{1,0:T(4,128)S(1)}, u32[]{:S(2)}, u32[]{:S(2)}) collective-permute-start(f32[4,768]{1,0:T(4,128)S(1)} %get-tuple-element.26), channel_id=1, source_target_pairs={{0,1},{1,0},{2,3},{3,2},{4,5},{5,4},{6,7},{7,6},{8,9},{9,8},{10,11... | collective-permute-start | bytes 36872 | tf_op jit(solution)/shard_map/ppermute | solution.py:254
  54.5 5.7 %collective-permute-start.12 = (f32[4,768]{1,0:T(4,128)S(1)}, f32[4,768]{1,0:T(4,128)S(1)}, u32[]{:S(2)}, u32[]{:S(2)}) collective-permute-start(f32[4,768]{1,0:T(4,128)S(1)} %log_add_fusion.1), channel_id=1, source_target_pairs={{0,6},{1,7},{2,4},{3,5},{4,2},{5,3},{6,0},{7,1},{8,14},{9,15},{10,... | collective-permute-start | bytes 36872 | tf_op jit(solution)/shard_map/ppermute | solution.py:254
  55.4 4.7 %collective-permute-start.11 = (f32[4,768]{1,0:T(4,128)S(1)}, f32[4,768]{1,0:T(4,128)S(1)}, u32[]{:S(2)}, u32[]{:S(2)}) collective-permute-start(f32[4,768]{1,0:T(4,128)S(1)} %log_add_fusion.1), channel_id=1, source_target_pairs={{0,4},{1,5},{2,6},{3,7},{4,0},{5,1},{6,2},{7,3},{8,12},{9,13},{10,... | collective-permute-start | bytes 36872 | tf_op jit(solution)/shard_map/ppermute | solution.py:254
  56.4 4.1 %collective-permute-start.10 = (f32[4,768]{1,0:T(4,128)S(1)}, f32[4,768]{1,0:T(4,128)S(1)}, u32[]{:S(2)}, u32[]{:S(2)}) collective-permute-start(f32[4,768]{1,0:T(4,128)S(1)} %log_add_fusion.1), channel_id=1, source_target_pairs={{0,2},{1,3},{2,0},{3,1},{4,6},{5,7},{6,4},{7,5},{8,10},{9,11},{10,... | collective-permute-start | bytes 36872 | tf_op jit(solution)/shard_map/ppermute | solution.py:254
  60.6 4.8 %collective-permute-start.15 = (f32[4,768]{1,0:T(4,128)S(1)}, f32[4,768]{1,0:T(4,128)S(1)}, u32[]{:S(2)}, u32[]{:S(2)}) collective-permute-start(f32[4,768]{1,0:T(4,128)S(1)} %log_add_fusion), channel_id=1, source_target_pairs={{0,24},{1,25},{2,26},{3,27},{4,28},{5,29},{6,30},{7,31},{8,16},{9,... | collective-permute-start | bytes 36872 | tf_op jit(solution)/shard_map/ppermute | solution.py:254
  61.6 3.8 %collective-permute-start.14 = (f32[4,768]{1,0:T(4,128)S(1)}, f32[4,768]{1,0:T(4,128)S(1)}, u32[]{:S(2)}, u32[]{:S(2)}) collective-permute-start(f32[4,768]{1,0:T(4,128)S(1)} %log_add_fusion), channel_id=1, source_target_pairs={{0,16},{1,17},{2,18},{3,19},{4,20},{5,21},{6,22},{7,23},{8,24},{9,... | collective-permute-start | bytes 36872 | tf_op jit(solution)/shard_map/ppermute | solution.py:254
  62.9 3.7 %collective-permute-start.13 = (f32[4,768]{1,0:T(4,128)S(1)}, f32[4,768]{1,0:T(4,128)S(1)}, u32[]{:S(2)}, u32[]{:S(2)}) collective-permute-start(f32[4,768]{1,0:T(4,128)S(1)} %log_add_fusion), channel_id=1, source_target_pairs={{0,8},{1,9},{2,10},{3,11},{4,12},{5,13},{6,14},{7,15},{8,0},{9,1},... | collective-permute-start | bytes 36872 | tf_op jit(solution)/shard_map/ppermute | solution.py:254

commit v9 on v8

--- a/solution.py
+++ b/solution.py
@@ -120,12 +120,10 @@
         logits = scores(c_ref[start : start + rows, :], v_ref[...], scale)
         peak = jnp.max(logits, axis=0, keepdims=True)
         parts.append(peak + jnp.log(jnp.sum(jnp.exp(logits - peak), axis=0, keepdims=True)))
-    part = merge(parts)
-    for i in range(out_ref.shape[0]):
-        out_ref[i] = part
-
-
-def partial(vectors, centroids, scale, copies):
+    out_ref[...] = merge(parts)
+
+
+def partial(vectors, centroids, scale):
     nv, dim = vectors.shape
     k = centroids.shape[0]
     vmem = pl.BlockSpec(memory_space=pltpu.VMEM)
@@ -133,7 +131,7 @@
         functools.partial(partial_kernel, scale, min(256, k)),
         in_specs=[vmem, vmem],
         out_specs=vmem,
-        out_shape=jax.ShapeDtypeStruct((copies, 1, nv), jnp.float32),
+        out_shape=jax.ShapeDtypeStruct((1, nv), jnp.float32),
         compiler_params=pltpu.CompilerParams(vmem_limit_bytes=12 * MIB),
         cost_estimate=pl.CostEstimate(
             flops=2 * nv * k * dim, bytes_accessed=2 * (nv + k) * dim, transcendentals=nv * k
@@ -149,12 +147,6 @@
     return lax.axis_index("item") ^ mask
 
 
-def row_lse(plan, parts, place):
-    n = plan["cents"]
-    first = index_of(plan, place) * n
-    return merge([parts[first + i] for i in range(n)])
-
-
 def weigh(resp, vectors):
     term = lax.dot_general(resp, vectors, NN, preferred_element_type=jnp.float32)
     return term, jnp.sum(resp.astype(jnp.float32), axis=1, keepdims=True)
@@ -178,14 +170,14 @@
     return c_ref[pl.ds(pl.multiple_of(lax.axis_index("item") * rows, rows), rows), :]
 
 
-def early_kernel(plan, scale, c_ref, parts, *refs):
+def early_kernel(plan, scale, c_ref, *refs):
     n = plan["pieces"]
+    rows, refs = refs[: plan["early"]], refs[plan["early"] :]
     pieces, arrived, outs = refs[:n], refs[n : n + plan["arrived"]], refs[n + plan["arrived"] :]
-    total, mass, done = outs[:3]
-    done[...] = jnp.zeros_like(done)
+    total, mass = outs[:2]
     own = own_rows(c_ref, total.shape[0])
     if arrived:
-        table, nv = outs[3], plan["nv"]
+        table, nv = outs[2], plan["nv"]
         core = core_index()
         half_lead, direct, swapped = leads(nv, core)
         places = [half_lead, direct, swapped]
@@ -197,7 +189,7 @@
     sums = weights = None
     for place in range(plan["early"]):
         vectors = vectors_of(plan, place, pieces)
-        sums, weights = absorb(own, vectors, row_lse(plan, parts, place), scale, sums, weights)
+        sums, weights = absorb(own, vectors, rows[place][...], scale, sums, weights)
     total[...], mass[...] = sums, weights
 
 
@@ -206,8 +198,9 @@
     return pieces[operand][pl.ds(start, plan["nv"]), :]
 
 
-def late_kernel(plan, scale, c_ref, parts, total, mass, *refs):
+def late_kernel(plan, scale, c_ref, total, mass, *refs):
     n, early = plan["pieces"], plan["early"]
+    rows, refs = refs[: plan["places"] - early], refs[plan["places"] - early :]
     pieces, refs = refs[:n], refs[n:]
     sums, weights = total[...], mass[...]
     if early < plan["places"]:
@@ -221,7 +214,7 @@
     own = own_rows(c_ref, new_ref.shape[0])
     for place in range(early, plan["places"]):
         vectors = vectors_of(plan, place, pieces)
-        sums, weights = absorb(own, vectors, row_lse(plan, parts, place), scale, sums, weights)
+        sums, weights = absorb(own, vectors, rows[place - early][...], scale, sums, weights)
     new_ref[...] = updated(sums, weights, own)
     for place in range(plan["places"]):
         logits = scores(new_ref[...], vectors_of(plan, place, pieces), scale)
@@ -286,23 +279,24 @@
         half, quarter = outgoing(vectors)
         near_quarter, near_half = go(quarter, (1, 2)), go(half, (1, 2))
         home, centroids = load(vectors, centroids)
-        part = partial(home, centroids, scale, items * cents)
-        parts = lax.all_to_all(part, BOTH, 0, 0, tiled=True)
-        near_quarter, near_half = after(near_quarter, part), after(near_half, part)
+        lse = merge_cent(partial(home, centroids, scale), go)
+        parts = [lse, go(lse, (1, 2)), go(lse, (2, 1)), go(lse, 3)]
+        near_quarter, near_half = after(near_quarter, lse), after(near_half, lse)
         swapped = go(near_quarter, 0, 2)
         far = go(near_half, (2, 1))
         over = [near_half[: nv // 4], near_half[nv // 4 :], near_quarter, swapped]
         near = [near_half, near_quarter, swapped] + [go(piece, 0, 1) for piece in over]
         pieces = [home]
-        plan = dict(exchange=True, cents=cents, early=3, blocks=[(0, 0), (1, 0), (1, nv), (2, 0)])
+        plan = dict(exchange=True, early=3, blocks=[(0, 0), (1, 0), (1, nv), (2, 0)])
     else:
         home, centroids = load(vectors, centroids)
-        parts = lax.all_gather(partial(home, centroids, scale, 1)[0], "cent", axis=0, tiled=False)
+        parts = lax.all_gather(partial(home, centroids, scale), "cent", axis=0, tiled=False)
         parts = merge([parts[i] for i in range(cents)])
         parts = lax.all_gather(parts, "item", axis=0, tiled=False)
+        parts = [parts[i] for i in range(items)]
         pieces = [lax.all_gather(vectors, "item", axis=0, tiled=True)]
         near = []
-        plan = dict(exchange=False, cents=1, early=items, blocks=[(0, i * nv) for i in range(items)])
+        plan = dict(exchange=False, early=items, blocks=[(0, i * nv) for i in range(items)])
     plan.update(nv=nv, places=items, pieces=len(pieces), arrived=len(near))
     pieces = [in_vmem(piece) for piece in pieces]
     centroids = in_vmem(centroids)
@@ -312,30 +306,29 @@
     early, late = plan["early"], items - plan["early"]
     params = pltpu.CompilerParams(vmem_limit_bytes=16 * MIB)
     tables = [pltpu.VMEM((2 * nv, dim), jnp.bfloat16)] if near else []
-    total, mass, done, *table = pl.pallas_call(
+    total, mass, *table = pl.pallas_call(
         functools.partial(early_kernel, dict(plan), scale),
-        in_specs=[vmem] * (2 + len(pieces) + len(near)),
-        out_specs=[vmem] * (3 + len(tables)),
+        in_specs=[vmem] * (1 + early + len(pieces) + len(near)),
+        out_specs=[vmem] * (2 + len(tables)),
         out_shape=[
             pltpu.VMEM((rows, dim), jnp.float32),
             pltpu.VMEM((rows, 1), jnp.float32),
-            jax.ShapeDtypeStruct((8, 128), jnp.float32),
         ]
         + tables,
         compiler_params=params,
         cost_estimate=pl.CostEstimate(flops=0, bytes_accessed=0, transcendentals=0),
         name="early_blocks",
-    )(centroids, parts, *pieces, *[in_vmem(piece) for piece in near])
+    )(centroids, *parts[:early], *pieces, *[in_vmem(piece) for piece in near])
     pieces += [in_vmem(piece) for piece in table]
     plan["pieces"] = len(pieces)
 
     arrived = []
     if late:
-        far = after(far, done)
+        far = after(far, *parts[1:], *near[3:])
         arrived = [in_vmem(far), in_vmem(go(far, 0, 1))]
     fresh, expo, peak, part, *block = pl.pallas_call(
         functools.partial(late_kernel, dict(plan), scale),
-        in_specs=[vmem] * (4 + len(pieces) + len(arrived)),
+        in_specs=[vmem] * (3 + late + len(pieces) + len(arrived)),
         out_specs=[vmem] * (4 + late),
         out_shape=[
             pltpu.VMEM((rows, dim), jnp.bfloat16),
@@ -351,7 +344,7 @@
             transcendentals=(items + late) * nv * rows,
         ),
         name="late_blocks",
-    )(centroids, parts, in_vmem(total), in_vmem(mass), *pieces, *arrived)
+    )(centroids, in_vmem(total), in_vmem(mass), *parts[early:], *pieces, *arrived)
     pieces += [in_vmem(piece) for piece in block]
 
     if small:

time: 69.5 us -> 61.8 us (0.89)
  blocking collectives: 13.6 us -> 0 us
  starting transfers between devices: 16.3 us -> 29.5 us
  waiting for transfers between devices: 22.8 us -> 15.4 us
    all_to_all x1 -> x0, blocking collectives: 13.6 us -> none  [shards(): parts = lax.all_to_all(part, BOTH, 0, 0, tiled=True)]
    ppermute x16 -> x23, starting transfers between devices: 16.3 us -> 29.5 us  [send(): return lax.ppermute(value, BOTH, pairs)]
    ppermute x16 -> x23, waiting for transfers between devices: 22.8 us -> 15.4 us  [send(): return lax.ppermute(value, BOTH, pairs)]
  transfers between devices with their start and end apart: 16 -> 23, of which waited for: 8 -> 14; matrix products, arithmetic and copies ran while one was open for 0% -> 0% of each run, Pallas kernels for 12% -> 13%
where the time goes in v9:
time: 61.8 us; the launch traced here: 61.6 us
  starting transfers between devices  29.5 us (48%)
  Pallas kernels  15.8 us (26%)
  waiting for transfers between devices  15.4 us (25%)
  between operations  0.71 us (1%)
    ppermute x23, starting transfers between devices, send(): return lax.ppermute(value, BOTH, pairs)  29.5 us
    ppermute x23, waiting for transfers between devices, send(): return lax.ppermute(value, BOTH, pairs)  15.4 us
    pallas_call x1, Pallas kernels, shards(): pl.pallas_call(functools.partial(late_kernel, dict(plan), scale), in_spec...  3.82 us
    pallas_call x1, Pallas kernels, shards(): pl.pallas_call(functools.partial(early_kernel, dict(plan), scale), in_spe...  3.48 us
    pallas_call x1, Pallas kernels, shards(): pl.pallas_call(functools.partial(last_kernel, dict(plan)), in_specs=[vmem...  2.71 us
    pallas_call x1, Pallas kernels, partial(): pl.pallas_call(functools.partial(partial_kernel, scale, min(256, k)), in_...  2.46 us
    pallas_call x1, Pallas kernels, load(): pl.pallas_call(load_kernel, in_specs=[hbm, hbm], out_specs=[vmem] * 2, ou...  2.09 us
    pallas_call x1, Pallas kernels, outgoing(): pl.pallas_call(outgoing_kernel, in_specs=[pl.BlockSpec(memory_space=pl.AN...  1.28 us
  transfers between devices with their start and end apart: 23, of which 14 were waited for; matrix products, arithmetic and copies ran while one was open for 0% of the time, Pallas kernels for 13%

profile of v9, /device:TPU:0, one launch (start us, length us, event | category | flops | bytes accessed | tf_op | source)
XLA Modules:
  0.0 61.6 jit_solution(13627440629080305380)
XLA Ops:
  0.6 1.3 %outgoing.1 = (bf16[384,1024]{1,0:T(8,128)(2,1)S(1)}, bf16[192,1024]{1,0:T(8,128)(2,1)S(1)}) custom-call(bf16[768,1024]{1,0:T(8,128)(2,1)} %v_hbm.3), custom_call_target="tpu_custom_call" | custom-call | bytes 1572864 | tf_op jit(solution)/shard_map/outgoing/pallas_call | solution.py:80
  1.9 3.0 %collective-permute-start.6 = (bf16[384,1024]{1,0:T(8,128)(2,1)S(1)}, bf16[384,1024]{1,0:T(8,128)(2,1)S(1)}, u32[]{:S(2)}, u32[]{:S(2)}) collective-permute-start(bf16[384,1024]{1,0:T(8,128)(2,1)S(1)} %get-tuple-element.16), channel_id=1, source_target_pairs={{0,8},{1,17},{2,10},{3,19},{4,12},{5,21},{6,14},{7,23},{8,0},{9,25... | collective-permute-start | bytes 2359304 | tf_op jit(solution)/shard_map/ppermute | solution.py:247
  4.9 2.1 %load.1 = (bf16[768,1024]{1,0:T(8,128)(2,1)S(1)}, bf16[1024,1024]{1,0:T(8,128)(2,1)S(1)}) custom-call(bf16[768,1024]{1,0:T(8,128)(2,1)} %v_hbm.3, bf16[1024,1024]{1,0:T(8,128)(2,1)} %c_hbm.1), custom_call_target="tpu_custom_call" | custom-call | bytes 7340032 | tf_op jit(solution)/shard_map/load/pallas_call | solution.py:103
  7.0 2.5 %partial_lse.1 = f32[1,768]{1,0:T(1,128)S(1)} custom-call(bf16[768,1024]{1,0:T(8,128)(2,1)S(1)} %get-tuple-element.15.v_ref.refs_3_.refs_1_.refs_0_, bf16[1024,1024]{1,0:T(8,128)(2,1)S(1)} %get-tuple-element.14.c_ref), custom_call_target="tpu_custom_call" | custom-call | flops 1610612736 | bytes 3670016 | tf_op jit(solution)/shard_map/partial_lse/pallas_call | solution.py:130
  9.6 1.1 %collective-permute-start.7 = (bf16[192,1024]{1,0:T(8,128)(2,1)S(1)}, bf16[192,1024]{1,0:T(8,128)(2,1)S(1)}, u32[]{:S(2)}, u32[]{:S(2)}) collective-permute-start(bf16[192,1024]{1,0:T(8,128)(2,1)S(1)} %get-tuple-element.17), channel_id=1, source_target_pairs={{0,8},{1,17},{2,10},{3,19},{4,12},{5,21},{6,14},{7,23},{8,0},{9,25... | collective-permute-start | bytes 1179656 | tf_op jit(solution)/shard_map/ppermute | solution.py:247
  10.7 3.7 %collective-permute-start.3 = (f32[1,768]{1,0:T(1,128)S(1)}, f32[1,768]{1,0:T(1,128)S(1)}, u32[]{:S(2)}, u32[]{:S(2)}) collective-permute-start(f32[1,768]{1,0:T(1,128)S(1)} %log_add_fusion.3), channel_id=1, source_target_pairs={{0,6},{1,7},{2,4},{3,5},{4,2},{5,3},{6,0},{7,1},{8,14},{9,15},{10,... | collective-permute-start | bytes 9224 | tf_op jit(solution)/shard_map/ppermute | solution.py:247
  16.2 2.7 %collective-permute-done.2 = f32[1,768]{1,0:T(1,128)S(1)} collective-permute-done((f32[1,768]{1,0:T(1,128)S(1)}, f32[1,768]{1,0:T(1,128)S(1)}, u32[]{:S(2)}, u32[]{:S(2)}) %collective-permute-start.2) | collective-permute-done | bytes 3104 | tf_op jit(solution)/shard_map/ppermute | solution.py:247
  19.1 2.1 %collective-permute-start.8 = (bf16[192,1024]{1,0:T(8,128)(2,1)S(1)}, bf16[192,1024]{1,0:T(8,128)(2,1)S(1)}, u32[]{:S(2)}, u32[]{:S(2)}) collective-permute-start(bf16[192,1024]{1,0:T(8,128)(2,1)S(1)} %after.4.refs_5_), channel_id=1, source_target_pairs={{0,2},{1,3},{2,0},{3,1},{4,6},{5,7},{6,4},{7,5},{8,10},{9,11},{10,... | collective-permute-start | bytes 1179656 | tf_op jit(solution)/shard_map/ppermute | solution.py:247
  21.2 1.5 %collective-permute-start.14 = (bf16[384,1024]{1,0:T(8,128)(2,1)S(1)}, bf16[384,1024]{1,0:T(8,128)(2,1)S(1)}, u32[]{:S(2)}, u32[]{:S(2)}) collective-permute-start(bf16[384,1024]{1,0:T(8,128)(2,1)S(1)} %after.3.refs_4_), channel_id=1, source_target_pairs={{0,16},{1,9},{2,18},{3,11},{4,20},{5,13},{6,22},{7,15},{8,24},{9,1... | collective-permute-start | bytes 2359304 | tf_op jit(solution)/shard_map/ppermute | solution.py:247
  22.7 1.4 %collective-permute-start.13 = (f32[1,768]{1,0:T(1,128)S(1)}, f32[1,768]{1,0:T(1,128)S(1)}, u32[]{:S(2)}, u32[]{:S(2)}) collective-permute-start(f32[1,768]{1,0:T(1,128)S(1)} %log_add_fusion.2.refs_1_.refs_0_), channel_id=1, source_target_pairs={{0,24},{1,25},{2,26},{3,27},{4,28},{5,29},{6,30},{7,31},{8,16},{9,... | collective-permute-start | bytes 9224 | tf_op jit(solution)/shard_map/ppermute | solution.py:247
  24.2 1.5 %collective-permute-start.5 = (f32[1,768]{1,0:T(1,128)S(1)}, f32[1,768]{1,0:T(1,128)S(1)}, u32[]{:S(2)}, u32[]{:S(2)}) collective-permute-start(f32[1,768]{1,0:T(1,128)S(1)} %log_add_fusion.2.refs_1_.refs_0_), channel_id=1, source_target_pairs={{0,16},{1,9},{2,18},{3,11},{4,20},{5,13},{6,22},{7,15},{8,24},{9,1... | collective-permute-start | bytes 9224 | tf_op jit(solution)/shard_map/ppermute | solution.py:247
  27.3 4.6 %collective-permute-start.11 = (bf16[192,1024]{1,0:T(8,128)(2,1)S(1)}, bf16[192,1024]{1,0:T(8,128)(2,1)S(1)}, u32[]{:S(2)}, u32[]{:S(2)}) collective-permute-start(bf16[192,1024]{1,0:T(8,128)(2,1)S(1)} %after.4.refs_5_), channel_id=1, source_target_pairs={{0,1},{1,0},{2,3},{3,2},{4,5},{5,4},{6,7},{7,6},{8,9},{9,8},{10,11... | collective-permute-start | bytes 1179656 | tf_op jit(solution)/shard_map/ppermute | solution.py:247
  31.9 1.4 %collective-permute-done.5.refs_2_ = f32[1,768]{1,0:T(1,128)S(1)} collective-permute-done((f32[1,768]{1,0:T(1,128)S(1)}, f32[1,768]{1,0:T(1,128)S(1)}, u32[]{:S(2)}, u32[]{:S(2)}) %collective-permute-start.5) | collective-permute-done | bytes 3104 | tf_op jit(solution)/shard_map/ppermute | solution.py:247
  33.9 1.7 %collective-permute-done.12.refs_10_.refs_7_ = bf16[192,1024]{1,0:T(8,128)(2,1)S(1)} collective-permute-done((bf16[192,1024]{1,0:T(8,128)(2,1)S(1)}, bf16[192,1024]{1,0:T(8,128)(2,1)S(1)}, u32[]{:S(2)}, u32[]{:S(2)}) %collective-permute-start.12) | collective-permute-done | bytes 393248 | tf_op jit(solution)/shard_map/ppermute | solution.py:247
  36.3 3.5 %early_blocks.1 = (f32[256,1024]{1,0:T(8,128)S(1)}, f32[256,1]{1,0:T(8,128)S(1)}, bf16[1536,1024]{1,0:T(8,128)(2,1)S(1)}) custom-call(bf16[1024,1024]{1,0:T(8,128)(2,1)S(1)} %get-tuple-element.14.c_ref, f32[1,768]{1,0:T(1,128)S(1)} %log_add_fusion.2.refs_1_.refs_0_, f32[1,768]{1,0:T(1,128)S(1)} %collective-permute-done.4.refs_1_, ...), custom_call_target="tpu_custom_call" | custom-call | tf_op jit(solution)/shard_map/early_blocks/pallas_call | solution.py:309
  39.8 3.8 %late_blocks.1 = (bf16[256,1024]{1,0:T(8,128)(2,1)S(1)}, f32[4,256,768]{2,1,0:T(8,128)S(1)}, f32[4,768]{1,0:T(4,128)S(1)}, f32[4,768]{1,0:T(4,128)S(1)}, bf16[768,1024]{1,0:T(8,128)(2,1)S(1)}) custom-call(bf16[1024,1024]{1,0:T(8,128)(2,1)S(1)} %get-tuple-element.14.c_ref, f32[256,1024]{1,0:T(8,128)S(1)} %get-tuple-element.18.total, ...), custom_call_target="tpu_custom_call" | custom-call | flops 2415919104 | bytes 1572864 | tf_op jit(solution)/shard_map/late_blocks/pallas_call | solution.py:329
  45.0 2.5 %collective-permute-start.19 = (f32[4,768]{1,0:T(4,128)S(1)}, f32[4,768]{1,0:T(4,128)S(1)}, u32[]{:S(2)}, u32[]{:S(2)}) collective-permute-start(f32[4,768]{1,0:T(4,128)S(1)} %log_add_fusion.1), channel_id=1, source_target_pairs={{0,6},{1,7},{2,4},{3,5},{4,2},{5,3},{6,0},{7,1},{8,14},{9,15},{10,... | collective-permute-start | bytes 36872 | tf_op jit(solution)/shard_map/ppermute | solution.py:247
  47.7 1.7 %collective-permute-start.17 = (f32[4,768]{1,0:T(4,128)S(1)}, f32[4,768]{1,0:T(4,128)S(1)}, u32[]{:S(2)}, u32[]{:S(2)}) collective-permute-start(f32[4,768]{1,0:T(4,128)S(1)} %log_add_fusion.1), channel_id=1, source_target_pairs={{0,2},{1,3},{2,0},{3,1},{4,6},{5,7},{6,4},{7,5},{8,10},{9,11},{10,... | collective-permute-start | bytes 36872 | tf_op jit(solution)/shard_map/ppermute | solution.py:247
  49.4 1.2 %collective-permute-done.19 = f32[4,768]{1,0:T(4,128)S(1)} collective-permute-done((f32[4,768]{1,0:T(4,128)S(1)}, f32[4,768]{1,0:T(4,128)S(1)}, u32[]{:S(2)}, u32[]{:S(2)}) %collective-permute-start.19) | collective-permute-done | bytes 12320 | tf_op jit(solution)/shard_map/ppermute | solution.py:247
  50.6 1.5 %collective-permute-done.18 = f32[4,768]{1,0:T(4,128)S(1)} collective-permute-done((f32[4,768]{1,0:T(4,128)S(1)}, f32[4,768]{1,0:T(4,128)S(1)}, u32[]{:S(2)}, u32[]{:S(2)}) %collective-permute-start.18) | collective-permute-done | bytes 12320 | tf_op jit(solution)/shard_map/ppermute | solution.py:247
  52.2 2.5 %collective-permute-start.22 = (f32[4,768]{1,0:T(4,128)S(1)}, f32[4,768]{1,0:T(4,128)S(1)}, u32[]{:S(2)}, u32[]{:S(2)}) collective-permute-start(f32[4,768]{1,0:T(4,128)S(1)} %log_add_fusion), channel_id=1, source_target_pairs={{0,24},{1,25},{2,26},{3,27},{4,28},{5,29},{6,30},{7,31},{8,16},{9,... | collective-permute-start | bytes 36872 | tf_op jit(solution)/shard_map/ppermute | solution.py:247
  55.7 1.1 %collective-permute-done.22 = f32[4,768]{1,0:T(4,128)S(1)} collective-permute-done((f32[4,768]{1,0:T(4,128)S(1)}, f32[4,768]{1,0:T(4,128)S(1)}, u32[]{:S(2)}, u32[]{:S(2)}) %collective-permute-start.22) | collective-permute-done | bytes 12320 | tf_op jit(solution)/shard_map/ppermute | solution.py:247
  56.8 1.5 %collective-permute-done.21 = f32[4,768]{1,0:T(4,128)S(1)} collective-permute-done((f32[4,768]{1,0:T(4,128)S(1)}, f32[4,768]{1,0:T(4,128)S(1)}, u32[]{:S(2)}, u32[]{:S(2)}) %collective-permute-start.21) | collective-permute-done | bytes 12320 | tf_op jit(solution)/shard_map/ppermute | solution.py:247
  58.9 2.7 %last_iteration.1 = (bf16[256,1024]{1,0:T(8,128)(2,1)}, f32[768]{0:T(1024)}) custom-call(bf16[256,1024]{1,0:T(8,128)(2,1)S(1)} %get-tuple-element.21.old_ref, f32[4,256,768]{2,1,0:T(8,128)S(1)} %get-tuple-element.22.expo_ref, f32[4,768]{1,0:T(4,128)S(1)} %get-tuple-element.23.peak_ref, f32[1,4,768]{2,1,0:T(4,128)S(1)} %add_bitcast_fusion.parts, ...), custom_call_target="tpu_custom_call" | custom-call | flops 1610612736 | bytes 524288 | tf_op jit(solution)/shard_map/last_iteration/pallas_call | solution.py:356
  (37 shorter events, 8.3 us)
Async XLA Ops:
  1.9 19.3 %collective-permute-start.6 = (bf16[384,1024]{1,0:T(8,128)(2,1)S(1)}, bf16[384,1024]{1,0:T(8,128)(2,1)S(1)}, u32[]{:S(2)}, u32[]{:S(2)}) collective-permute-start(bf16[384,1024]{1,0:T(8,128)(2,1)S(1)} %get-tuple-element.16), channel_id=1, source_target_pairs={{0,8},{1,17},{2,10},{3,19},{4,12},{5,21},{6,14},{7,23},{8,0},{9,25... | collective-permute-start | bytes 2359304 | tf_op jit(solution)/shard_map/ppermute | solution.py:247
  9.5 1.2 %collective-permute-start = (f32[1,768]{1,0:T(1,128)S(1)}, f32[1,768]{1,0:T(1,128)S(1)}, u32[]{:S(2)}, u32[]{:S(2)}) collective-permute-start(f32[1,768]{1,0:T(1,128)S(1)} %partial_lse.1), channel_id=1, source_target_pairs={{0,1},{1,0},{2,3},{3,2},{4,5},{5,4},{6,7},{7,6},{8,9},{9,8},{10,11... | collective-permute-start | bytes 9224 | tf_op jit(solution)/shard_map/ppermute | solution.py:247
  9.6 9.5 %collective-permute-start.7 = (bf16[192,1024]{1,0:T(8,128)(2,1)S(1)}, bf16[192,1024]{1,0:T(8,128)(2,1)S(1)}, u32[]{:S(2)}, u32[]{:S(2)}) collective-permute-start(bf16[192,1024]{1,0:T(8,128)(2,1)S(1)} %get-tuple-element.17), channel_id=1, source_target_pairs={{0,8},{1,17},{2,10},{3,19},{4,12},{5,21},{6,14},{7,23},{8,0},{9,25... | collective-permute-start | bytes 1179656 | tf_op jit(solution)/shard_map/ppermute | solution.py:247
  10.7 5.5 %collective-permute-start.3 = (f32[1,768]{1,0:T(1,128)S(1)}, f32[1,768]{1,0:T(1,128)S(1)}, u32[]{:S(2)}, u32[]{:S(2)}) collective-permute-start(f32[1,768]{1,0:T(1,128)S(1)} %log_add_fusion.3), channel_id=1, source_target_pairs={{0,6},{1,7},{2,4},{3,5},{4,2},{5,3},{6,0},{7,1},{8,14},{9,15},{10,... | collective-permute-start | bytes 9224 | tf_op jit(solution)/shard_map/ppermute | solution.py:247
  14.4 4.5 %collective-permute-start.2 = (f32[1,768]{1,0:T(1,128)S(1)}, f32[1,768]{1,0:T(1,128)S(1)}, u32[]{:S(2)}, u32[]{:S(2)}) collective-permute-start(f32[1,768]{1,0:T(1,128)S(1)} %log_add_fusion.3), channel_id=1, source_target_pairs={{0,4},{1,5},{2,6},{3,7},{4,0},{5,1},{6,2},{7,3},{8,12},{9,13},{10,... | collective-permute-start | bytes 9224 | tf_op jit(solution)/shard_map/ppermute | solution.py:247
  14.4 4.5 %collective-permute-start.1 = (f32[1,768]{1,0:T(1,128)S(1)}, f32[1,768]{1,0:T(1,128)S(1)}, u32[]{:S(2)}, u32[]{:S(2)}) collective-permute-start(f32[1,768]{1,0:T(1,128)S(1)} %log_add_fusion.3), channel_id=1, source_target_pairs={{0,2},{1,3},{2,0},{3,1},{4,6},{5,7},{6,4},{7,5},{8,10},{9,11},{10,... | collective-permute-start | bytes 9224 | tf_op jit(solution)/shard_map/ppermute | solution.py:247
  19.1 14.2 %collective-permute-start.8 = (bf16[192,1024]{1,0:T(8,128)(2,1)S(1)}, bf16[192,1024]{1,0:T(8,128)(2,1)S(1)}, u32[]{:S(2)}, u32[]{:S(2)}) collective-permute-start(bf16[192,1024]{1,0:T(8,128)(2,1)S(1)} %after.4.refs_5_), channel_id=1, source_target_pairs={{0,2},{1,3},{2,0},{3,1},{4,6},{5,7},{6,4},{7,5},{8,10},{9,11},{10,... | collective-permute-start | bytes 1179656 | tf_op jit(solution)/shard_map/ppermute | solution.py:247
  21.2 15.0 %collective-permute-start.14 = (bf16[384,1024]{1,0:T(8,128)(2,1)S(1)}, bf16[384,1024]{1,0:T(8,128)(2,1)S(1)}, u32[]{:S(2)}, u32[]{:S(2)}) collective-permute-start(bf16[384,1024]{1,0:T(8,128)(2,1)S(1)} %after.3.refs_4_), channel_id=1, source_target_pairs={{0,16},{1,9},{2,18},{3,11},{4,20},{5,13},{6,22},{7,15},{8,24},{9,1... | collective-permute-start | bytes 2359304 | tf_op jit(solution)/shard_map/ppermute | solution.py:247
  22.7 4.6 %collective-permute-start.13 = (f32[1,768]{1,0:T(1,128)S(1)}, f32[1,768]{1,0:T(1,128)S(1)}, u32[]{:S(2)}, u32[]{:S(2)}) collective-permute-start(f32[1,768]{1,0:T(1,128)S(1)} %log_add_fusion.2.refs_1_.refs_0_), channel_id=1, source_target_pairs={{0,24},{1,25},{2,26},{3,27},{4,28},{5,29},{6,30},{7,31},{8,16},{9,... | collective-permute-start | bytes 9224 | tf_op jit(solution)/shard_map/ppermute | solution.py:247
  24.2 9.2 %collective-permute-start.5 = (f32[1,768]{1,0:T(1,128)S(1)}, f32[1,768]{1,0:T(1,128)S(1)}, u32[]{:S(2)}, u32[]{:S(2)}) collective-permute-start(f32[1,768]{1,0:T(1,128)S(1)} %log_add_fusion.2.refs_1_.refs_0_), channel_id=1, source_target_pairs={{0,16},{1,9},{2,18},{3,11},{4,20},{5,13},{6,22},{7,15},{8,24},{9,1... | collective-permute-start | bytes 9224 | tf_op jit(solution)/shard_map/ppermute | solution.py:247
  25.7 8.2 %collective-permute-start.4 = (f32[1,768]{1,0:T(1,128)S(1)}, f32[1,768]{1,0:T(1,128)S(1)}, u32[]{:S(2)}, u32[]{:S(2)}) collective-permute-start(f32[1,768]{1,0:T(1,128)S(1)} %log_add_fusion.2.refs_1_.refs_0_), channel_id=1, source_target_pairs={{0,8},{1,17},{2,10},{3,19},{4,12},{5,21},{6,14},{7,23},{8,0},{9,25... | collective-permute-start | bytes 9224 | tf_op jit(solution)/shard_map/ppermute | solution.py:247
  27.3 6.6 %collective-permute-start.11 = (bf16[192,1024]{1,0:T(8,128)(2,1)S(1)}, bf16[192,1024]{1,0:T(8,128)(2,1)S(1)}, u32[]{:S(2)}, u32[]{:S(2)}) collective-permute-start(bf16[192,1024]{1,0:T(8,128)(2,1)S(1)} %after.4.refs_5_), channel_id=1, source_target_pairs={{0,1},{1,0},{2,3},{3,2},{4,5},{5,4},{6,7},{7,6},{8,9},{9,8},{10,11... | collective-permute-start | bytes 1179656 | tf_op jit(solution)/shard_map/ppermute | solution.py:247
  33.3 2.3 %collective-permute-start.10 = (bf16[192,1024]{1,0:T(8,128)(2,1)S(1)}, bf16[192,1024]{1,0:T(8,128)(2,1)S(1)}, u32[]{:S(2)}, u32[]{:S(2)}) collective-permute-start(bf16[192,1024]{1,0:T(8,128)(2,1)S(1)} %get-tuple-element.26), channel_id=1, source_target_pairs={{0,1},{1,0},{2,3},{3,2},{4,5},{5,4},{6,7},{7,6},{8,9},{9,8},{10,11... | collective-permute-start | bytes 1179656 | tf_op jit(solution)/shard_map/ppermute | solution.py:247
  33.3 2.3 %collective-permute-start.12 = (bf16[192,1024]{1,0:T(8,128)(2,1)S(1)}, bf16[192,1024]{1,0:T(8,128)(2,1)S(1)}, u32[]{:S(2)}, u32[]{:S(2)}) collective-permute-start(bf16[192,1024]{1,0:T(8,128)(2,1)S(1)} %collective-permute-done.8.refs_6_), channel_id=1, source_target_pairs={{0,1},{1,0},{2,3},{3,2},{4,5},{5,4},{6,7},{7,6},{8,9},{9,8},{10,11... | collective-permute-start | bytes 1179656 | tf_op jit(solution)/shard_map/ppermute | solution.py:247
  33.9 2.3 %collective-permute-start.9 = (bf16[192,1024]{1,0:T(8,128)(2,1)S(1)}, bf16[192,1024]{1,0:T(8,128)(2,1)S(1)}, u32[]{:S(2)}, u32[]{:S(2)}) collective-permute-start(bf16[192,1024]{1,0:T(8,128)(2,1)S(1)} %get-tuple-element.27), channel_id=1, source_target_pairs={{0,1},{1,0},{2,3},{3,2},{4,5},{5,4},{6,7},{7,6},{8,9},{9,8},{10,11... | collective-permute-start | bytes 1179656 | tf_op jit(solution)/shard_map/ppermute | solution.py:247
  36.2 3.6 %collective-permute-start.15 = (bf16[384,1024]{1,0:T(8,128)(2,1)S(1)}, bf16[384,1024]{1,0:T(8,128)(2,1)S(1)}, u32[]{:S(2)}, u32[]{:S(2)}) collective-permute-start(bf16[384,1024]{1,0:T(8,128)(2,1)S(1)} %after.5.refs_3_), channel_id=1, source_target_pairs={{0,1},{1,0},{2,3},{3,2},{4,5},{5,4},{6,7},{7,6},{8,9},{9,8},{10,11... | collective-permute-start | bytes 2359304 | tf_op jit(solution)/shard_map/ppermute | solution.py:247
  43.6 1.3 %collective-permute-start.16 = (f32[4,768]{1,0:T(4,128)S(1)}, f32[4,768]{1,0:T(4,128)S(1)}, u32[]{:S(2)}, u32[]{:S(2)}) collective-permute-start(f32[4,768]{1,0:T(4,128)S(1)} %get-tuple-element.24), channel_id=1, source_target_pairs={{0,1},{1,0},{2,3},{3,2},{4,5},{5,4},{6,7},{7,6},{8,9},{9,8},{10,11... | collective-permute-start | bytes 36872 | tf_op jit(solution)/shard_map/ppermute | solution.py:247
  45.0 5.7 %collective-permute-start.19 = (f32[4,768]{1,0:T(4,128)S(1)}, f32[4,768]{1,0:T(4,128)S(1)}, u32[]{:S(2)}, u32[]{:S(2)}) collective-permute-start(f32[4,768]{1,0:T(4,128)S(1)} %log_add_fusion.1), channel_id=1, source_target_pairs={{0,6},{1,7},{2,4},{3,5},{4,2},{5,3},{6,0},{7,1},{8,14},{9,15},{10,... | collective-permute-start | bytes 36872 | tf_op jit(solution)/shard_map/ppermute | solution.py:247
  47.5 4.6 %collective-permute-start.18 = (f32[4,768]{1,0:T(4,128)S(1)}, f32[4,768]{1,0:T(4,128)S(1)}, u32[]{:S(2)}, u32[]{:S(2)}) collective-permute-start(f32[4,768]{1,0:T(4,128)S(1)} %log_add_fusion.1), channel_id=1, source_target_pairs={{0,4},{1,5},{2,6},{3,7},{4,0},{5,1},{6,2},{7,3},{8,12},{9,13},{10,... | collective-permute-start | bytes 36872 | tf_op jit(solution)/shard_map/ppermute | solution.py:247
  47.7 4.4 %collective-permute-start.17 = (f32[4,768]{1,0:T(4,128)S(1)}, f32[4,768]{1,0:T(4,128)S(1)}, u32[]{:S(2)}, u32[]{:S(2)}) collective-permute-start(f32[4,768]{1,0:T(4,128)S(1)} %log_add_fusion.1), channel_id=1, source_target_pairs={{0,2},{1,3},{2,0},{3,1},{4,6},{5,7},{6,4},{7,5},{8,10},{9,11},{10,... | collective-permute-start | bytes 36872 | tf_op jit(solution)/shard_map/ppermute | solution.py:247
  52.2 4.7 %collective-permute-start.22 = (f32[4,768]{1,0:T(4,128)S(1)}, f32[4,768]{1,0:T(4,128)S(1)}, u32[]{:S(2)}, u32[]{:S(2)}) collective-permute-start(f32[4,768]{1,0:T(4,128)S(1)} %log_add_fusion), channel_id=1, source_target_pairs={{0,24},{1,25},{2,26},{3,27},{4,28},{5,29},{6,30},{7,31},{8,16},{9,... | collective-permute-start | bytes 36872 | tf_op jit(solution)/shard_map/ppermute | solution.py:247
  54.6 3.7 %collective-permute-start.21 = (f32[4,768]{1,0:T(4,128)S(1)}, f32[4,768]{1,0:T(4,128)S(1)}, u32[]{:S(2)}, u32[]{:S(2)}) collective-permute-start(f32[4,768]{1,0:T(4,128)S(1)} %log_add_fusion), channel_id=1, source_target_pairs={{0,16},{1,17},{2,18},{3,19},{4,20},{5,21},{6,22},{7,23},{8,24},{9,... | collective-permute-start | bytes 36872 | tf_op jit(solution)/shard_map/ppermute | solution.py:247
  55.2 3.7 %collective-permute-start.20 = (f32[4,768]{1,0:T(4,128)S(1)}, f32[4,768]{1,0:T(4,128)S(1)}, u32[]{:S(2)}, u32[]{:S(2)}) collective-permute-start(f32[4,768]{1,0:T(4,128)S(1)} %log_add_fusion), channel_id=1, source_target_pairs={{0,8},{1,9},{2,10},{3,11},{4,12},{5,13},{6,14},{7,15},{8,0},{9,1},... | collective-permute-start | bytes 36872 | tf_op jit(solution)/shard_map/ppermute | solution.py:247

commit v10 on v9

--- a/solution.py
+++ b/solution.py
@@ -170,9 +170,18 @@
     return c_ref[pl.ds(pl.multiple_of(lax.axis_index("item") * rows, rows), rows), :]
 
 
+def home_kernel(scale, c_ref, home, row, _, total, mass):
+    own = own_rows(c_ref, total.shape[0])
+    total[...], mass[...] = absorb(own, home[...], row[...], scale, None, None)
+
+
 def early_kernel(plan, scale, c_ref, *refs):
     n = plan["pieces"]
-    rows, refs = refs[: plan["early"]], refs[plan["early"] :]
+    first = plan["first"]
+    sums = weights = None
+    if first:
+        sums, weights, refs = refs[0][...], refs[1][...], refs[2:]
+    rows, refs = refs[: plan["early"] - first], refs[plan["early"] - first :]
     pieces, arrived, outs = refs[:n], refs[n : n + plan["arrived"]], refs[n + plan["arrived"] :]
     total, mass = outs[:2]
     own = own_rows(c_ref, total.shape[0])
@@ -186,10 +195,9 @@
         for lead, ref in zip(places, arrived):
             table[pl.ds(pl.multiple_of(lead, 64), ref.shape[0]), :] = ref[...]
         pieces += (table,)
-    sums = weights = None
-    for place in range(plan["early"]):
+    for place in range(first, plan["early"]):
         vectors = vectors_of(plan, place, pieces)
-        sums, weights = absorb(own, vectors, rows[place][...], scale, sums, weights)
+        sums, weights = absorb(own, vectors, rows[place - first][...], scale, sums, weights)
     total[...], mass[...] = sums, weights
 
 
@@ -287,7 +295,7 @@
         over = [near_half[: nv // 4], near_half[nv // 4 :], near_quarter, swapped]
         near = [near_half, near_quarter, swapped] + [go(piece, 0, 1) for piece in over]
         pieces = [home]
-        plan = dict(exchange=True, early=3, blocks=[(0, 0), (1, 0), (1, nv), (2, 0)])
+        plan = dict(exchange=True, first=1, early=3, blocks=[(0, 0), (1, 0), (1, nv), (2, 0)])
     else:
         home, centroids = load(vectors, centroids)
         parts = lax.all_gather(partial(home, centroids, scale), "cent", axis=0, tiled=False)
@@ -296,7 +304,7 @@
         parts = [parts[i] for i in range(items)]
         pieces = [lax.all_gather(vectors, "item", axis=0, tiled=True)]
         near = []
-        plan = dict(exchange=False, early=items, blocks=[(0, i * nv) for i in range(items)])
+        plan = dict(exchange=False, first=0, early=items, blocks=[(0, i * nv) for i in range(items)])
     plan.update(nv=nv, places=items, pieces=len(pieces), arrived=len(near))
     pieces = [in_vmem(piece) for piece in pieces]
     centroids = in_vmem(centroids)
@@ -306,9 +314,21 @@
     early, late = plan["early"], items - plan["early"]
     params = pltpu.CompilerParams(vmem_limit_bytes=16 * MIB)
     tables = [pltpu.VMEM((2 * nv, dim), jnp.bfloat16)] if near else []
+    begun = []
+    if plan["first"]:
+        begun = pl.pallas_call(
+            functools.partial(home_kernel, scale),
+            in_specs=[vmem] * 3 + [pl.BlockSpec(memory_space=pl.ANY)],
+            out_specs=[vmem] * 2,
+            out_shape=[pltpu.VMEM((rows, dim), jnp.float32), pltpu.VMEM((rows, 1), jnp.float32)],
+            compiler_params=params,
+            cost_estimate=pl.CostEstimate(flops=2 * flops, bytes_accessed=2 * nv * dim, transcendentals=nv * rows),
+            name="home_block",
+        )(centroids, pieces[0], parts[0], parts[3])
+        begun = [in_vmem(value) for value in begun]
     total, mass, *table = pl.pallas_call(
         functools.partial(early_kernel, dict(plan), scale),
-        in_specs=[vmem] * (1 + early + len(pieces) + len(near)),
+        in_specs=[vmem] * (1 + len(begun) + early - plan["first"] + len(pieces) + len(near)),
         out_specs=[vmem] * (2 + len(tables)),
         out_shape=[
             pltpu.VMEM((rows, dim), jnp.float32),
@@ -318,13 +338,13 @@
         compiler_params=params,
         cost_estimate=pl.CostEstimate(flops=0, bytes_accessed=0, transcendentals=0),
         name="early_blocks",
-    )(centroids, *parts[:early], *pieces, *[in_vmem(piece) for piece in near])
+    )(centroids, *begun, *parts[plan["first"] : early], *pieces, *[in_vmem(piece) for piece in near])
     pieces += [in_vmem(piece) for piece in table]
     plan["pieces"] = len(pieces)
 
     arrived = []
     if late:
-        far = after(far, *parts[1:], *near[3:])
+        far = after(far, *parts[1:])
         arrived = [in_vmem(far), in_vmem(go(far, 0, 1))]
     fresh, expo, peak, part, *block = pl.pallas_call(
         functools.partial(late_kernel, dict(plan), scale),

time: 61.8 us -> 65.5 us (1.060)
  waiting for transfers between devices: 15.4 us -> 25.3 us
  starting transfers between devices: 29.5 us -> 22.6 us
  Pallas kernels: 15.8 us -> 16.5 us
    ppermute x23, waiting for transfers between devices: 15.4 us -> 25.3 us  [send(): return lax.ppermute(value, BOTH, pairs)]
    ppermute x23, starting transfers between devices: 29.5 us -> 22.6 us  [send(): return lax.ppermute(value, BOTH, pairs)]
    pallas_call x0 -> x1, Pallas kernels: none -> 1.36 us  [shards(): pl.pallas_call(functools.partial(home_kernel, scale), in_specs=[vmem] * 3...]
    pallas_call x1, Pallas kernels: 3.48 us -> 2.79 us  [shards(): pl.pallas_call(functools.partial(early_kernel, dict(plan), scale), in_spe...]
where the time goes in v10:
time: 65.5 us; the launch traced here: 65.4 us
  waiting for transfers between devices  25.3 us (39%)
  starting transfers between devices  22.6 us (35%)
  Pallas kernels  16.5 us (25%)
  between operations  0.76 us (1%)
    ppermute x23, waiting for transfers between devices, send(): return lax.ppermute(value, BOTH, pairs)  25.3 us
    ppermute x23, starting transfers between devices, send(): return lax.ppermute(value, BOTH, pairs)  22.6 us
    pallas_call x1, Pallas kernels, shards(): pl.pallas_call(functools.partial(late_kernel, dict(plan), scale), in_spec...  3.81 us
    pallas_call x1, Pallas kernels, shards(): pl.pallas_call(functools.partial(early_kernel, dict(plan), scale), in_spe...  2.79 us
    pallas_call x1, Pallas kernels, shards(): pl.pallas_call(functools.partial(last_kernel, dict(plan)), in_specs=[vmem...  2.71 us
    pallas_call x1, Pallas kernels, partial(): pl.pallas_call(functools.partial(partial_kernel, scale, min(256, k)), in_...  2.46 us
    pallas_call x1, Pallas kernels, load(): pl.pallas_call(load_kernel, in_specs=[hbm, hbm], out_specs=[vmem] * 2, ou...  2.09 us
    pallas_call x1, Pallas kernels, shards(): pl.pallas_call(functools.partial(home_kernel, scale), in_specs=[vmem] * 3...  1.36 us
  transfers between devices with their start and end apart: 23, of which 14 were waited for; matrix products, arithmetic and copies ran while one was open for 0% of the time, Pallas kernels for 13%

profile of v10, /device:TPU:0, one launch (start us, length us, event | category | flops | bytes accessed | tf_op | source)
XLA Modules:
  0.0 65.4 jit_solution(15556270341064023024)
XLA Ops:
  0.6 1.3 %outgoing.1 = (bf16[384,1024]{1,0:T(8,128)(2,1)S(1)}, bf16[192,1024]{1,0:T(8,128)(2,1)S(1)}) custom-call(bf16[768,1024]{1,0:T(8,128)(2,1)} %v_hbm.3), custom_call_target="tpu_custom_call" | custom-call | bytes 1572864 | tf_op jit(solution)/shard_map/outgoing/pallas_call | solution.py:80
  1.9 3.0 %collective-permute-start.7 = (bf16[384,1024]{1,0:T(8,128)(2,1)S(1)}, bf16[384,1024]{1,0:T(8,128)(2,1)S(1)}, u32[]{:S(2)}, u32[]{:S(2)}) collective-permute-start(bf16[384,1024]{1,0:T(8,128)(2,1)S(1)} %get-tuple-element.20), channel_id=1, source_target_pairs={{0,8},{1,17},{2,10},{3,19},{4,12},{5,21},{6,14},{7,23},{8,0},{9,25... | collective-permute-start | bytes 2359304 | tf_op jit(solution)/shard_map/ppermute | solution.py:255
  4.9 2.1 %load.1 = (bf16[768,1024]{1,0:T(8,128)(2,1)S(1)}, bf16[1024,1024]{1,0:T(8,128)(2,1)S(1)}) custom-call(bf16[768,1024]{1,0:T(8,128)(2,1)} %v_hbm.3, bf16[1024,1024]{1,0:T(8,128)(2,1)} %c_hbm.1), custom_call_target="tpu_custom_call" | custom-call | bytes 7340032 | tf_op jit(solution)/shard_map/load/pallas_call | solution.py:103
  7.0 2.5 %partial_lse.1 = f32[1,768]{1,0:T(1,128)S(1)} custom-call(bf16[768,1024]{1,0:T(8,128)(2,1)S(1)} %get-tuple-element.17.v_ref.home.refs_4_.refs_1_.refs_0_, bf16[1024,1024]{1,0:T(8,128)(2,1)S(1)} %get-tuple-element.16.c_ref), custom_call_target="tpu_custom_call" | custom-call | flops 1610612736 | bytes 3670016 | tf_op jit(solution)/shard_map/partial_lse/pallas_call | solution.py:130
  9.6 1.1 %collective-permute-done = f32[1,768]{1,0:T(1,128)S(1)} collective-permute-done((f32[1,768]{1,0:T(1,128)S(1)}, f32[1,768]{1,0:T(1,128)S(1)}, u32[]{:S(2)}, u32[]{:S(2)}) %collective-permute-start) | collective-permute-done | bytes 3104 | tf_op jit(solution)/shard_map/ppermute | solution.py:255
  10.7 3.7 %collective-permute-start.3 = (f32[1,768]{1,0:T(1,128)S(1)}, f32[1,768]{1,0:T(1,128)S(1)}, u32[]{:S(2)}, u32[]{:S(2)}) collective-permute-start(f32[1,768]{1,0:T(1,128)S(1)} %log_add_fusion.3), channel_id=1, source_target_pairs={{0,6},{1,7},{2,4},{3,5},{4,2},{5,3},{6,0},{7,1},{8,14},{9,15},{10,... | collective-permute-start | bytes 9224 | tf_op jit(solution)/shard_map/ppermute | solution.py:255
  16.2 2.7 %collective-permute-done.2 = f32[1,768]{1,0:T(1,128)S(1)} collective-permute-done((f32[1,768]{1,0:T(1,128)S(1)}, f32[1,768]{1,0:T(1,128)S(1)}, u32[]{:S(2)}, u32[]{:S(2)}) %collective-permute-start.2) | collective-permute-done | bytes 3104 | tf_op jit(solution)/shard_map/ppermute | solution.py:255
  19.0 1.6 %collective-permute-start.14 = (bf16[384,1024]{1,0:T(8,128)(2,1)S(1)}, bf16[384,1024]{1,0:T(8,128)(2,1)S(1)}, u32[]{:S(2)}, u32[]{:S(2)}) collective-permute-start(bf16[384,1024]{1,0:T(8,128)(2,1)S(1)} %after.3.refs_5_), channel_id=1, source_target_pairs={{0,16},{1,9},{2,18},{3,11},{4,20},{5,13},{6,22},{7,15},{8,24},{9,1... | collective-permute-start | bytes 2359304 | tf_op jit(solution)/shard_map/ppermute | solution.py:255
  21.8 1.3 %collective-permute-start.5 = (f32[1,768]{1,0:T(1,128)S(1)}, f32[1,768]{1,0:T(1,128)S(1)}, u32[]{:S(2)}, u32[]{:S(2)}) collective-permute-start(f32[1,768]{1,0:T(1,128)S(1)} %log_add_fusion.2.row.refs_1_), channel_id=1, source_target_pairs={{0,8},{1,17},{2,10},{3,19},{4,12},{5,21},{6,14},{7,23},{8,0},{9,25... | collective-permute-start | bytes 9224 | tf_op jit(solution)/shard_map/ppermute | solution.py:255
  23.1 1.5 %collective-permute-start.4 = (f32[1,768]{1,0:T(1,128)S(1)}, f32[1,768]{1,0:T(1,128)S(1)}, u32[]{:S(2)}, u32[]{:S(2)}) collective-permute-start(f32[1,768]{1,0:T(1,128)S(1)} %log_add_fusion.2.row.refs_1_), channel_id=1, source_target_pairs={{0,24},{1,25},{2,26},{3,27},{4,28},{5,29},{6,30},{7,31},{8,16},{9,... | collective-permute-start | bytes 9224 | tf_op jit(solution)/shard_map/ppermute | solution.py:255
  24.6 8.0 %collective-permute-done.8.refs_0_ = bf16[192,1024]{1,0:T(8,128)(2,1)S(1)} collective-permute-done((bf16[192,1024]{1,0:T(8,128)(2,1)S(1)}, bf16[192,1024]{1,0:T(8,128)(2,1)S(1)}, u32[]{:S(2)}, u32[]{:S(2)}) %collective-permute-start.8) | collective-permute-done | bytes 393248 | tf_op jit(solution)/shard_map/ppermute | solution.py:255
  32.6 1.1 %collective-permute-done.6.refs_3_.refs_2_ = f32[1,768]{1,0:T(1,128)S(1)} collective-permute-done((f32[1,768]{1,0:T(1,128)S(1)}, f32[1,768]{1,0:T(1,128)S(1)}, u32[]{:S(2)}, u32[]{:S(2)}) %collective-permute-start.6) | collective-permute-done | bytes 3104 | tf_op jit(solution)/shard_map/ppermute | solution.py:255
  34.5 5.8 %collective-permute-done.9.refs_7_ = bf16[192,1024]{1,0:T(8,128)(2,1)S(1)} collective-permute-done((bf16[192,1024]{1,0:T(8,128)(2,1)S(1)}, bf16[192,1024]{1,0:T(8,128)(2,1)S(1)}, u32[]{:S(2)}, u32[]{:S(2)}) %collective-permute-start.9) | collective-permute-done | bytes 393248 | tf_op jit(solution)/shard_map/ppermute | solution.py:255
  40.9 1.4 %home_block.1 = (f32[256,1024]{1,0:T(8,128)S(1)}, f32[256,1]{1,0:T(8,128)S(1)}) custom-call(bf16[1024,1024]{1,0:T(8,128)(2,1)S(1)} %get-tuple-element.16.c_ref, bf16[768,1024]{1,0:T(8,128)(2,1)S(1)} %get-tuple-element.17.v_ref.home.refs_4_.refs_1_.refs_0_, f32[1,768]{1,0:T(1,128)S(1)} %log_add_fusion.2.row.refs_1_, ...), custom_call_target="tpu_custom_call" | custom-call | flops 805306368 | bytes 1572864 | tf_op jit(solution)/shard_map/home_block/pallas_call | solution.py:319
  42.7 2.8 %early_blocks.1 = (f32[256,1024]{1,0:T(8,128)S(1)}, f32[256,1]{1,0:T(8,128)S(1)}, bf16[1536,1024]{1,0:T(8,128)(2,1)S(1)}) custom-call(bf16[1024,1024]{1,0:T(8,128)(2,1)S(1)} %get-tuple-element.16.c_ref, f32[256,1024]{1,0:T(8,128)S(1)} %get-tuple-element.18.refs_0_, f32[256,1]{1,0:T(8,128)S(1)} %get-tuple-element.19.refs_1_, ...), custom_call_target="tpu_custom_call" | custom-call | tf_op jit(solution)/shard_map/early_blocks/pallas_call | solution.py:329
  45.5 3.8 %late_blocks.1 = (bf16[256,1024]{1,0:T(8,128)(2,1)S(1)}, f32[4,256,768]{2,1,0:T(8,128)S(1)}, f32[4,768]{1,0:T(4,128)S(1)}, f32[4,768]{1,0:T(4,128)S(1)}, bf16[768,1024]{1,0:T(8,128)(2,1)S(1)}) custom-call(bf16[1024,1024]{1,0:T(8,128)(2,1)S(1)} %get-tuple-element.16.c_ref, f32[256,1024]{1,0:T(8,128)S(1)} %get-tuple-element.22.total, ...), custom_call_target="tpu_custom_call" | custom-call | flops 2415919104 | bytes 1572864 | tf_op jit(solution)/shard_map/late_blocks/pallas_call | solution.py:349
  49.5 1.0 %collective-permute-done.16 = f32[4,768]{1,0:T(4,128)S(1)} collective-permute-done((f32[4,768]{1,0:T(4,128)S(1)}, f32[4,768]{1,0:T(4,128)S(1)}, u32[]{:S(2)}, u32[]{:S(2)}) %collective-permute-start.16) | collective-permute-done | bytes 12320 | tf_op jit(solution)/shard_map/ppermute | solution.py:255
  50.6 1.5 %collective-permute-start.19 = (f32[4,768]{1,0:T(4,128)S(1)}, f32[4,768]{1,0:T(4,128)S(1)}, u32[]{:S(2)}, u32[]{:S(2)}) collective-permute-start(f32[4,768]{1,0:T(4,128)S(1)} %log_add_fusion.1), channel_id=1, source_target_pairs={{0,6},{1,7},{2,4},{3,5},{4,2},{5,3},{6,0},{7,1},{8,14},{9,15},{10,... | collective-permute-start | bytes 36872 | tf_op jit(solution)/shard_map/ppermute | solution.py:255
  52.7 2.3 %collective-permute-start.17 = (f32[4,768]{1,0:T(4,128)S(1)}, f32[4,768]{1,0:T(4,128)S(1)}, u32[]{:S(2)}, u32[]{:S(2)}) collective-permute-start(f32[4,768]{1,0:T(4,128)S(1)} %log_add_fusion.1), channel_id=1, source_target_pairs={{0,2},{1,3},{2,0},{3,1},{4,6},{5,7},{6,4},{7,5},{8,10},{9,11},{10,... | collective-permute-start | bytes 36872 | tf_op jit(solution)/shard_map/ppermute | solution.py:255
  55.0 1.2 %collective-permute-done.19 = f32[4,768]{1,0:T(4,128)S(1)} collective-permute-done((f32[4,768]{1,0:T(4,128)S(1)}, f32[4,768]{1,0:T(4,128)S(1)}, u32[]{:S(2)}, u32[]{:S(2)}) %collective-permute-start.19) | collective-permute-done | bytes 12320 | tf_op jit(solution)/shard_map/ppermute | solution.py:255
  56.8 1.8 %collective-permute-start.22 = (f32[4,768]{1,0:T(4,128)S(1)}, f32[4,768]{1,0:T(4,128)S(1)}, u32[]{:S(2)}, u32[]{:S(2)}) collective-permute-start(f32[4,768]{1,0:T(4,128)S(1)} %log_add_fusion), channel_id=1, source_target_pairs={{0,24},{1,25},{2,26},{3,27},{4,28},{5,29},{6,30},{7,31},{8,16},{9,... | collective-permute-start | bytes 36872 | tf_op jit(solution)/shard_map/ppermute | solution.py:255
  58.9 1.5 %collective-permute-start.20 = (f32[4,768]{1,0:T(4,128)S(1)}, f32[4,768]{1,0:T(4,128)S(1)}, u32[]{:S(2)}, u32[]{:S(2)}) collective-permute-start(f32[4,768]{1,0:T(4,128)S(1)} %log_add_fusion), channel_id=1, source_target_pairs={{0,8},{1,9},{2,10},{3,11},{4,12},{5,13},{6,14},{7,15},{8,0},{9,1},... | collective-permute-start | bytes 36872 | tf_op jit(solution)/shard_map/ppermute | solution.py:255
  60.4 1.1 %collective-permute-done.22 = f32[4,768]{1,0:T(4,128)S(1)} collective-permute-done((f32[4,768]{1,0:T(4,128)S(1)}, f32[4,768]{1,0:T(4,128)S(1)}, u32[]{:S(2)}, u32[]{:S(2)}) %collective-permute-start.22) | collective-permute-done | bytes 12320 | tf_op jit(solution)/shard_map/ppermute | solution.py:255
  62.7 2.7 %last_iteration.1 = (bf16[256,1024]{1,0:T(8,128)(2,1)}, f32[768]{0:T(1024)}) custom-call(bf16[256,1024]{1,0:T(8,128)(2,1)S(1)} %get-tuple-element.25.old_ref, f32[4,256,768]{2,1,0:T(8,128)S(1)} %get-tuple-element.26.expo_ref, f32[4,768]{1,0:T(4,128)S(1)} %get-tuple-element.27.peak_ref, f32[1,4,768]{2,1,0:T(4,128)S(1)} %add_bitcast_fusion.parts, ...), custom_call_target="tpu_custom_call" | custom-call | flops 1610612736 | bytes 524288 | tf_op jit(solution)/shard_map/last_iteration/pallas_call | solution.py:376
  (38 shorter events, 7.8 us)
Async XLA Ops:
  1.9 17.0 %collective-permute-start.7 = (bf16[384,1024]{1,0:T(8,128)(2,1)S(1)}, bf16[384,1024]{1,0:T(8,128)(2,1)S(1)}, u32[]{:S(2)}, u32[]{:S(2)}) collective-permute-start(bf16[384,1024]{1,0:T(8,128)(2,1)S(1)} %get-tuple-element.20), channel_id=1, source_target_pairs={{0,8},{1,17},{2,10},{3,19},{4,12},{5,21},{6,14},{7,23},{8,0},{9,25... | collective-permute-start | bytes 2359304 | tf_op jit(solution)/shard_map/ppermute | solution.py:255
  9.5 1.2 %collective-permute-start = (f32[1,768]{1,0:T(1,128)S(1)}, f32[1,768]{1,0:T(1,128)S(1)}, u32[]{:S(2)}, u32[]{:S(2)}) collective-permute-start(f32[1,768]{1,0:T(1,128)S(1)} %partial_lse.1), channel_id=1, source_target_pairs={{0,1},{1,0},{2,3},{3,2},{4,5},{5,4},{6,7},{7,6},{8,9},{9,8},{10,11... | collective-permute-start | bytes 9224 | tf_op jit(solution)/shard_map/ppermute | solution.py:255
  10.7 5.5 %collective-permute-start.3 = (f32[1,768]{1,0:T(1,128)S(1)}, f32[1,768]{1,0:T(1,128)S(1)}, u32[]{:S(2)}, u32[]{:S(2)}) collective-permute-start(f32[1,768]{1,0:T(1,128)S(1)} %log_add_fusion.3), channel_id=1, source_target_pairs={{0,6},{1,7},{2,4},{3,5},{4,2},{5,3},{6,0},{7,1},{8,14},{9,15},{10,... | collective-permute-start | bytes 9224 | tf_op jit(solution)/shard_map/ppermute | solution.py:255
  14.4 4.5 %collective-permute-start.2 = (f32[1,768]{1,0:T(1,128)S(1)}, f32[1,768]{1,0:T(1,128)S(1)}, u32[]{:S(2)}, u32[]{:S(2)}) collective-permute-start(f32[1,768]{1,0:T(1,128)S(1)} %log_add_fusion.3), channel_id=1, source_target_pairs={{0,4},{1,5},{2,6},{3,7},{4,0},{5,1},{6,2},{7,3},{8,12},{9,13},{10,... | collective-permute-start | bytes 9224 | tf_op jit(solution)/shard_map/ppermute | solution.py:255
  14.4 4.5 %collective-permute-start.1 = (f32[1,768]{1,0:T(1,128)S(1)}, f32[1,768]{1,0:T(1,128)S(1)}, u32[]{:S(2)}, u32[]{:S(2)}) collective-permute-start(f32[1,768]{1,0:T(1,128)S(1)} %log_add_fusion.3), channel_id=1, source_target_pairs={{0,2},{1,3},{2,0},{3,1},{4,6},{5,7},{6,4},{7,5},{8,10},{9,11},{10,... | collective-permute-start | bytes 9224 | tf_op jit(solution)/shard_map/ppermute | solution.py:255
  19.0 14.8 %collective-permute-start.14 = (bf16[384,1024]{1,0:T(8,128)(2,1)S(1)}, bf16[384,1024]{1,0:T(8,128)(2,1)S(1)}, u32[]{:S(2)}, u32[]{:S(2)}) collective-permute-start(bf16[384,1024]{1,0:T(8,128)(2,1)S(1)} %after.3.refs_5_), channel_id=1, source_target_pairs={{0,16},{1,9},{2,18},{3,11},{4,20},{5,13},{6,22},{7,15},{8,24},{9,1... | collective-permute-start | bytes 2359304 | tf_op jit(solution)/shard_map/ppermute | solution.py:255
  20.6 12.1 %collective-permute-start.8 = (bf16[192,1024]{1,0:T(8,128)(2,1)S(1)}, bf16[192,1024]{1,0:T(8,128)(2,1)S(1)}, u32[]{:S(2)}, u32[]{:S(2)}) collective-permute-start(bf16[192,1024]{1,0:T(8,128)(2,1)S(1)} %get-tuple-element.21), channel_id=1, source_target_pairs={{0,8},{1,17},{2,10},{3,19},{4,12},{5,21},{6,14},{7,23},{8,0},{9,25... | collective-permute-start | bytes 1179656 | tf_op jit(solution)/shard_map/ppermute | solution.py:255
  21.1 12.6 %collective-permute-start.6 = (f32[1,768]{1,0:T(1,128)S(1)}, f32[1,768]{1,0:T(1,128)S(1)}, u32[]{:S(2)}, u32[]{:S(2)}) collective-permute-start(f32[1,768]{1,0:T(1,128)S(1)} %log_add_fusion.2.row.refs_1_), channel_id=1, source_target_pairs={{0,16},{1,9},{2,18},{3,11},{4,20},{5,13},{6,22},{7,15},{8,24},{9,1... | collective-permute-start | bytes 9224 | tf_op jit(solution)/shard_map/ppermute | solution.py:255
  21.8 11.9 %collective-permute-start.5 = (f32[1,768]{1,0:T(1,128)S(1)}, f32[1,768]{1,0:T(1,128)S(1)}, u32[]{:S(2)}, u32[]{:S(2)}) collective-permute-start(f32[1,768]{1,0:T(1,128)S(1)} %log_add_fusion.2.row.refs_1_), channel_id=1, source_target_pairs={{0,8},{1,17},{2,10},{3,19},{4,12},{5,21},{6,14},{7,23},{8,0},{9,25... | collective-permute-start | bytes 9224 | tf_op jit(solution)/shard_map/ppermute | solution.py:255
  23.1 10.6 %collective-permute-start.4 = (f32[1,768]{1,0:T(1,128)S(1)}, f32[1,768]{1,0:T(1,128)S(1)}, u32[]{:S(2)}, u32[]{:S(2)}) collective-permute-start(f32[1,768]{1,0:T(1,128)S(1)} %log_add_fusion.2.row.refs_1_), channel_id=1, source_target_pairs={{0,24},{1,25},{2,26},{3,27},{4,28},{5,29},{6,30},{7,31},{8,16},{9,... | collective-permute-start | bytes 9224 | tf_op jit(solution)/shard_map/ppermute | solution.py:255
  32.6 7.8 %collective-permute-start.9 = (bf16[192,1024]{1,0:T(8,128)(2,1)S(1)}, bf16[192,1024]{1,0:T(8,128)(2,1)S(1)}, u32[]{:S(2)}, u32[]{:S(2)}) collective-permute-start(bf16[192,1024]{1,0:T(8,128)(2,1)S(1)} %after.4.refs_6_), channel_id=1, source_target_pairs={{0,2},{1,3},{2,0},{3,1},{4,6},{5,7},{6,4},{7,5},{8,10},{9,11},{10,... | collective-permute-start | bytes 1179656 | tf_op jit(solution)/shard_map/ppermute | solution.py:255
  33.8 11.7 %collective-permute-start.15 = (bf16[384,1024]{1,0:T(8,128)(2,1)S(1)}, bf16[384,1024]{1,0:T(8,128)(2,1)S(1)}, u32[]{:S(2)}, u32[]{:S(2)}) collective-permute-start(bf16[384,1024]{1,0:T(8,128)(2,1)S(1)} %after.5.refs_3_), channel_id=1, source_target_pairs={{0,1},{1,0},{2,3},{3,2},{4,5},{5,4},{6,7},{7,6},{8,9},{9,8},{10,11... | collective-permute-start | bytes 2359304 | tf_op jit(solution)/shard_map/ppermute | solution.py:255
  33.9 8.3 %collective-permute-start.12 = (bf16[192,1024]{1,0:T(8,128)(2,1)S(1)}, bf16[192,1024]{1,0:T(8,128)(2,1)S(1)}, u32[]{:S(2)}, u32[]{:S(2)}) collective-permute-start(bf16[192,1024]{1,0:T(8,128)(2,1)S(1)} %after.4.refs_6_), channel_id=1, source_target_pairs={{0,1},{1,0},{2,3},{3,2},{4,5},{5,4},{6,7},{7,6},{8,9},{9,8},{10,11... | collective-permute-start | bytes 1179656 | tf_op jit(solution)/shard_map/ppermute | solution.py:255
  34.4 7.9 %collective-permute-start.11 = (bf16[192,1024]{1,0:T(8,128)(2,1)S(1)}, bf16[192,1024]{1,0:T(8,128)(2,1)S(1)}, u32[]{:S(2)}, u32[]{:S(2)}) collective-permute-start(bf16[192,1024]{1,0:T(8,128)(2,1)S(1)} %get-tuple-element.30), channel_id=1, source_target_pairs={{0,1},{1,0},{2,3},{3,2},{4,5},{5,4},{6,7},{7,6},{8,9},{9,8},{10,11... | collective-permute-start | bytes 1179656 | tf_op jit(solution)/shard_map/ppermute | solution.py:255
  40.4 1.9 %collective-permute-start.13 = (bf16[192,1024]{1,0:T(8,128)(2,1)S(1)}, bf16[192,1024]{1,0:T(8,128)(2,1)S(1)}, u32[]{:S(2)}, u32[]{:S(2)}) collective-permute-start(bf16[192,1024]{1,0:T(8,128)(2,1)S(1)} %collective-permute-done.9.refs_7_), channel_id=1, source_target_pairs={{0,1},{1,0},{2,3},{3,2},{4,5},{5,4},{6,7},{7,6},{8,9},{9,8},{10,11... | collective-permute-start | bytes 1179656 | tf_op jit(solution)/shard_map/ppermute | solution.py:255
  40.4 2.3 %collective-permute-start.10 = (bf16[192,1024]{1,0:T(8,128)(2,1)S(1)}, bf16[192,1024]{1,0:T(8,128)(2,1)S(1)}, u32[]{:S(2)}, u32[]{:S(2)}) collective-permute-start(bf16[192,1024]{1,0:T(8,128)(2,1)S(1)} %get-tuple-element.31), channel_id=1, source_target_pairs={{0,1},{1,0},{2,3},{3,2},{4,5},{5,4},{6,7},{7,6},{8,9},{9,8},{10,11... | collective-permute-start | bytes 1179656 | tf_op jit(solution)/shard_map/ppermute | solution.py:255
  49.3 1.2 %collective-permute-start.16 = (f32[4,768]{1,0:T(4,128)S(1)}, f32[4,768]{1,0:T(4,128)S(1)}, u32[]{:S(2)}, u32[]{:S(2)}) collective-permute-start(f32[4,768]{1,0:T(4,128)S(1)} %get-tuple-element.28), channel_id=1, source_target_pairs={{0,1},{1,0},{2,3},{3,2},{4,5},{5,4},{6,7},{7,6},{8,9},{9,8},{10,11... | collective-permute-start | bytes 36872 | tf_op jit(solution)/shard_map/ppermute | solution.py:255
  50.6 5.7 %collective-permute-start.19 = (f32[4,768]{1,0:T(4,128)S(1)}, f32[4,768]{1,0:T(4,128)S(1)}, u32[]{:S(2)}, u32[]{:S(2)}) collective-permute-start(f32[4,768]{1,0:T(4,128)S(1)} %log_add_fusion.1), channel_id=1, source_target_pairs={{0,6},{1,7},{2,4},{3,5},{4,2},{5,3},{6,0},{7,1},{8,14},{9,15},{10,... | collective-permute-start | bytes 36872 | tf_op jit(solution)/shard_map/ppermute | solution.py:255
  52.1 4.6 %collective-permute-start.18 = (f32[4,768]{1,0:T(4,128)S(1)}, f32[4,768]{1,0:T(4,128)S(1)}, u32[]{:S(2)}, u32[]{:S(2)}) collective-permute-start(f32[4,768]{1,0:T(4,128)S(1)} %log_add_fusion.1), channel_id=1, source_target_pairs={{0,4},{1,5},{2,6},{3,7},{4,0},{5,1},{6,2},{7,3},{8,12},{9,13},{10,... | collective-permute-start | bytes 36872 | tf_op jit(solution)/shard_map/ppermute | solution.py:255
  52.7 4.1 %collective-permute-start.17 = (f32[4,768]{1,0:T(4,128)S(1)}, f32[4,768]{1,0:T(4,128)S(1)}, u32[]{:S(2)}, u32[]{:S(2)}) collective-permute-start(f32[4,768]{1,0:T(4,128)S(1)} %log_add_fusion.1), channel_id=1, source_target_pairs={{0,2},{1,3},{2,0},{3,1},{4,6},{5,7},{6,4},{7,5},{8,10},{9,11},{10,... | collective-permute-start | bytes 36872 | tf_op jit(solution)/shard_map/ppermute | solution.py:255
  56.8 4.7 %collective-permute-start.22 = (f32[4,768]{1,0:T(4,128)S(1)}, f32[4,768]{1,0:T(4,128)S(1)}, u32[]{:S(2)}, u32[]{:S(2)}) collective-permute-start(f32[4,768]{1,0:T(4,128)S(1)} %log_add_fusion), channel_id=1, source_target_pairs={{0,24},{1,25},{2,26},{3,27},{4,28},{5,29},{6,30},{7,31},{8,16},{9,... | collective-permute-start | bytes 36872 | tf_op jit(solution)/shard_map/ppermute | solution.py:255
  58.6 3.7 %collective-permute-start.21 = (f32[4,768]{1,0:T(4,128)S(1)}, f32[4,768]{1,0:T(4,128)S(1)}, u32[]{:S(2)}, u32[]{:S(2)}) collective-permute-start(f32[4,768]{1,0:T(4,128)S(1)} %log_add_fusion), channel_id=1, source_target_pairs={{0,16},{1,17},{2,18},{3,19},{4,20},{5,21},{6,22},{7,23},{8,24},{9,... | collective-permute-start | bytes 36872 | tf_op jit(solution)/shard_map/ppermute | solution.py:255
  58.9 3.7 %collective-permute-start.20 = (f32[4,768]{1,0:T(4,128)S(1)}, f32[4,768]{1,0:T(4,128)S(1)}, u32[]{:S(2)}, u32[]{:S(2)}) collective-permute-start(f32[4,768]{1,0:T(4,128)S(1)} %log_add_fusion), channel_id=1, source_target_pairs={{0,8},{1,9},{2,10},{3,11},{4,12},{5,13},{6,14},{7,15},{8,0},{9,1},... | collective-permute-start | bytes 36872 | tf_op jit(solution)/shard_map/ppermute | solution.py:255

commit v11 on v10

--- a/solution.py
+++ b/solution.py
@@ -61,14 +61,14 @@
     return [pl.multiple_of(lead, 64) for lead in (core * half, direct, swapped)]
 
 
-def outgoing_kernel(v_hbm, half_ref, quarter_ref, sems):
+def outgoing_kernel(v_hbm, out_ref, sems):
     half_lead, direct, _ = leads(v_hbm.shape[0], core_index())
-    rows = quarter_ref.shape[0]
+    rows = out_ref.shape[0] // 3
+    starts = (half_lead, half_lead + rows, direct)
     copy_rows(
         [
-            (v_hbm.at[pl.ds(direct, rows), :], quarter_ref),
-            (v_hbm.at[pl.ds(half_lead, rows), :], half_ref.at[pl.ds(0, rows), :]),
-            (v_hbm.at[pl.ds(half_lead + rows, rows), :], half_ref.at[pl.ds(rows, rows), :]),
+            (v_hbm.at[pl.ds(pl.multiple_of(start, 64), rows), :], out_ref.at[pl.ds(i * rows, rows), :])
+            for i, start in enumerate(starts)
         ],
         sems,
     )
@@ -76,12 +76,11 @@
 
 def outgoing(vectors):
     nv, dim = vectors.shape
-    vmem = pl.BlockSpec(memory_space=pltpu.VMEM)
     return pl.pallas_call(
         outgoing_kernel,
         in_specs=[pl.BlockSpec(memory_space=pl.ANY)],
-        out_specs=[vmem] * 2,
-        out_shape=[pltpu.VMEM((nv // 2, dim), jnp.bfloat16), pltpu.VMEM((nv // 4, dim), jnp.bfloat16)],
+        out_specs=pl.BlockSpec(memory_space=pltpu.VMEM),
+        out_shape=pltpu.VMEM((3 * (nv // 4), dim), jnp.bfloat16),
         scratch_shapes=[pltpu.SemaphoreType.DMA((3,))],
         compiler_params=pltpu.CompilerParams(vmem_limit_bytes=2 * MIB),
         cost_estimate=pl.CostEstimate(flops=0, bytes_accessed=2 * nv * dim, transcendentals=0),
@@ -189,11 +188,15 @@
         table, nv = outs[2], plan["nv"]
         core = core_index()
         half_lead, direct, swapped = leads(nv, core)
-        places = [half_lead, direct, swapped]
+        quarter = nv // 4
+        near, arrived = arrived[0], arrived[1:]
+        table[pl.ds(half_lead, 2 * quarter), :] = near[: 2 * quarter, :]
+        table[pl.ds(direct, quarter), :] = near[2 * quarter :, :]
+        places = [swapped]
         half_lead, direct, swapped = leads(nv, 1 - core)
-        places += [nv + half_lead, nv + half_lead + nv // 4, nv + direct, nv + swapped]
+        places += [nv + half_lead, nv + half_lead + quarter, nv + direct, nv + swapped]
         for lead, ref in zip(places, arrived):
-            table[pl.ds(pl.multiple_of(lead, 64), ref.shape[0]), :] = ref[...]
+            table[pl.ds(pl.multiple_of(lead, 64), quarter), :] = ref[...]
         pieces += (table,)
     for place in range(first, plan["early"]):
         vectors = vectors_of(plan, place, pieces)
@@ -284,16 +287,15 @@
 
     small = items == 4 and cents == 8
     if small:
-        half, quarter = outgoing(vectors)
-        near_quarter, near_half = go(quarter, (1, 2)), go(half, (1, 2))
+        near = go(outgoing(vectors), (1, 2))
         home, centroids = load(vectors, centroids)
         lse = merge_cent(partial(home, centroids, scale), go)
         parts = [lse, go(lse, (1, 2)), go(lse, (2, 1)), go(lse, 3)]
-        near_quarter, near_half = after(near_quarter, lse), after(near_half, lse)
-        swapped = go(near_quarter, 0, 2)
-        far = go(near_half, (2, 1))
-        over = [near_half[: nv // 4], near_half[nv // 4 :], near_quarter, swapped]
-        near = [near_half, near_quarter, swapped] + [go(piece, 0, 1) for piece in over]
+        near = after(near, lse)
+        quarters = [near[i : i + nv // 4] for i in range(0, near.shape[0], nv // 4)]
+        swapped = go(quarters[2], 0, 2)
+        far = go(near[: nv // 2], (2, 1))
+        near = [near, swapped] + [go(piece, 0, 1) for piece in quarters + [swapped]]
         pieces = [home]
         plan = dict(exchange=True, first=1, early=3, blocks=[(0, 0), (1, 0), (1, nv), (2, 0)])
     else:
@@ -324,7 +326,7 @@
             compiler_params=params,
             cost_estimate=pl.CostEstimate(flops=2 * flops, bytes_accessed=2 * nv * dim, transcendentals=nv * rows),
             name="home_block",
-        )(centroids, pieces[0], parts[0], parts[3])
+        )(centroids, pieces[0], parts[0], near[2])
         begun = [in_vmem(value) for value in begun]
     total, mass, *table = pl.pallas_call(
         functools.partial(early_kernel, dict(plan), scale),
@@ -344,7 +346,7 @@
 
     arrived = []
     if late:
-        far = after(far, *parts[1:])
+        far = after(far, *parts[1:], *near[2:], begun[1])
         arrived = [in_vmem(far), in_vmem(go(far, 0, 1))]
     fresh, expo, peak, part, *block = pl.pallas_call(
         functools.partial(late_kernel, dict(plan), scale),

time: 65.5 us -> 62.2 us (0.950)
  waiting for transfers between devices: 25.3 us -> 15.5 us
  starting transfers between devices: 22.6 us -> 28.9 us
    ppermute x23 -> x22, waiting for transfers between devices: 25.3 us -> 15.5 us  [send(): return lax.ppermute(value, BOTH, pairs)]
    ppermute x23 -> x22, starting transfers between devices: 22.6 us -> 28.9 us  [send(): return lax.ppermute(value, BOTH, pairs)]
  transfers between devices with their start and end apart: 23 -> 22, of which waited for: 14 -> 13; matrix products, arithmetic and copies ran while one was open for 0% -> 0% of each run, Pallas kernels for 13% -> 14%
where the time goes in v11:
time: 62.2 us; the launch traced here: 62 us
  starting transfers between devices  28.9 us (46%)
  Pallas kernels  16.5 us (27%)
  waiting for transfers between devices  15.5 us (25%)
  between operations  0.75 us (1%)
    ppermute x22, starting transfers between devices, send(): return lax.ppermute(value, BOTH, pairs)  28.9 us
    ppermute x22, waiting for transfers between devices, send(): return lax.ppermute(value, BOTH, pairs)  15.5 us
    pallas_call x1, Pallas kernels, shards(): pl.pallas_call(functools.partial(late_kernel, dict(plan), scale), in_spec...  3.82 us
    pallas_call x1, Pallas kernels, shards(): pl.pallas_call(functools.partial(early_kernel, dict(plan), scale), in_spe...  2.81 us
    pallas_call x1, Pallas kernels, shards(): pl.pallas_call(functools.partial(last_kernel, dict(plan)), in_specs=[vmem...  2.71 us
    pallas_call x1, Pallas kernels, partial(): pl.pallas_call(functools.partial(partial_kernel, scale, min(256, k)), in_...  2.46 us
    pallas_call x1, Pallas kernels, load(): pl.pallas_call(load_kernel, in_specs=[hbm, hbm], out_specs=[vmem] * 2, ou...  2.09 us
    pallas_call x1, Pallas kernels, shards(): pl.pallas_call(functools.partial(home_kernel, scale), in_specs=[vmem] * 3...  1.36 us
  transfers between devices with their start and end apart: 22, of which 13 were waited for; matrix products, arithmetic and copies ran while one was open for 0% of the time, Pallas kernels for 14%

profile of v11, /device:TPU:0, one launch (start us, length us, event | category | flops | bytes accessed | tf_op | source)
XLA Modules:
  0.0 62.0 jit_solution(14154889506025536080)
XLA Ops:
  0.6 1.3 %outgoing.1 = bf16[576,1024]{1,0:T(8,128)(2,1)S(1)} custom-call(bf16[768,1024]{1,0:T(8,128)(2,1)} %v_hbm.3), custom_call_target="tpu_custom_call" | custom-call | bytes 1572864 | tf_op jit(solution)/shard_map/outgoing/pallas_call | solution.py:79
  1.9 3.0 %collective-permute-start.4 = (bf16[576,1024]{1,0:T(8,128)(2,1)S(1)}, bf16[576,1024]{1,0:T(8,128)(2,1)S(1)}, u32[]{:S(2)}, u32[]{:S(2)}) collective-permute-start(bf16[576,1024]{1,0:T(8,128)(2,1)S(1)} %outgoing.1), channel_id=1, source_target_pairs={{0,8},{1,17},{2,10},{3,19},{4,12},{5,21},{6,14},{7,23},{8,0},{9,25... | collective-permute-start | bytes 3538952 | tf_op jit(solution)/shard_map/ppermute | solution.py:258
  4.9 2.1 %load.1 = (bf16[768,1024]{1,0:T(8,128)(2,1)S(1)}, bf16[1024,1024]{1,0:T(8,128)(2,1)S(1)}) custom-call(bf16[768,1024]{1,0:T(8,128)(2,1)} %v_hbm.3, bf16[1024,1024]{1,0:T(8,128)(2,1)} %c_hbm.1), custom_call_target="tpu_custom_call" | custom-call | bytes 7340032 | tf_op jit(solution)/shard_map/load/pallas_call | solution.py:102
  7.0 2.5 %partial_lse.1 = f32[1,768]{1,0:T(1,128)S(1)} custom-call(bf16[768,1024]{1,0:T(8,128)(2,1)S(1)} %get-tuple-element.15.v_ref.home.refs_4_.refs_1_.refs_0_, bf16[1024,1024]{1,0:T(8,128)(2,1)S(1)} %get-tuple-element.14.c_ref), custom_call_target="tpu_custom_call" | custom-call | flops 1610612736 | bytes 3670016 | tf_op jit(solution)/shard_map/partial_lse/pallas_call | solution.py:129
  9.6 1.1 %collective-permute-done = f32[1,768]{1,0:T(1,128)S(1)} collective-permute-done((f32[1,768]{1,0:T(1,128)S(1)}, f32[1,768]{1,0:T(1,128)S(1)}, u32[]{:S(2)}, u32[]{:S(2)}) %collective-permute-start) | collective-permute-done | bytes 3104 | tf_op jit(solution)/shard_map/ppermute | solution.py:258
  10.7 3.7 %collective-permute-start.3 = (f32[1,768]{1,0:T(1,128)S(1)}, f32[1,768]{1,0:T(1,128)S(1)}, u32[]{:S(2)}, u32[]{:S(2)}) collective-permute-start(f32[1,768]{1,0:T(1,128)S(1)} %log_add_fusion.3), channel_id=1, source_target_pairs={{0,6},{1,7},{2,4},{3,5},{4,2},{5,3},{6,0},{7,1},{8,14},{9,15},{10,... | collective-permute-start | bytes 9224 | tf_op jit(solution)/shard_map/ppermute | solution.py:258
  16.2 2.7 %collective-permute-done.2 = f32[1,768]{1,0:T(1,128)S(1)} collective-permute-done((f32[1,768]{1,0:T(1,128)S(1)}, f32[1,768]{1,0:T(1,128)S(1)}, u32[]{:S(2)}, u32[]{:S(2)}) %collective-permute-start.2) | collective-permute-done | bytes 3104 | tf_op jit(solution)/shard_map/ppermute | solution.py:258
  19.2 2.1 %collective-permute-start.13 = (bf16[384,1024]{1,0:T(8,128)(2,1)S(1)}, bf16[384,1024]{1,0:T(8,128)(2,1)S(1)}, u32[]{:S(2)}, u32[]{:S(2)}) collective-permute-start(bf16[384,1024]{1,0:T(8,128)(2,1)S(1)} %slice.19), channel_id=1, source_target_pairs={{0,16},{1,9},{2,18},{3,11},{4,20},{5,13},{6,22},{7,15},{8,24},{9,1... | collective-permute-start | bytes 2359304 | tf_op jit(solution)/shard_map/ppermute | solution.py:258
  21.4 1.6 %collective-permute-start.8 = (bf16[192,1024]{1,0:T(8,128)(2,1)S(1)}, bf16[192,1024]{1,0:T(8,128)(2,1)S(1)}, u32[]{:S(2)}, u32[]{:S(2)}) collective-permute-start(bf16[192,1024]{1,0:T(8,128)(2,1)S(1)} %get-tuple-element.27), channel_id=1, source_target_pairs={{0,2},{1,3},{2,0},{3,1},{4,6},{5,7},{6,4},{7,5},{8,10},{9,11},{10,... | collective-permute-start | bytes 1179656 | tf_op jit(solution)/shard_map/ppermute | solution.py:258
  22.9 1.4 %collective-permute-start.12 = (f32[1,768]{1,0:T(1,128)S(1)}, f32[1,768]{1,0:T(1,128)S(1)}, u32[]{:S(2)}, u32[]{:S(2)}) collective-permute-start(f32[1,768]{1,0:T(1,128)S(1)} %log_add_fusion.2.refs_1_.row), channel_id=1, source_target_pairs={{0,24},{1,25},{2,26},{3,27},{4,28},{5,29},{6,30},{7,31},{8,16},{9,... | collective-permute-start | bytes 9224 | tf_op jit(solution)/shard_map/ppermute | solution.py:258
  24.4 1.5 %collective-permute-start.7 = (f32[1,768]{1,0:T(1,128)S(1)}, f32[1,768]{1,0:T(1,128)S(1)}, u32[]{:S(2)}, u32[]{:S(2)}) collective-permute-start(f32[1,768]{1,0:T(1,128)S(1)} %log_add_fusion.2.refs_1_.row), channel_id=1, source_target_pairs={{0,16},{1,9},{2,18},{3,11},{4,20},{5,13},{6,22},{7,15},{8,24},{9,1... | collective-permute-start | bytes 9224 | tf_op jit(solution)/shard_map/ppermute | solution.py:258
  25.9 1.6 %collective-permute-done.12.refs_3_.refs_0_ = f32[1,768]{1,0:T(1,128)S(1)} collective-permute-done((f32[1,768]{1,0:T(1,128)S(1)}, f32[1,768]{1,0:T(1,128)S(1)}, u32[]{:S(2)}, u32[]{:S(2)}) %collective-permute-start.12) | collective-permute-done | bytes 3104 | tf_op jit(solution)/shard_map/ppermute | solution.py:258
  27.5 3.2 %collective-permute-start.9 = (bf16[192,1024]{1,0:T(8,128)(2,1)S(1)}, bf16[192,1024]{1,0:T(8,128)(2,1)S(1)}, u32[]{:S(2)}, u32[]{:S(2)}) collective-permute-start(bf16[192,1024]{1,0:T(8,128)(2,1)S(1)} %get-tuple-element.26), channel_id=1, source_target_pairs={{0,1},{1,0},{2,3},{3,2},{4,5},{5,4},{6,7},{7,6},{8,9},{9,8},{10,11... | collective-permute-start | bytes 1179656 | tf_op jit(solution)/shard_map/ppermute | solution.py:258
  31.9 2.0 %collective-permute-start.6 = (f32[1,768]{1,0:T(1,128)S(1)}, f32[1,768]{1,0:T(1,128)S(1)}, u32[]{:S(2)}, u32[]{:S(2)}) collective-permute-start(f32[1,768]{1,0:T(1,128)S(1)} %log_add_fusion.2.refs_1_.row), channel_id=1, source_target_pairs={{0,8},{1,17},{2,10},{3,19},{4,12},{5,21},{6,14},{7,23},{8,0},{9,25... | collective-permute-start | bytes 9224 | tf_op jit(solution)/shard_map/ppermute | solution.py:258
  33.9 1.4 %home_block.1 = (f32[256,1024]{1,0:T(8,128)S(1)}, f32[256,1]{1,0:T(8,128)S(1)}) custom-call(bf16[1024,1024]{1,0:T(8,128)(2,1)S(1)} %get-tuple-element.14.c_ref, bf16[768,1024]{1,0:T(8,128)(2,1)S(1)} %get-tuple-element.15.v_ref.home.refs_4_.refs_1_.refs_0_, f32[1,768]{1,0:T(1,128)S(1)} %log_add_fusion.2.refs_1_.row, ...), custom_call_target="tpu_custom_call" | custom-call | flops 805306368 | bytes 1572864 | tf_op jit(solution)/shard_map/home_block/pallas_call | solution.py:321
  35.7 2.8 %early_blocks.1 = (f32[256,1024]{1,0:T(8,128)S(1)}, f32[256,1]{1,0:T(8,128)S(1)}, bf16[1536,1024]{1,0:T(8,128)(2,1)S(1)}) custom-call(bf16[1024,1024]{1,0:T(8,128)(2,1)S(1)} %get-tuple-element.14.c_ref, f32[256,1024]{1,0:T(8,128)S(1)} %get-tuple-element.16.refs_0_, f32[256,1]{1,0:T(8,128)S(1)} %get-tuple-element.17.refs_1_.refs_8_, ...), custom_call_target="tpu_custom_call" | custom-call | tf_op jit(solution)/shard_map/early_blocks/pallas_call | solution.py:331
  38.5 3.8 %late_blocks.1 = (bf16[256,1024]{1,0:T(8,128)(2,1)S(1)}, f32[4,256,768]{2,1,0:T(8,128)S(1)}, f32[4,768]{1,0:T(4,128)S(1)}, f32[4,768]{1,0:T(4,128)S(1)}, bf16[768,1024]{1,0:T(8,128)(2,1)S(1)}) custom-call(bf16[1024,1024]{1,0:T(8,128)(2,1)S(1)} %get-tuple-element.14.c_ref, f32[256,1024]{1,0:T(8,128)S(1)} %get-tuple-element.18.total, ...), custom_call_target="tpu_custom_call" | custom-call | flops 2415919104 | bytes 1572864 | tf_op jit(solution)/shard_map/late_blocks/pallas_call | solution.py:351
  43.8 4.2 %collective-permute-start.18 = (f32[4,768]{1,0:T(4,128)S(1)}, f32[4,768]{1,0:T(4,128)S(1)}, u32[]{:S(2)}, u32[]{:S(2)}) collective-permute-start(f32[4,768]{1,0:T(4,128)S(1)} %log_add_fusion.1), channel_id=1, source_target_pairs={{0,6},{1,7},{2,4},{3,5},{4,2},{5,3},{6,0},{7,1},{8,14},{9,15},{10,... | collective-permute-start | bytes 36872 | tf_op jit(solution)/shard_map/ppermute | solution.py:258
  48.6 1.0 %collective-permute-done.18 = f32[4,768]{1,0:T(4,128)S(1)} collective-permute-done((f32[4,768]{1,0:T(4,128)S(1)}, f32[4,768]{1,0:T(4,128)S(1)}, u32[]{:S(2)}, u32[]{:S(2)}) %collective-permute-start.18) | collective-permute-done | bytes 12320 | tf_op jit(solution)/shard_map/ppermute | solution.py:258
  49.6 2.9 %collective-permute-done.17 = f32[4,768]{1,0:T(4,128)S(1)} collective-permute-done((f32[4,768]{1,0:T(4,128)S(1)}, f32[4,768]{1,0:T(4,128)S(1)}, u32[]{:S(2)}, u32[]{:S(2)}) %collective-permute-start.17) | collective-permute-done | bytes 12320 | tf_op jit(solution)/shard_map/ppermute | solution.py:258
  52.6 2.5 %collective-permute-start.21 = (f32[4,768]{1,0:T(4,128)S(1)}, f32[4,768]{1,0:T(4,128)S(1)}, u32[]{:S(2)}, u32[]{:S(2)}) collective-permute-start(f32[4,768]{1,0:T(4,128)S(1)} %log_add_fusion), channel_id=1, source_target_pairs={{0,24},{1,25},{2,26},{3,27},{4,28},{5,29},{6,30},{7,31},{8,16},{9,... | collective-permute-start | bytes 36872 | tf_op jit(solution)/shard_map/ppermute | solution.py:258
  56.1 1.1 %collective-permute-done.21 = f32[4,768]{1,0:T(4,128)S(1)} collective-permute-done((f32[4,768]{1,0:T(4,128)S(1)}, f32[4,768]{1,0:T(4,128)S(1)}, u32[]{:S(2)}, u32[]{:S(2)}) %collective-permute-start.21) | collective-permute-done | bytes 12320 | tf_op jit(solution)/shard_map/ppermute | solution.py:258
  57.2 1.5 %collective-permute-done.20 = f32[4,768]{1,0:T(4,128)S(1)} collective-permute-done((f32[4,768]{1,0:T(4,128)S(1)}, f32[4,768]{1,0:T(4,128)S(1)}, u32[]{:S(2)}, u32[]{:S(2)}) %collective-permute-start.20) | collective-permute-done | bytes 12320 | tf_op jit(solution)/shard_map/ppermute | solution.py:258
  59.3 2.7 %last_iteration.1 = (bf16[256,1024]{1,0:T(8,128)(2,1)}, f32[768]{0:T(1024)}) custom-call(bf16[256,1024]{1,0:T(8,128)(2,1)S(1)} %get-tuple-element.21.old_ref, f32[4,256,768]{2,1,0:T(8,128)S(1)} %get-tuple-element.22.expo_ref, f32[4,768]{1,0:T(4,128)S(1)} %get-tuple-element.23.peak_ref, f32[1,4,768]{2,1,0:T(4,128)S(1)} %add_bitcast_fusion.parts, ...), custom_call_target="tpu_custom_call" | custom-call | flops 1610612736 | bytes 524288 | tf_op jit(solution)/shard_map/last_iteration/pallas_call | solution.py:378
  (36 shorter events, 7.4 us)
Async XLA Ops:
  1.9 17.2 %collective-permute-start.4 = (bf16[576,1024]{1,0:T(8,128)(2,1)S(1)}, bf16[576,1024]{1,0:T(8,128)(2,1)S(1)}, u32[]{:S(2)}, u32[]{:S(2)}) collective-permute-start(bf16[576,1024]{1,0:T(8,128)(2,1)S(1)} %outgoing.1), channel_id=1, source_target_pairs={{0,8},{1,17},{2,10},{3,19},{4,12},{5,21},{6,14},{7,23},{8,0},{9,25... | collective-permute-start | bytes 3538952 | tf_op jit(solution)/shard_map/ppermute | solution.py:258
  9.5 1.2 %collective-permute-start = (f32[1,768]{1,0:T(1,128)S(1)}, f32[1,768]{1,0:T(1,128)S(1)}, u32[]{:S(2)}, u32[]{:S(2)}) collective-permute-start(f32[1,768]{1,0:T(1,128)S(1)} %partial_lse.1), channel_id=1, source_target_pairs={{0,1},{1,0},{2,3},{3,2},{4,5},{5,4},{6,7},{7,6},{8,9},{9,8},{10,11... | collective-permute-start | bytes 9224 | tf_op jit(solution)/shard_map/ppermute | solution.py:258
  10.7 5.5 %collective-permute-start.3 = (f32[1,768]{1,0:T(1,128)S(1)}, f32[1,768]{1,0:T(1,128)S(1)}, u32[]{:S(2)}, u32[]{:S(2)}) collective-permute-start(f32[1,768]{1,0:T(1,128)S(1)} %log_add_fusion.3), channel_id=1, source_target_pairs={{0,6},{1,7},{2,4},{3,5},{4,2},{5,3},{6,0},{7,1},{8,14},{9,15},{10,... | collective-permute-start | bytes 9224 | tf_op jit(solution)/shard_map/ppermute | solution.py:258
  14.4 4.5 %collective-permute-start.2 = (f32[1,768]{1,0:T(1,128)S(1)}, f32[1,768]{1,0:T(1,128)S(1)}, u32[]{:S(2)}, u32[]{:S(2)}) collective-permute-start(f32[1,768]{1,0:T(1,128)S(1)} %log_add_fusion.3), channel_id=1, source_target_pairs={{0,4},{1,5},{2,6},{3,7},{4,0},{5,1},{6,2},{7,3},{8,12},{9,13},{10,... | collective-permute-start | bytes 9224 | tf_op jit(solution)/shard_map/ppermute | solution.py:258
  14.4 4.5 %collective-permute-start.1 = (f32[1,768]{1,0:T(1,128)S(1)}, f32[1,768]{1,0:T(1,128)S(1)}, u32[]{:S(2)}, u32[]{:S(2)}) collective-permute-start(f32[1,768]{1,0:T(1,128)S(1)} %log_add_fusion.3), channel_id=1, source_target_pairs={{0,2},{1,3},{2,0},{3,1},{4,6},{5,7},{6,4},{7,5},{8,10},{9,11},{10,... | collective-permute-start | bytes 9224 | tf_op jit(solution)/shard_map/ppermute | solution.py:258
  19.2 16.3 %collective-permute-start.13 = (bf16[384,1024]{1,0:T(8,128)(2,1)S(1)}, bf16[384,1024]{1,0:T(8,128)(2,1)S(1)}, u32[]{:S(2)}, u32[]{:S(2)}) collective-permute-start(bf16[384,1024]{1,0:T(8,128)(2,1)S(1)} %slice.19), channel_id=1, source_target_pairs={{0,16},{1,9},{2,18},{3,11},{4,20},{5,13},{6,22},{7,15},{8,24},{9,1... | collective-permute-start | bytes 2359304 | tf_op jit(solution)/shard_map/ppermute | solution.py:258
  21.4 10.1 %collective-permute-start.8 = (bf16[192,1024]{1,0:T(8,128)(2,1)S(1)}, bf16[192,1024]{1,0:T(8,128)(2,1)S(1)}, u32[]{:S(2)}, u32[]{:S(2)}) collective-permute-start(bf16[192,1024]{1,0:T(8,128)(2,1)S(1)} %get-tuple-element.27), channel_id=1, source_target_pairs={{0,2},{1,3},{2,0},{3,1},{4,6},{5,7},{6,4},{7,5},{8,10},{9,11},{10,... | collective-permute-start | bytes 1179656 | tf_op jit(solution)/shard_map/ppermute | solution.py:258
  22.9 9.0 %collective-permute-start.5 = (bf16[192,1024]{1,0:T(8,128)(2,1)S(1)}, bf16[192,1024]{1,0:T(8,128)(2,1)S(1)}, u32[]{:S(2)}, u32[]{:S(2)}) collective-permute-start(bf16[192,1024]{1,0:T(8,128)(2,1)S(1)} %get-tuple-element.28), channel_id=1, source_target_pairs={{0,1},{1,0},{2,3},{3,2},{4,5},{5,4},{6,7},{7,6},{8,9},{9,8},{10,11... | collective-permute-start | bytes 1179656 | tf_op jit(solution)/shard_map/ppermute | solution.py:258
  22.9 4.6 %collective-permute-start.12 = (f32[1,768]{1,0:T(1,128)S(1)}, f32[1,768]{1,0:T(1,128)S(1)}, u32[]{:S(2)}, u32[]{:S(2)}) collective-permute-start(f32[1,768]{1,0:T(1,128)S(1)} %log_add_fusion.2.refs_1_.row), channel_id=1, source_target_pairs={{0,24},{1,25},{2,26},{3,27},{4,28},{5,29},{6,30},{7,31},{8,16},{9,... | collective-permute-start | bytes 9224 | tf_op jit(solution)/shard_map/ppermute | solution.py:258
  24.4 7.1 %collective-permute-start.7 = (f32[1,768]{1,0:T(1,128)S(1)}, f32[1,768]{1,0:T(1,128)S(1)}, u32[]{:S(2)}, u32[]{:S(2)}) collective-permute-start(f32[1,768]{1,0:T(1,128)S(1)} %log_add_fusion.2.refs_1_.row), channel_id=1, source_target_pairs={{0,16},{1,9},{2,18},{3,11},{4,20},{5,13},{6,22},{7,15},{8,24},{9,1... | collective-permute-start | bytes 9224 | tf_op jit(solution)/shard_map/ppermute | solution.py:258
  27.5 8.0 %collective-permute-start.9 = (bf16[192,1024]{1,0:T(8,128)(2,1)S(1)}, bf16[192,1024]{1,0:T(8,128)(2,1)S(1)}, u32[]{:S(2)}, u32[]{:S(2)}) collective-permute-start(bf16[192,1024]{1,0:T(8,128)(2,1)S(1)} %get-tuple-element.26), channel_id=1, source_target_pairs={{0,1},{1,0},{2,3},{3,2},{4,5},{5,4},{6,7},{7,6},{8,9},{9,8},{10,11... | collective-permute-start | bytes 1179656 | tf_op jit(solution)/shard_map/ppermute | solution.py:258
  31.4 4.1 %collective-permute-start.10 = (bf16[192,1024]{1,0:T(8,128)(2,1)S(1)}, bf16[192,1024]{1,0:T(8,128)(2,1)S(1)}, u32[]{:S(2)}, u32[]{:S(2)}) collective-permute-start(bf16[192,1024]{1,0:T(8,128)(2,1)S(1)} %get-tuple-element.27), channel_id=1, source_target_pairs={{0,1},{1,0},{2,3},{3,2},{4,5},{5,4},{6,7},{7,6},{8,9},{9,8},{10,11... | collective-permute-start | bytes 1179656 | tf_op jit(solution)/shard_map/ppermute | solution.py:258
  31.4 4.1 %collective-permute-start.11 = (bf16[192,1024]{1,0:T(8,128)(2,1)S(1)}, bf16[192,1024]{1,0:T(8,128)(2,1)S(1)}, u32[]{:S(2)}, u32[]{:S(2)}) collective-permute-start(bf16[192,1024]{1,0:T(8,128)(2,1)S(1)} %collective-permute-done.8.refs_6_), channel_id=1, source_target_pairs={{0,1},{1,0},{2,3},{3,2},{4,5},{5,4},{6,7},{7,6},{8,9},{9,8},{10,11... | collective-permute-start | bytes 1179656 | tf_op jit(solution)/shard_map/ppermute | solution.py:258
  31.9 3.6 %collective-permute-start.6 = (f32[1,768]{1,0:T(1,128)S(1)}, f32[1,768]{1,0:T(1,128)S(1)}, u32[]{:S(2)}, u32[]{:S(2)}) collective-permute-start(f32[1,768]{1,0:T(1,128)S(1)} %log_add_fusion.2.refs_1_.row), channel_id=1, source_target_pairs={{0,8},{1,17},{2,10},{3,19},{4,12},{5,21},{6,14},{7,23},{8,0},{9,25... | collective-permute-start | bytes 9224 | tf_op jit(solution)/shard_map/ppermute | solution.py:258
  35.6 2.9 %collective-permute-start.14 = (bf16[384,1024]{1,0:T(8,128)(2,1)S(1)}, bf16[384,1024]{1,0:T(8,128)(2,1)S(1)}, u32[]{:S(2)}, u32[]{:S(2)}) collective-permute-start(bf16[384,1024]{1,0:T(8,128)(2,1)S(1)} %after.3.refs_3_), channel_id=1, source_target_pairs={{0,1},{1,0},{2,3},{3,2},{4,5},{5,4},{6,7},{7,6},{8,9},{9,8},{10,11... | collective-permute-start | bytes 2359304 | tf_op jit(solution)/shard_map/ppermute | solution.py:258
  42.3 1.4 %collective-permute-start.15 = (f32[4,768]{1,0:T(4,128)S(1)}, f32[4,768]{1,0:T(4,128)S(1)}, u32[]{:S(2)}, u32[]{:S(2)}) collective-permute-start(f32[4,768]{1,0:T(4,128)S(1)} %get-tuple-element.24), channel_id=1, source_target_pairs={{0,1},{1,0},{2,3},{3,2},{4,5},{5,4},{6,7},{7,6},{8,9},{9,8},{10,11... | collective-permute-start | bytes 36872 | tf_op jit(solution)/shard_map/ppermute | solution.py:258
  43.8 5.8 %collective-permute-start.18 = (f32[4,768]{1,0:T(4,128)S(1)}, f32[4,768]{1,0:T(4,128)S(1)}, u32[]{:S(2)}, u32[]{:S(2)}) collective-permute-start(f32[4,768]{1,0:T(4,128)S(1)} %log_add_fusion.1), channel_id=1, source_target_pairs={{0,6},{1,7},{2,4},{3,5},{4,2},{5,3},{6,0},{7,1},{8,14},{9,15},{10,... | collective-permute-start | bytes 36872 | tf_op jit(solution)/shard_map/ppermute | solution.py:258
  47.9 4.6 %collective-permute-start.17 = (f32[4,768]{1,0:T(4,128)S(1)}, f32[4,768]{1,0:T(4,128)S(1)}, u32[]{:S(2)}, u32[]{:S(2)}) collective-permute-start(f32[4,768]{1,0:T(4,128)S(1)} %log_add_fusion.1), channel_id=1, source_target_pairs={{0,4},{1,5},{2,6},{3,7},{4,0},{5,1},{6,2},{7,3},{8,12},{9,13},{10,... | collective-permute-start | bytes 36872 | tf_op jit(solution)/shard_map/ppermute | solution.py:258
  47.9 4.6 %collective-permute-start.16 = (f32[4,768]{1,0:T(4,128)S(1)}, f32[4,768]{1,0:T(4,128)S(1)}, u32[]{:S(2)}, u32[]{:S(2)}) collective-permute-start(f32[4,768]{1,0:T(4,128)S(1)} %log_add_fusion.1), channel_id=1, source_target_pairs={{0,2},{1,3},{2,0},{3,1},{4,6},{5,7},{6,4},{7,5},{8,10},{9,11},{10,... | collective-permute-start | bytes 36872 | tf_op jit(solution)/shard_map/ppermute | solution.py:258
  52.6 4.7 %collective-permute-start.21 = (f32[4,768]{1,0:T(4,128)S(1)}, f32[4,768]{1,0:T(4,128)S(1)}, u32[]{:S(2)}, u32[]{:S(2)}) collective-permute-start(f32[4,768]{1,0:T(4,128)S(1)} %log_add_fusion), channel_id=1, source_target_pairs={{0,24},{1,25},{2,26},{3,27},{4,28},{5,29},{6,30},{7,31},{8,16},{9,... | collective-permute-start | bytes 36872 | tf_op jit(solution)/shard_map/ppermute | solution.py:258
  55.1 3.7 %collective-permute-start.20 = (f32[4,768]{1,0:T(4,128)S(1)}, f32[4,768]{1,0:T(4,128)S(1)}, u32[]{:S(2)}, u32[]{:S(2)}) collective-permute-start(f32[4,768]{1,0:T(4,128)S(1)} %log_add_fusion), channel_id=1, source_target_pairs={{0,16},{1,17},{2,18},{3,19},{4,20},{5,21},{6,22},{7,23},{8,24},{9,... | collective-permute-start | bytes 36872 | tf_op jit(solution)/shard_map/ppermute | solution.py:258
  55.6 3.7 %collective-permute-start.19 = (f32[4,768]{1,0:T(4,128)S(1)}, f32[4,768]{1,0:T(4,128)S(1)}, u32[]{:S(2)}, u32[]{:S(2)}) collective-permute-start(f32[4,768]{1,0:T(4,128)S(1)} %log_add_fusion), channel_id=1, source_target_pairs={{0,8},{1,9},{2,10},{3,11},{4,12},{5,13},{6,14},{7,15},{8,0},{9,1},... | collective-permute-start | bytes 36872 | tf_op jit(solution)/shard_map/ppermute | solution.py:258

commit v12 on v11

--- a/solution.py
+++ b/solution.py
@@ -250,10 +250,13 @@
     new_ref[...] = updated(total, mass, old_ref[...])
 
 
-def send(value, items, cents, item_mask, cent_mask=0):
+def send(value, items, cents, item_mask, cent_mask=0, cores=(0, 1)):
     masks = item_mask if isinstance(item_mask, tuple) else (item_mask, item_mask)
     pairs = [
-        (i * cents + c, (i ^ masks[c % 2]) * cents + (c ^ cent_mask)) for i in range(items) for c in range(cents)
+        (i * cents + c, (i ^ masks[c % 2]) * cents + (c ^ cent_mask))
+        for i in range(items)
+        for c in range(cents)
+        if c % 2 in cores
     ]
     return lax.ppermute(value, BOTH, pairs)
 
@@ -282,8 +285,8 @@
     rows = centroids.shape[0] // items
     scale = BETA / math.sqrt(dim)
 
-    def go(value, item_mask, cent_mask=0):
-        return send(value, items, cents, item_mask, cent_mask)
+    def go(value, item_mask, cent_mask=0, cores=(0, 1)):
+        return send(value, items, cents, item_mask, cent_mask, cores)
 
     small = items == 4 and cents == 8
     if small:
@@ -370,8 +373,10 @@
     pieces += [in_vmem(piece) for piece in block]
 
     if small:
-        lse = merge_cent(part, go)
-        parts = merge([lse] + [go(lse, mask) for mask in (1, 2, 3)])[None]
+        lse = merge([part, go(part, 0, 1)])
+        lse = merge([lse] + [go(lse, 0, mask, (1,)) for mask in (2, 4, 6)])
+        lse = merge([lse] + [go(lse, mask, 0, (1,)) for mask in (1, 2, 3)])
+        parts = jnp.where(core_index() == 1, lse, go(lse, 0, 1, (1,)))[None]
     else:
         gathered = lax.all_gather(part, "cent", axis=0, tiled=False)
         parts = lax.all_gather(merge([gathered[i] for i in range(cents)]), "item", axis=0, tiled=False)

time: 62.2 us -> 80.2 us (1.29)
  waiting for transfers between devices: 15.5 us -> 31.6 us
  local copies, waits for them, and re-layouts: 0.13 us -> 7.38 us
  starting transfers between devices: 28.9 us -> 23.3 us
    ppermute x22 -> x23, waiting for transfers between devices: 15.5 us -> 31.6 us  [send(): return lax.ppermute(value, BOTH, pairs)]
    unnamed x0 -> x12, local copies, waits for them, and re-layouts: none -> 7.24 us
    ppermute x22 -> x23, starting transfers between devices: 28.9 us -> 23.3 us  [send(): return lax.ppermute(value, BOTH, pairs)]
  transfers between devices with their start and end apart: 22 -> 23, of which waited for: 13 -> 7; matrix products, arithmetic and copies ran while one was open for 0% -> 0% of each run, Pallas kernels for 14% -> 11%
where the time goes in v12:
time: 80.2 us; the launch traced here: 79.8 us
  waiting for transfers between devices  31.6 us (39%)
  starting transfers between devices  23.3 us (29%)
  Pallas kernels  16.4 us (20%)
  local copies, waits for them, and re-layouts  7.38 us (9%)
  between operations  0.9 us (1%)
    ppermute x23, waiting for transfers between devices, send(): return lax.ppermute(value, BOTH, pairs)  31.6 us
    ppermute x23, starting transfers between devices, send(): return lax.ppermute(value, BOTH, pairs)  23.3 us
    unnamed x12, local copies, waits for them, and re-layouts  7.24 us
    pallas_call x1, Pallas kernels, shards(): pl.pallas_call(functools.partial(late_kernel, dict(plan), scale), in_spec...  3.78 us
    pallas_call x1, Pallas kernels, shards(): pl.pallas_call(functools.partial(early_kernel, dict(plan), scale), in_spe...  2.77 us
    pallas_call x1, Pallas kernels, shards(): pl.pallas_call(functools.partial(last_kernel, dict(plan)), in_specs=[vmem...  2.63 us
    pallas_call x1, Pallas kernels, partial(): pl.pallas_call(functools.partial(partial_kernel, scale, min(256, k)), in_...  2.46 us
    pallas_call x1, Pallas kernels, load(): pl.pallas_call(load_kernel, in_specs=[hbm, hbm], out_specs=[vmem] * 2, ou...  2.09 us
  transfers between devices with their start and end apart: 23, of which 7 were waited for; matrix products, arithmetic and copies ran while one was open for 0% of the time, Pallas kernels for 11%

profile of v12, /device:TPU:0, one launch (start us, length us, event | category | flops | bytes accessed | tf_op | source)
XLA Modules:
  0.0 79.8 jit_solution(6167765362133251064)
XLA Ops:
  0.6 1.3 %outgoing.1 = bf16[576,1024]{1,0:T(8,128)(2,1)S(1)} custom-call(bf16[768,1024]{1,0:T(8,128)(2,1)} %v_hbm.3), custom_call_target="tpu_custom_call" | custom-call | bytes 1572864 | tf_op jit(solution)/shard_map/outgoing/pallas_call | solution.py:79
  1.9 3.0 %collective-permute-start.4 = (bf16[576,1024]{1,0:T(8,128)(2,1)S(1)}, bf16[576,1024]{1,0:T(8,128)(2,1)S(1)}, u32[]{:S(2)}, u32[]{:S(2)}) collective-permute-start(bf16[576,1024]{1,0:T(8,128)(2,1)S(1)} %outgoing.1), channel_id=1, source_target_pairs={{0,8},{1,17},{2,10},{3,19},{4,12},{5,21},{6,14},{7,23},{8,0},{9,25... | collective-permute-start | bytes 3538952 | tf_op jit(solution)/shard_map/ppermute | solution.py:261
  4.9 2.1 %load.1 = (bf16[768,1024]{1,0:T(8,128)(2,1)S(1)}, bf16[1024,1024]{1,0:T(8,128)(2,1)S(1)}) custom-call(bf16[768,1024]{1,0:T(8,128)(2,1)} %v_hbm.3, bf16[1024,1024]{1,0:T(8,128)(2,1)} %c_hbm.1), custom_call_target="tpu_custom_call" | custom-call | bytes 7340032 | tf_op jit(solution)/shard_map/load/pallas_call | solution.py:102
  7.0 2.5 %partial_lse.1 = f32[1,768]{1,0:T(1,128)S(1)} custom-call(bf16[768,1024]{1,0:T(8,128)(2,1)S(1)} %get-tuple-element.15.v_ref.home.refs_4_.refs_1_.refs_0_, bf16[1024,1024]{1,0:T(8,128)(2,1)S(1)} %get-tuple-element.14.c_ref), custom_call_target="tpu_custom_call" | custom-call | flops 1610612736 | bytes 3670016 | tf_op jit(solution)/shard_map/partial_lse/pallas_call | solution.py:129
  9.6 1.1 %collective-permute-done = f32[1,768]{1,0:T(1,128)S(1)} collective-permute-done((f32[1,768]{1,0:T(1,128)S(1)}, f32[1,768]{1,0:T(1,128)S(1)}, u32[]{:S(2)}, u32[]{:S(2)}) %collective-permute-start) | collective-permute-done | bytes 3104 | tf_op jit(solution)/shard_map/ppermute | solution.py:261
  10.7 1.6 %collective-permute-start.1 = (f32[1,768]{1,0:T(1,128)S(1)}, f32[1,768]{1,0:T(1,128)S(1)}, u32[]{:S(2)}, u32[]{:S(2)}) collective-permute-start(f32[1,768]{1,0:T(1,128)S(1)} %log_add_fusion.4), channel_id=1, source_target_pairs={{0,2},{1,3},{2,0},{3,1},{4,6},{5,7},{6,4},{7,5},{8,10},{9,11},{10,... | collective-permute-start | bytes 9224 | tf_op jit(solution)/shard_map/ppermute | solution.py:261
  12.4 2.6 %collective-permute-start.2 = (f32[1,768]{1,0:T(1,128)S(1)}, f32[1,768]{1,0:T(1,128)S(1)}, u32[]{:S(2)}, u32[]{:S(2)}) collective-permute-start(f32[1,768]{1,0:T(1,128)S(1)} %log_add_fusion.4), channel_id=1, source_target_pairs={{0,4},{1,5},{2,6},{3,7},{4,0},{5,1},{6,2},{7,3},{8,12},{9,13},{10,... | collective-permute-start | bytes 9224 | tf_op jit(solution)/shard_map/ppermute | solution.py:261
  15.2 1.7 %collective-permute-done.2 = f32[1,768]{1,0:T(1,128)S(1)} collective-permute-done((f32[1,768]{1,0:T(1,128)S(1)}, f32[1,768]{1,0:T(1,128)S(1)}, u32[]{:S(2)}, u32[]{:S(2)}) %collective-permute-start.2) | collective-permute-done | bytes 3104 | tf_op jit(solution)/shard_map/ppermute | solution.py:261
  16.9 3.5 %collective-permute-done.3 = f32[1,768]{1,0:T(1,128)S(1)} collective-permute-done((f32[1,768]{1,0:T(1,128)S(1)}, f32[1,768]{1,0:T(1,128)S(1)}, u32[]{:S(2)}, u32[]{:S(2)}) %collective-permute-start.3) | collective-permute-done | bytes 3104 | tf_op jit(solution)/shard_map/ppermute | solution.py:261
  21.4 1.6 %collective-permute-start.13 = (bf16[384,1024]{1,0:T(8,128)(2,1)S(1)}, bf16[384,1024]{1,0:T(8,128)(2,1)S(1)}, u32[]{:S(2)}, u32[]{:S(2)}) collective-permute-start(bf16[384,1024]{1,0:T(8,128)(2,1)S(1)} %slice.19), channel_id=1, source_target_pairs={{0,16},{1,9},{2,18},{3,11},{4,20},{5,13},{6,22},{7,15},{8,24},{9,1... | collective-permute-start | bytes 2359304 | tf_op jit(solution)/shard_map/ppermute | solution.py:261
  23.0 1.4 %collective-permute-start.12 = (f32[1,768]{1,0:T(1,128)S(1)}, f32[1,768]{1,0:T(1,128)S(1)}, u32[]{:S(2)}, u32[]{:S(2)}) collective-permute-start(f32[1,768]{1,0:T(1,128)S(1)} %log_add_fusion.3.refs_1_.row), channel_id=1, source_target_pairs={{0,24},{1,25},{2,26},{3,27},{4,28},{5,29},{6,30},{7,31},{8,16},{9,... | collective-permute-start | bytes 9224 | tf_op jit(solution)/shard_map/ppermute | solution.py:261
  25.0 2.6 %collective-permute-done.12.refs_3_.refs_0_ = f32[1,768]{1,0:T(1,128)S(1)} collective-permute-done((f32[1,768]{1,0:T(1,128)S(1)}, f32[1,768]{1,0:T(1,128)S(1)}, u32[]{:S(2)}, u32[]{:S(2)}) %collective-permute-start.12) | collective-permute-done | bytes 3104 | tf_op jit(solution)/shard_map/ppermute | solution.py:261
  27.6 4.6 %collective-permute-start.10 = (bf16[192,1024]{1,0:T(8,128)(2,1)S(1)}, bf16[192,1024]{1,0:T(8,128)(2,1)S(1)}, u32[]{:S(2)}, u32[]{:S(2)}) collective-permute-start(bf16[192,1024]{1,0:T(8,128)(2,1)S(1)} %get-tuple-element.27), channel_id=1, source_target_pairs={{0,1},{1,0},{2,3},{3,2},{4,5},{5,4},{6,7},{7,6},{8,9},{9,8},{10,11... | collective-permute-start | bytes 1179656 | tf_op jit(solution)/shard_map/ppermute | solution.py:261
  33.2 1.4 %home_block.1 = (f32[256,1024]{1,0:T(8,128)S(1)}, f32[256,1]{1,0:T(8,128)S(1)}) custom-call(bf16[1024,1024]{1,0:T(8,128)(2,1)S(1)} %get-tuple-element.14.c_ref, bf16[768,1024]{1,0:T(8,128)(2,1)S(1)} %get-tuple-element.15.v_ref.home.refs_4_.refs_1_.refs_0_, f32[1,768]{1,0:T(1,128)S(1)} %log_add_fusion.3.refs_1_.row, ...), custom_call_target="tpu_custom_call" | custom-call | flops 805306368 | bytes 1572864 | tf_op jit(solution)/shard_map/home_block/pallas_call | solution.py:324
  34.6 1.7 %collective-permute-done.7.refs_3_.refs_2_ = f32[1,768]{1,0:T(1,128)S(1)} collective-permute-done((f32[1,768]{1,0:T(1,128)S(1)}, f32[1,768]{1,0:T(1,128)S(1)}, u32[]{:S(2)}, u32[]{:S(2)}) %collective-permute-start.7) | collective-permute-done | bytes 3104 | tf_op jit(solution)/shard_map/ppermute | solution.py:261
  36.4 2.8 %early_blocks.1 = (f32[256,1024]{1,0:T(8,128)S(1)}, f32[256,1]{1,0:T(8,128)S(1)}, bf16[1536,1024]{1,0:T(8,128)(2,1)S(1)}) custom-call(bf16[1024,1024]{1,0:T(8,128)(2,1)S(1)} %get-tuple-element.14.c_ref, f32[256,1024]{1,0:T(8,128)S(1)} %get-tuple-element.16.refs_0_, f32[256,1]{1,0:T(8,128)S(1)} %get-tuple-element.17.refs_1_.refs_8_, ...), custom_call_target="tpu_custom_call" | custom-call | tf_op jit(solution)/shard_map/early_blocks/pallas_call | solution.py:334
  39.2 3.8 %late_blocks.1 = (bf16[256,1024]{1,0:T(8,128)(2,1)S(1)}, f32[4,256,768]{2,1,0:T(8,128)S(1)}, f32[4,768]{1,0:T(4,128)S(1)}, f32[4,768]{1,0:T(4,128)S(1)}, bf16[768,1024]{1,0:T(8,128)(2,1)S(1)}) custom-call(bf16[1024,1024]{1,0:T(8,128)(2,1)S(1)} %get-tuple-element.14.c_ref, f32[256,1024]{1,0:T(8,128)S(1)} %get-tuple-element.18.total, ...), custom_call_target="tpu_custom_call" | custom-call | flops 2415919104 | bytes 1572864 | tf_op jit(solution)/shard_map/late_blocks/pallas_call | solution.py:354
  43.0 1.6 %copy-done.2 = f32[4,256,768]{2,1,0:T(8,128)} copy-done((f32[4,256,768]{2,1,0:T(8,128)}, f32[4,256,768]{2,1,0:T(8,128)S(1)}, u32[]{:S(2)}) %copy-start.2) | copy-done | bytes 3145752
  50.9 1.3 %collective-permute-start.22 = (f32[4,768]{1,0:T(4,128)S(1)}, f32[4,768]{1,0:T(4,128)S(1)}, u32[]{:S(2)}, u32[]{:S(2)}) collective-permute-start(f32[4,768]{1,0:T(4,128)S(1)} %log_add_fusion), channel_id=1, source_target_pairs={{1,0},{3,2},{5,4},{7,6},{9,8},{11,10},{13,12},{15,14},{17,16},{19,... | collective-permute-start | bytes 36872 | tf_op jit(solution)/shard_map/ppermute | solution.py:261
  52.3 20.1 %collective-permute-done.22 = f32[4,768]{1,0:T(4,128)S(1)} collective-permute-done((f32[4,768]{1,0:T(4,128)S(1)}, f32[4,768]{1,0:T(4,128)S(1)}, u32[]{:S(2)}, u32[]{:S(2)}) %collective-permute-start.22) | collective-permute-done | bytes 12320 | tf_op jit(solution)/shard_map/ppermute | solution.py:261
  72.3 1.9 %copy-done.1 = bf16[1536,1024]{1,0:T(8,128)(2,1)S(1)} copy-done((bf16[1536,1024]{1,0:T(8,128)(2,1)S(1)}, bf16[1536,1024]{1,0:T(8,128)(2,1)}, u32[]{:S(2)}) %copy-start.1) | copy-done | bytes 3145752
  74.2 1.9 %copy-done.3 = f32[4,256,768]{2,1,0:T(8,128)S(1)} copy-done((f32[4,256,768]{2,1,0:T(8,128)S(1)}, f32[4,256,768]{2,1,0:T(8,128)}, u32[]{:S(2)}) %copy-start.3) | copy-done | bytes 3145752
  76.1 1.0 %copy-done.5 = bf16[256,1024]{1,0:T(8,128)(2,1)S(1)} copy-done((bf16[256,1024]{1,0:T(8,128)(2,1)S(1)}, bf16[256,1024]{1,0:T(8,128)(2,1)}, u32[]{:S(2)}) %copy-start.5) | copy-done | bytes 524312
  77.1 2.6 %last_iteration.1 = (bf16[256,1024]{1,0:T(8,128)(2,1)}, f32[768]{0:T(1024)}) custom-call(bf16[256,1024]{1,0:T(8,128)(2,1)S(1)} %copy-done.5, f32[4,256,768]{2,1,0:T(8,128)S(1)} %copy-done.3, f32[4,768]{1,0:T(4,128)S(1)} %get-tuple-element.23.peak_ref, f32[1,4,768]{2,1,0:T(4,128)S(1)} %select_bitcast_fusion.parts, ...), custom_call_target="tpu_custom_call" | custom-call | flops 1610612736 | bytes 524288 | tf_op jit(solution)/shard_map/last_iteration/pallas_call | solution.py:383
  (51 shorter events, 9.2 us)
Async XLA Ops:
  1.9 18.5 %collective-permute-start.4 = (bf16[576,1024]{1,0:T(8,128)(2,1)S(1)}, bf16[576,1024]{1,0:T(8,128)(2,1)S(1)}, u32[]{:S(2)}, u32[]{:S(2)}) collective-permute-start(bf16[576,1024]{1,0:T(8,128)(2,1)S(1)} %outgoing.1), channel_id=1, source_target_pairs={{0,8},{1,17},{2,10},{3,19},{4,12},{5,21},{6,14},{7,23},{8,0},{9,25... | collective-permute-start | bytes 3538952 | tf_op jit(solution)/shard_map/ppermute | solution.py:261
  9.5 1.2 %collective-permute-start = (f32[1,768]{1,0:T(1,128)S(1)}, f32[1,768]{1,0:T(1,128)S(1)}, u32[]{:S(2)}, u32[]{:S(2)}) collective-permute-start(f32[1,768]{1,0:T(1,128)S(1)} %partial_lse.1), channel_id=1, source_target_pairs={{0,1},{1,0},{2,3},{3,2},{4,5},{5,4},{6,7},{7,6},{8,9},{9,8},{10,11... | collective-permute-start | bytes 9224 | tf_op jit(solution)/shard_map/ppermute | solution.py:261
  10.7 4.5 %collective-permute-start.1 = (f32[1,768]{1,0:T(1,128)S(1)}, f32[1,768]{1,0:T(1,128)S(1)}, u32[]{:S(2)}, u32[]{:S(2)}) collective-permute-start(f32[1,768]{1,0:T(1,128)S(1)} %log_add_fusion.4), channel_id=1, source_target_pairs={{0,2},{1,3},{2,0},{3,1},{4,6},{5,7},{6,4},{7,5},{8,10},{9,11},{10,... | collective-permute-start | bytes 9224 | tf_op jit(solution)/shard_map/ppermute | solution.py:261
  12.4 4.5 %collective-permute-start.2 = (f32[1,768]{1,0:T(1,128)S(1)}, f32[1,768]{1,0:T(1,128)S(1)}, u32[]{:S(2)}, u32[]{:S(2)}) collective-permute-start(f32[1,768]{1,0:T(1,128)S(1)} %log_add_fusion.4), channel_id=1, source_target_pairs={{0,4},{1,5},{2,6},{3,7},{4,0},{5,1},{6,2},{7,3},{8,12},{9,13},{10,... | collective-permute-start | bytes 9224 | tf_op jit(solution)/shard_map/ppermute | solution.py:261
  15.0 5.4 %collective-permute-start.3 = (f32[1,768]{1,0:T(1,128)S(1)}, f32[1,768]{1,0:T(1,128)S(1)}, u32[]{:S(2)}, u32[]{:S(2)}) collective-permute-start(f32[1,768]{1,0:T(1,128)S(1)} %log_add_fusion.4), channel_id=1, source_target_pairs={{0,6},{1,7},{2,4},{3,5},{4,2},{5,3},{6,0},{7,1},{8,14},{9,15},{10,... | collective-permute-start | bytes 9224 | tf_op jit(solution)/shard_map/ppermute | solution.py:261
  20.5 11.7 %collective-permute-start.8 = (bf16[192,1024]{1,0:T(8,128)(2,1)S(1)}, bf16[192,1024]{1,0:T(8,128)(2,1)S(1)}, u32[]{:S(2)}, u32[]{:S(2)}) collective-permute-start(bf16[192,1024]{1,0:T(8,128)(2,1)S(1)} %get-tuple-element.27), channel_id=1, source_target_pairs={{0,2},{1,3},{2,0},{3,1},{4,6},{5,7},{6,4},{7,5},{8,10},{9,11},{10,... | collective-permute-start | bytes 1179656 | tf_op jit(solution)/shard_map/ppermute | solution.py:261
  21.4 14.9 %collective-permute-start.13 = (bf16[384,1024]{1,0:T(8,128)(2,1)S(1)}, bf16[384,1024]{1,0:T(8,128)(2,1)S(1)}, u32[]{:S(2)}, u32[]{:S(2)}) collective-permute-start(bf16[384,1024]{1,0:T(8,128)(2,1)S(1)} %slice.19), channel_id=1, source_target_pairs={{0,16},{1,9},{2,18},{3,11},{4,20},{5,13},{6,22},{7,15},{8,24},{9,1... | collective-permute-start | bytes 2359304 | tf_op jit(solution)/shard_map/ppermute | solution.py:261
  23.0 9.7 %collective-permute-start.5 = (bf16[192,1024]{1,0:T(8,128)(2,1)S(1)}, bf16[192,1024]{1,0:T(8,128)(2,1)S(1)}, u32[]{:S(2)}, u32[]{:S(2)}) collective-permute-start(bf16[192,1024]{1,0:T(8,128)(2,1)S(1)} %get-tuple-element.28), channel_id=1, source_target_pairs={{0,1},{1,0},{2,3},{3,2},{4,5},{5,4},{6,7},{7,6},{8,9},{9,8},{10,11... | collective-permute-start | bytes 1179656 | tf_op jit(solution)/shard_map/ppermute | solution.py:261
  23.0 4.6 %collective-permute-start.12 = (f32[1,768]{1,0:T(1,128)S(1)}, f32[1,768]{1,0:T(1,128)S(1)}, u32[]{:S(2)}, u32[]{:S(2)}) collective-permute-start(f32[1,768]{1,0:T(1,128)S(1)} %log_add_fusion.3.refs_1_.row), channel_id=1, source_target_pairs={{0,24},{1,25},{2,26},{3,27},{4,28},{5,29},{6,30},{7,31},{8,16},{9,... | collective-permute-start | bytes 9224 | tf_op jit(solution)/shard_map/ppermute | solution.py:261
  24.4 7.7 %collective-permute-start.6 = (f32[1,768]{1,0:T(1,128)S(1)}, f32[1,768]{1,0:T(1,128)S(1)}, u32[]{:S(2)}, u32[]{:S(2)}) collective-permute-start(f32[1,768]{1,0:T(1,128)S(1)} %log_add_fusion.3.refs_1_.row), channel_id=1, source_target_pairs={{0,8},{1,17},{2,10},{3,19},{4,12},{5,21},{6,14},{7,23},{8,0},{9,25... | collective-permute-start | bytes 9224 | tf_op jit(solution)/shard_map/ppermute | solution.py:261
  27.6 8.7 %collective-permute-start.10 = (bf16[192,1024]{1,0:T(8,128)(2,1)S(1)}, bf16[192,1024]{1,0:T(8,128)(2,1)S(1)}, u32[]{:S(2)}, u32[]{:S(2)}) collective-permute-start(bf16[192,1024]{1,0:T(8,128)(2,1)S(1)} %get-tuple-element.27), channel_id=1, source_target_pairs={{0,1},{1,0},{2,3},{3,2},{4,5},{5,4},{6,7},{7,6},{8,9},{9,8},{10,11... | collective-permute-start | bytes 1179656 | tf_op jit(solution)/shard_map/ppermute | solution.py:261
  32.2 4.1 %collective-permute-start.9 = (bf16[192,1024]{1,0:T(8,128)(2,1)S(1)}, bf16[192,1024]{1,0:T(8,128)(2,1)S(1)}, u32[]{:S(2)}, u32[]{:S(2)}) collective-permute-start(bf16[192,1024]{1,0:T(8,128)(2,1)S(1)} %get-tuple-element.26), channel_id=1, source_target_pairs={{0,1},{1,0},{2,3},{3,2},{4,5},{5,4},{6,7},{7,6},{8,9},{9,8},{10,11... | collective-permute-start | bytes 1179656 | tf_op jit(solution)/shard_map/ppermute | solution.py:261
  32.2 4.1 %collective-permute-start.11 = (bf16[192,1024]{1,0:T(8,128)(2,1)S(1)}, bf16[192,1024]{1,0:T(8,128)(2,1)S(1)}, u32[]{:S(2)}, u32[]{:S(2)}) collective-permute-start(bf16[192,1024]{1,0:T(8,128)(2,1)S(1)} %collective-permute-done.8.refs_6_), channel_id=1, source_target_pairs={{0,1},{1,0},{2,3},{3,2},{4,5},{5,4},{6,7},{7,6},{8,9},{9,8},{10,11... | collective-permute-start | bytes 1179656 | tf_op jit(solution)/shard_map/ppermute | solution.py:261
  32.7 3.6 %collective-permute-start.7 = (f32[1,768]{1,0:T(1,128)S(1)}, f32[1,768]{1,0:T(1,128)S(1)}, u32[]{:S(2)}, u32[]{:S(2)}) collective-permute-start(f32[1,768]{1,0:T(1,128)S(1)} %log_add_fusion.3.refs_1_.row), channel_id=1, source_target_pairs={{0,16},{1,9},{2,18},{3,11},{4,20},{5,13},{6,22},{7,15},{8,24},{9,1... | collective-permute-start | bytes 9224 | tf_op jit(solution)/shard_map/ppermute | solution.py:261
  36.3 2.9 %collective-permute-start.14 = (bf16[384,1024]{1,0:T(8,128)(2,1)S(1)}, bf16[384,1024]{1,0:T(8,128)(2,1)S(1)}, u32[]{:S(2)}, u32[]{:S(2)}) collective-permute-start(bf16[384,1024]{1,0:T(8,128)(2,1)S(1)} %after.3.refs_3_), channel_id=1, source_target_pairs={{0,1},{1,0},{2,3},{3,2},{4,5},{5,4},{6,7},{7,6},{8,9},{9,8},{10,11... | collective-permute-start | bytes 2359304 | tf_op jit(solution)/shard_map/ppermute | solution.py:261
  39.2 3.8 %copy-start = (bf16[1536,1024]{1,0:T(8,128)(2,1)}, bf16[1536,1024]{1,0:T(8,128)(2,1)S(1)}, u32[]{:S(2)}) copy-start(bf16[1536,1024]{1,0:T(8,128)(2,1)S(1)} %get-tuple-element.20.refs_2_.refs_1_) | copy-start | bytes 9437188
  45.4 1.3 %collective-permute-start.15 = (f32[4,768]{1,0:T(4,128)S(1)}, f32[4,768]{1,0:T(4,128)S(1)}, u32[]{:S(2)}, u32[]{:S(2)}) collective-permute-start(f32[4,768]{1,0:T(4,128)S(1)} %get-tuple-element.24), channel_id=1, source_target_pairs={{0,1},{1,0},{2,3},{3,2},{4,5},{5,4},{6,7},{7,6},{8,9},{9,8},{10,11... | collective-permute-start | bytes 36872 | tf_op jit(solution)/shard_map/ppermute | solution.py:261
  46.8 2.0 %collective-permute-start.16 = (f32[4,768]{1,0:T(4,128)S(1)}, f32[4,768]{1,0:T(4,128)S(1)}, u32[]{:S(2)}, u32[]{:S(2)}) collective-permute-start(f32[4,768]{1,0:T(4,128)S(1)} %log_add_fusion.2), channel_id=1, source_target_pairs={{1,3},{3,1},{5,7},{7,5},{9,11},{11,9},{13,15},{15,13},{17,19},{19,... | collective-permute-start | bytes 36872 | tf_op jit(solution)/shard_map/ppermute | solution.py:261
  47.5 1.4 %collective-permute-start.17 = (f32[4,768]{1,0:T(4,128)S(1)}, f32[4,768]{1,0:T(4,128)S(1)}, u32[]{:S(2)}, u32[]{:S(2)}) collective-permute-start(f32[4,768]{1,0:T(4,128)S(1)} %log_add_fusion.2), channel_id=1, source_target_pairs={{1,5},{3,7},{5,1},{7,3},{9,13},{11,15},{13,9},{15,11},{17,21},{19,... | collective-permute-start | bytes 36872 | tf_op jit(solution)/shard_map/ppermute | solution.py:261
  48.1 0.7 collective-permute-start.18
  48.9 2.0 %collective-permute-start.19 = (f32[4,768]{1,0:T(4,128)S(1)}, f32[4,768]{1,0:T(4,128)S(1)}, u32[]{:S(2)}, u32[]{:S(2)}) collective-permute-start(f32[4,768]{1,0:T(4,128)S(1)} %log_add_fusion.1), channel_id=1, source_target_pairs={{1,9},{3,11},{5,13},{7,15},{9,1},{11,3},{13,5},{15,7},{17,25},{19,... | collective-permute-start | bytes 36872 | tf_op jit(solution)/shard_map/ppermute | solution.py:261
  49.5 1.4 %collective-permute-start.20 = (f32[4,768]{1,0:T(4,128)S(1)}, f32[4,768]{1,0:T(4,128)S(1)}, u32[]{:S(2)}, u32[]{:S(2)}) collective-permute-start(f32[4,768]{1,0:T(4,128)S(1)} %log_add_fusion.1), channel_id=1, source_target_pairs={{1,17},{3,19},{5,21},{7,23},{9,25},{11,27},{13,29},{15,31},{17,1},... | collective-permute-start | bytes 36872 | tf_op jit(solution)/shard_map/ppermute | solution.py:261
  50.2 0.7 collective-permute-start.21
  50.9 21.4 %collective-permute-start.22 = (f32[4,768]{1,0:T(4,128)S(1)}, f32[4,768]{1,0:T(4,128)S(1)}, u32[]{:S(2)}, u32[]{:S(2)}) collective-permute-start(f32[4,768]{1,0:T(4,128)S(1)} %log_add_fusion), channel_id=1, source_target_pairs={{1,0},{3,2},{5,4},{7,6},{9,8},{11,10},{13,12},{15,14},{17,16},{19,... | collective-permute-start | bytes 36872 | tf_op jit(solution)/shard_map/ppermute | solution.py:261
  (5 other events, 7.2 us)

commit v13 on v11

--- a/solution.py
+++ b/solution.py
@@ -167,6 +167,22 @@
 
 def own_rows(c_ref, rows):
     return c_ref[pl.ds(pl.multiple_of(lax.axis_index("item") * rows, rows), rows), :]
+
+
+def begin(centroids, home, lse, other, rows, scale):
+    nv, dim = home.shape
+    vmem = pl.BlockSpec(memory_space=pltpu.VMEM)
+    return pl.pallas_call(
+        functools.partial(home_kernel, scale),
+        in_specs=[vmem] * 3 + [pl.BlockSpec(memory_space=pl.ANY)],
+        out_specs=[vmem] * 2,
+        out_shape=[pltpu.VMEM((rows, dim), jnp.float32), pltpu.VMEM((rows, 1), jnp.float32)],
+        compiler_params=pltpu.CompilerParams(vmem_limit_bytes=16 * MIB),
+        cost_estimate=pl.CostEstimate(
+            flops=4 * nv * rows * dim, bytes_accessed=2 * nv * dim, transcendentals=nv * rows
+        ),
+        name="home_block",
+    )(in_vmem(centroids), in_vmem(home), lse, other)
 
 
 def home_kernel(scale, c_ref, home, row, _, total, mass):
@@ -295,6 +311,8 @@
         quarters = [near[i : i + nv // 4] for i in range(0, near.shape[0], nv // 4)]
         swapped = go(quarters[2], 0, 2)
         far = go(near[: nv // 2], (2, 1))
+        begun = begin(centroids, home, lse, parts[3], rows, scale)
+        swapped = after(swapped, begun[1])
         near = [near, swapped] + [go(piece, 0, 1) for piece in quarters + [swapped]]
         pieces = [home]
         plan = dict(exchange=True, first=1, early=3, blocks=[(0, 0), (1, 0), (1, nv), (2, 0)])
@@ -305,7 +323,7 @@
         parts = lax.all_gather(parts, "item", axis=0, tiled=False)
         parts = [parts[i] for i in range(items)]
         pieces = [lax.all_gather(vectors, "item", axis=0, tiled=True)]
-        near = []
+        near = begun = []
         plan = dict(exchange=False, first=0, early=items, blocks=[(0, i * nv) for i in range(items)])
     plan.update(nv=nv, places=items, pieces=len(pieces), arrived=len(near))
     pieces = [in_vmem(piece) for piece in pieces]
@@ -316,18 +334,6 @@
     early, late = plan["early"], items - plan["early"]
     params = pltpu.CompilerParams(vmem_limit_bytes=16 * MIB)
     tables = [pltpu.VMEM((2 * nv, dim), jnp.bfloat16)] if near else []
-    begun = []
-    if plan["first"]:
-        begun = pl.pallas_call(
-            functools.partial(home_kernel, scale),
-            in_specs=[vmem] * 3 + [pl.BlockSpec(memory_space=pl.ANY)],
-            out_specs=[vmem] * 2,
-            out_shape=[pltpu.VMEM((rows, dim), jnp.float32), pltpu.VMEM((rows, 1), jnp.float32)],
-            compiler_params=params,
-            cost_estimate=pl.CostEstimate(flops=2 * flops, bytes_accessed=2 * nv * dim, transcendentals=nv * rows),
-            name="home_block",
-        )(centroids, pieces[0], parts[0], near[2])
-        begun = [in_vmem(value) for value in begun]
     total, mass, *table = pl.pallas_call(
         functools.partial(early_kernel, dict(plan), scale),
         in_specs=[vmem] * (1 + len(begun) + early - plan["first"] + len(pieces) + len(near)),
@@ -340,13 +346,13 @@
         compiler_params=params,
         cost_estimate=pl.CostEstimate(flops=0, bytes_accessed=0, transcendentals=0),
         name="early_blocks",
-    )(centroids, *begun, *parts[plan["first"] : early], *pieces, *[in_vmem(piece) for piece in near])
+    )(centroids, *[in_vmem(value) for value in begun], *parts[plan["first"] : early], *pieces, *[in_vmem(piece) for piece in near])
     pieces += [in_vmem(piece) for piece in table]
     plan["pieces"] = len(pieces)
 
     arrived = []
     if late:
-        far = after(far, *parts[1:], *near[2:], begun[1])
+        far = after(far, *parts[1:], *near[2:])
         arrived = [in_vmem(far), in_vmem(go(far, 0, 1))]
     fresh, expo, peak, part, *block = pl.pallas_call(
         functools.partial(late_kernel, dict(plan), scale),

time: 62.2 us -> 61.8 us (level)
  transfers between devices with their start and end apart: 22 -> 22, of which waited for: 13 -> 15; matrix products, arithmetic and copies ran while one was open for 0% -> 0% of each run, Pallas kernels for 14% -> 14%
where the time goes in v13:
time: 61.8 us; the launch traced here: 61.6 us
  starting transfers between devices  28.6 us (46%)
  Pallas kernels  16.6 us (27%)
  waiting for transfers between devices  15.4 us (25%)
  between operations  0.72 us (1%)
    ppermute x22, starting transfers between devices, send(): return lax.ppermute(value, BOTH, pairs)  28.6 us
    ppermute x22, waiting for transfers between devices, send(): return lax.ppermute(value, BOTH, pairs)  15.4 us
    pallas_call x1, Pallas kernels, shards(): pl.pallas_call(functools.partial(late_kernel, dict(plan), scale), in_spec...  3.87 us
    pallas_call x1, Pallas kernels, shards(): pl.pallas_call(functools.partial(early_kernel, dict(plan), scale), in_spe...  2.8 us
    pallas_call x1, Pallas kernels, shards(): pl.pallas_call(functools.partial(last_kernel, dict(plan)), in_specs=[vmem...  2.72 us
    pallas_call x1, Pallas kernels, partial(): pl.pallas_call(functools.partial(partial_kernel, scale, min(256, k)), in_...  2.46 us
    pallas_call x1, Pallas kernels, load(): pl.pallas_call(load_kernel, in_specs=[hbm, hbm], out_specs=[vmem] * 2, ou...  2.09 us
    pallas_call x1, Pallas kernels, begin(): pl.pallas_call(functools.partial(home_kernel, scale), in_specs=[vmem] * 3...  1.36 us
  transfers between devices with their start and end apart: 22, of which 15 were waited for; matrix products, arithmetic and copies ran while one was open for 0% of the time, Pallas kernels for 14%

profile of v13, /device:TPU:0, one launch (start us, length us, event | category | flops | bytes accessed | tf_op | source)
XLA Modules:
  0.0 61.6 jit_solution(12774981077429133722)
XLA Ops:
  0.6 1.3 %outgoing.1 = bf16[576,1024]{1,0:T(8,128)(2,1)S(1)} custom-call(bf16[768,1024]{1,0:T(8,128)(2,1)} %v_hbm.3), custom_call_target="tpu_custom_call" | custom-call | bytes 1572864 | tf_op jit(solution)/shard_map/outgoing/pallas_call | solution.py:79
  1.9 3.0 %collective-permute-start.7 = (bf16[576,1024]{1,0:T(8,128)(2,1)S(1)}, bf16[576,1024]{1,0:T(8,128)(2,1)S(1)}, u32[]{:S(2)}, u32[]{:S(2)}) collective-permute-start(bf16[576,1024]{1,0:T(8,128)(2,1)S(1)} %outgoing.1), channel_id=1, source_target_pairs={{0,8},{1,17},{2,10},{3,19},{4,12},{5,21},{6,14},{7,23},{8,0},{9,25... | collective-permute-start | bytes 3538952 | tf_op jit(solution)/shard_map/ppermute | solution.py:274
  4.9 2.1 %load.1 = (bf16[768,1024]{1,0:T(8,128)(2,1)S(1)}, bf16[1024,1024]{1,0:T(8,128)(2,1)S(1)}) custom-call(bf16[768,1024]{1,0:T(8,128)(2,1)} %v_hbm.3, bf16[1024,1024]{1,0:T(8,128)(2,1)} %c_hbm.1), custom_call_target="tpu_custom_call" | custom-call | bytes 7340032 | tf_op jit(solution)/shard_map/load/pallas_call | solution.py:102
  7.0 2.5 %partial_lse.1 = f32[1,768]{1,0:T(1,128)S(1)} custom-call(bf16[768,1024]{1,0:T(8,128)(2,1)S(1)} %get-tuple-element.15.v_ref.home.refs_4_.refs_1_.refs_0_, bf16[1024,1024]{1,0:T(8,128)(2,1)S(1)} %get-tuple-element.14.c_ref), custom_call_target="tpu_custom_call" | custom-call | flops 1610612736 | bytes 3670016 | tf_op jit(solution)/shard_map/partial_lse/pallas_call | solution.py:129
  9.6 1.1 %collective-permute-done = f32[1,768]{1,0:T(1,128)S(1)} collective-permute-done((f32[1,768]{1,0:T(1,128)S(1)}, f32[1,768]{1,0:T(1,128)S(1)}, u32[]{:S(2)}, u32[]{:S(2)}) %collective-permute-start) | collective-permute-done | bytes 3104 | tf_op jit(solution)/shard_map/ppermute | solution.py:274
  10.7 3.7 %collective-permute-start.3 = (f32[1,768]{1,0:T(1,128)S(1)}, f32[1,768]{1,0:T(1,128)S(1)}, u32[]{:S(2)}, u32[]{:S(2)}) collective-permute-start(f32[1,768]{1,0:T(1,128)S(1)} %log_add_fusion.3), channel_id=1, source_target_pairs={{0,6},{1,7},{2,4},{3,5},{4,2},{5,3},{6,0},{7,1},{8,14},{9,15},{10,... | collective-permute-start | bytes 9224 | tf_op jit(solution)/shard_map/ppermute | solution.py:274
  16.2 2.7 %collective-permute-done.2 = f32[1,768]{1,0:T(1,128)S(1)} collective-permute-done((f32[1,768]{1,0:T(1,128)S(1)}, f32[1,768]{1,0:T(1,128)S(1)}, u32[]{:S(2)}, u32[]{:S(2)}) %collective-permute-start.2) | collective-permute-done | bytes 3104 | tf_op jit(solution)/shard_map/ppermute | solution.py:274
  19.2 2.2 %collective-permute-start.8 = (bf16[192,1024]{1,0:T(8,128)(2,1)S(1)}, bf16[192,1024]{1,0:T(8,128)(2,1)S(1)}, u32[]{:S(2)}, u32[]{:S(2)}) collective-permute-start(bf16[192,1024]{1,0:T(8,128)(2,1)S(1)} %get-tuple-element.28), channel_id=1, source_target_pairs={{0,2},{1,3},{2,0},{3,1},{4,6},{5,7},{6,4},{7,5},{8,10},{9,11},{10,... | collective-permute-start | bytes 1179656 | tf_op jit(solution)/shard_map/ppermute | solution.py:274
  21.4 1.6 %collective-permute-start.13 = (bf16[384,1024]{1,0:T(8,128)(2,1)S(1)}, bf16[384,1024]{1,0:T(8,128)(2,1)S(1)}, u32[]{:S(2)}, u32[]{:S(2)}) collective-permute-start(bf16[384,1024]{1,0:T(8,128)(2,1)S(1)} %slice.19), channel_id=1, source_target_pairs={{0,16},{1,9},{2,18},{3,11},{4,20},{5,13},{6,22},{7,15},{8,24},{9,1... | collective-permute-start | bytes 2359304 | tf_op jit(solution)/shard_map/ppermute | solution.py:274
  23.0 1.4 %collective-permute-start.4 = (f32[1,768]{1,0:T(1,128)S(1)}, f32[1,768]{1,0:T(1,128)S(1)}, u32[]{:S(2)}, u32[]{:S(2)}) collective-permute-start(f32[1,768]{1,0:T(1,128)S(1)} %log_add_fusion.2.row.refs_1_), channel_id=1, source_target_pairs={{0,24},{1,25},{2,26},{3,27},{4,28},{5,29},{6,30},{7,31},{8,16},{9,... | collective-permute-start | bytes 9224 | tf_op jit(solution)/shard_map/ppermute | solution.py:274
  24.4 1.5 %collective-permute-start.6 = (f32[1,768]{1,0:T(1,128)S(1)}, f32[1,768]{1,0:T(1,128)S(1)}, u32[]{:S(2)}, u32[]{:S(2)}) collective-permute-start(f32[1,768]{1,0:T(1,128)S(1)} %log_add_fusion.2.row.refs_1_), channel_id=1, source_target_pairs={{0,16},{1,9},{2,18},{3,11},{4,20},{5,13},{6,22},{7,15},{8,24},{9,1... | collective-permute-start | bytes 9224 | tf_op jit(solution)/shard_map/ppermute | solution.py:274
  27.6 1.4 %home_block.1 = (f32[256,1024]{1,0:T(8,128)S(1)}, f32[256,1]{1,0:T(8,128)S(1)}) custom-call(bf16[1024,1024]{1,0:T(8,128)(2,1)S(1)} %get-tuple-element.14.c_ref, bf16[768,1024]{1,0:T(8,128)(2,1)S(1)} %get-tuple-element.15.v_ref.home.refs_4_.refs_1_.refs_0_, f32[1,768]{1,0:T(1,128)S(1)} %log_add_fusion.2.row.refs_1_, ...), custom_call_target="tpu_custom_call" | custom-call | flops 805306368 | bytes 1572864 | tf_op jit(solution)/shard_map/home_block/pallas_call | solution.py:175
  29.0 4.6 %collective-permute-start.10 = (bf16[192,1024]{1,0:T(8,128)(2,1)S(1)}, bf16[192,1024]{1,0:T(8,128)(2,1)S(1)}, u32[]{:S(2)}, u32[]{:S(2)}) collective-permute-start(bf16[192,1024]{1,0:T(8,128)(2,1)S(1)} %get-tuple-element.26), channel_id=1, source_target_pairs={{0,1},{1,0},{2,3},{3,2},{4,5},{5,4},{6,7},{7,6},{8,9},{9,8},{10,11... | collective-permute-start | bytes 1179656 | tf_op jit(solution)/shard_map/ppermute | solution.py:274
  37.0 2.8 %early_blocks.1 = (f32[256,1024]{1,0:T(8,128)S(1)}, f32[256,1]{1,0:T(8,128)S(1)}, bf16[1536,1024]{1,0:T(8,128)(2,1)S(1)}) custom-call(bf16[1024,1024]{1,0:T(8,128)(2,1)S(1)} %get-tuple-element.14.c_ref, f32[256,1024]{1,0:T(8,128)S(1)} %get-tuple-element.16.refs_0_, f32[256,1]{1,0:T(8,128)S(1)} %get-tuple-element.17.refs_1_, ...), custom_call_target="tpu_custom_call" | custom-call | tf_op jit(solution)/shard_map/early_blocks/pallas_call | solution.py:337
  39.8 3.9 %late_blocks.1 = (bf16[256,1024]{1,0:T(8,128)(2,1)S(1)}, f32[4,256,768]{2,1,0:T(8,128)S(1)}, f32[4,768]{1,0:T(4,128)S(1)}, f32[4,768]{1,0:T(4,128)S(1)}, bf16[768,1024]{1,0:T(8,128)(2,1)S(1)}) custom-call(bf16[1024,1024]{1,0:T(8,128)(2,1)S(1)} %get-tuple-element.14.c_ref, f32[256,1024]{1,0:T(8,128)S(1)} %get-tuple-element.18.total, ...), custom_call_target="tpu_custom_call" | custom-call | flops 2415919104 | bytes 1572864 | tf_op jit(solution)/shard_map/late_blocks/pallas_call | solution.py:357
  45.0 2.5 %collective-permute-start.18 = (f32[4,768]{1,0:T(4,128)S(1)}, f32[4,768]{1,0:T(4,128)S(1)}, u32[]{:S(2)}, u32[]{:S(2)}) collective-permute-start(f32[4,768]{1,0:T(4,128)S(1)} %log_add_fusion.1), channel_id=1, source_target_pairs={{0,6},{1,7},{2,4},{3,5},{4,2},{5,3},{6,0},{7,1},{8,14},{9,15},{10,... | collective-permute-start | bytes 36872 | tf_op jit(solution)/shard_map/ppermute | solution.py:274
  47.7 1.7 %collective-permute-start.16 = (f32[4,768]{1,0:T(4,128)S(1)}, f32[4,768]{1,0:T(4,128)S(1)}, u32[]{:S(2)}, u32[]{:S(2)}) collective-permute-start(f32[4,768]{1,0:T(4,128)S(1)} %log_add_fusion.1), channel_id=1, source_target_pairs={{0,2},{1,3},{2,0},{3,1},{4,6},{5,7},{6,4},{7,5},{8,10},{9,11},{10,... | collective-permute-start | bytes 36872 | tf_op jit(solution)/shard_map/ppermute | solution.py:274
  49.4 1.1 %collective-permute-done.18 = f32[4,768]{1,0:T(4,128)S(1)} collective-permute-done((f32[4,768]{1,0:T(4,128)S(1)}, f32[4,768]{1,0:T(4,128)S(1)}, u32[]{:S(2)}, u32[]{:S(2)}) %collective-permute-start.18) | collective-permute-done | bytes 12320 | tf_op jit(solution)/shard_map/ppermute | solution.py:274
  50.5 1.6 %collective-permute-done.17 = f32[4,768]{1,0:T(4,128)S(1)} collective-permute-done((f32[4,768]{1,0:T(4,128)S(1)}, f32[4,768]{1,0:T(4,128)S(1)}, u32[]{:S(2)}, u32[]{:S(2)}) %collective-permute-start.17) | collective-permute-done | bytes 12320 | tf_op jit(solution)/shard_map/ppermute | solution.py:274
  52.2 1.6 %collective-permute-start.21 = (f32[4,768]{1,0:T(4,128)S(1)}, f32[4,768]{1,0:T(4,128)S(1)}, u32[]{:S(2)}, u32[]{:S(2)}) collective-permute-start(f32[4,768]{1,0:T(4,128)S(1)} %log_add_fusion), channel_id=1, source_target_pairs={{0,24},{1,25},{2,26},{3,27},{4,28},{5,29},{6,30},{7,31},{8,16},{9,... | collective-permute-start | bytes 36872 | tf_op jit(solution)/shard_map/ppermute | solution.py:274
  53.7 1.5 %collective-permute-start.20 = (f32[4,768]{1,0:T(4,128)S(1)}, f32[4,768]{1,0:T(4,128)S(1)}, u32[]{:S(2)}, u32[]{:S(2)}) collective-permute-start(f32[4,768]{1,0:T(4,128)S(1)} %log_add_fusion), channel_id=1, source_target_pairs={{0,16},{1,17},{2,18},{3,19},{4,20},{5,21},{6,22},{7,23},{8,24},{9,... | collective-permute-start | bytes 36872 | tf_op jit(solution)/shard_map/ppermute | solution.py:274
  55.7 1.1 %collective-permute-done.21 = f32[4,768]{1,0:T(4,128)S(1)} collective-permute-done((f32[4,768]{1,0:T(4,128)S(1)}, f32[4,768]{1,0:T(4,128)S(1)}, u32[]{:S(2)}, u32[]{:S(2)}) %collective-permute-start.21) | collective-permute-done | bytes 12320 | tf_op jit(solution)/shard_map/ppermute | solution.py:274
  57.4 1.5 %collective-permute-done.19 = f32[4,768]{1,0:T(4,128)S(1)} collective-permute-done((f32[4,768]{1,0:T(4,128)S(1)}, f32[4,768]{1,0:T(4,128)S(1)}, u32[]{:S(2)}, u32[]{:S(2)}) %collective-permute-start.19) | collective-permute-done | bytes 12320 | tf_op jit(solution)/shard_map/ppermute | solution.py:274
  58.9 2.7 %last_iteration.1 = (bf16[256,1024]{1,0:T(8,128)(2,1)}, f32[768]{0:T(1024)}) custom-call(bf16[256,1024]{1,0:T(8,128)(2,1)S(1)} %get-tuple-element.21.old_ref, f32[4,256,768]{2,1,0:T(8,128)S(1)} %get-tuple-element.22.expo_ref, f32[4,768]{1,0:T(4,128)S(1)} %get-tuple-element.23.peak_ref, f32[1,4,768]{2,1,0:T(4,128)S(1)} %add_bitcast_fusion.parts, ...), custom_call_target="tpu_custom_call" | custom-call | flops 1610612736 | bytes 524288 | tf_op jit(solution)/shard_map/last_iteration/pallas_call | solution.py:384
  (37 shorter events, 9.9 us)
Async XLA Ops:
  1.9 17.2 %collective-permute-start.7 = (bf16[576,1024]{1,0:T(8,128)(2,1)S(1)}, bf16[576,1024]{1,0:T(8,128)(2,1)S(1)}, u32[]{:S(2)}, u32[]{:S(2)}) collective-permute-start(bf16[576,1024]{1,0:T(8,128)(2,1)S(1)} %outgoing.1), channel_id=1, source_target_pairs={{0,8},{1,17},{2,10},{3,19},{4,12},{5,21},{6,14},{7,23},{8,0},{9,25... | collective-permute-start | bytes 3538952 | tf_op jit(solution)/shard_map/ppermute | solution.py:274
  9.5 1.2 %collective-permute-start = (f32[1,768]{1,0:T(1,128)S(1)}, f32[1,768]{1,0:T(1,128)S(1)}, u32[]{:S(2)}, u32[]{:S(2)}) collective-permute-start(f32[1,768]{1,0:T(1,128)S(1)} %partial_lse.1), channel_id=1, source_target_pairs={{0,1},{1,0},{2,3},{3,2},{4,5},{5,4},{6,7},{7,6},{8,9},{9,8},{10,11... | collective-permute-start | bytes 9224 | tf_op jit(solution)/shard_map/ppermute | solution.py:274
  10.7 5.5 %collective-permute-start.3 = (f32[1,768]{1,0:T(1,128)S(1)}, f32[1,768]{1,0:T(1,128)S(1)}, u32[]{:S(2)}, u32[]{:S(2)}) collective-permute-start(f32[1,768]{1,0:T(1,128)S(1)} %log_add_fusion.3), channel_id=1, source_target_pairs={{0,6},{1,7},{2,4},{3,5},{4,2},{5,3},{6,0},{7,1},{8,14},{9,15},{10,... | collective-permute-start | bytes 9224 | tf_op jit(solution)/shard_map/ppermute | solution.py:274
  14.4 4.5 %collective-permute-start.2 = (f32[1,768]{1,0:T(1,128)S(1)}, f32[1,768]{1,0:T(1,128)S(1)}, u32[]{:S(2)}, u32[]{:S(2)}) collective-permute-start(f32[1,768]{1,0:T(1,128)S(1)} %log_add_fusion.3), channel_id=1, source_target_pairs={{0,4},{1,5},{2,6},{3,7},{4,0},{5,1},{6,2},{7,3},{8,12},{9,13},{10,... | collective-permute-start | bytes 9224 | tf_op jit(solution)/shard_map/ppermute | solution.py:274
  14.4 4.5 %collective-permute-start.1 = (f32[1,768]{1,0:T(1,128)S(1)}, f32[1,768]{1,0:T(1,128)S(1)}, u32[]{:S(2)}, u32[]{:S(2)}) collective-permute-start(f32[1,768]{1,0:T(1,128)S(1)} %log_add_fusion.3), channel_id=1, source_target_pairs={{0,2},{1,3},{2,0},{3,1},{4,6},{5,7},{6,4},{7,5},{8,10},{9,11},{10,... | collective-permute-start | bytes 9224 | tf_op jit(solution)/shard_map/ppermute | solution.py:274
  19.2 14.4 %collective-permute-start.8 = (bf16[192,1024]{1,0:T(8,128)(2,1)S(1)}, bf16[192,1024]{1,0:T(8,128)(2,1)S(1)}, u32[]{:S(2)}, u32[]{:S(2)}) collective-permute-start(bf16[192,1024]{1,0:T(8,128)(2,1)S(1)} %get-tuple-element.28), channel_id=1, source_target_pairs={{0,2},{1,3},{2,0},{3,1},{4,6},{5,7},{6,4},{7,5},{8,10},{9,11},{10,... | collective-permute-start | bytes 1179656 | tf_op jit(solution)/shard_map/ppermute | solution.py:274
  21.4 14.7 %collective-permute-start.13 = (bf16[384,1024]{1,0:T(8,128)(2,1)S(1)}, bf16[384,1024]{1,0:T(8,128)(2,1)S(1)}, u32[]{:S(2)}, u32[]{:S(2)}) collective-permute-start(bf16[384,1024]{1,0:T(8,128)(2,1)S(1)} %slice.19), channel_id=1, source_target_pairs={{0,16},{1,9},{2,18},{3,11},{4,20},{5,13},{6,22},{7,15},{8,24},{9,1... | collective-permute-start | bytes 2359304 | tf_op jit(solution)/shard_map/ppermute | solution.py:274
  23.0 4.6 %collective-permute-start.4 = (f32[1,768]{1,0:T(1,128)S(1)}, f32[1,768]{1,0:T(1,128)S(1)}, u32[]{:S(2)}, u32[]{:S(2)}) collective-permute-start(f32[1,768]{1,0:T(1,128)S(1)} %log_add_fusion.2.row.refs_1_), channel_id=1, source_target_pairs={{0,24},{1,25},{2,26},{3,27},{4,28},{5,29},{6,30},{7,31},{8,16},{9,... | collective-permute-start | bytes 9224 | tf_op jit(solution)/shard_map/ppermute | solution.py:274
  24.4 9.3 %collective-permute-start.6 = (f32[1,768]{1,0:T(1,128)S(1)}, f32[1,768]{1,0:T(1,128)S(1)}, u32[]{:S(2)}, u32[]{:S(2)}) collective-permute-start(f32[1,768]{1,0:T(1,128)S(1)} %log_add_fusion.2.row.refs_1_), channel_id=1, source_target_pairs={{0,16},{1,9},{2,18},{3,11},{4,20},{5,13},{6,22},{7,15},{8,24},{9,1... | collective-permute-start | bytes 9224 | tf_op jit(solution)/shard_map/ppermute | solution.py:274
  26.0 8.2 %collective-permute-start.5 = (f32[1,768]{1,0:T(1,128)S(1)}, f32[1,768]{1,0:T(1,128)S(1)}, u32[]{:S(2)}, u32[]{:S(2)}) collective-permute-start(f32[1,768]{1,0:T(1,128)S(1)} %log_add_fusion.2.row.refs_1_), channel_id=1, source_target_pairs={{0,8},{1,17},{2,10},{3,19},{4,12},{5,21},{6,14},{7,23},{8,0},{9,25... | collective-permute-start | bytes 9224 | tf_op jit(solution)/shard_map/ppermute | solution.py:274
  29.0 6.0 %collective-permute-start.10 = (bf16[192,1024]{1,0:T(8,128)(2,1)S(1)}, bf16[192,1024]{1,0:T(8,128)(2,1)S(1)}, u32[]{:S(2)}, u32[]{:S(2)}) collective-permute-start(bf16[192,1024]{1,0:T(8,128)(2,1)S(1)} %get-tuple-element.26), channel_id=1, source_target_pairs={{0,1},{1,0},{2,3},{3,2},{4,5},{5,4},{6,7},{7,6},{8,9},{9,8},{10,11... | collective-permute-start | bytes 1179656 | tf_op jit(solution)/shard_map/ppermute | solution.py:274
  33.6 1.9 %collective-permute-start.9 = (bf16[192,1024]{1,0:T(8,128)(2,1)S(1)}, bf16[192,1024]{1,0:T(8,128)(2,1)S(1)}, u32[]{:S(2)}, u32[]{:S(2)}) collective-permute-start(bf16[192,1024]{1,0:T(8,128)(2,1)S(1)} %get-tuple-element.27), channel_id=1, source_target_pairs={{0,1},{1,0},{2,3},{3,2},{4,5},{5,4},{6,7},{7,6},{8,9},{9,8},{10,11... | collective-permute-start | bytes 1179656 | tf_op jit(solution)/shard_map/ppermute | solution.py:274
  33.7 2.4 %collective-permute-start.11 = (bf16[192,1024]{1,0:T(8,128)(2,1)S(1)}, bf16[192,1024]{1,0:T(8,128)(2,1)S(1)}, u32[]{:S(2)}, u32[]{:S(2)}) collective-permute-start(bf16[192,1024]{1,0:T(8,128)(2,1)S(1)} %get-tuple-element.28), channel_id=1, source_target_pairs={{0,1},{1,0},{2,3},{3,2},{4,5},{5,4},{6,7},{7,6},{8,9},{9,8},{10,11... | collective-permute-start | bytes 1179656 | tf_op jit(solution)/shard_map/ppermute | solution.py:274
  34.1 2.5 %collective-permute-start.12 = (bf16[192,1024]{1,0:T(8,128)(2,1)S(1)}, bf16[192,1024]{1,0:T(8,128)(2,1)S(1)}, u32[]{:S(2)}, u32[]{:S(2)}) collective-permute-start(bf16[192,1024]{1,0:T(8,128)(2,1)S(1)} %after.4.refs_6_), channel_id=1, source_target_pairs={{0,1},{1,0},{2,3},{3,2},{4,5},{5,4},{6,7},{7,6},{8,9},{9,8},{10,11... | collective-permute-start | bytes 1179656 | tf_op jit(solution)/shard_map/ppermute | solution.py:274
  36.6 3.2 %collective-permute-start.14 = (bf16[384,1024]{1,0:T(8,128)(2,1)S(1)}, bf16[384,1024]{1,0:T(8,128)(2,1)S(1)}, u32[]{:S(2)}, u32[]{:S(2)}) collective-permute-start(bf16[384,1024]{1,0:T(8,128)(2,1)S(1)} %after.5.refs_3_), channel_id=1, source_target_pairs={{0,1},{1,0},{2,3},{3,2},{4,5},{5,4},{6,7},{7,6},{8,9},{9,8},{10,11... | collective-permute-start | bytes 2359304 | tf_op jit(solution)/shard_map/ppermute | solution.py:274
  43.7 1.2 %collective-permute-start.15 = (f32[4,768]{1,0:T(4,128)S(1)}, f32[4,768]{1,0:T(4,128)S(1)}, u32[]{:S(2)}, u32[]{:S(2)}) collective-permute-start(f32[4,768]{1,0:T(4,128)S(1)} %get-tuple-element.24), channel_id=1, source_target_pairs={{0,1},{1,0},{2,3},{3,2},{4,5},{5,4},{6,7},{7,6},{8,9},{9,8},{10,11... | collective-permute-start | bytes 36872 | tf_op jit(solution)/shard_map/ppermute | solution.py:274
  45.0 5.6 %collective-permute-start.18 = (f32[4,768]{1,0:T(4,128)S(1)}, f32[4,768]{1,0:T(4,128)S(1)}, u32[]{:S(2)}, u32[]{:S(2)}) collective-permute-start(f32[4,768]{1,0:T(4,128)S(1)} %log_add_fusion.1), channel_id=1, source_target_pairs={{0,6},{1,7},{2,4},{3,5},{4,2},{5,3},{6,0},{7,1},{8,14},{9,15},{10,... | collective-permute-start | bytes 36872 | tf_op jit(solution)/shard_map/ppermute | solution.py:274
  47.5 4.6 %collective-permute-start.17 = (f32[4,768]{1,0:T(4,128)S(1)}, f32[4,768]{1,0:T(4,128)S(1)}, u32[]{:S(2)}, u32[]{:S(2)}) collective-permute-start(f32[4,768]{1,0:T(4,128)S(1)} %log_add_fusion.1), channel_id=1, source_target_pairs={{0,4},{1,5},{2,6},{3,7},{4,0},{5,1},{6,2},{7,3},{8,12},{9,13},{10,... | collective-permute-start | bytes 36872 | tf_op jit(solution)/shard_map/ppermute | solution.py:274
  47.7 4.4 %collective-permute-start.16 = (f32[4,768]{1,0:T(4,128)S(1)}, f32[4,768]{1,0:T(4,128)S(1)}, u32[]{:S(2)}, u32[]{:S(2)}) collective-permute-start(f32[4,768]{1,0:T(4,128)S(1)} %log_add_fusion.1), channel_id=1, source_target_pairs={{0,2},{1,3},{2,0},{3,1},{4,6},{5,7},{6,4},{7,5},{8,10},{9,11},{10,... | collective-permute-start | bytes 36872 | tf_op jit(solution)/shard_map/ppermute | solution.py:274
  52.2 4.7 %collective-permute-start.21 = (f32[4,768]{1,0:T(4,128)S(1)}, f32[4,768]{1,0:T(4,128)S(1)}, u32[]{:S(2)}, u32[]{:S(2)}) collective-permute-start(f32[4,768]{1,0:T(4,128)S(1)} %log_add_fusion), channel_id=1, source_target_pairs={{0,24},{1,25},{2,26},{3,27},{4,28},{5,29},{6,30},{7,31},{8,16},{9,... | collective-permute-start | bytes 36872 | tf_op jit(solution)/shard_map/ppermute | solution.py:274
  53.7 3.7 %collective-permute-start.20 = (f32[4,768]{1,0:T(4,128)S(1)}, f32[4,768]{1,0:T(4,128)S(1)}, u32[]{:S(2)}, u32[]{:S(2)}) collective-permute-start(f32[4,768]{1,0:T(4,128)S(1)} %log_add_fusion), channel_id=1, source_target_pairs={{0,16},{1,17},{2,18},{3,19},{4,20},{5,21},{6,22},{7,23},{8,24},{9,... | collective-permute-start | bytes 36872 | tf_op jit(solution)/shard_map/ppermute | solution.py:274
  55.2 3.7 %collective-permute-start.19 = (f32[4,768]{1,0:T(4,128)S(1)}, f32[4,768]{1,0:T(4,128)S(1)}, u32[]{:S(2)}, u32[]{:S(2)}) collective-permute-start(f32[4,768]{1,0:T(4,128)S(1)} %log_add_fusion), channel_id=1, source_target_pairs={{0,8},{1,9},{2,10},{3,11},{4,12},{5,13},{6,14},{7,15},{8,0},{9,1},... | collective-permute-start | bytes 36872 | tf_op jit(solution)/shard_map/ppermute | solution.py:274

commit v14 on v13

--- a/solution.py
+++ b/solution.py
@@ -306,14 +306,16 @@
         near = go(outgoing(vectors), (1, 2))
         home, centroids = load(vectors, centroids)
         lse = merge_cent(partial(home, centroids, scale), go)
-        parts = [lse, go(lse, (1, 2)), go(lse, (2, 1)), go(lse, 3)]
         near = after(near, lse)
         quarters = [near[i : i + nv // 4] for i in range(0, near.shape[0], nv // 4)]
         swapped = go(quarters[2], 0, 2)
         far = go(near[: nv // 2], (2, 1))
-        begun = begin(centroids, home, lse, parts[3], rows, scale)
+        crossed = [go(piece, 0, 1) for piece in quarters]
+        lse = after(lse, *crossed)
+        parts = [lse, go(lse, (1, 2)), go(lse, (2, 1)), go(lse, 3)]
+        begun = begin(centroids, home, lse, crossed[2], rows, scale)
         swapped = after(swapped, begun[1])
-        near = [near, swapped] + [go(piece, 0, 1) for piece in quarters + [swapped]]
+        near = [near, swapped] + crossed + [go(swapped, 0, 1)]
         pieces = [home]
         plan = dict(exchange=True, first=1, early=3, blocks=[(0, 0), (1, 0), (1, nv), (2, 0)])
     else:

time: 61.8 us -> 63.5 us (1.028)
  waiting for transfers between devices: 15.4 us -> 21.8 us
  starting transfers between devices: 28.6 us -> 24 us
    ppermute x22, waiting for transfers between devices: 15.4 us -> 21.8 us  [send(): return lax.ppermute(value, BOTH, pairs)]
    ppermute x22, starting transfers between devices: 28.6 us -> 24 us  [send(): return lax.ppermute(value, BOTH, pairs)]
  transfers between devices with their start and end apart: 22 -> 22, of which waited for: 15 -> 14; matrix products, arithmetic and copies ran while one was open for 0% -> 0% of each run, Pallas kernels for 14% -> 14%
where the time goes in v14:
time: 63.5 us; the launch traced here: 63.4 us
  starting transfers between devices  24 us (38%)
  waiting for transfers between devices  21.8 us (34%)
  Pallas kernels  16.6 us (26%)
  between operations  0.74 us (1%)
    ppermute x22, starting transfers between devices, send(): return lax.ppermute(value, BOTH, pairs)  24 us
    ppermute x22, waiting for transfers between devices, send(): return lax.ppermute(value, BOTH, pairs)  21.8 us
    pallas_call x1, Pallas kernels, shards(): pl.pallas_call(functools.partial(late_kernel, dict(plan), scale), in_spec...  3.84 us
    pallas_call x1, Pallas kernels, shards(): pl.pallas_call(functools.partial(early_kernel, dict(plan), scale), in_spe...  2.81 us
    pallas_call x1, Pallas kernels, shards(): pl.pallas_call(functools.partial(last_kernel, dict(plan)), in_specs=[vmem...  2.71 us
    pallas_call x1, Pallas kernels, partial(): pl.pallas_call(functools.partial(partial_kernel, scale, min(256, k)), in_...  2.46 us
    pallas_call x1, Pallas kernels, load(): pl.pallas_call(load_kernel, in_specs=[hbm, hbm], out_specs=[vmem] * 2, ou...  2.09 us
    pallas_call x1, Pallas kernels, begin(): pl.pallas_call(functools.partial(home_kernel, scale), in_specs=[vmem] * 3...  1.36 us
  transfers between devices with their start and end apart: 22, of which 14 were waited for; matrix products, arithmetic and copies ran while one was open for 0% of the time, Pallas kernels for 14%

profile of v14, /device:TPU:0, one launch (start us, length us, event | category | flops | bytes accessed | tf_op | source)
XLA Modules:
  0.0 63.4 jit_solution(4227520596492610572)
XLA Ops:
  0.6 1.3 %outgoing.1 = bf16[576,1024]{1,0:T(8,128)(2,1)S(1)} custom-call(bf16[768,1024]{1,0:T(8,128)(2,1)} %v_hbm.3), custom_call_target="tpu_custom_call" | custom-call | bytes 1572864 | tf_op jit(solution)/shard_map/outgoing/pallas_call | solution.py:79
  1.9 3.0 %collective-permute-start.4 = (bf16[576,1024]{1,0:T(8,128)(2,1)S(1)}, bf16[576,1024]{1,0:T(8,128)(2,1)S(1)}, u32[]{:S(2)}, u32[]{:S(2)}) collective-permute-start(bf16[576,1024]{1,0:T(8,128)(2,1)S(1)} %outgoing.1), channel_id=1, source_target_pairs={{0,8},{1,17},{2,10},{3,19},{4,12},{5,21},{6,14},{7,23},{8,0},{9,25... | collective-permute-start | bytes 3538952 | tf_op jit(solution)/shard_map/ppermute | solution.py:274
  4.9 2.1 %load.1 = (bf16[768,1024]{1,0:T(8,128)(2,1)S(1)}, bf16[1024,1024]{1,0:T(8,128)(2,1)S(1)}) custom-call(bf16[768,1024]{1,0:T(8,128)(2,1)} %v_hbm.3, bf16[1024,1024]{1,0:T(8,128)(2,1)} %c_hbm.1), custom_call_target="tpu_custom_call" | custom-call | bytes 7340032 | tf_op jit(solution)/shard_map/load/pallas_call | solution.py:102
  7.0 2.5 %partial_lse.1 = f32[1,768]{1,0:T(1,128)S(1)} custom-call(bf16[768,1024]{1,0:T(8,128)(2,1)S(1)} %get-tuple-element.15.v_ref.home.refs_4_.refs_1_.refs_0_, bf16[1024,1024]{1,0:T(8,128)(2,1)S(1)} %get-tuple-element.14.c_ref), custom_call_target="tpu_custom_call" | custom-call | flops 1610612736 | bytes 3670016 | tf_op jit(solution)/shard_map/partial_lse/pallas_call | solution.py:129
  9.6 1.1 %collective-permute-done = f32[1,768]{1,0:T(1,128)S(1)} collective-permute-done((f32[1,768]{1,0:T(1,128)S(1)}, f32[1,768]{1,0:T(1,128)S(1)}, u32[]{:S(2)}, u32[]{:S(2)}) %collective-permute-start) | collective-permute-done | bytes 3104 | tf_op jit(solution)/shard_map/ppermute | solution.py:274
  10.7 3.7 %collective-permute-start.3 = (f32[1,768]{1,0:T(1,128)S(1)}, f32[1,768]{1,0:T(1,128)S(1)}, u32[]{:S(2)}, u32[]{:S(2)}) collective-permute-start(f32[1,768]{1,0:T(1,128)S(1)} %log_add_fusion.3), channel_id=1, source_target_pairs={{0,6},{1,7},{2,4},{3,5},{4,2},{5,3},{6,0},{7,1},{8,14},{9,15},{10,... | collective-permute-start | bytes 9224 | tf_op jit(solution)/shard_map/ppermute | solution.py:274
  15.2 1.0 %collective-permute-done.3 = f32[1,768]{1,0:T(1,128)S(1)} collective-permute-done((f32[1,768]{1,0:T(1,128)S(1)}, f32[1,768]{1,0:T(1,128)S(1)}, u32[]{:S(2)}, u32[]{:S(2)}) %collective-permute-start.3) | collective-permute-done | bytes 3104 | tf_op jit(solution)/shard_map/ppermute | solution.py:274
  16.2 2.7 %collective-permute-done.2 = f32[1,768]{1,0:T(1,128)S(1)} collective-permute-done((f32[1,768]{1,0:T(1,128)S(1)}, f32[1,768]{1,0:T(1,128)S(1)}, u32[]{:S(2)}, u32[]{:S(2)}) %collective-permute-start.2) | collective-permute-done | bytes 3104 | tf_op jit(solution)/shard_map/ppermute | solution.py:274
  19.8 2.1 %collective-permute-start.10 = (bf16[192,1024]{1,0:T(8,128)(2,1)S(1)}, bf16[192,1024]{1,0:T(8,128)(2,1)S(1)}, u32[]{:S(2)}, u32[]{:S(2)}) collective-permute-start(bf16[192,1024]{1,0:T(8,128)(2,1)S(1)} %get-tuple-element.26), channel_id=1, source_target_pairs={{0,2},{1,3},{2,0},{3,1},{4,6},{5,7},{6,4},{7,5},{8,10},{9,11},{10,... | collective-permute-start | bytes 1179656 | tf_op jit(solution)/shard_map/ppermute | solution.py:274
  22.0 1.6 %collective-permute-start.13 = (bf16[384,1024]{1,0:T(8,128)(2,1)S(1)}, bf16[384,1024]{1,0:T(8,128)(2,1)S(1)}, u32[]{:S(2)}, u32[]{:S(2)}) collective-permute-start(bf16[384,1024]{1,0:T(8,128)(2,1)S(1)} %slice.19), channel_id=1, source_target_pairs={{0,16},{1,9},{2,18},{3,11},{4,20},{5,13},{6,22},{7,15},{8,24},{9,1... | collective-permute-start | bytes 2359304 | tf_op jit(solution)/shard_map/ppermute | solution.py:274
  23.6 1.4 %home_block.1 = (f32[256,1024]{1,0:T(8,128)S(1)}, f32[256,1]{1,0:T(8,128)S(1)}) custom-call(bf16[1024,1024]{1,0:T(8,128)(2,1)S(1)} %get-tuple-element.14.c_ref, bf16[768,1024]{1,0:T(8,128)(2,1)S(1)} %get-tuple-element.15.v_ref.home.refs_4_.refs_1_.refs_0_, f32[1,768]{1,0:T(1,128)S(1)} %after.5.row, ...), custom_call_target="tpu_custom_call" | custom-call | flops 805306368 | bytes 1572864 | tf_op jit(solution)/shard_map/home_block/pallas_call | solution.py:175
  25.0 6.7 %collective-permute-done.10.refs_0_ = bf16[192,1024]{1,0:T(8,128)(2,1)S(1)} collective-permute-done((bf16[192,1024]{1,0:T(8,128)(2,1)S(1)}, bf16[192,1024]{1,0:T(8,128)(2,1)S(1)}, u32[]{:S(2)}, u32[]{:S(2)}) %collective-permute-start.10) | collective-permute-done | bytes 393248 | tf_op jit(solution)/shard_map/ppermute | solution.py:274
  31.7 2.6 %collective-permute-start.12 = (f32[1,768]{1,0:T(1,128)S(1)}, f32[1,768]{1,0:T(1,128)S(1)}, u32[]{:S(2)}, u32[]{:S(2)}) collective-permute-start(f32[1,768]{1,0:T(1,128)S(1)} %after.5.row), channel_id=1, source_target_pairs={{0,24},{1,25},{2,26},{3,27},{4,28},{5,29},{6,30},{7,31},{8,16},{9,... | collective-permute-start | bytes 9224 | tf_op jit(solution)/shard_map/ppermute | solution.py:274
  35.1 1.0 %collective-permute-done.12.refs_3_.refs_0_ = f32[1,768]{1,0:T(1,128)S(1)} collective-permute-done((f32[1,768]{1,0:T(1,128)S(1)}, f32[1,768]{1,0:T(1,128)S(1)}, u32[]{:S(2)}, u32[]{:S(2)}) %collective-permute-start.12) | collective-permute-done | bytes 3104 | tf_op jit(solution)/shard_map/ppermute | solution.py:274
  36.2 1.7 %collective-permute-done.9.refs_3_.refs_2_ = f32[1,768]{1,0:T(1,128)S(1)} collective-permute-done((f32[1,768]{1,0:T(1,128)S(1)}, f32[1,768]{1,0:T(1,128)S(1)}, u32[]{:S(2)}, u32[]{:S(2)}) %collective-permute-start.9) | collective-permute-done | bytes 3104 | tf_op jit(solution)/shard_map/ppermute | solution.py:274
  38.5 2.8 %early_blocks.1 = (f32[256,1024]{1,0:T(8,128)S(1)}, f32[256,1]{1,0:T(8,128)S(1)}, bf16[1536,1024]{1,0:T(8,128)(2,1)S(1)}) custom-call(bf16[1024,1024]{1,0:T(8,128)(2,1)S(1)} %get-tuple-element.14.c_ref, f32[256,1024]{1,0:T(8,128)S(1)} %get-tuple-element.16.refs_0_, f32[256,1]{1,0:T(8,128)S(1)} %get-tuple-element.17.refs_1_, ...), custom_call_target="tpu_custom_call" | custom-call | tf_op jit(solution)/shard_map/early_blocks/pallas_call | solution.py:339
  41.3 3.8 %late_blocks.1 = (bf16[256,1024]{1,0:T(8,128)(2,1)S(1)}, f32[4,256,768]{2,1,0:T(8,128)S(1)}, f32[4,768]{1,0:T(4,128)S(1)}, f32[4,768]{1,0:T(4,128)S(1)}, bf16[768,1024]{1,0:T(8,128)(2,1)S(1)}) custom-call(bf16[1024,1024]{1,0:T(8,128)(2,1)S(1)} %get-tuple-element.14.c_ref, f32[256,1024]{1,0:T(8,128)S(1)} %get-tuple-element.18.total, ...), custom_call_target="tpu_custom_call" | custom-call | flops 2415919104 | bytes 1572864 | tf_op jit(solution)/shard_map/late_blocks/pallas_call | solution.py:359
  46.6 3.7 %collective-permute-start.18 = (f32[4,768]{1,0:T(4,128)S(1)}, f32[4,768]{1,0:T(4,128)S(1)}, u32[]{:S(2)}, u32[]{:S(2)}) collective-permute-start(f32[4,768]{1,0:T(4,128)S(1)} %log_add_fusion.1), channel_id=1, source_target_pairs={{0,6},{1,7},{2,4},{3,5},{4,2},{5,3},{6,0},{7,1},{8,14},{9,15},{10,... | collective-permute-start | bytes 36872 | tf_op jit(solution)/shard_map/ppermute | solution.py:274
  51.0 1.1 %collective-permute-done.18 = f32[4,768]{1,0:T(4,128)S(1)} collective-permute-done((f32[4,768]{1,0:T(4,128)S(1)}, f32[4,768]{1,0:T(4,128)S(1)}, u32[]{:S(2)}, u32[]{:S(2)}) %collective-permute-start.18) | collective-permute-done | bytes 12320 | tf_op jit(solution)/shard_map/ppermute | solution.py:274
  52.1 2.7 %collective-permute-done.17 = f32[4,768]{1,0:T(4,128)S(1)} collective-permute-done((f32[4,768]{1,0:T(4,128)S(1)}, f32[4,768]{1,0:T(4,128)S(1)}, u32[]{:S(2)}, u32[]{:S(2)}) %collective-permute-start.17) | collective-permute-done | bytes 12320 | tf_op jit(solution)/shard_map/ppermute | solution.py:274
  54.9 1.6 %collective-permute-start.21 = (f32[4,768]{1,0:T(4,128)S(1)}, f32[4,768]{1,0:T(4,128)S(1)}, u32[]{:S(2)}, u32[]{:S(2)}) collective-permute-start(f32[4,768]{1,0:T(4,128)S(1)} %log_add_fusion), channel_id=1, source_target_pairs={{0,24},{1,25},{2,26},{3,27},{4,28},{5,29},{6,30},{7,31},{8,16},{9,... | collective-permute-start | bytes 36872 | tf_op jit(solution)/shard_map/ppermute | solution.py:274
  56.9 1.5 %collective-permute-start.19 = (f32[4,768]{1,0:T(4,128)S(1)}, f32[4,768]{1,0:T(4,128)S(1)}, u32[]{:S(2)}, u32[]{:S(2)}) collective-permute-start(f32[4,768]{1,0:T(4,128)S(1)} %log_add_fusion), channel_id=1, source_target_pairs={{0,8},{1,9},{2,10},{3,11},{4,12},{5,13},{6,14},{7,15},{8,0},{9,1},... | collective-permute-start | bytes 36872 | tf_op jit(solution)/shard_map/ppermute | solution.py:274
  58.4 1.1 %collective-permute-done.21 = f32[4,768]{1,0:T(4,128)S(1)} collective-permute-done((f32[4,768]{1,0:T(4,128)S(1)}, f32[4,768]{1,0:T(4,128)S(1)}, u32[]{:S(2)}, u32[]{:S(2)}) %collective-permute-start.21) | collective-permute-done | bytes 12320 | tf_op jit(solution)/shard_map/ppermute | solution.py:274
  60.7 2.7 %last_iteration.1 = (bf16[256,1024]{1,0:T(8,128)(2,1)}, f32[768]{0:T(1024)}) custom-call(bf16[256,1024]{1,0:T(8,128)(2,1)S(1)} %get-tuple-element.21.old_ref, f32[4,256,768]{2,1,0:T(8,128)S(1)} %get-tuple-element.22.expo_ref, f32[4,768]{1,0:T(4,128)S(1)} %get-tuple-element.23.peak_ref, f32[1,4,768]{2,1,0:T(4,128)S(1)} %add_bitcast_fusion.parts, ...), custom_call_target="tpu_custom_call" | custom-call | flops 1610612736 | bytes 524288 | tf_op jit(solution)/shard_map/last_iteration/pallas_call | solution.py:386
  (38 shorter events, 7.2 us)
Async XLA Ops:
  1.9 17.2 %collective-permute-start.4 = (bf16[576,1024]{1,0:T(8,128)(2,1)S(1)}, bf16[576,1024]{1,0:T(8,128)(2,1)S(1)}, u32[]{:S(2)}, u32[]{:S(2)}) collective-permute-start(bf16[576,1024]{1,0:T(8,128)(2,1)S(1)} %outgoing.1), channel_id=1, source_target_pairs={{0,8},{1,17},{2,10},{3,19},{4,12},{5,21},{6,14},{7,23},{8,0},{9,25... | collective-permute-start | bytes 3538952 | tf_op jit(solution)/shard_map/ppermute | solution.py:274
  9.5 1.2 %collective-permute-start = (f32[1,768]{1,0:T(1,128)S(1)}, f32[1,768]{1,0:T(1,128)S(1)}, u32[]{:S(2)}, u32[]{:S(2)}) collective-permute-start(f32[1,768]{1,0:T(1,128)S(1)} %partial_lse.1), channel_id=1, source_target_pairs={{0,1},{1,0},{2,3},{3,2},{4,5},{5,4},{6,7},{7,6},{8,9},{9,8},{10,11... | collective-permute-start | bytes 9224 | tf_op jit(solution)/shard_map/ppermute | solution.py:274
  10.7 5.5 %collective-permute-start.3 = (f32[1,768]{1,0:T(1,128)S(1)}, f32[1,768]{1,0:T(1,128)S(1)}, u32[]{:S(2)}, u32[]{:S(2)}) collective-permute-start(f32[1,768]{1,0:T(1,128)S(1)} %log_add_fusion.3), channel_id=1, source_target_pairs={{0,6},{1,7},{2,4},{3,5},{4,2},{5,3},{6,0},{7,1},{8,14},{9,15},{10,... | collective-permute-start | bytes 9224 | tf_op jit(solution)/shard_map/ppermute | solution.py:274
  14.4 4.5 %collective-permute-start.2 = (f32[1,768]{1,0:T(1,128)S(1)}, f32[1,768]{1,0:T(1,128)S(1)}, u32[]{:S(2)}, u32[]{:S(2)}) collective-permute-start(f32[1,768]{1,0:T(1,128)S(1)} %log_add_fusion.3), channel_id=1, source_target_pairs={{0,4},{1,5},{2,6},{3,7},{4,0},{5,1},{6,2},{7,3},{8,12},{9,13},{10,... | collective-permute-start | bytes 9224 | tf_op jit(solution)/shard_map/ppermute | solution.py:274
  14.4 4.5 %collective-permute-start.1 = (f32[1,768]{1,0:T(1,128)S(1)}, f32[1,768]{1,0:T(1,128)S(1)}, u32[]{:S(2)}, u32[]{:S(2)}) collective-permute-start(f32[1,768]{1,0:T(1,128)S(1)} %log_add_fusion.3), channel_id=1, source_target_pairs={{0,2},{1,3},{2,0},{3,1},{4,6},{5,7},{6,4},{7,5},{8,10},{9,11},{10,... | collective-permute-start | bytes 9224 | tf_op jit(solution)/shard_map/ppermute | solution.py:274
  19.2 4.4 %collective-permute-start.6 = (bf16[192,1024]{1,0:T(8,128)(2,1)S(1)}, bf16[192,1024]{1,0:T(8,128)(2,1)S(1)}, u32[]{:S(2)}, u32[]{:S(2)}) collective-permute-start(bf16[192,1024]{1,0:T(8,128)(2,1)S(1)} %get-tuple-element.27), channel_id=1, source_target_pairs={{0,1},{1,0},{2,3},{3,2},{4,5},{5,4},{6,7},{7,6},{8,9},{9,8},{10,11... | collective-permute-start | bytes 1179656 | tf_op jit(solution)/shard_map/ppermute | solution.py:274
  19.3 4.3 %collective-permute-start.5 = (bf16[192,1024]{1,0:T(8,128)(2,1)S(1)}, bf16[192,1024]{1,0:T(8,128)(2,1)S(1)}, u32[]{:S(2)}, u32[]{:S(2)}) collective-permute-start(bf16[192,1024]{1,0:T(8,128)(2,1)S(1)} %get-tuple-element.28), channel_id=1, source_target_pairs={{0,1},{1,0},{2,3},{3,2},{4,5},{5,4},{6,7},{7,6},{8,9},{9,8},{10,11... | collective-permute-start | bytes 1179656 | tf_op jit(solution)/shard_map/ppermute | solution.py:274
  19.8 3.8 %collective-permute-start.7 = (bf16[192,1024]{1,0:T(8,128)(2,1)S(1)}, bf16[192,1024]{1,0:T(8,128)(2,1)S(1)}, u32[]{:S(2)}, u32[]{:S(2)}) collective-permute-start(bf16[192,1024]{1,0:T(8,128)(2,1)S(1)} %get-tuple-element.26), channel_id=1, source_target_pairs={{0,1},{1,0},{2,3},{3,2},{4,5},{5,4},{6,7},{7,6},{8,9},{9,8},{10,11... | collective-permute-start | bytes 1179656 | tf_op jit(solution)/shard_map/ppermute | solution.py:274
  19.8 11.8 %collective-permute-start.10 = (bf16[192,1024]{1,0:T(8,128)(2,1)S(1)}, bf16[192,1024]{1,0:T(8,128)(2,1)S(1)}, u32[]{:S(2)}, u32[]{:S(2)}) collective-permute-start(bf16[192,1024]{1,0:T(8,128)(2,1)S(1)} %get-tuple-element.26), channel_id=1, source_target_pairs={{0,2},{1,3},{2,0},{3,1},{4,6},{5,7},{6,4},{7,5},{8,10},{9,11},{10,... | collective-permute-start | bytes 1179656 | tf_op jit(solution)/shard_map/ppermute | solution.py:274
  22.0 16.4 %collective-permute-start.13 = (bf16[384,1024]{1,0:T(8,128)(2,1)S(1)}, bf16[384,1024]{1,0:T(8,128)(2,1)S(1)}, u32[]{:S(2)}, u32[]{:S(2)}) collective-permute-start(bf16[384,1024]{1,0:T(8,128)(2,1)S(1)} %slice.19), channel_id=1, source_target_pairs={{0,16},{1,9},{2,18},{3,11},{4,20},{5,13},{6,22},{7,15},{8,24},{9,1... | collective-permute-start | bytes 2359304 | tf_op jit(solution)/shard_map/ppermute | solution.py:274
  31.7 6.7 %collective-permute-start.11 = (bf16[192,1024]{1,0:T(8,128)(2,1)S(1)}, bf16[192,1024]{1,0:T(8,128)(2,1)S(1)}, u32[]{:S(2)}, u32[]{:S(2)}) collective-permute-start(bf16[192,1024]{1,0:T(8,128)(2,1)S(1)} %after.6.refs_6_), channel_id=1, source_target_pairs={{0,1},{1,0},{2,3},{3,2},{4,5},{5,4},{6,7},{7,6},{8,9},{9,8},{10,11... | collective-permute-start | bytes 1179656 | tf_op jit(solution)/shard_map/ppermute | solution.py:274
  31.7 4.5 %collective-permute-start.12 = (f32[1,768]{1,0:T(1,128)S(1)}, f32[1,768]{1,0:T(1,128)S(1)}, u32[]{:S(2)}, u32[]{:S(2)}) collective-permute-start(f32[1,768]{1,0:T(1,128)S(1)} %after.5.row), channel_id=1, source_target_pairs={{0,24},{1,25},{2,26},{3,27},{4,28},{5,29},{6,30},{7,31},{8,16},{9,... | collective-permute-start | bytes 9224 | tf_op jit(solution)/shard_map/ppermute | solution.py:274
  34.3 3.6 %collective-permute-start.9 = (f32[1,768]{1,0:T(1,128)S(1)}, f32[1,768]{1,0:T(1,128)S(1)}, u32[]{:S(2)}, u32[]{:S(2)}) collective-permute-start(f32[1,768]{1,0:T(1,128)S(1)} %after.5.row), channel_id=1, source_target_pairs={{0,16},{1,9},{2,18},{3,11},{4,20},{5,13},{6,22},{7,15},{8,24},{9,1... | collective-permute-start | bytes 9224 | tf_op jit(solution)/shard_map/ppermute | solution.py:274
  34.8 3.6 %collective-permute-start.8 = (f32[1,768]{1,0:T(1,128)S(1)}, f32[1,768]{1,0:T(1,128)S(1)}, u32[]{:S(2)}, u32[]{:S(2)}) collective-permute-start(f32[1,768]{1,0:T(1,128)S(1)} %after.5.row), channel_id=1, source_target_pairs={{0,8},{1,17},{2,10},{3,19},{4,12},{5,21},{6,14},{7,23},{8,0},{9,25... | collective-permute-start | bytes 9224 | tf_op jit(solution)/shard_map/ppermute | solution.py:274
  38.4 2.9 %collective-permute-start.14 = (bf16[384,1024]{1,0:T(8,128)(2,1)S(1)}, bf16[384,1024]{1,0:T(8,128)(2,1)S(1)}, u32[]{:S(2)}, u32[]{:S(2)}) collective-permute-start(bf16[384,1024]{1,0:T(8,128)(2,1)S(1)} %after.7.refs_3_), channel_id=1, source_target_pairs={{0,1},{1,0},{2,3},{3,2},{4,5},{5,4},{6,7},{7,6},{8,9},{9,8},{10,11... | collective-permute-start | bytes 2359304 | tf_op jit(solution)/shard_map/ppermute | solution.py:274
  45.1 1.4 %collective-permute-start.15 = (f32[4,768]{1,0:T(4,128)S(1)}, f32[4,768]{1,0:T(4,128)S(1)}, u32[]{:S(2)}, u32[]{:S(2)}) collective-permute-start(f32[4,768]{1,0:T(4,128)S(1)} %get-tuple-element.24), channel_id=1, source_target_pairs={{0,1},{1,0},{2,3},{3,2},{4,5},{5,4},{6,7},{7,6},{8,9},{9,8},{10,11... | collective-permute-start | bytes 36872 | tf_op jit(solution)/shard_map/ppermute | solution.py:274
  46.6 5.6 %collective-permute-start.18 = (f32[4,768]{1,0:T(4,128)S(1)}, f32[4,768]{1,0:T(4,128)S(1)}, u32[]{:S(2)}, u32[]{:S(2)}) collective-permute-start(f32[4,768]{1,0:T(4,128)S(1)} %log_add_fusion.1), channel_id=1, source_target_pairs={{0,6},{1,7},{2,4},{3,5},{4,2},{5,3},{6,0},{7,1},{8,14},{9,15},{10,... | collective-permute-start | bytes 36872 | tf_op jit(solution)/shard_map/ppermute | solution.py:274
  50.2 4.6 %collective-permute-start.17 = (f32[4,768]{1,0:T(4,128)S(1)}, f32[4,768]{1,0:T(4,128)S(1)}, u32[]{:S(2)}, u32[]{:S(2)}) collective-permute-start(f32[4,768]{1,0:T(4,128)S(1)} %log_add_fusion.1), channel_id=1, source_target_pairs={{0,4},{1,5},{2,6},{3,7},{4,0},{5,1},{6,2},{7,3},{8,12},{9,13},{10,... | collective-permute-start | bytes 36872 | tf_op jit(solution)/shard_map/ppermute | solution.py:274
  50.2 4.6 %collective-permute-start.16 = (f32[4,768]{1,0:T(4,128)S(1)}, f32[4,768]{1,0:T(4,128)S(1)}, u32[]{:S(2)}, u32[]{:S(2)}) collective-permute-start(f32[4,768]{1,0:T(4,128)S(1)} %log_add_fusion.1), channel_id=1, source_target_pairs={{0,2},{1,3},{2,0},{3,1},{4,6},{5,7},{6,4},{7,5},{8,10},{9,11},{10,... | collective-permute-start | bytes 36872 | tf_op jit(solution)/shard_map/ppermute | solution.py:274
  54.9 4.7 %collective-permute-start.21 = (f32[4,768]{1,0:T(4,128)S(1)}, f32[4,768]{1,0:T(4,128)S(1)}, u32[]{:S(2)}, u32[]{:S(2)}) collective-permute-start(f32[4,768]{1,0:T(4,128)S(1)} %log_add_fusion), channel_id=1, source_target_pairs={{0,24},{1,25},{2,26},{3,27},{4,28},{5,29},{6,30},{7,31},{8,16},{9,... | collective-permute-start | bytes 36872 | tf_op jit(solution)/shard_map/ppermute | solution.py:274
  56.4 3.7 %collective-permute-start.20 = (f32[4,768]{1,0:T(4,128)S(1)}, f32[4,768]{1,0:T(4,128)S(1)}, u32[]{:S(2)}, u32[]{:S(2)}) collective-permute-start(f32[4,768]{1,0:T(4,128)S(1)} %log_add_fusion), channel_id=1, source_target_pairs={{0,16},{1,17},{2,18},{3,19},{4,20},{5,21},{6,22},{7,23},{8,24},{9,... | collective-permute-start | bytes 36872 | tf_op jit(solution)/shard_map/ppermute | solution.py:274
  56.9 3.7 %collective-permute-start.19 = (f32[4,768]{1,0:T(4,128)S(1)}, f32[4,768]{1,0:T(4,128)S(1)}, u32[]{:S(2)}, u32[]{:S(2)}) collective-permute-start(f32[4,768]{1,0:T(4,128)S(1)} %log_add_fusion), channel_id=1, source_target_pairs={{0,8},{1,9},{2,10},{3,11},{4,12},{5,13},{6,14},{7,15},{8,0},{9,1},... | collective-permute-start | bytes 36872 | tf_op jit(solution)/shard_map/ppermute | solution.py:274

commit v15 on v14

--- a/solution.py
+++ b/solution.py
@@ -314,7 +314,7 @@
         lse = after(lse, *crossed)
         parts = [lse, go(lse, (1, 2)), go(lse, (2, 1)), go(lse, 3)]
         begun = begin(centroids, home, lse, crossed[2], rows, scale)
-        swapped = after(swapped, begun[1])
+        swapped = after(swapped, begun[1], *parts[1:])
         near = [near, swapped] + crossed + [go(swapped, 0, 1)]
         pieces = [home]
         plan = dict(exchange=True, first=1, early=3, blocks=[(0, 0), (1, 0), (1, nv), (2, 0)])

time: 63.5 us -> 60.8 us (0.957)
  waiting for transfers between devices: 21.8 us -> 19 us
    ppermute x22, waiting for transfers between devices: 21.8 us -> 19 us  [send(): return lax.ppermute(value, BOTH, pairs)]
  transfers between devices with their start and end apart: 22 -> 22, of which waited for: 14 -> 13; matrix products, arithmetic and copies ran while one was open for 0% -> 0% of each run, Pallas kernels for 14% -> 14%
where the time goes in v15:
time: 60.8 us; the launch traced here: 60.7 us
  starting transfers between devices  24 us (39%)
  waiting for transfers between devices  19 us (31%)
  Pallas kernels  16.5 us (27%)
  between operations  0.74 us (1%)
    ppermute x22, starting transfers between devices, send(): return lax.ppermute(value, BOTH, pairs)  24 us
    ppermute x22, waiting for transfers between devices, send(): return lax.ppermute(value, BOTH, pairs)  19 us
    pallas_call x1, Pallas kernels, shards(): pl.pallas_call(functools.partial(late_kernel, dict(plan), scale), in_spec...  3.83 us
    pallas_call x1, Pallas kernels, shards(): pl.pallas_call(functools.partial(early_kernel, dict(plan), scale), in_spe...  2.81 us
    pallas_call x1, Pallas kernels, shards(): pl.pallas_call(functools.partial(last_kernel, dict(plan)), in_specs=[vmem...  2.71 us
    pallas_call x1, Pallas kernels, partial(): pl.pallas_call(functools.partial(partial_kernel, scale, min(256, k)), in_...  2.46 us
    pallas_call x1, Pallas kernels, load(): pl.pallas_call(load_kernel, in_specs=[hbm, hbm], out_specs=[vmem] * 2, ou...  2.09 us
    pallas_call x1, Pallas kernels, begin(): pl.pallas_call(functools.partial(home_kernel, scale), in_specs=[vmem] * 3...  1.36 us
  transfers between devices with their start and end apart: 22, of which 13 were waited for; matrix products, arithmetic and copies ran while one was open for 0% of the time, Pallas kernels for 14%

profile of v15, /device:TPU:0, one launch (start us, length us, event | category | flops | bytes accessed | tf_op | source)
XLA Modules:
  0.0 60.7 jit_solution(8481377032547466727)
XLA Ops:
  0.6 1.3 %outgoing.1 = bf16[576,1024]{1,0:T(8,128)(2,1)S(1)} custom-call(bf16[768,1024]{1,0:T(8,128)(2,1)} %v_hbm.3), custom_call_target="tpu_custom_call" | custom-call | bytes 1572864 | tf_op jit(solution)/shard_map/outgoing/pallas_call | solution.py:79
  1.9 3.0 %collective-permute-start.4 = (bf16[576,1024]{1,0:T(8,128)(2,1)S(1)}, bf16[576,1024]{1,0:T(8,128)(2,1)S(1)}, u32[]{:S(2)}, u32[]{:S(2)}) collective-permute-start(bf16[576,1024]{1,0:T(8,128)(2,1)S(1)} %outgoing.1), channel_id=1, source_target_pairs={{0,8},{1,17},{2,10},{3,19},{4,12},{5,21},{6,14},{7,23},{8,0},{9,25... | collective-permute-start | bytes 3538952 | tf_op jit(solution)/shard_map/ppermute | solution.py:274
  4.9 2.1 %load.1 = (bf16[768,1024]{1,0:T(8,128)(2,1)S(1)}, bf16[1024,1024]{1,0:T(8,128)(2,1)S(1)}) custom-call(bf16[768,1024]{1,0:T(8,128)(2,1)} %v_hbm.3, bf16[1024,1024]{1,0:T(8,128)(2,1)} %c_hbm.1), custom_call_target="tpu_custom_call" | custom-call | bytes 7340032 | tf_op jit(solution)/shard_map/load/pallas_call | solution.py:102
  7.0 2.5 %partial_lse.1 = f32[1,768]{1,0:T(1,128)S(1)} custom-call(bf16[768,1024]{1,0:T(8,128)(2,1)S(1)} %get-tuple-element.15.v_ref.home.refs_4_.refs_1_.refs_0_, bf16[1024,1024]{1,0:T(8,128)(2,1)S(1)} %get-tuple-element.14.c_ref), custom_call_target="tpu_custom_call" | custom-call | flops 1610612736 | bytes 3670016 | tf_op jit(solution)/shard_map/partial_lse/pallas_call | solution.py:129
  9.6 1.1 %collective-permute-done = f32[1,768]{1,0:T(1,128)S(1)} collective-permute-done((f32[1,768]{1,0:T(1,128)S(1)}, f32[1,768]{1,0:T(1,128)S(1)}, u32[]{:S(2)}, u32[]{:S(2)}) %collective-permute-start) | collective-permute-done | bytes 3104 | tf_op jit(solution)/shard_map/ppermute | solution.py:274
  10.7 3.7 %collective-permute-start.3 = (f32[1,768]{1,0:T(1,128)S(1)}, f32[1,768]{1,0:T(1,128)S(1)}, u32[]{:S(2)}, u32[]{:S(2)}) collective-permute-start(f32[1,768]{1,0:T(1,128)S(1)} %log_add_fusion.3), channel_id=1, source_target_pairs={{0,6},{1,7},{2,4},{3,5},{4,2},{5,3},{6,0},{7,1},{8,14},{9,15},{10,... | collective-permute-start | bytes 9224 | tf_op jit(solution)/shard_map/ppermute | solution.py:274
  16.2 2.7 %collective-permute-done.2 = f32[1,768]{1,0:T(1,128)S(1)} collective-permute-done((f32[1,768]{1,0:T(1,128)S(1)}, f32[1,768]{1,0:T(1,128)S(1)}, u32[]{:S(2)}, u32[]{:S(2)}) %collective-permute-start.2) | collective-permute-done | bytes 3104 | tf_op jit(solution)/shard_map/ppermute | solution.py:274
  19.8 2.1 %collective-permute-start.10 = (bf16[192,1024]{1,0:T(8,128)(2,1)S(1)}, bf16[192,1024]{1,0:T(8,128)(2,1)S(1)}, u32[]{:S(2)}, u32[]{:S(2)}) collective-permute-start(bf16[192,1024]{1,0:T(8,128)(2,1)S(1)} %get-tuple-element.26), channel_id=1, source_target_pairs={{0,2},{1,3},{2,0},{3,1},{4,6},{5,7},{6,4},{7,5},{8,10},{9,11},{10,... | collective-permute-start | bytes 1179656 | tf_op jit(solution)/shard_map/ppermute | solution.py:274
  22.0 1.6 %collective-permute-start.13 = (bf16[384,1024]{1,0:T(8,128)(2,1)S(1)}, bf16[384,1024]{1,0:T(8,128)(2,1)S(1)}, u32[]{:S(2)}, u32[]{:S(2)}) collective-permute-start(bf16[384,1024]{1,0:T(8,128)(2,1)S(1)} %slice.19), channel_id=1, source_target_pairs={{0,16},{1,9},{2,18},{3,11},{4,20},{5,13},{6,22},{7,15},{8,24},{9,1... | collective-permute-start | bytes 2359304 | tf_op jit(solution)/shard_map/ppermute | solution.py:274
  23.6 1.5 %collective-permute-start.11 = (f32[1,768]{1,0:T(1,128)S(1)}, f32[1,768]{1,0:T(1,128)S(1)}, u32[]{:S(2)}, u32[]{:S(2)}) collective-permute-start(f32[1,768]{1,0:T(1,128)S(1)} %after.5.row), channel_id=1, source_target_pairs={{0,24},{1,25},{2,26},{3,27},{4,28},{5,29},{6,30},{7,31},{8,16},{9,... | collective-permute-start | bytes 9224 | tf_op jit(solution)/shard_map/ppermute | solution.py:274
  25.1 1.5 %collective-permute-start.9 = (f32[1,768]{1,0:T(1,128)S(1)}, f32[1,768]{1,0:T(1,128)S(1)}, u32[]{:S(2)}, u32[]{:S(2)}) collective-permute-start(f32[1,768]{1,0:T(1,128)S(1)} %after.5.row), channel_id=1, source_target_pairs={{0,16},{1,9},{2,18},{3,11},{4,20},{5,13},{6,22},{7,15},{8,24},{9,1... | collective-permute-start | bytes 9224 | tf_op jit(solution)/shard_map/ppermute | solution.py:274
  27.2 1.4 %home_block.1 = (f32[256,1024]{1,0:T(8,128)S(1)}, f32[256,1]{1,0:T(8,128)S(1)}) custom-call(bf16[1024,1024]{1,0:T(8,128)(2,1)S(1)} %get-tuple-element.14.c_ref, bf16[768,1024]{1,0:T(8,128)(2,1)S(1)} %get-tuple-element.15.v_ref.home.refs_4_.refs_1_.refs_0_, f32[1,768]{1,0:T(1,128)S(1)} %after.5.row, ...), custom_call_target="tpu_custom_call" | custom-call | flops 805306368 | bytes 1572864 | tf_op jit(solution)/shard_map/home_block/pallas_call | solution.py:175
  28.5 3.1 %collective-permute-done.10.refs_0_ = bf16[192,1024]{1,0:T(8,128)(2,1)S(1)} collective-permute-done((bf16[192,1024]{1,0:T(8,128)(2,1)S(1)}, bf16[192,1024]{1,0:T(8,128)(2,1)S(1)}, u32[]{:S(2)}, u32[]{:S(2)}) %collective-permute-start.10) | collective-permute-done | bytes 393248 | tf_op jit(solution)/shard_map/ppermute | solution.py:274
  31.7 2.5 %collective-permute-done.9.refs_3_.refs_2_ = f32[1,768]{1,0:T(1,128)S(1)} collective-permute-done((f32[1,768]{1,0:T(1,128)S(1)}, f32[1,768]{1,0:T(1,128)S(1)}, u32[]{:S(2)}, u32[]{:S(2)}) %collective-permute-start.9) | collective-permute-done | bytes 3104 | tf_op jit(solution)/shard_map/ppermute | solution.py:274
  34.2 1.7 %collective-permute-done.12.refs_10_.refs_7_ = bf16[192,1024]{1,0:T(8,128)(2,1)S(1)} collective-permute-done((bf16[192,1024]{1,0:T(8,128)(2,1)S(1)}, bf16[192,1024]{1,0:T(8,128)(2,1)S(1)}, u32[]{:S(2)}, u32[]{:S(2)}) %collective-permute-start.12) | collective-permute-done | bytes 393248 | tf_op jit(solution)/shard_map/ppermute | solution.py:274
  36.0 2.8 %early_blocks.1 = (f32[256,1024]{1,0:T(8,128)S(1)}, f32[256,1]{1,0:T(8,128)S(1)}, bf16[1536,1024]{1,0:T(8,128)(2,1)S(1)}) custom-call(bf16[1024,1024]{1,0:T(8,128)(2,1)S(1)} %get-tuple-element.14.c_ref, f32[256,1024]{1,0:T(8,128)S(1)} %get-tuple-element.16.refs_0_, f32[256,1]{1,0:T(8,128)S(1)} %get-tuple-element.17.refs_1_, ...), custom_call_target="tpu_custom_call" | custom-call | tf_op jit(solution)/shard_map/early_blocks/pallas_call | solution.py:339
  38.8 3.8 %late_blocks.1 = (bf16[256,1024]{1,0:T(8,128)(2,1)S(1)}, f32[4,256,768]{2,1,0:T(8,128)S(1)}, f32[4,768]{1,0:T(4,128)S(1)}, f32[4,768]{1,0:T(4,128)S(1)}, bf16[768,1024]{1,0:T(8,128)(2,1)S(1)}) custom-call(bf16[1024,1024]{1,0:T(8,128)(2,1)S(1)} %get-tuple-element.14.c_ref, f32[256,1024]{1,0:T(8,128)S(1)} %get-tuple-element.18.total, ...), custom_call_target="tpu_custom_call" | custom-call | flops 2415919104 | bytes 1572864 | tf_op jit(solution)/shard_map/late_blocks/pallas_call | solution.py:359
  44.0 2.5 %collective-permute-start.18 = (f32[4,768]{1,0:T(4,128)S(1)}, f32[4,768]{1,0:T(4,128)S(1)}, u32[]{:S(2)}, u32[]{:S(2)}) collective-permute-start(f32[4,768]{1,0:T(4,128)S(1)} %log_add_fusion.1), channel_id=1, source_target_pairs={{0,6},{1,7},{2,4},{3,5},{4,2},{5,3},{6,0},{7,1},{8,14},{9,15},{10,... | collective-permute-start | bytes 36872 | tf_op jit(solution)/shard_map/ppermute | solution.py:274
  46.7 1.7 %collective-permute-start.16 = (f32[4,768]{1,0:T(4,128)S(1)}, f32[4,768]{1,0:T(4,128)S(1)}, u32[]{:S(2)}, u32[]{:S(2)}) collective-permute-start(f32[4,768]{1,0:T(4,128)S(1)} %log_add_fusion.1), channel_id=1, source_target_pairs={{0,2},{1,3},{2,0},{3,1},{4,6},{5,7},{6,4},{7,5},{8,10},{9,11},{10,... | collective-permute-start | bytes 36872 | tf_op jit(solution)/shard_map/ppermute | solution.py:274
  48.4 1.2 %collective-permute-done.18 = f32[4,768]{1,0:T(4,128)S(1)} collective-permute-done((f32[4,768]{1,0:T(4,128)S(1)}, f32[4,768]{1,0:T(4,128)S(1)}, u32[]{:S(2)}, u32[]{:S(2)}) %collective-permute-start.18) | collective-permute-done | bytes 12320 | tf_op jit(solution)/shard_map/ppermute | solution.py:274
  49.6 1.5 %collective-permute-done.17 = f32[4,768]{1,0:T(4,128)S(1)} collective-permute-done((f32[4,768]{1,0:T(4,128)S(1)}, f32[4,768]{1,0:T(4,128)S(1)}, u32[]{:S(2)}, u32[]{:S(2)}) %collective-permute-start.17) | collective-permute-done | bytes 12320 | tf_op jit(solution)/shard_map/ppermute | solution.py:274
  51.2 2.5 %collective-permute-start.21 = (f32[4,768]{1,0:T(4,128)S(1)}, f32[4,768]{1,0:T(4,128)S(1)}, u32[]{:S(2)}, u32[]{:S(2)}) collective-permute-start(f32[4,768]{1,0:T(4,128)S(1)} %log_add_fusion), channel_id=1, source_target_pairs={{0,24},{1,25},{2,26},{3,27},{4,28},{5,29},{6,30},{7,31},{8,16},{9,... | collective-permute-start | bytes 36872 | tf_op jit(solution)/shard_map/ppermute | solution.py:274
  55.8 1.6 %collective-permute-done.20 = f32[4,768]{1,0:T(4,128)S(1)} collective-permute-done((f32[4,768]{1,0:T(4,128)S(1)}, f32[4,768]{1,0:T(4,128)S(1)}, u32[]{:S(2)}, u32[]{:S(2)}) %collective-permute-start.20) | collective-permute-done | bytes 12320 | tf_op jit(solution)/shard_map/ppermute | solution.py:274
  57.9 2.7 %last_iteration.1 = (bf16[256,1024]{1,0:T(8,128)(2,1)}, f32[768]{0:T(1024)}) custom-call(bf16[256,1024]{1,0:T(8,128)(2,1)S(1)} %get-tuple-element.21.old_ref, f32[4,256,768]{2,1,0:T(8,128)S(1)} %get-tuple-element.22.expo_ref, f32[4,768]{1,0:T(4,128)S(1)} %get-tuple-element.23.peak_ref, f32[1,4,768]{2,1,0:T(4,128)S(1)} %add_bitcast_fusion.parts, ...), custom_call_target="tpu_custom_call" | custom-call | flops 1610612736 | bytes 524288 | tf_op jit(solution)/shard_map/last_iteration/pallas_call | solution.py:386
  (38 shorter events, 7.8 us)
Async XLA Ops:
  1.9 17.2 %collective-permute-start.4 = (bf16[576,1024]{1,0:T(8,128)(2,1)S(1)}, bf16[576,1024]{1,0:T(8,128)(2,1)S(1)}, u32[]{:S(2)}, u32[]{:S(2)}) collective-permute-start(bf16[576,1024]{1,0:T(8,128)(2,1)S(1)} %outgoing.1), channel_id=1, source_target_pairs={{0,8},{1,17},{2,10},{3,19},{4,12},{5,21},{6,14},{7,23},{8,0},{9,25... | collective-permute-start | bytes 3538952 | tf_op jit(solution)/shard_map/ppermute | solution.py:274
  9.5 1.2 %collective-permute-start = (f32[1,768]{1,0:T(1,128)S(1)}, f32[1,768]{1,0:T(1,128)S(1)}, u32[]{:S(2)}, u32[]{:S(2)}) collective-permute-start(f32[1,768]{1,0:T(1,128)S(1)} %partial_lse.1), channel_id=1, source_target_pairs={{0,1},{1,0},{2,3},{3,2},{4,5},{5,4},{6,7},{7,6},{8,9},{9,8},{10,11... | collective-permute-start | bytes 9224 | tf_op jit(solution)/shard_map/ppermute | solution.py:274
  10.7 5.5 %collective-permute-start.3 = (f32[1,768]{1,0:T(1,128)S(1)}, f32[1,768]{1,0:T(1,128)S(1)}, u32[]{:S(2)}, u32[]{:S(2)}) collective-permute-start(f32[1,768]{1,0:T(1,128)S(1)} %log_add_fusion.3), channel_id=1, source_target_pairs={{0,6},{1,7},{2,4},{3,5},{4,2},{5,3},{6,0},{7,1},{8,14},{9,15},{10,... | collective-permute-start | bytes 9224 | tf_op jit(solution)/shard_map/ppermute | solution.py:274
  14.4 4.5 %collective-permute-start.2 = (f32[1,768]{1,0:T(1,128)S(1)}, f32[1,768]{1,0:T(1,128)S(1)}, u32[]{:S(2)}, u32[]{:S(2)}) collective-permute-start(f32[1,768]{1,0:T(1,128)S(1)} %log_add_fusion.3), channel_id=1, source_target_pairs={{0,4},{1,5},{2,6},{3,7},{4,0},{5,1},{6,2},{7,3},{8,12},{9,13},{10,... | collective-permute-start | bytes 9224 | tf_op jit(solution)/shard_map/ppermute | solution.py:274
  14.4 4.5 %collective-permute-start.1 = (f32[1,768]{1,0:T(1,128)S(1)}, f32[1,768]{1,0:T(1,128)S(1)}, u32[]{:S(2)}, u32[]{:S(2)}) collective-permute-start(f32[1,768]{1,0:T(1,128)S(1)} %log_add_fusion.3), channel_id=1, source_target_pairs={{0,2},{1,3},{2,0},{3,1},{4,6},{5,7},{6,4},{7,5},{8,10},{9,11},{10,... | collective-permute-start | bytes 9224 | tf_op jit(solution)/shard_map/ppermute | solution.py:274
  19.2 4.4 %collective-permute-start.6 = (bf16[192,1024]{1,0:T(8,128)(2,1)S(1)}, bf16[192,1024]{1,0:T(8,128)(2,1)S(1)}, u32[]{:S(2)}, u32[]{:S(2)}) collective-permute-start(bf16[192,1024]{1,0:T(8,128)(2,1)S(1)} %get-tuple-element.27), channel_id=1, source_target_pairs={{0,1},{1,0},{2,3},{3,2},{4,5},{5,4},{6,7},{7,6},{8,9},{9,8},{10,11... | collective-permute-start | bytes 1179656 | tf_op jit(solution)/shard_map/ppermute | solution.py:274
  19.3 4.3 %collective-permute-start.5 = (bf16[192,1024]{1,0:T(8,128)(2,1)S(1)}, bf16[192,1024]{1,0:T(8,128)(2,1)S(1)}, u32[]{:S(2)}, u32[]{:S(2)}) collective-permute-start(bf16[192,1024]{1,0:T(8,128)(2,1)S(1)} %get-tuple-element.28), channel_id=1, source_target_pairs={{0,1},{1,0},{2,3},{3,2},{4,5},{5,4},{6,7},{7,6},{8,9},{9,8},{10,11... | collective-permute-start | bytes 1179656 | tf_op jit(solution)/shard_map/ppermute | solution.py:274
  19.8 3.8 %collective-permute-start.7 = (bf16[192,1024]{1,0:T(8,128)(2,1)S(1)}, bf16[192,1024]{1,0:T(8,128)(2,1)S(1)}, u32[]{:S(2)}, u32[]{:S(2)}) collective-permute-start(bf16[192,1024]{1,0:T(8,128)(2,1)S(1)} %get-tuple-element.26), channel_id=1, source_target_pairs={{0,1},{1,0},{2,3},{3,2},{4,5},{5,4},{6,7},{7,6},{8,9},{9,8},{10,11... | collective-permute-start | bytes 1179656 | tf_op jit(solution)/shard_map/ppermute | solution.py:274
  19.8 11.8 %collective-permute-start.10 = (bf16[192,1024]{1,0:T(8,128)(2,1)S(1)}, bf16[192,1024]{1,0:T(8,128)(2,1)S(1)}, u32[]{:S(2)}, u32[]{:S(2)}) collective-permute-start(bf16[192,1024]{1,0:T(8,128)(2,1)S(1)} %get-tuple-element.26), channel_id=1, source_target_pairs={{0,2},{1,3},{2,0},{3,1},{4,6},{5,7},{6,4},{7,5},{8,10},{9,11},{10,... | collective-permute-start | bytes 1179656 | tf_op jit(solution)/shard_map/ppermute | solution.py:274
  22.0 12.2 %collective-permute-start.13 = (bf16[384,1024]{1,0:T(8,128)(2,1)S(1)}, bf16[384,1024]{1,0:T(8,128)(2,1)S(1)}, u32[]{:S(2)}, u32[]{:S(2)}) collective-permute-start(bf16[384,1024]{1,0:T(8,128)(2,1)S(1)} %slice.19), channel_id=1, source_target_pairs={{0,16},{1,9},{2,18},{3,11},{4,20},{5,13},{6,22},{7,15},{8,24},{9,1... | collective-permute-start | bytes 2359304 | tf_op jit(solution)/shard_map/ppermute | solution.py:274
  23.6 8.0 %collective-permute-start.11 = (f32[1,768]{1,0:T(1,128)S(1)}, f32[1,768]{1,0:T(1,128)S(1)}, u32[]{:S(2)}, u32[]{:S(2)}) collective-permute-start(f32[1,768]{1,0:T(1,128)S(1)} %after.5.row), channel_id=1, source_target_pairs={{0,24},{1,25},{2,26},{3,27},{4,28},{5,29},{6,30},{7,31},{8,16},{9,... | collective-permute-start | bytes 9224 | tf_op jit(solution)/shard_map/ppermute | solution.py:274
  25.1 9.0 %collective-permute-start.9 = (f32[1,768]{1,0:T(1,128)S(1)}, f32[1,768]{1,0:T(1,128)S(1)}, u32[]{:S(2)}, u32[]{:S(2)}) collective-permute-start(f32[1,768]{1,0:T(1,128)S(1)} %after.5.row), channel_id=1, source_target_pairs={{0,16},{1,9},{2,18},{3,11},{4,20},{5,13},{6,22},{7,15},{8,24},{9,1... | collective-permute-start | bytes 9224 | tf_op jit(solution)/shard_map/ppermute | solution.py:274
  26.6 7.5 %collective-permute-start.8 = (f32[1,768]{1,0:T(1,128)S(1)}, f32[1,768]{1,0:T(1,128)S(1)}, u32[]{:S(2)}, u32[]{:S(2)}) collective-permute-start(f32[1,768]{1,0:T(1,128)S(1)} %after.5.row), channel_id=1, source_target_pairs={{0,8},{1,17},{2,10},{3,19},{4,12},{5,21},{6,14},{7,23},{8,0},{9,25... | collective-permute-start | bytes 9224 | tf_op jit(solution)/shard_map/ppermute | solution.py:274
  34.2 1.7 %collective-permute-start.12 = (bf16[192,1024]{1,0:T(8,128)(2,1)S(1)}, bf16[192,1024]{1,0:T(8,128)(2,1)S(1)}, u32[]{:S(2)}, u32[]{:S(2)}) collective-permute-start(bf16[192,1024]{1,0:T(8,128)(2,1)S(1)} %after.6.refs_6_), channel_id=1, source_target_pairs={{0,1},{1,0},{2,3},{3,2},{4,5},{5,4},{6,7},{7,6},{8,9},{9,8},{10,11... | collective-permute-start | bytes 1179656 | tf_op jit(solution)/shard_map/ppermute | solution.py:274
  35.9 3.0 %collective-permute-start.14 = (bf16[384,1024]{1,0:T(8,128)(2,1)S(1)}, bf16[384,1024]{1,0:T(8,128)(2,1)S(1)}, u32[]{:S(2)}, u32[]{:S(2)}) collective-permute-start(bf16[384,1024]{1,0:T(8,128)(2,1)S(1)} %after.7.refs_3_), channel_id=1, source_target_pairs={{0,1},{1,0},{2,3},{3,2},{4,5},{5,4},{6,7},{7,6},{8,9},{9,8},{10,11... | collective-permute-start | bytes 2359304 | tf_op jit(solution)/shard_map/ppermute | solution.py:274
  42.7 1.3 %collective-permute-start.15 = (f32[4,768]{1,0:T(4,128)S(1)}, f32[4,768]{1,0:T(4,128)S(1)}, u32[]{:S(2)}, u32[]{:S(2)}) collective-permute-start(f32[4,768]{1,0:T(4,128)S(1)} %get-tuple-element.24), channel_id=1, source_target_pairs={{0,1},{1,0},{2,3},{3,2},{4,5},{5,4},{6,7},{7,6},{8,9},{9,8},{10,11... | collective-permute-start | bytes 36872 | tf_op jit(solution)/shard_map/ppermute | solution.py:274
  44.0 5.7 %collective-permute-start.18 = (f32[4,768]{1,0:T(4,128)S(1)}, f32[4,768]{1,0:T(4,128)S(1)}, u32[]{:S(2)}, u32[]{:S(2)}) collective-permute-start(f32[4,768]{1,0:T(4,128)S(1)} %log_add_fusion.1), channel_id=1, source_target_pairs={{0,6},{1,7},{2,4},{3,5},{4,2},{5,3},{6,0},{7,1},{8,14},{9,15},{10,... | collective-permute-start | bytes 36872 | tf_op jit(solution)/shard_map/ppermute | solution.py:274
  46.5 4.6 %collective-permute-start.17 = (f32[4,768]{1,0:T(4,128)S(1)}, f32[4,768]{1,0:T(4,128)S(1)}, u32[]{:S(2)}, u32[]{:S(2)}) collective-permute-start(f32[4,768]{1,0:T(4,128)S(1)} %log_add_fusion.1), channel_id=1, source_target_pairs={{0,4},{1,5},{2,6},{3,7},{4,0},{5,1},{6,2},{7,3},{8,12},{9,13},{10,... | collective-permute-start | bytes 36872 | tf_op jit(solution)/shard_map/ppermute | solution.py:274
  46.7 4.4 %collective-permute-start.16 = (f32[4,768]{1,0:T(4,128)S(1)}, f32[4,768]{1,0:T(4,128)S(1)}, u32[]{:S(2)}, u32[]{:S(2)}) collective-permute-start(f32[4,768]{1,0:T(4,128)S(1)} %log_add_fusion.1), channel_id=1, source_target_pairs={{0,2},{1,3},{2,0},{3,1},{4,6},{5,7},{6,4},{7,5},{8,10},{9,11},{10,... | collective-permute-start | bytes 36872 | tf_op jit(solution)/shard_map/ppermute | solution.py:274
  51.2 4.7 %collective-permute-start.21 = (f32[4,768]{1,0:T(4,128)S(1)}, f32[4,768]{1,0:T(4,128)S(1)}, u32[]{:S(2)}, u32[]{:S(2)}) collective-permute-start(f32[4,768]{1,0:T(4,128)S(1)} %log_add_fusion), channel_id=1, source_target_pairs={{0,24},{1,25},{2,26},{3,27},{4,28},{5,29},{6,30},{7,31},{8,16},{9,... | collective-permute-start | bytes 36872 | tf_op jit(solution)/shard_map/ppermute | solution.py:274
  53.7 3.7 %collective-permute-start.20 = (f32[4,768]{1,0:T(4,128)S(1)}, f32[4,768]{1,0:T(4,128)S(1)}, u32[]{:S(2)}, u32[]{:S(2)}) collective-permute-start(f32[4,768]{1,0:T(4,128)S(1)} %log_add_fusion), channel_id=1, source_target_pairs={{0,16},{1,17},{2,18},{3,19},{4,20},{5,21},{6,22},{7,23},{8,24},{9,... | collective-permute-start | bytes 36872 | tf_op jit(solution)/shard_map/ppermute | solution.py:274
  54.2 3.7 %collective-permute-start.19 = (f32[4,768]{1,0:T(4,128)S(1)}, f32[4,768]{1,0:T(4,128)S(1)}, u32[]{:S(2)}, u32[]{:S(2)}) collective-permute-start(f32[4,768]{1,0:T(4,128)S(1)} %log_add_fusion), channel_id=1, source_target_pairs={{0,8},{1,9},{2,10},{3,11},{4,12},{5,13},{6,14},{7,15},{8,0},{9,1},... | collective-permute-start | bytes 36872 | tf_op jit(solution)/shard_map/ppermute | solution.py:274

commit v16 on v14

--- a/solution.py
+++ b/solution.py
@@ -313,7 +313,7 @@
         crossed = [go(piece, 0, 1) for piece in quarters]
         lse = after(lse, *crossed)
         parts = [lse, go(lse, (1, 2)), go(lse, (2, 1)), go(lse, 3)]
-        begun = begin(centroids, home, lse, crossed[2], rows, scale)
+        begun = begin(centroids, home, lse, parts[3], rows, scale)
         swapped = after(swapped, begun[1])
         near = [near, swapped] + crossed + [go(swapped, 0, 1)]
         pieces = [home]

time: 63.5 us -> 64.7 us (1.019)
  starting transfers between devices: 24 us -> 28 us
  waiting for transfers between devices: 21.8 us -> 19 us
    ppermute x22, starting transfers between devices: 24 us -> 28 us  [send(): return lax.ppermute(value, BOTH, pairs)]
    ppermute x22, waiting for transfers between devices: 21.8 us -> 19 us  [send(): return lax.ppermute(value, BOTH, pairs)]
where the time goes in v16:
time: 64.7 us; the launch traced here: 64.6 us
  starting transfers between devices  28 us (43%)
  waiting for transfers between devices  19 us (29%)
  Pallas kernels  16.5 us (26%)
  between operations  0.74 us (1%)
    ppermute x22, starting transfers between devices, send(): return lax.ppermute(value, BOTH, pairs)  28 us
    ppermute x22, waiting for transfers between devices, send(): return lax.ppermute(value, BOTH, pairs)  19 us
    pallas_call x1, Pallas kernels, shards(): pl.pallas_call(functools.partial(late_kernel, dict(plan), scale), in_spec...  3.8 us
    pallas_call x1, Pallas kernels, shards(): pl.pallas_call(functools.partial(early_kernel, dict(plan), scale), in_spe...  2.8 us
    pallas_call x1, Pallas kernels, shards(): pl.pallas_call(functools.partial(last_kernel, dict(plan)), in_specs=[vmem...  2.71 us
    pallas_call x1, Pallas kernels, partial(): pl.pallas_call(functools.partial(partial_kernel, scale, min(256, k)), in_...  2.46 us
    pallas_call x1, Pallas kernels, load(): pl.pallas_call(load_kernel, in_specs=[hbm, hbm], out_specs=[vmem] * 2, ou...  2.09 us
    pallas_call x1, Pallas kernels, begin(): pl.pallas_call(functools.partial(home_kernel, scale), in_specs=[vmem] * 3...  1.36 us
  transfers between devices with their start and end apart: 22, of which 14 were waited for; matrix products, arithmetic and copies ran while one was open for 0% of the time, Pallas kernels for 14%

profile of v16, /device:TPU:0, one launch (start us, length us, event | category | flops | bytes accessed | tf_op | source)
XLA Modules:
  0.0 64.6 jit_solution(8267911261453042454)
XLA Ops:
  0.6 1.3 %outgoing.1 = bf16[576,1024]{1,0:T(8,128)(2,1)S(1)} custom-call(bf16[768,1024]{1,0:T(8,128)(2,1)} %v_hbm.3), custom_call_target="tpu_custom_call" | custom-call | bytes 1572864 | tf_op jit(solution)/shard_map/outgoing/pallas_call | solution.py:79
  1.9 3.0 %collective-permute-start.4 = (bf16[576,1024]{1,0:T(8,128)(2,1)S(1)}, bf16[576,1024]{1,0:T(8,128)(2,1)S(1)}, u32[]{:S(2)}, u32[]{:S(2)}) collective-permute-start(bf16[576,1024]{1,0:T(8,128)(2,1)S(1)} %outgoing.1), channel_id=1, source_target_pairs={{0,8},{1,17},{2,10},{3,19},{4,12},{5,21},{6,14},{7,23},{8,0},{9,25... | collective-permute-start | bytes 3538952 | tf_op jit(solution)/shard_map/ppermute | solution.py:274
  4.9 2.1 %load.1 = (bf16[768,1024]{1,0:T(8,128)(2,1)S(1)}, bf16[1024,1024]{1,0:T(8,128)(2,1)S(1)}) custom-call(bf16[768,1024]{1,0:T(8,128)(2,1)} %v_hbm.3, bf16[1024,1024]{1,0:T(8,128)(2,1)} %c_hbm.1), custom_call_target="tpu_custom_call" | custom-call | bytes 7340032 | tf_op jit(solution)/shard_map/load/pallas_call | solution.py:102
  7.0 2.5 %partial_lse.1 = f32[1,768]{1,0:T(1,128)S(1)} custom-call(bf16[768,1024]{1,0:T(8,128)(2,1)S(1)} %get-tuple-element.15.v_ref.home.refs_4_.refs_1_.refs_0_, bf16[1024,1024]{1,0:T(8,128)(2,1)S(1)} %get-tuple-element.14.c_ref), custom_call_target="tpu_custom_call" | custom-call | flops 1610612736 | bytes 3670016 | tf_op jit(solution)/shard_map/partial_lse/pallas_call | solution.py:129
  10.7 3.7 %collective-permute-start.3 = (f32[1,768]{1,0:T(1,128)S(1)}, f32[1,768]{1,0:T(1,128)S(1)}, u32[]{:S(2)}, u32[]{:S(2)}) collective-permute-start(f32[1,768]{1,0:T(1,128)S(1)} %log_add_fusion.3), channel_id=1, source_target_pairs={{0,6},{1,7},{2,4},{3,5},{4,2},{5,3},{6,0},{7,1},{8,14},{9,15},{10,... | collective-permute-start | bytes 9224 | tf_op jit(solution)/shard_map/ppermute | solution.py:274
  16.2 2.7 %collective-permute-done.2 = f32[1,768]{1,0:T(1,128)S(1)} collective-permute-done((f32[1,768]{1,0:T(1,128)S(1)}, f32[1,768]{1,0:T(1,128)S(1)}, u32[]{:S(2)}, u32[]{:S(2)}) %collective-permute-start.2) | collective-permute-done | bytes 3104 | tf_op jit(solution)/shard_map/ppermute | solution.py:274
  19.8 2.1 %collective-permute-start.11 = (bf16[192,1024]{1,0:T(8,128)(2,1)S(1)}, bf16[192,1024]{1,0:T(8,128)(2,1)S(1)}, u32[]{:S(2)}, u32[]{:S(2)}) collective-permute-start(bf16[192,1024]{1,0:T(8,128)(2,1)S(1)} %get-tuple-element.26), channel_id=1, source_target_pairs={{0,2},{1,3},{2,0},{3,1},{4,6},{5,7},{6,4},{7,5},{8,10},{9,11},{10,... | collective-permute-start | bytes 1179656 | tf_op jit(solution)/shard_map/ppermute | solution.py:274
  22.0 1.6 %collective-permute-start.13 = (bf16[384,1024]{1,0:T(8,128)(2,1)S(1)}, bf16[384,1024]{1,0:T(8,128)(2,1)S(1)}, u32[]{:S(2)}, u32[]{:S(2)}) collective-permute-start(bf16[384,1024]{1,0:T(8,128)(2,1)S(1)} %slice.19), channel_id=1, source_target_pairs={{0,16},{1,9},{2,18},{3,11},{4,20},{5,13},{6,22},{7,15},{8,24},{9,1... | collective-permute-start | bytes 2359304 | tf_op jit(solution)/shard_map/ppermute | solution.py:274
  23.6 1.5 %collective-permute-start.8 = (f32[1,768]{1,0:T(1,128)S(1)}, f32[1,768]{1,0:T(1,128)S(1)}, u32[]{:S(2)}, u32[]{:S(2)}) collective-permute-start(f32[1,768]{1,0:T(1,128)S(1)} %after.5.row), channel_id=1, source_target_pairs={{0,24},{1,25},{2,26},{3,27},{4,28},{5,29},{6,30},{7,31},{8,16},{9,... | collective-permute-start | bytes 9224 | tf_op jit(solution)/shard_map/ppermute | solution.py:274
  25.1 3.2 %collective-permute-done.8._.refs_3_.refs_0_ = f32[1,768]{1,0:T(1,128)S(1)} collective-permute-done((f32[1,768]{1,0:T(1,128)S(1)}, f32[1,768]{1,0:T(1,128)S(1)}, u32[]{:S(2)}, u32[]{:S(2)}) %collective-permute-start.8) | collective-permute-done | bytes 3104 | tf_op jit(solution)/shard_map/ppermute | solution.py:274
  28.3 1.4 %home_block.1 = (f32[256,1024]{1,0:T(8,128)S(1)}, f32[256,1]{1,0:T(8,128)S(1)}) custom-call(bf16[1024,1024]{1,0:T(8,128)(2,1)S(1)} %get-tuple-element.14.c_ref, bf16[768,1024]{1,0:T(8,128)(2,1)S(1)} %get-tuple-element.15.v_ref.home.refs_4_.refs_1_.refs_0_, f32[1,768]{1,0:T(1,128)S(1)} %after.5.row, f32[1,768]{1,0:T(1,128)S(1)} %collective-permute-done.8._.refs_3_.refs_0_), custom_call_target="tpu_custom_call" | custom-call | flops 805306368 | bytes 1572864 | tf_op jit(solution)/shard_map/home_block/pallas_call | solution.py:175
  29.6 2.0 %collective-permute-done.11.refs_0_ = bf16[192,1024]{1,0:T(8,128)(2,1)S(1)} collective-permute-done((bf16[192,1024]{1,0:T(8,128)(2,1)S(1)}, bf16[192,1024]{1,0:T(8,128)(2,1)S(1)}, u32[]{:S(2)}, u32[]{:S(2)}) %collective-permute-start.11) | collective-permute-done | bytes 393248 | tf_op jit(solution)/shard_map/ppermute | solution.py:274
  31.7 3.9 %collective-permute-start.12 = (bf16[192,1024]{1,0:T(8,128)(2,1)S(1)}, bf16[192,1024]{1,0:T(8,128)(2,1)S(1)}, u32[]{:S(2)}, u32[]{:S(2)}) collective-permute-start(bf16[192,1024]{1,0:T(8,128)(2,1)S(1)} %after.6.refs_6_), channel_id=1, source_target_pairs={{0,1},{1,0},{2,3},{3,2},{4,5},{5,4},{6,7},{7,6},{8,9},{9,8},{10,11... | collective-permute-start | bytes 1179656 | tf_op jit(solution)/shard_map/ppermute | solution.py:274
  36.2 1.5 %collective-permute-start.9 = (f32[1,768]{1,0:T(1,128)S(1)}, f32[1,768]{1,0:T(1,128)S(1)}, u32[]{:S(2)}, u32[]{:S(2)}) collective-permute-start(f32[1,768]{1,0:T(1,128)S(1)} %after.5.row), channel_id=1, source_target_pairs={{0,8},{1,17},{2,10},{3,19},{4,12},{5,21},{6,14},{7,23},{8,0},{9,25... | collective-permute-start | bytes 9224 | tf_op jit(solution)/shard_map/ppermute | solution.py:274
  37.7 1.5 %collective-permute-done.10.refs_3_.refs_2_ = f32[1,768]{1,0:T(1,128)S(1)} collective-permute-done((f32[1,768]{1,0:T(1,128)S(1)}, f32[1,768]{1,0:T(1,128)S(1)}, u32[]{:S(2)}, u32[]{:S(2)}) %collective-permute-start.10) | collective-permute-done | bytes 3104 | tf_op jit(solution)/shard_map/ppermute | solution.py:274
  39.8 2.8 %early_blocks.1 = (f32[256,1024]{1,0:T(8,128)S(1)}, f32[256,1]{1,0:T(8,128)S(1)}, bf16[1536,1024]{1,0:T(8,128)(2,1)S(1)}) custom-call(bf16[1024,1024]{1,0:T(8,128)(2,1)S(1)} %get-tuple-element.14.c_ref, f32[256,1024]{1,0:T(8,128)S(1)} %get-tuple-element.16.refs_0_, f32[256,1]{1,0:T(8,128)S(1)} %get-tuple-element.17.refs_1_, ...), custom_call_target="tpu_custom_call" | custom-call | tf_op jit(solution)/shard_map/early_blocks/pallas_call | solution.py:339
  42.7 3.8 %late_blocks.1 = (bf16[256,1024]{1,0:T(8,128)(2,1)S(1)}, f32[4,256,768]{2,1,0:T(8,128)S(1)}, f32[4,768]{1,0:T(4,128)S(1)}, f32[4,768]{1,0:T(4,128)S(1)}, bf16[768,1024]{1,0:T(8,128)(2,1)S(1)}) custom-call(bf16[1024,1024]{1,0:T(8,128)(2,1)S(1)} %get-tuple-element.14.c_ref, f32[256,1024]{1,0:T(8,128)S(1)} %get-tuple-element.18.total, ...), custom_call_target="tpu_custom_call" | custom-call | flops 2415919104 | bytes 1572864 | tf_op jit(solution)/shard_map/late_blocks/pallas_call | solution.py:359
  47.9 2.5 %collective-permute-start.18 = (f32[4,768]{1,0:T(4,128)S(1)}, f32[4,768]{1,0:T(4,128)S(1)}, u32[]{:S(2)}, u32[]{:S(2)}) collective-permute-start(f32[4,768]{1,0:T(4,128)S(1)} %log_add_fusion.1), channel_id=1, source_target_pairs={{0,6},{1,7},{2,4},{3,5},{4,2},{5,3},{6,0},{7,1},{8,14},{9,15},{10,... | collective-permute-start | bytes 36872 | tf_op jit(solution)/shard_map/ppermute | solution.py:274
  50.6 1.7 %collective-permute-start.16 = (f32[4,768]{1,0:T(4,128)S(1)}, f32[4,768]{1,0:T(4,128)S(1)}, u32[]{:S(2)}, u32[]{:S(2)}) collective-permute-start(f32[4,768]{1,0:T(4,128)S(1)} %log_add_fusion.1), channel_id=1, source_target_pairs={{0,2},{1,3},{2,0},{3,1},{4,6},{5,7},{6,4},{7,5},{8,10},{9,11},{10,... | collective-permute-start | bytes 36872 | tf_op jit(solution)/shard_map/ppermute | solution.py:274
  52.4 1.2 %collective-permute-done.18 = f32[4,768]{1,0:T(4,128)S(1)} collective-permute-done((f32[4,768]{1,0:T(4,128)S(1)}, f32[4,768]{1,0:T(4,128)S(1)}, u32[]{:S(2)}, u32[]{:S(2)}) %collective-permute-start.18) | collective-permute-done | bytes 12320 | tf_op jit(solution)/shard_map/ppermute | solution.py:274
  53.6 1.5 %collective-permute-done.17 = f32[4,768]{1,0:T(4,128)S(1)} collective-permute-done((f32[4,768]{1,0:T(4,128)S(1)}, f32[4,768]{1,0:T(4,128)S(1)}, u32[]{:S(2)}, u32[]{:S(2)}) %collective-permute-start.17) | collective-permute-done | bytes 12320 | tf_op jit(solution)/shard_map/ppermute | solution.py:274
  55.1 2.4 %collective-permute-start.21 = (f32[4,768]{1,0:T(4,128)S(1)}, f32[4,768]{1,0:T(4,128)S(1)}, u32[]{:S(2)}, u32[]{:S(2)}) collective-permute-start(f32[4,768]{1,0:T(4,128)S(1)} %log_add_fusion), channel_id=1, source_target_pairs={{0,24},{1,25},{2,26},{3,27},{4,28},{5,29},{6,30},{7,31},{8,16},{9,... | collective-permute-start | bytes 36872 | tf_op jit(solution)/shard_map/ppermute | solution.py:274
  59.8 1.4 %collective-permute-done.20 = f32[4,768]{1,0:T(4,128)S(1)} collective-permute-done((f32[4,768]{1,0:T(4,128)S(1)}, f32[4,768]{1,0:T(4,128)S(1)}, u32[]{:S(2)}, u32[]{:S(2)}) %collective-permute-start.20) | collective-permute-done | bytes 12320 | tf_op jit(solution)/shard_map/ppermute | solution.py:274
  61.9 2.7 %last_iteration.1 = (bf16[256,1024]{1,0:T(8,128)(2,1)}, f32[768]{0:T(1024)}) custom-call(bf16[256,1024]{1,0:T(8,128)(2,1)S(1)} %get-tuple-element.21.old_ref, f32[4,256,768]{2,1,0:T(8,128)S(1)} %get-tuple-element.22.expo_ref, f32[4,768]{1,0:T(4,128)S(1)} %get-tuple-element.23.peak_ref, f32[1,4,768]{2,1,0:T(4,128)S(1)} %add_bitcast_fusion.parts, ...), custom_call_target="tpu_custom_call" | custom-call | flops 1610612736 | bytes 524288 | tf_op jit(solution)/shard_map/last_iteration/pallas_call | solution.py:386
  (38 shorter events, 9.9 us)
Async XLA Ops:
  1.9 17.2 %collective-permute-start.4 = (bf16[576,1024]{1,0:T(8,128)(2,1)S(1)}, bf16[576,1024]{1,0:T(8,128)(2,1)S(1)}, u32[]{:S(2)}, u32[]{:S(2)}) collective-permute-start(bf16[576,1024]{1,0:T(8,128)(2,1)S(1)} %outgoing.1), channel_id=1, source_target_pairs={{0,8},{1,17},{2,10},{3,19},{4,12},{5,21},{6,14},{7,23},{8,0},{9,25... | collective-permute-start | bytes 3538952 | tf_op jit(solution)/shard_map/ppermute | solution.py:274
  9.5 1.2 %collective-permute-start = (f32[1,768]{1,0:T(1,128)S(1)}, f32[1,768]{1,0:T(1,128)S(1)}, u32[]{:S(2)}, u32[]{:S(2)}) collective-permute-start(f32[1,768]{1,0:T(1,128)S(1)} %partial_lse.1), channel_id=1, source_target_pairs={{0,1},{1,0},{2,3},{3,2},{4,5},{5,4},{6,7},{7,6},{8,9},{9,8},{10,11... | collective-permute-start | bytes 9224 | tf_op jit(solution)/shard_map/ppermute | solution.py:274
  10.7 5.5 %collective-permute-start.3 = (f32[1,768]{1,0:T(1,128)S(1)}, f32[1,768]{1,0:T(1,128)S(1)}, u32[]{:S(2)}, u32[]{:S(2)}) collective-permute-start(f32[1,768]{1,0:T(1,128)S(1)} %log_add_fusion.3), channel_id=1, source_target_pairs={{0,6},{1,7},{2,4},{3,5},{4,2},{5,3},{6,0},{7,1},{8,14},{9,15},{10,... | collective-permute-start | bytes 9224 | tf_op jit(solution)/shard_map/ppermute | solution.py:274
  14.4 4.5 %collective-permute-start.2 = (f32[1,768]{1,0:T(1,128)S(1)}, f32[1,768]{1,0:T(1,128)S(1)}, u32[]{:S(2)}, u32[]{:S(2)}) collective-permute-start(f32[1,768]{1,0:T(1,128)S(1)} %log_add_fusion.3), channel_id=1, source_target_pairs={{0,4},{1,5},{2,6},{3,7},{4,0},{5,1},{6,2},{7,3},{8,12},{9,13},{10,... | collective-permute-start | bytes 9224 | tf_op jit(solution)/shard_map/ppermute | solution.py:274
  14.4 4.5 %collective-permute-start.1 = (f32[1,768]{1,0:T(1,128)S(1)}, f32[1,768]{1,0:T(1,128)S(1)}, u32[]{:S(2)}, u32[]{:S(2)}) collective-permute-start(f32[1,768]{1,0:T(1,128)S(1)} %log_add_fusion.3), channel_id=1, source_target_pairs={{0,2},{1,3},{2,0},{3,1},{4,6},{5,7},{6,4},{7,5},{8,10},{9,11},{10,... | collective-permute-start | bytes 9224 | tf_op jit(solution)/shard_map/ppermute | solution.py:274
  19.2 4.4 %collective-permute-start.6 = (bf16[192,1024]{1,0:T(8,128)(2,1)S(1)}, bf16[192,1024]{1,0:T(8,128)(2,1)S(1)}, u32[]{:S(2)}, u32[]{:S(2)}) collective-permute-start(bf16[192,1024]{1,0:T(8,128)(2,1)S(1)} %get-tuple-element.27), channel_id=1, source_target_pairs={{0,1},{1,0},{2,3},{3,2},{4,5},{5,4},{6,7},{7,6},{8,9},{9,8},{10,11... | collective-permute-start | bytes 1179656 | tf_op jit(solution)/shard_map/ppermute | solution.py:274
  19.3 4.3 %collective-permute-start.5 = (bf16[192,1024]{1,0:T(8,128)(2,1)S(1)}, bf16[192,1024]{1,0:T(8,128)(2,1)S(1)}, u32[]{:S(2)}, u32[]{:S(2)}) collective-permute-start(bf16[192,1024]{1,0:T(8,128)(2,1)S(1)} %get-tuple-element.28), channel_id=1, source_target_pairs={{0,1},{1,0},{2,3},{3,2},{4,5},{5,4},{6,7},{7,6},{8,9},{9,8},{10,11... | collective-permute-start | bytes 1179656 | tf_op jit(solution)/shard_map/ppermute | solution.py:274
  19.8 3.8 %collective-permute-start.7 = (bf16[192,1024]{1,0:T(8,128)(2,1)S(1)}, bf16[192,1024]{1,0:T(8,128)(2,1)S(1)}, u32[]{:S(2)}, u32[]{:S(2)}) collective-permute-start(bf16[192,1024]{1,0:T(8,128)(2,1)S(1)} %get-tuple-element.26), channel_id=1, source_target_pairs={{0,1},{1,0},{2,3},{3,2},{4,5},{5,4},{6,7},{7,6},{8,9},{9,8},{10,11... | collective-permute-start | bytes 1179656 | tf_op jit(solution)/shard_map/ppermute | solution.py:274
  19.8 11.8 %collective-permute-start.11 = (bf16[192,1024]{1,0:T(8,128)(2,1)S(1)}, bf16[192,1024]{1,0:T(8,128)(2,1)S(1)}, u32[]{:S(2)}, u32[]{:S(2)}) collective-permute-start(bf16[192,1024]{1,0:T(8,128)(2,1)S(1)} %get-tuple-element.26), channel_id=1, source_target_pairs={{0,2},{1,3},{2,0},{3,1},{4,6},{5,7},{6,4},{7,5},{8,10},{9,11},{10,... | collective-permute-start | bytes 1179656 | tf_op jit(solution)/shard_map/ppermute | solution.py:274
  22.0 17.8 %collective-permute-start.13 = (bf16[384,1024]{1,0:T(8,128)(2,1)S(1)}, bf16[384,1024]{1,0:T(8,128)(2,1)S(1)}, u32[]{:S(2)}, u32[]{:S(2)}) collective-permute-start(bf16[384,1024]{1,0:T(8,128)(2,1)S(1)} %slice.19), channel_id=1, source_target_pairs={{0,16},{1,9},{2,18},{3,11},{4,20},{5,13},{6,22},{7,15},{8,24},{9,1... | collective-permute-start | bytes 2359304 | tf_op jit(solution)/shard_map/ppermute | solution.py:274
  23.6 4.7 %collective-permute-start.8 = (f32[1,768]{1,0:T(1,128)S(1)}, f32[1,768]{1,0:T(1,128)S(1)}, u32[]{:S(2)}, u32[]{:S(2)}) collective-permute-start(f32[1,768]{1,0:T(1,128)S(1)} %after.5.row), channel_id=1, source_target_pairs={{0,24},{1,25},{2,26},{3,27},{4,28},{5,29},{6,30},{7,31},{8,16},{9,... | collective-permute-start | bytes 9224 | tf_op jit(solution)/shard_map/ppermute | solution.py:274
  31.7 8.1 %collective-permute-start.12 = (bf16[192,1024]{1,0:T(8,128)(2,1)S(1)}, bf16[192,1024]{1,0:T(8,128)(2,1)S(1)}, u32[]{:S(2)}, u32[]{:S(2)}) collective-permute-start(bf16[192,1024]{1,0:T(8,128)(2,1)S(1)} %after.6.refs_6_), channel_id=1, source_target_pairs={{0,1},{1,0},{2,3},{3,2},{4,5},{5,4},{6,7},{7,6},{8,9},{9,8},{10,11... | collective-permute-start | bytes 1179656 | tf_op jit(solution)/shard_map/ppermute | solution.py:274
  35.5 3.6 %collective-permute-start.10 = (f32[1,768]{1,0:T(1,128)S(1)}, f32[1,768]{1,0:T(1,128)S(1)}, u32[]{:S(2)}, u32[]{:S(2)}) collective-permute-start(f32[1,768]{1,0:T(1,128)S(1)} %after.5.row), channel_id=1, source_target_pairs={{0,16},{1,9},{2,18},{3,11},{4,20},{5,13},{6,22},{7,15},{8,24},{9,1... | collective-permute-start | bytes 9224 | tf_op jit(solution)/shard_map/ppermute | solution.py:274
  36.2 3.6 %collective-permute-start.9 = (f32[1,768]{1,0:T(1,128)S(1)}, f32[1,768]{1,0:T(1,128)S(1)}, u32[]{:S(2)}, u32[]{:S(2)}) collective-permute-start(f32[1,768]{1,0:T(1,128)S(1)} %after.5.row), channel_id=1, source_target_pairs={{0,8},{1,17},{2,10},{3,19},{4,12},{5,21},{6,14},{7,23},{8,0},{9,25... | collective-permute-start | bytes 9224 | tf_op jit(solution)/shard_map/ppermute | solution.py:274
  39.8 2.9 %collective-permute-start.14 = (bf16[384,1024]{1,0:T(8,128)(2,1)S(1)}, bf16[384,1024]{1,0:T(8,128)(2,1)S(1)}, u32[]{:S(2)}, u32[]{:S(2)}) collective-permute-start(bf16[384,1024]{1,0:T(8,128)(2,1)S(1)} %after.7.refs_3_), channel_id=1, source_target_pairs={{0,1},{1,0},{2,3},{3,2},{4,5},{5,4},{6,7},{7,6},{8,9},{9,8},{10,11... | collective-permute-start | bytes 2359304 | tf_op jit(solution)/shard_map/ppermute | solution.py:274
  46.5 1.4 %collective-permute-start.15 = (f32[4,768]{1,0:T(4,128)S(1)}, f32[4,768]{1,0:T(4,128)S(1)}, u32[]{:S(2)}, u32[]{:S(2)}) collective-permute-start(f32[4,768]{1,0:T(4,128)S(1)} %get-tuple-element.24), channel_id=1, source_target_pairs={{0,1},{1,0},{2,3},{3,2},{4,5},{5,4},{6,7},{7,6},{8,9},{9,8},{10,11... | collective-permute-start | bytes 36872 | tf_op jit(solution)/shard_map/ppermute | solution.py:274
  47.9 5.7 %collective-permute-start.18 = (f32[4,768]{1,0:T(4,128)S(1)}, f32[4,768]{1,0:T(4,128)S(1)}, u32[]{:S(2)}, u32[]{:S(2)}) collective-permute-start(f32[4,768]{1,0:T(4,128)S(1)} %log_add_fusion.1), channel_id=1, source_target_pairs={{0,6},{1,7},{2,4},{3,5},{4,2},{5,3},{6,0},{7,1},{8,14},{9,15},{10,... | collective-permute-start | bytes 36872 | tf_op jit(solution)/shard_map/ppermute | solution.py:274
  50.4 4.6 %collective-permute-start.17 = (f32[4,768]{1,0:T(4,128)S(1)}, f32[4,768]{1,0:T(4,128)S(1)}, u32[]{:S(2)}, u32[]{:S(2)}) collective-permute-start(f32[4,768]{1,0:T(4,128)S(1)} %log_add_fusion.1), channel_id=1, source_target_pairs={{0,4},{1,5},{2,6},{3,7},{4,0},{5,1},{6,2},{7,3},{8,12},{9,13},{10,... | collective-permute-start | bytes 36872 | tf_op jit(solution)/shard_map/ppermute | solution.py:274
  50.6 4.4 %collective-permute-start.16 = (f32[4,768]{1,0:T(4,128)S(1)}, f32[4,768]{1,0:T(4,128)S(1)}, u32[]{:S(2)}, u32[]{:S(2)}) collective-permute-start(f32[4,768]{1,0:T(4,128)S(1)} %log_add_fusion.1), channel_id=1, source_target_pairs={{0,2},{1,3},{2,0},{3,1},{4,6},{5,7},{6,4},{7,5},{8,10},{9,11},{10,... | collective-permute-start | bytes 36872 | tf_op jit(solution)/shard_map/ppermute | solution.py:274
  55.1 4.7 %collective-permute-start.21 = (f32[4,768]{1,0:T(4,128)S(1)}, f32[4,768]{1,0:T(4,128)S(1)}, u32[]{:S(2)}, u32[]{:S(2)}) collective-permute-start(f32[4,768]{1,0:T(4,128)S(1)} %log_add_fusion), channel_id=1, source_target_pairs={{0,24},{1,25},{2,26},{3,27},{4,28},{5,29},{6,30},{7,31},{8,16},{9,... | collective-permute-start | bytes 36872 | tf_op jit(solution)/shard_map/ppermute | solution.py:274
  57.5 3.7 %collective-permute-start.20 = (f32[4,768]{1,0:T(4,128)S(1)}, f32[4,768]{1,0:T(4,128)S(1)}, u32[]{:S(2)}, u32[]{:S(2)}) collective-permute-start(f32[4,768]{1,0:T(4,128)S(1)} %log_add_fusion), channel_id=1, source_target_pairs={{0,16},{1,17},{2,18},{3,19},{4,20},{5,21},{6,22},{7,23},{8,24},{9,... | collective-permute-start | bytes 36872 | tf_op jit(solution)/shard_map/ppermute | solution.py:274
  58.1 3.7 %collective-permute-start.19 = (f32[4,768]{1,0:T(4,128)S(1)}, f32[4,768]{1,0:T(4,128)S(1)}, u32[]{:S(2)}, u32[]{:S(2)}) collective-permute-start(f32[4,768]{1,0:T(4,128)S(1)} %log_add_fusion), channel_id=1, source_target_pairs={{0,8},{1,9},{2,10},{3,11},{4,12},{5,13},{6,14},{7,15},{8,0},{9,1},... | collective-permute-start | bytes 36872 | tf_op jit(solution)/shard_map/ppermute | solution.py:274

commit v17 on v15

--- a/solution.py
+++ b/solution.py
@@ -183,6 +183,37 @@
         ),
         name="home_block",
     )(in_vmem(centroids), in_vmem(home), lse, other)
+
+
+def near_kernel(scale, c_ref, near, last, row, total, mass, table, new_total, new_mass):
+    half_lead, direct, swapped = leads(table.shape[0], core_index())
+    quarter = last.shape[0]
+    table[pl.ds(half_lead, 2 * quarter), :] = near[: 2 * quarter, :]
+    table[pl.ds(direct, quarter), :] = near[2 * quarter :, :]
+    table[pl.ds(swapped, quarter), :] = last[...]
+    own = own_rows(c_ref, total.shape[0])
+    new_total[...], new_mass[...] = absorb(own, table[...], row[...], scale, total[...], mass[...])
+
+
+def add_near(centroids, near, swapped, row, begun, scale):
+    quarter, dim = swapped.shape
+    rows = begun[0].shape[0]
+    vmem = pl.BlockSpec(memory_space=pltpu.VMEM)
+    return pl.pallas_call(
+        functools.partial(near_kernel, scale),
+        in_specs=[vmem] * 6,
+        out_specs=[vmem] * 3,
+        out_shape=[
+            pltpu.VMEM((4 * quarter, dim), jnp.bfloat16),
+            pltpu.VMEM((rows, dim), jnp.float32),
+            pltpu.VMEM((rows, 1), jnp.float32),
+        ],
+        compiler_params=pltpu.CompilerParams(vmem_limit_bytes=16 * MIB),
+        cost_estimate=pl.CostEstimate(
+            flops=16 * quarter * rows * dim, bytes_accessed=8 * quarter * dim, transcendentals=4 * quarter * rows
+        ),
+        name="near_block",
+    )(in_vmem(centroids), in_vmem(near), in_vmem(swapped), row, *[in_vmem(value) for value in begun])
 
 
 def home_kernel(scale, c_ref, home, row, _, total, mass):
@@ -202,16 +233,9 @@
     own = own_rows(c_ref, total.shape[0])
     if arrived:
         table, nv = outs[2], plan["nv"]
-        core = core_index()
-        half_lead, direct, swapped = leads(nv, core)
         quarter = nv // 4
-        near, arrived = arrived[0], arrived[1:]
-        table[pl.ds(half_lead, 2 * quarter), :] = near[: 2 * quarter, :]
-        table[pl.ds(direct, quarter), :] = near[2 * quarter :, :]
-        places = [swapped]
-        half_lead, direct, swapped = leads(nv, 1 - core)
-        places += [nv + half_lead, nv + half_lead + quarter, nv + direct, nv + swapped]
-        for lead, ref in zip(places, arrived):
+        half_lead, direct, swapped = leads(nv, 1 - core_index())
+        for lead, ref in zip((half_lead, half_lead + quarter, direct, swapped), arrived):
             table[pl.ds(pl.multiple_of(lead, 64), quarter), :] = ref[...]
         pieces += (table,)
     for place in range(first, plan["early"]):
@@ -315,9 +339,11 @@
         parts = [lse, go(lse, (1, 2)), go(lse, (2, 1)), go(lse, 3)]
         begun = begin(centroids, home, lse, crossed[2], rows, scale)
         swapped = after(swapped, begun[1], *parts[1:])
-        near = [near, swapped] + crossed + [go(swapped, 0, 1)]
-        pieces = [home]
-        plan = dict(exchange=True, first=1, early=3, blocks=[(0, 0), (1, 0), (1, nv), (2, 0)])
+        crossed = crossed + [go(swapped, 0, 1)]
+        near, *begun = add_near(centroids, near, swapped, parts[1], begun, scale)
+        home, near = [home, near], crossed
+        pieces = home
+        plan = dict(exchange=True, first=2, early=3, blocks=[(i, 0) for i in range(4)])
     else:
         home, centroids = load(vectors, centroids)
         parts = lax.all_gather(partial(home, centroids, scale), "cent", axis=0, tiled=False)
@@ -335,7 +361,7 @@
     flops = 2 * nv * rows * dim
     early, late = plan["early"], items - plan["early"]
     params = pltpu.CompilerParams(vmem_limit_bytes=16 * MIB)
-    tables = [pltpu.VMEM((2 * nv, dim), jnp.bfloat16)] if near else []
+    tables = [pltpu.VMEM((nv, dim), jnp.bfloat16)] if near else []
     total, mass, *table = pl.pallas_call(
         functools.partial(early_kernel, dict(plan), scale),
         in_specs=[vmem] * (1 + len(begun) + early - plan["first"] + len(pieces) + len(near)),
@@ -354,7 +380,7 @@
 
     arrived = []
     if late:
-        far = after(far, *parts[1:], *near[2:])
+        far = after(far, swapped)
         arrived = [in_vmem(far), in_vmem(go(far, 0, 1))]
     fresh, expo, peak, part, *block = pl.pallas_call(
         functools.partial(late_kernel, dict(plan), scale),

time: 60.8 us -> 61 us (level)
    pallas_call x0 -> x1, Pallas kernels: none -> 1.55 us  [add_near(): pl.pallas_call(functools.partial(near_kernel, scale), in_specs=[vmem] * 6...]
    pallas_call x1, Pallas kernels: 2.81 us -> 1.55 us  [shards(): pl.pallas_call(functools.partial(early_kernel, dict(plan), scale), in_spe...]
  transfers between devices with their start and end apart: 22 -> 22, of which waited for: 13 -> 14; matrix products, arithmetic and copies ran while one was open for 0% -> 0% of each run, Pallas kernels for 14% -> 15%
where the time goes in v17:
time: 61 us; the launch traced here: 60.9 us
  starting transfers between devices  24.1 us (40%)
  waiting for transfers between devices  18.8 us (31%)
  Pallas kernels  16.8 us (28%)
  between operations  0.77 us (1%)
    ppermute x22, starting transfers between devices, send(): return lax.ppermute(value, BOTH, pairs)  24.1 us
    ppermute x22, waiting for transfers between devices, send(): return lax.ppermute(value, BOTH, pairs)  18.8 us
    pallas_call x1, Pallas kernels, shards(): pl.pallas_call(functools.partial(late_kernel, dict(plan), scale), in_spec...  3.82 us
    pallas_call x1, Pallas kernels, shards(): pl.pallas_call(functools.partial(last_kernel, dict(plan)), in_specs=[vmem...  2.71 us
    pallas_call x1, Pallas kernels, partial(): pl.pallas_call(functools.partial(partial_kernel, scale, min(256, k)), in_...  2.46 us
    pallas_call x1, Pallas kernels, load(): pl.pallas_call(load_kernel, in_specs=[hbm, hbm], out_specs=[vmem] * 2, ou...  2.09 us
    pallas_call x1, Pallas kernels, shards(): pl.pallas_call(functools.partial(early_kernel, dict(plan), scale), in_spe...  1.55 us
    pallas_call x1, Pallas kernels, add_near(): pl.pallas_call(functools.partial(near_kernel, scale), in_specs=[vmem] * 6...  1.55 us
  transfers between devices with their start and end apart: 22, of which 14 were waited for; matrix products, arithmetic and copies ran while one was open for 0% of the time, Pallas kernels for 15%

profile of v17, /device:TPU:0, one launch (start us, length us, event | category | flops | bytes accessed | tf_op | source)
XLA Modules:
  0.0 60.9 jit_solution(5324119086490468849)
XLA Ops:
  0.6 1.3 %outgoing.1 = bf16[576,1024]{1,0:T(8,128)(2,1)S(1)} custom-call(bf16[768,1024]{1,0:T(8,128)(2,1)} %v_hbm.3), custom_call_target="tpu_custom_call" | custom-call | bytes 1572864 | tf_op jit(solution)/shard_map/outgoing/pallas_call | solution.py:79
  1.9 3.0 %collective-permute-start = (bf16[576,1024]{1,0:T(8,128)(2,1)S(1)}, bf16[576,1024]{1,0:T(8,128)(2,1)S(1)}, u32[]{:S(2)}, u32[]{:S(2)}) collective-permute-start(bf16[576,1024]{1,0:T(8,128)(2,1)S(1)} %outgoing.1), channel_id=1, source_target_pairs={{0,8},{1,17},{2,10},{3,19},{4,12},{5,21},{6,14},{7,23},{8,0},{9,25... | collective-permute-start | bytes 3538952 | tf_op jit(solution)/shard_map/ppermute | solution.py:298
  4.9 2.1 %load.1 = (bf16[768,1024]{1,0:T(8,128)(2,1)S(1)}, bf16[1024,1024]{1,0:T(8,128)(2,1)S(1)}) custom-call(bf16[768,1024]{1,0:T(8,128)(2,1)} %v_hbm.3, bf16[1024,1024]{1,0:T(8,128)(2,1)} %c_hbm.1), custom_call_target="tpu_custom_call" | custom-call | bytes 7340032 | tf_op jit(solution)/shard_map/load/pallas_call | solution.py:102
  7.0 2.5 %partial_lse.1 = f32[1,768]{1,0:T(1,128)S(1)} custom-call(bf16[768,1024]{1,0:T(8,128)(2,1)S(1)} %get-tuple-element.18.v_ref.home.refs_3_.refs_1_.refs_0_, bf16[1024,1024]{1,0:T(8,128)(2,1)S(1)} %get-tuple-element.17.c_ref), custom_call_target="tpu_custom_call" | custom-call | flops 1610612736 | bytes 3670016 | tf_op jit(solution)/shard_map/partial_lse/pallas_call | solution.py:129
  9.6 1.1 %collective-permute-done.1 = f32[1,768]{1,0:T(1,128)S(1)} collective-permute-done((f32[1,768]{1,0:T(1,128)S(1)}, f32[1,768]{1,0:T(1,128)S(1)}, u32[]{:S(2)}, u32[]{:S(2)}) %collective-permute-start.1) | collective-permute-done | bytes 3104 | tf_op jit(solution)/shard_map/ppermute | solution.py:298
  10.7 3.7 %collective-permute-start.4 = (f32[1,768]{1,0:T(1,128)S(1)}, f32[1,768]{1,0:T(1,128)S(1)}, u32[]{:S(2)}, u32[]{:S(2)}) collective-permute-start(f32[1,768]{1,0:T(1,128)S(1)} %log_add_fusion.3), channel_id=1, source_target_pairs={{0,6},{1,7},{2,4},{3,5},{4,2},{5,3},{6,0},{7,1},{8,14},{9,15},{10,... | collective-permute-start | bytes 9224 | tf_op jit(solution)/shard_map/ppermute | solution.py:298
  16.2 2.7 %collective-permute-done.3 = f32[1,768]{1,0:T(1,128)S(1)} collective-permute-done((f32[1,768]{1,0:T(1,128)S(1)}, f32[1,768]{1,0:T(1,128)S(1)}, u32[]{:S(2)}, u32[]{:S(2)}) %collective-permute-start.3) | collective-permute-done | bytes 3104 | tf_op jit(solution)/shard_map/ppermute | solution.py:298
  19.2 2.1 %collective-permute-start.13 = (bf16[384,1024]{1,0:T(8,128)(2,1)S(1)}, bf16[384,1024]{1,0:T(8,128)(2,1)S(1)}, u32[]{:S(2)}, u32[]{:S(2)}) collective-permute-start(bf16[384,1024]{1,0:T(8,128)(2,1)S(1)} %slice.19), channel_id=1, source_target_pairs={{0,16},{1,9},{2,18},{3,11},{4,20},{5,13},{6,22},{7,15},{8,24},{9,1... | collective-permute-start | bytes 2359304 | tf_op jit(solution)/shard_map/ppermute | solution.py:298
  22.0 1.6 %collective-permute-start.5 = (bf16[192,1024]{1,0:T(8,128)(2,1)S(1)}, bf16[192,1024]{1,0:T(8,128)(2,1)S(1)}, u32[]{:S(2)}, u32[]{:S(2)}) collective-permute-start(bf16[192,1024]{1,0:T(8,128)(2,1)S(1)} %get-tuple-element.34), channel_id=1, source_target_pairs={{0,2},{1,3},{2,0},{3,1},{4,6},{5,7},{6,4},{7,5},{8,10},{9,11},{10,... | collective-permute-start | bytes 1179656 | tf_op jit(solution)/shard_map/ppermute | solution.py:298
  24.3 1.4 %collective-permute-start.11 = (f32[1,768]{1,0:T(1,128)S(1)}, f32[1,768]{1,0:T(1,128)S(1)}, u32[]{:S(2)}, u32[]{:S(2)}) collective-permute-start(f32[1,768]{1,0:T(1,128)S(1)} %after.5.row), channel_id=1, source_target_pairs={{0,24},{1,25},{2,26},{3,27},{4,28},{5,29},{6,30},{7,31},{8,16},{9,... | collective-permute-start | bytes 9224 | tf_op jit(solution)/shard_map/ppermute | solution.py:298
  25.7 1.5 %collective-permute-start.10 = (f32[1,768]{1,0:T(1,128)S(1)}, f32[1,768]{1,0:T(1,128)S(1)}, u32[]{:S(2)}, u32[]{:S(2)}) collective-permute-start(f32[1,768]{1,0:T(1,128)S(1)} %after.5.row), channel_id=1, source_target_pairs={{0,16},{1,9},{2,18},{3,11},{4,20},{5,13},{6,22},{7,15},{8,24},{9,1... | collective-permute-start | bytes 9224 | tf_op jit(solution)/shard_map/ppermute | solution.py:298
  27.8 1.4 %home_block.1 = (f32[256,1024]{1,0:T(8,128)S(1)}, f32[256,1]{1,0:T(8,128)S(1)}) custom-call(bf16[1024,1024]{1,0:T(8,128)(2,1)S(1)} %get-tuple-element.17.c_ref, bf16[768,1024]{1,0:T(8,128)(2,1)S(1)} %get-tuple-element.18.v_ref.home.refs_3_.refs_1_.refs_0_, f32[1,768]{1,0:T(1,128)S(1)} %after.5.row, bf16[192,1024]{1,0:T(8,128)(2,1)S(1)} %collective-permute-done.8.refs_3_._.refs_7_), custom_call_target="tpu_custom_call" | custom-call | flops 805306368 | bytes 1572864 | tf_op jit(solution)/shard_map/home_block/pallas_call | solution.py:175
  29.1 4.3 %collective-permute-done.5.refs_0_ = bf16[192,1024]{1,0:T(8,128)(2,1)S(1)} collective-permute-done((bf16[192,1024]{1,0:T(8,128)(2,1)S(1)}, bf16[192,1024]{1,0:T(8,128)(2,1)S(1)}, u32[]{:S(2)}, u32[]{:S(2)}) %collective-permute-start.5) | collective-permute-done | bytes 393248 | tf_op jit(solution)/shard_map/ppermute | solution.py:298
  34.1 1.6 %near_block.1 = (bf16[768,1024]{1,0:T(8,128)(2,1)S(1)}, f32[256,1024]{1,0:T(8,128)S(1)}, f32[256,1]{1,0:T(8,128)S(1)}) custom-call(bf16[1024,1024]{1,0:T(8,128)(2,1)S(1)} %get-tuple-element.17.c_ref, bf16[576,1024]{1,0:T(8,128)(2,1)S(1)} %after.4.near, bf16[192,1024]{1,0:T(8,128)(2,1)S(1)} %after.6.last.refs_1_, ...), custom_call_target="tpu_custom_call" | custom-call | flops 805306368 | bytes 1572864 | tf_op jit(solution)/shard_map/near_block/pallas_call | solution.py:202
  36.4 1.6 %early_blocks.1 = (f32[256,1024]{1,0:T(8,128)S(1)}, f32[256,1]{1,0:T(8,128)S(1)}, bf16[768,1024]{1,0:T(8,128)(2,1)S(1)}) custom-call(bf16[1024,1024]{1,0:T(8,128)(2,1)S(1)} %get-tuple-element.17.c_ref, f32[256,1024]{1,0:T(8,128)S(1)} %get-tuple-element.21.refs_0_, f32[256,1]{1,0:T(8,128)S(1)} %get-tuple-element.22.refs_1_, ...), custom_call_target="tpu_custom_call" | custom-call | tf_op jit(solution)/shard_map/early_blocks/pallas_call | solution.py:365
  38.0 3.8 %late_blocks.1 = (bf16[256,1024]{1,0:T(8,128)(2,1)S(1)}, f32[4,256,768]{2,1,0:T(8,128)S(1)}, f32[4,768]{1,0:T(4,128)S(1)}, f32[4,768]{1,0:T(4,128)S(1)}, bf16[768,1024]{1,0:T(8,128)(2,1)S(1)}) custom-call(bf16[1024,1024]{1,0:T(8,128)(2,1)S(1)} %get-tuple-element.17.c_ref, f32[256,1024]{1,0:T(8,128)S(1)} %get-tuple-element.24.total, ...), custom_call_target="tpu_custom_call" | custom-call | flops 2415919104 | bytes 1572864 | tf_op jit(solution)/shard_map/late_blocks/pallas_call | solution.py:385
  43.1 3.7 %collective-permute-start.18 = (f32[4,768]{1,0:T(4,128)S(1)}, f32[4,768]{1,0:T(4,128)S(1)}, u32[]{:S(2)}, u32[]{:S(2)}) collective-permute-start(f32[4,768]{1,0:T(4,128)S(1)} %log_add_fusion.1), channel_id=1, source_target_pairs={{0,6},{1,7},{2,4},{3,5},{4,2},{5,3},{6,0},{7,1},{8,14},{9,15},{10,... | collective-permute-start | bytes 36872 | tf_op jit(solution)/shard_map/ppermute | solution.py:298
  47.5 1.1 %collective-permute-done.18 = f32[4,768]{1,0:T(4,128)S(1)} collective-permute-done((f32[4,768]{1,0:T(4,128)S(1)}, f32[4,768]{1,0:T(4,128)S(1)}, u32[]{:S(2)}, u32[]{:S(2)}) %collective-permute-start.18) | collective-permute-done | bytes 12320 | tf_op jit(solution)/shard_map/ppermute | solution.py:298
  48.6 2.7 %collective-permute-done.17 = f32[4,768]{1,0:T(4,128)S(1)} collective-permute-done((f32[4,768]{1,0:T(4,128)S(1)}, f32[4,768]{1,0:T(4,128)S(1)}, u32[]{:S(2)}, u32[]{:S(2)}) %collective-permute-start.17) | collective-permute-done | bytes 12320 | tf_op jit(solution)/shard_map/ppermute | solution.py:298
  51.4 1.5 %collective-permute-start.21 = (f32[4,768]{1,0:T(4,128)S(1)}, f32[4,768]{1,0:T(4,128)S(1)}, u32[]{:S(2)}, u32[]{:S(2)}) collective-permute-start(f32[4,768]{1,0:T(4,128)S(1)} %log_add_fusion), channel_id=1, source_target_pairs={{0,24},{1,25},{2,26},{3,27},{4,28},{5,29},{6,30},{7,31},{8,16},{9,... | collective-permute-start | bytes 36872 | tf_op jit(solution)/shard_map/ppermute | solution.py:298
  52.9 1.5 %collective-permute-start.20 = (f32[4,768]{1,0:T(4,128)S(1)}, f32[4,768]{1,0:T(4,128)S(1)}, u32[]{:S(2)}, u32[]{:S(2)}) collective-permute-start(f32[4,768]{1,0:T(4,128)S(1)} %log_add_fusion), channel_id=1, source_target_pairs={{0,16},{1,17},{2,18},{3,19},{4,20},{5,21},{6,22},{7,23},{8,24},{9,... | collective-permute-start | bytes 36872 | tf_op jit(solution)/shard_map/ppermute | solution.py:298
  55.0 1.1 %collective-permute-done.21 = f32[4,768]{1,0:T(4,128)S(1)} collective-permute-done((f32[4,768]{1,0:T(4,128)S(1)}, f32[4,768]{1,0:T(4,128)S(1)}, u32[]{:S(2)}, u32[]{:S(2)}) %collective-permute-start.21) | collective-permute-done | bytes 12320 | tf_op jit(solution)/shard_map/ppermute | solution.py:298
  56.6 1.5 %collective-permute-done.19 = f32[4,768]{1,0:T(4,128)S(1)} collective-permute-done((f32[4,768]{1,0:T(4,128)S(1)}, f32[4,768]{1,0:T(4,128)S(1)}, u32[]{:S(2)}, u32[]{:S(2)}) %collective-permute-start.19) | collective-permute-done | bytes 12320 | tf_op jit(solution)/shard_map/ppermute | solution.py:298
  58.1 2.7 %last_iteration.1 = (bf16[256,1024]{1,0:T(8,128)(2,1)}, f32[768]{0:T(1024)}) custom-call(bf16[256,1024]{1,0:T(8,128)(2,1)S(1)} %get-tuple-element.27.old_ref, f32[4,256,768]{2,1,0:T(8,128)S(1)} %get-tuple-element.28.expo_ref, f32[4,768]{1,0:T(4,128)S(1)} %get-tuple-element.29.peak_ref, f32[1,4,768]{2,1,0:T(4,128)S(1)} %add_bitcast_fusion.parts, ...), custom_call_target="tpu_custom_call" | custom-call | flops 1610612736 | bytes 524288 | tf_op jit(solution)/shard_map/last_iteration/pallas_call | solution.py:412
  (39 shorter events, 8.6 us)
Async XLA Ops:
  1.9 17.2 %collective-permute-start = (bf16[576,1024]{1,0:T(8,128)(2,1)S(1)}, bf16[576,1024]{1,0:T(8,128)(2,1)S(1)}, u32[]{:S(2)}, u32[]{:S(2)}) collective-permute-start(bf16[576,1024]{1,0:T(8,128)(2,1)S(1)} %outgoing.1), channel_id=1, source_target_pairs={{0,8},{1,17},{2,10},{3,19},{4,12},{5,21},{6,14},{7,23},{8,0},{9,25... | collective-permute-start | bytes 3538952 | tf_op jit(solution)/shard_map/ppermute | solution.py:298
  9.5 1.2 %collective-permute-start.1 = (f32[1,768]{1,0:T(1,128)S(1)}, f32[1,768]{1,0:T(1,128)S(1)}, u32[]{:S(2)}, u32[]{:S(2)}) collective-permute-start(f32[1,768]{1,0:T(1,128)S(1)} %partial_lse.1), channel_id=1, source_target_pairs={{0,1},{1,0},{2,3},{3,2},{4,5},{5,4},{6,7},{7,6},{8,9},{9,8},{10,11... | collective-permute-start | bytes 9224 | tf_op jit(solution)/shard_map/ppermute | solution.py:298
  10.7 5.5 %collective-permute-start.4 = (f32[1,768]{1,0:T(1,128)S(1)}, f32[1,768]{1,0:T(1,128)S(1)}, u32[]{:S(2)}, u32[]{:S(2)}) collective-permute-start(f32[1,768]{1,0:T(1,128)S(1)} %log_add_fusion.3), channel_id=1, source_target_pairs={{0,6},{1,7},{2,4},{3,5},{4,2},{5,3},{6,0},{7,1},{8,14},{9,15},{10,... | collective-permute-start | bytes 9224 | tf_op jit(solution)/shard_map/ppermute | solution.py:298
  14.4 4.5 %collective-permute-start.3 = (f32[1,768]{1,0:T(1,128)S(1)}, f32[1,768]{1,0:T(1,128)S(1)}, u32[]{:S(2)}, u32[]{:S(2)}) collective-permute-start(f32[1,768]{1,0:T(1,128)S(1)} %log_add_fusion.3), channel_id=1, source_target_pairs={{0,4},{1,5},{2,6},{3,7},{4,0},{5,1},{6,2},{7,3},{8,12},{9,13},{10,... | collective-permute-start | bytes 9224 | tf_op jit(solution)/shard_map/ppermute | solution.py:298
  14.4 4.5 %collective-permute-start.2 = (f32[1,768]{1,0:T(1,128)S(1)}, f32[1,768]{1,0:T(1,128)S(1)}, u32[]{:S(2)}, u32[]{:S(2)}) collective-permute-start(f32[1,768]{1,0:T(1,128)S(1)} %log_add_fusion.3), channel_id=1, source_target_pairs={{0,2},{1,3},{2,0},{3,1},{4,6},{5,7},{6,4},{7,5},{8,10},{9,11},{10,... | collective-permute-start | bytes 9224 | tf_op jit(solution)/shard_map/ppermute | solution.py:298
  19.2 14.3 %collective-permute-start.13 = (bf16[384,1024]{1,0:T(8,128)(2,1)S(1)}, bf16[384,1024]{1,0:T(8,128)(2,1)S(1)}, u32[]{:S(2)}, u32[]{:S(2)}) collective-permute-start(bf16[384,1024]{1,0:T(8,128)(2,1)S(1)} %slice.19), channel_id=1, source_target_pairs={{0,16},{1,9},{2,18},{3,11},{4,20},{5,13},{6,22},{7,15},{8,24},{9,1... | collective-permute-start | bytes 2359304 | tf_op jit(solution)/shard_map/ppermute | solution.py:298
  21.4 2.2 %collective-permute-start.7 = (bf16[192,1024]{1,0:T(8,128)(2,1)S(1)}, bf16[192,1024]{1,0:T(8,128)(2,1)S(1)}, u32[]{:S(2)}, u32[]{:S(2)}) collective-permute-start(bf16[192,1024]{1,0:T(8,128)(2,1)S(1)} %get-tuple-element.32), channel_id=1, source_target_pairs={{0,1},{1,0},{2,3},{3,2},{4,5},{5,4},{6,7},{7,6},{8,9},{9,8},{10,11... | collective-permute-start | bytes 1179656 | tf_op jit(solution)/shard_map/ppermute | solution.py:298
  21.4 2.3 %collective-permute-start.6 = (bf16[192,1024]{1,0:T(8,128)(2,1)S(1)}, bf16[192,1024]{1,0:T(8,128)(2,1)S(1)}, u32[]{:S(2)}, u32[]{:S(2)}) collective-permute-start(bf16[192,1024]{1,0:T(8,128)(2,1)S(1)} %get-tuple-element.33), channel_id=1, source_target_pairs={{0,1},{1,0},{2,3},{3,2},{4,5},{5,4},{6,7},{7,6},{8,9},{9,8},{10,11... | collective-permute-start | bytes 1179656 | tf_op jit(solution)/shard_map/ppermute | solution.py:298
  21.9 2.3 %collective-permute-start.8 = (bf16[192,1024]{1,0:T(8,128)(2,1)S(1)}, bf16[192,1024]{1,0:T(8,128)(2,1)S(1)}, u32[]{:S(2)}, u32[]{:S(2)}) collective-permute-start(bf16[192,1024]{1,0:T(8,128)(2,1)S(1)} %get-tuple-element.34), channel_id=1, source_target_pairs={{0,1},{1,0},{2,3},{3,2},{4,5},{5,4},{6,7},{7,6},{8,9},{9,8},{10,11... | collective-permute-start | bytes 1179656 | tf_op jit(solution)/shard_map/ppermute | solution.py:298
  22.0 11.5 %collective-permute-start.5 = (bf16[192,1024]{1,0:T(8,128)(2,1)S(1)}, bf16[192,1024]{1,0:T(8,128)(2,1)S(1)}, u32[]{:S(2)}, u32[]{:S(2)}) collective-permute-start(bf16[192,1024]{1,0:T(8,128)(2,1)S(1)} %get-tuple-element.34), channel_id=1, source_target_pairs={{0,2},{1,3},{2,0},{3,1},{4,6},{5,7},{6,4},{7,5},{8,10},{9,11},{10,... | collective-permute-start | bytes 1179656 | tf_op jit(solution)/shard_map/ppermute | solution.py:298
  24.3 9.2 %collective-permute-start.11 = (f32[1,768]{1,0:T(1,128)S(1)}, f32[1,768]{1,0:T(1,128)S(1)}, u32[]{:S(2)}, u32[]{:S(2)}) collective-permute-start(f32[1,768]{1,0:T(1,128)S(1)} %after.5.row), channel_id=1, source_target_pairs={{0,24},{1,25},{2,26},{3,27},{4,28},{5,29},{6,30},{7,31},{8,16},{9,... | collective-permute-start | bytes 9224 | tf_op jit(solution)/shard_map/ppermute | solution.py:298
  25.7 7.8 %collective-permute-start.10 = (f32[1,768]{1,0:T(1,128)S(1)}, f32[1,768]{1,0:T(1,128)S(1)}, u32[]{:S(2)}, u32[]{:S(2)}) collective-permute-start(f32[1,768]{1,0:T(1,128)S(1)} %after.5.row), channel_id=1, source_target_pairs={{0,16},{1,9},{2,18},{3,11},{4,20},{5,13},{6,22},{7,15},{8,24},{9,1... | collective-permute-start | bytes 9224 | tf_op jit(solution)/shard_map/ppermute | solution.py:298
  27.2 6.3 %collective-permute-start.9 = (f32[1,768]{1,0:T(1,128)S(1)}, f32[1,768]{1,0:T(1,128)S(1)}, u32[]{:S(2)}, u32[]{:S(2)}) collective-permute-start(f32[1,768]{1,0:T(1,128)S(1)} %after.5.row), channel_id=1, source_target_pairs={{0,8},{1,17},{2,10},{3,19},{4,12},{5,21},{6,14},{7,23},{8,0},{9,25... | collective-permute-start | bytes 9224 | tf_op jit(solution)/shard_map/ppermute | solution.py:298
  33.5 4.5 %collective-permute-start.14 = (bf16[384,1024]{1,0:T(8,128)(2,1)S(1)}, bf16[384,1024]{1,0:T(8,128)(2,1)S(1)}, u32[]{:S(2)}, u32[]{:S(2)}) collective-permute-start(bf16[384,1024]{1,0:T(8,128)(2,1)S(1)} %after.7.refs_4_), channel_id=1, source_target_pairs={{0,1},{1,0},{2,3},{3,2},{4,5},{5,4},{6,7},{7,6},{8,9},{9,8},{10,11... | collective-permute-start | bytes 2359304 | tf_op jit(solution)/shard_map/ppermute | solution.py:298
  33.6 2.8 %collective-permute-start.12 = (bf16[192,1024]{1,0:T(8,128)(2,1)S(1)}, bf16[192,1024]{1,0:T(8,128)(2,1)S(1)}, u32[]{:S(2)}, u32[]{:S(2)}) collective-permute-start(bf16[192,1024]{1,0:T(8,128)(2,1)S(1)} %after.6.last.refs_1_), channel_id=1, source_target_pairs={{0,1},{1,0},{2,3},{3,2},{4,5},{5,4},{6,7},{7,6},{8,9},{9,8},{10,11... | collective-permute-start | bytes 1179656 | tf_op jit(solution)/shard_map/ppermute | solution.py:298
  41.8 1.2 %collective-permute-start.15 = (f32[4,768]{1,0:T(4,128)S(1)}, f32[4,768]{1,0:T(4,128)S(1)}, u32[]{:S(2)}, u32[]{:S(2)}) collective-permute-start(f32[4,768]{1,0:T(4,128)S(1)} %get-tuple-element.30), channel_id=1, source_target_pairs={{0,1},{1,0},{2,3},{3,2},{4,5},{5,4},{6,7},{7,6},{8,9},{9,8},{10,11... | collective-permute-start | bytes 36872 | tf_op jit(solution)/shard_map/ppermute | solution.py:298
  43.1 5.6 %collective-permute-start.18 = (f32[4,768]{1,0:T(4,128)S(1)}, f32[4,768]{1,0:T(4,128)S(1)}, u32[]{:S(2)}, u32[]{:S(2)}) collective-permute-start(f32[4,768]{1,0:T(4,128)S(1)} %log_add_fusion.1), channel_id=1, source_target_pairs={{0,6},{1,7},{2,4},{3,5},{4,2},{5,3},{6,0},{7,1},{8,14},{9,15},{10,... | collective-permute-start | bytes 36872 | tf_op jit(solution)/shard_map/ppermute | solution.py:298
  46.8 4.6 %collective-permute-start.17 = (f32[4,768]{1,0:T(4,128)S(1)}, f32[4,768]{1,0:T(4,128)S(1)}, u32[]{:S(2)}, u32[]{:S(2)}) collective-permute-start(f32[4,768]{1,0:T(4,128)S(1)} %log_add_fusion.1), channel_id=1, source_target_pairs={{0,4},{1,5},{2,6},{3,7},{4,0},{5,1},{6,2},{7,3},{8,12},{9,13},{10,... | collective-permute-start | bytes 36872 | tf_op jit(solution)/shard_map/ppermute | solution.py:298
  46.8 4.6 %collective-permute-start.16 = (f32[4,768]{1,0:T(4,128)S(1)}, f32[4,768]{1,0:T(4,128)S(1)}, u32[]{:S(2)}, u32[]{:S(2)}) collective-permute-start(f32[4,768]{1,0:T(4,128)S(1)} %log_add_fusion.1), channel_id=1, source_target_pairs={{0,2},{1,3},{2,0},{3,1},{4,6},{5,7},{6,4},{7,5},{8,10},{9,11},{10,... | collective-permute-start | bytes 36872 | tf_op jit(solution)/shard_map/ppermute | solution.py:298
  51.4 4.7 %collective-permute-start.21 = (f32[4,768]{1,0:T(4,128)S(1)}, f32[4,768]{1,0:T(4,128)S(1)}, u32[]{:S(2)}, u32[]{:S(2)}) collective-permute-start(f32[4,768]{1,0:T(4,128)S(1)} %log_add_fusion), channel_id=1, source_target_pairs={{0,24},{1,25},{2,26},{3,27},{4,28},{5,29},{6,30},{7,31},{8,16},{9,... | collective-permute-start | bytes 36872 | tf_op jit(solution)/shard_map/ppermute | solution.py:298
  52.9 3.7 %collective-permute-start.20 = (f32[4,768]{1,0:T(4,128)S(1)}, f32[4,768]{1,0:T(4,128)S(1)}, u32[]{:S(2)}, u32[]{:S(2)}) collective-permute-start(f32[4,768]{1,0:T(4,128)S(1)} %log_add_fusion), channel_id=1, source_target_pairs={{0,16},{1,17},{2,18},{3,19},{4,20},{5,21},{6,22},{7,23},{8,24},{9,... | collective-permute-start | bytes 36872 | tf_op jit(solution)/shard_map/ppermute | solution.py:298
  54.4 3.7 %collective-permute-start.19 = (f32[4,768]{1,0:T(4,128)S(1)}, f32[4,768]{1,0:T(4,128)S(1)}, u32[]{:S(2)}, u32[]{:S(2)}) collective-permute-start(f32[4,768]{1,0:T(4,128)S(1)} %log_add_fusion), channel_id=1, source_target_pairs={{0,8},{1,9},{2,10},{3,11},{4,12},{5,13},{6,14},{7,15},{8,0},{9,1},... | collective-permute-start | bytes 36872 | tf_op jit(solution)/shard_map/ppermute | solution.py:298

commit v18 on v17

--- a/solution.py
+++ b/solution.py
@@ -380,7 +380,7 @@
 
     arrived = []
     if late:
-        far = after(far, swapped)
+        far = after(far, begun[1])
         arrived = [in_vmem(far), in_vmem(go(far, 0, 1))]
     fresh, expo, peak, part, *block = pl.pallas_call(
         functools.partial(late_kernel, dict(plan), scale),

time: 61 us -> 62.6 us (1.026)
  waiting for transfers between devices: 18.8 us -> 20.4 us
    ppermute x22, waiting for transfers between devices: 18.8 us -> 20.4 us  [send(): return lax.ppermute(value, BOTH, pairs)]
  transfers between devices with their start and end apart: 22 -> 22, of which waited for: 14 -> 14; matrix products, arithmetic and copies ran while one was open for 0% -> 0% of each run, Pallas kernels for 15% -> 14%
where the time goes in v18:
time: 62.6 us; the launch traced here: 62.4 us
  starting transfers between devices  24.1 us (38%)
  waiting for transfers between devices  20.4 us (33%)
  Pallas kernels  16.8 us (27%)
  between operations  0.77 us (1%)
    ppermute x22, starting transfers between devices, send(): return lax.ppermute(value, BOTH, pairs)  24.1 us
    ppermute x22, waiting for transfers between devices, send(): return lax.ppermute(value, BOTH, pairs)  20.4 us
    pallas_call x1, Pallas kernels, shards(): pl.pallas_call(functools.partial(late_kernel, dict(plan), scale), in_spec...  3.83 us
    pallas_call x1, Pallas kernels, shards(): pl.pallas_call(functools.partial(last_kernel, dict(plan)), in_specs=[vmem...  2.71 us
    pallas_call x1, Pallas kernels, partial(): pl.pallas_call(functools.partial(partial_kernel, scale, min(256, k)), in_...  2.46 us
    pallas_call x1, Pallas kernels, load(): pl.pallas_call(load_kernel, in_specs=[hbm, hbm], out_specs=[vmem] * 2, ou...  2.09 us
    pallas_call x1, Pallas kernels, shards(): pl.pallas_call(functools.partial(early_kernel, dict(plan), scale), in_spe...  1.55 us
    pallas_call x1, Pallas kernels, add_near(): pl.pallas_call(functools.partial(near_kernel, scale), in_specs=[vmem] * 6...  1.54 us
  transfers between devices with their start and end apart: 22, of which 14 were waited for; matrix products, arithmetic and copies ran while one was open for 0% of the time, Pallas kernels for 14%

profile of v18, /device:TPU:0, one launch (start us, length us, event | category | flops | bytes accessed | tf_op | source)
XLA Modules:
  0.0 62.4 jit_solution(12724923597652402094)
XLA Ops:
  0.6 1.3 %outgoing.1 = bf16[576,1024]{1,0:T(8,128)(2,1)S(1)} custom-call(bf16[768,1024]{1,0:T(8,128)(2,1)} %v_hbm.3), custom_call_target="tpu_custom_call" | custom-call | bytes 1572864 | tf_op jit(solution)/shard_map/outgoing/pallas_call | solution.py:79
  1.9 3.0 %collective-permute-start = (bf16[576,1024]{1,0:T(8,128)(2,1)S(1)}, bf16[576,1024]{1,0:T(8,128)(2,1)S(1)}, u32[]{:S(2)}, u32[]{:S(2)}) collective-permute-start(bf16[576,1024]{1,0:T(8,128)(2,1)S(1)} %outgoing.1), channel_id=1, source_target_pairs={{0,8},{1,17},{2,10},{3,19},{4,12},{5,21},{6,14},{7,23},{8,0},{9,25... | collective-permute-start | bytes 3538952 | tf_op jit(solution)/shard_map/ppermute | solution.py:298
  4.9 2.1 %load.1 = (bf16[768,1024]{1,0:T(8,128)(2,1)S(1)}, bf16[1024,1024]{1,0:T(8,128)(2,1)S(1)}) custom-call(bf16[768,1024]{1,0:T(8,128)(2,1)} %v_hbm.3, bf16[1024,1024]{1,0:T(8,128)(2,1)} %c_hbm.1), custom_call_target="tpu_custom_call" | custom-call | bytes 7340032 | tf_op jit(solution)/shard_map/load/pallas_call | solution.py:102
  7.0 2.5 %partial_lse.1 = f32[1,768]{1,0:T(1,128)S(1)} custom-call(bf16[768,1024]{1,0:T(8,128)(2,1)S(1)} %get-tuple-element.18.v_ref.home.refs_3_.refs_1_.refs_0_, bf16[1024,1024]{1,0:T(8,128)(2,1)S(1)} %get-tuple-element.17.c_ref), custom_call_target="tpu_custom_call" | custom-call | flops 1610612736 | bytes 3670016 | tf_op jit(solution)/shard_map/partial_lse/pallas_call | solution.py:129
  9.6 1.1 %collective-permute-done.1 = f32[1,768]{1,0:T(1,128)S(1)} collective-permute-done((f32[1,768]{1,0:T(1,128)S(1)}, f32[1,768]{1,0:T(1,128)S(1)}, u32[]{:S(2)}, u32[]{:S(2)}) %collective-permute-start.1) | collective-permute-done | bytes 3104 | tf_op jit(solution)/shard_map/ppermute | solution.py:298
  10.7 3.7 %collective-permute-start.4 = (f32[1,768]{1,0:T(1,128)S(1)}, f32[1,768]{1,0:T(1,128)S(1)}, u32[]{:S(2)}, u32[]{:S(2)}) collective-permute-start(f32[1,768]{1,0:T(1,128)S(1)} %log_add_fusion.3), channel_id=1, source_target_pairs={{0,6},{1,7},{2,4},{3,5},{4,2},{5,3},{6,0},{7,1},{8,14},{9,15},{10,... | collective-permute-start | bytes 9224 | tf_op jit(solution)/shard_map/ppermute | solution.py:298
  16.2 2.7 %collective-permute-done.3 = f32[1,768]{1,0:T(1,128)S(1)} collective-permute-done((f32[1,768]{1,0:T(1,128)S(1)}, f32[1,768]{1,0:T(1,128)S(1)}, u32[]{:S(2)}, u32[]{:S(2)}) %collective-permute-start.3) | collective-permute-done | bytes 3104 | tf_op jit(solution)/shard_map/ppermute | solution.py:298
  19.2 2.1 %collective-permute-start.13 = (bf16[384,1024]{1,0:T(8,128)(2,1)S(1)}, bf16[384,1024]{1,0:T(8,128)(2,1)S(1)}, u32[]{:S(2)}, u32[]{:S(2)}) collective-permute-start(bf16[384,1024]{1,0:T(8,128)(2,1)S(1)} %slice.19), channel_id=1, source_target_pairs={{0,16},{1,9},{2,18},{3,11},{4,20},{5,13},{6,22},{7,15},{8,24},{9,1... | collective-permute-start | bytes 2359304 | tf_op jit(solution)/shard_map/ppermute | solution.py:298
  22.0 1.6 %collective-permute-start.5 = (bf16[192,1024]{1,0:T(8,128)(2,1)S(1)}, bf16[192,1024]{1,0:T(8,128)(2,1)S(1)}, u32[]{:S(2)}, u32[]{:S(2)}) collective-permute-start(bf16[192,1024]{1,0:T(8,128)(2,1)S(1)} %get-tuple-element.34), channel_id=1, source_target_pairs={{0,2},{1,3},{2,0},{3,1},{4,6},{5,7},{6,4},{7,5},{8,10},{9,11},{10,... | collective-permute-start | bytes 1179656 | tf_op jit(solution)/shard_map/ppermute | solution.py:298
  24.3 1.4 %collective-permute-start.11 = (f32[1,768]{1,0:T(1,128)S(1)}, f32[1,768]{1,0:T(1,128)S(1)}, u32[]{:S(2)}, u32[]{:S(2)}) collective-permute-start(f32[1,768]{1,0:T(1,128)S(1)} %after.5.row), channel_id=1, source_target_pairs={{0,24},{1,25},{2,26},{3,27},{4,28},{5,29},{6,30},{7,31},{8,16},{9,... | collective-permute-start | bytes 9224 | tf_op jit(solution)/shard_map/ppermute | solution.py:298
  25.7 1.5 %collective-permute-start.10 = (f32[1,768]{1,0:T(1,128)S(1)}, f32[1,768]{1,0:T(1,128)S(1)}, u32[]{:S(2)}, u32[]{:S(2)}) collective-permute-start(f32[1,768]{1,0:T(1,128)S(1)} %after.5.row), channel_id=1, source_target_pairs={{0,16},{1,9},{2,18},{3,11},{4,20},{5,13},{6,22},{7,15},{8,24},{9,1... | collective-permute-start | bytes 9224 | tf_op jit(solution)/shard_map/ppermute | solution.py:298
  27.8 1.4 %home_block.1 = (f32[256,1024]{1,0:T(8,128)S(1)}, f32[256,1]{1,0:T(8,128)S(1)}) custom-call(bf16[1024,1024]{1,0:T(8,128)(2,1)S(1)} %get-tuple-element.17.c_ref, bf16[768,1024]{1,0:T(8,128)(2,1)S(1)} %get-tuple-element.18.v_ref.home.refs_3_.refs_1_.refs_0_, f32[1,768]{1,0:T(1,128)S(1)} %after.5.row, bf16[192,1024]{1,0:T(8,128)(2,1)S(1)} %collective-permute-done.8.refs_3_._.refs_7_), custom_call_target="tpu_custom_call" | custom-call | flops 805306368 | bytes 1572864 | tf_op jit(solution)/shard_map/home_block/pallas_call | solution.py:175
  29.1 4.3 %collective-permute-done.5.refs_0_ = bf16[192,1024]{1,0:T(8,128)(2,1)S(1)} collective-permute-done((bf16[192,1024]{1,0:T(8,128)(2,1)S(1)}, bf16[192,1024]{1,0:T(8,128)(2,1)S(1)}, u32[]{:S(2)}, u32[]{:S(2)}) %collective-permute-start.5) | collective-permute-done | bytes 393248 | tf_op jit(solution)/shard_map/ppermute | solution.py:298
  33.5 1.5 %near_block.1 = (bf16[768,1024]{1,0:T(8,128)(2,1)S(1)}, f32[256,1024]{1,0:T(8,128)S(1)}, f32[256,1]{1,0:T(8,128)S(1)}) custom-call(bf16[1024,1024]{1,0:T(8,128)(2,1)S(1)} %get-tuple-element.17.c_ref, bf16[576,1024]{1,0:T(8,128)(2,1)S(1)} %after.4.near, bf16[192,1024]{1,0:T(8,128)(2,1)S(1)} %after.6.last, f32[1,768]{1,0:T(1,128)S(1)} %collective-permute-done.9.refs_2_.row, ...), custom_call_target="tpu_custom_call" | custom-call | flops 805306368 | bytes 1572864 | tf_op jit(solution)/shard_map/near_block/pallas_call | solution.py:202
  35.6 2.3 %collective-permute-done.12.refs_8_ = bf16[192,1024]{1,0:T(8,128)(2,1)S(1)} collective-permute-done((bf16[192,1024]{1,0:T(8,128)(2,1)S(1)}, bf16[192,1024]{1,0:T(8,128)(2,1)S(1)}, u32[]{:S(2)}, u32[]{:S(2)}) %collective-permute-start.12) | collective-permute-done | bytes 393248 | tf_op jit(solution)/shard_map/ppermute | solution.py:298
  38.0 1.6 %early_blocks.1 = (f32[256,1024]{1,0:T(8,128)S(1)}, f32[256,1]{1,0:T(8,128)S(1)}, bf16[768,1024]{1,0:T(8,128)(2,1)S(1)}) custom-call(bf16[1024,1024]{1,0:T(8,128)(2,1)S(1)} %get-tuple-element.17.c_ref, f32[256,1024]{1,0:T(8,128)S(1)} %get-tuple-element.21.refs_0_, f32[256,1]{1,0:T(8,128)S(1)} %get-tuple-element.22.refs_1_, ...), custom_call_target="tpu_custom_call" | custom-call | tf_op jit(solution)/shard_map/early_blocks/pallas_call | solution.py:365
  39.5 3.8 %late_blocks.1 = (bf16[256,1024]{1,0:T(8,128)(2,1)S(1)}, f32[4,256,768]{2,1,0:T(8,128)S(1)}, f32[4,768]{1,0:T(4,128)S(1)}, f32[4,768]{1,0:T(4,128)S(1)}, bf16[768,1024]{1,0:T(8,128)(2,1)S(1)}) custom-call(bf16[1024,1024]{1,0:T(8,128)(2,1)S(1)} %get-tuple-element.17.c_ref, f32[256,1024]{1,0:T(8,128)S(1)} %get-tuple-element.24.total, ...), custom_call_target="tpu_custom_call" | custom-call | flops 2415919104 | bytes 1572864 | tf_op jit(solution)/shard_map/late_blocks/pallas_call | solution.py:385
  44.6 3.7 %collective-permute-start.18 = (f32[4,768]{1,0:T(4,128)S(1)}, f32[4,768]{1,0:T(4,128)S(1)}, u32[]{:S(2)}, u32[]{:S(2)}) collective-permute-start(f32[4,768]{1,0:T(4,128)S(1)} %log_add_fusion.1), channel_id=1, source_target_pairs={{0,6},{1,7},{2,4},{3,5},{4,2},{5,3},{6,0},{7,1},{8,14},{9,15},{10,... | collective-permute-start | bytes 36872 | tf_op jit(solution)/shard_map/ppermute | solution.py:298
  49.1 1.1 %collective-permute-done.18 = f32[4,768]{1,0:T(4,128)S(1)} collective-permute-done((f32[4,768]{1,0:T(4,128)S(1)}, f32[4,768]{1,0:T(4,128)S(1)}, u32[]{:S(2)}, u32[]{:S(2)}) %collective-permute-start.18) | collective-permute-done | bytes 12320 | tf_op jit(solution)/shard_map/ppermute | solution.py:298
  50.2 2.7 %collective-permute-done.17 = f32[4,768]{1,0:T(4,128)S(1)} collective-permute-done((f32[4,768]{1,0:T(4,128)S(1)}, f32[4,768]{1,0:T(4,128)S(1)}, u32[]{:S(2)}, u32[]{:S(2)}) %collective-permute-start.17) | collective-permute-done | bytes 12320 | tf_op jit(solution)/shard_map/ppermute | solution.py:298
  52.9 1.5 %collective-permute-start.21 = (f32[4,768]{1,0:T(4,128)S(1)}, f32[4,768]{1,0:T(4,128)S(1)}, u32[]{:S(2)}, u32[]{:S(2)}) collective-permute-start(f32[4,768]{1,0:T(4,128)S(1)} %log_add_fusion), channel_id=1, source_target_pairs={{0,24},{1,25},{2,26},{3,27},{4,28},{5,29},{6,30},{7,31},{8,16},{9,... | collective-permute-start | bytes 36872 | tf_op jit(solution)/shard_map/ppermute | solution.py:298
  54.4 1.5 %collective-permute-start.20 = (f32[4,768]{1,0:T(4,128)S(1)}, f32[4,768]{1,0:T(4,128)S(1)}, u32[]{:S(2)}, u32[]{:S(2)}) collective-permute-start(f32[4,768]{1,0:T(4,128)S(1)} %log_add_fusion), channel_id=1, source_target_pairs={{0,16},{1,17},{2,18},{3,19},{4,20},{5,21},{6,22},{7,23},{8,24},{9,... | collective-permute-start | bytes 36872 | tf_op jit(solution)/shard_map/ppermute | solution.py:298
  58.1 1.5 %collective-permute-done.19 = f32[4,768]{1,0:T(4,128)S(1)} collective-permute-done((f32[4,768]{1,0:T(4,128)S(1)}, f32[4,768]{1,0:T(4,128)S(1)}, u32[]{:S(2)}, u32[]{:S(2)}) %collective-permute-start.19) | collective-permute-done | bytes 12320 | tf_op jit(solution)/shard_map/ppermute | solution.py:298
  59.7 2.7 %last_iteration.1 = (bf16[256,1024]{1,0:T(8,128)(2,1)}, f32[768]{0:T(1024)}) custom-call(bf16[256,1024]{1,0:T(8,128)(2,1)S(1)} %get-tuple-element.27.old_ref, f32[4,256,768]{2,1,0:T(8,128)S(1)} %get-tuple-element.28.expo_ref, f32[4,768]{1,0:T(4,128)S(1)} %get-tuple-element.29.peak_ref, f32[1,4,768]{2,1,0:T(4,128)S(1)} %add_bitcast_fusion.parts, ...), custom_call_target="tpu_custom_call" | custom-call | flops 1610612736 | bytes 524288 | tf_op jit(solution)/shard_map/last_iteration/pallas_call | solution.py:412
  (39 shorter events, 9.0 us)
Async XLA Ops:
  1.9 17.2 %collective-permute-start = (bf16[576,1024]{1,0:T(8,128)(2,1)S(1)}, bf16[576,1024]{1,0:T(8,128)(2,1)S(1)}, u32[]{:S(2)}, u32[]{:S(2)}) collective-permute-start(bf16[576,1024]{1,0:T(8,128)(2,1)S(1)} %outgoing.1), channel_id=1, source_target_pairs={{0,8},{1,17},{2,10},{3,19},{4,12},{5,21},{6,14},{7,23},{8,0},{9,25... | collective-permute-start | bytes 3538952 | tf_op jit(solution)/shard_map/ppermute | solution.py:298
  9.5 1.2 %collective-permute-start.1 = (f32[1,768]{1,0:T(1,128)S(1)}, f32[1,768]{1,0:T(1,128)S(1)}, u32[]{:S(2)}, u32[]{:S(2)}) collective-permute-start(f32[1,768]{1,0:T(1,128)S(1)} %partial_lse.1), channel_id=1, source_target_pairs={{0,1},{1,0},{2,3},{3,2},{4,5},{5,4},{6,7},{7,6},{8,9},{9,8},{10,11... | collective-permute-start | bytes 9224 | tf_op jit(solution)/shard_map/ppermute | solution.py:298
  10.7 5.5 %collective-permute-start.4 = (f32[1,768]{1,0:T(1,128)S(1)}, f32[1,768]{1,0:T(1,128)S(1)}, u32[]{:S(2)}, u32[]{:S(2)}) collective-permute-start(f32[1,768]{1,0:T(1,128)S(1)} %log_add_fusion.3), channel_id=1, source_target_pairs={{0,6},{1,7},{2,4},{3,5},{4,2},{5,3},{6,0},{7,1},{8,14},{9,15},{10,... | collective-permute-start | bytes 9224 | tf_op jit(solution)/shard_map/ppermute | solution.py:298
  14.4 4.5 %collective-permute-start.3 = (f32[1,768]{1,0:T(1,128)S(1)}, f32[1,768]{1,0:T(1,128)S(1)}, u32[]{:S(2)}, u32[]{:S(2)}) collective-permute-start(f32[1,768]{1,0:T(1,128)S(1)} %log_add_fusion.3), channel_id=1, source_target_pairs={{0,4},{1,5},{2,6},{3,7},{4,0},{5,1},{6,2},{7,3},{8,12},{9,13},{10,... | collective-permute-start | bytes 9224 | tf_op jit(solution)/shard_map/ppermute | solution.py:298
  14.4 4.5 %collective-permute-start.2 = (f32[1,768]{1,0:T(1,128)S(1)}, f32[1,768]{1,0:T(1,128)S(1)}, u32[]{:S(2)}, u32[]{:S(2)}) collective-permute-start(f32[1,768]{1,0:T(1,128)S(1)} %log_add_fusion.3), channel_id=1, source_target_pairs={{0,2},{1,3},{2,0},{3,1},{4,6},{5,7},{6,4},{7,5},{8,10},{9,11},{10,... | collective-permute-start | bytes 9224 | tf_op jit(solution)/shard_map/ppermute | solution.py:298
  19.2 15.9 %collective-permute-start.13 = (bf16[384,1024]{1,0:T(8,128)(2,1)S(1)}, bf16[384,1024]{1,0:T(8,128)(2,1)S(1)}, u32[]{:S(2)}, u32[]{:S(2)}) collective-permute-start(bf16[384,1024]{1,0:T(8,128)(2,1)S(1)} %slice.19), channel_id=1, source_target_pairs={{0,16},{1,9},{2,18},{3,11},{4,20},{5,13},{6,22},{7,15},{8,24},{9,1... | collective-permute-start | bytes 2359304 | tf_op jit(solution)/shard_map/ppermute | solution.py:298
  21.4 2.2 %collective-permute-start.7 = (bf16[192,1024]{1,0:T(8,128)(2,1)S(1)}, bf16[192,1024]{1,0:T(8,128)(2,1)S(1)}, u32[]{:S(2)}, u32[]{:S(2)}) collective-permute-start(bf16[192,1024]{1,0:T(8,128)(2,1)S(1)} %get-tuple-element.32), channel_id=1, source_target_pairs={{0,1},{1,0},{2,3},{3,2},{4,5},{5,4},{6,7},{7,6},{8,9},{9,8},{10,11... | collective-permute-start | bytes 1179656 | tf_op jit(solution)/shard_map/ppermute | solution.py:298
  21.4 2.3 %collective-permute-start.6 = (bf16[192,1024]{1,0:T(8,128)(2,1)S(1)}, bf16[192,1024]{1,0:T(8,128)(2,1)S(1)}, u32[]{:S(2)}, u32[]{:S(2)}) collective-permute-start(bf16[192,1024]{1,0:T(8,128)(2,1)S(1)} %get-tuple-element.33), channel_id=1, source_target_pairs={{0,1},{1,0},{2,3},{3,2},{4,5},{5,4},{6,7},{7,6},{8,9},{9,8},{10,11... | collective-permute-start | bytes 1179656 | tf_op jit(solution)/shard_map/ppermute | solution.py:298
  21.9 2.3 %collective-permute-start.8 = (bf16[192,1024]{1,0:T(8,128)(2,1)S(1)}, bf16[192,1024]{1,0:T(8,128)(2,1)S(1)}, u32[]{:S(2)}, u32[]{:S(2)}) collective-permute-start(bf16[192,1024]{1,0:T(8,128)(2,1)S(1)} %get-tuple-element.34), channel_id=1, source_target_pairs={{0,1},{1,0},{2,3},{3,2},{4,5},{5,4},{6,7},{7,6},{8,9},{9,8},{10,11... | collective-permute-start | bytes 1179656 | tf_op jit(solution)/shard_map/ppermute | solution.py:298
  22.0 11.5 %collective-permute-start.5 = (bf16[192,1024]{1,0:T(8,128)(2,1)S(1)}, bf16[192,1024]{1,0:T(8,128)(2,1)S(1)}, u32[]{:S(2)}, u32[]{:S(2)}) collective-permute-start(bf16[192,1024]{1,0:T(8,128)(2,1)S(1)} %get-tuple-element.34), channel_id=1, source_target_pairs={{0,2},{1,3},{2,0},{3,1},{4,6},{5,7},{6,4},{7,5},{8,10},{9,11},{10,... | collective-permute-start | bytes 1179656 | tf_op jit(solution)/shard_map/ppermute | solution.py:298
  24.3 9.2 %collective-permute-start.11 = (f32[1,768]{1,0:T(1,128)S(1)}, f32[1,768]{1,0:T(1,128)S(1)}, u32[]{:S(2)}, u32[]{:S(2)}) collective-permute-start(f32[1,768]{1,0:T(1,128)S(1)} %after.5.row), channel_id=1, source_target_pairs={{0,24},{1,25},{2,26},{3,27},{4,28},{5,29},{6,30},{7,31},{8,16},{9,... | collective-permute-start | bytes 9224 | tf_op jit(solution)/shard_map/ppermute | solution.py:298
  25.7 7.8 %collective-permute-start.10 = (f32[1,768]{1,0:T(1,128)S(1)}, f32[1,768]{1,0:T(1,128)S(1)}, u32[]{:S(2)}, u32[]{:S(2)}) collective-permute-start(f32[1,768]{1,0:T(1,128)S(1)} %after.5.row), channel_id=1, source_target_pairs={{0,16},{1,9},{2,18},{3,11},{4,20},{5,13},{6,22},{7,15},{8,24},{9,1... | collective-permute-start | bytes 9224 | tf_op jit(solution)/shard_map/ppermute | solution.py:298
  27.2 6.3 %collective-permute-start.9 = (f32[1,768]{1,0:T(1,128)S(1)}, f32[1,768]{1,0:T(1,128)S(1)}, u32[]{:S(2)}, u32[]{:S(2)}) collective-permute-start(f32[1,768]{1,0:T(1,128)S(1)} %after.5.row), channel_id=1, source_target_pairs={{0,8},{1,17},{2,10},{3,19},{4,12},{5,21},{6,14},{7,23},{8,0},{9,25... | collective-permute-start | bytes 9224 | tf_op jit(solution)/shard_map/ppermute | solution.py:298
  35.1 4.5 %collective-permute-start.14 = (bf16[384,1024]{1,0:T(8,128)(2,1)S(1)}, bf16[384,1024]{1,0:T(8,128)(2,1)S(1)}, u32[]{:S(2)}, u32[]{:S(2)}) collective-permute-start(bf16[384,1024]{1,0:T(8,128)(2,1)S(1)} %after.7.refs_4_), channel_id=1, source_target_pairs={{0,1},{1,0},{2,3},{3,2},{4,5},{5,4},{6,7},{7,6},{8,9},{9,8},{10,11... | collective-permute-start | bytes 2359304 | tf_op jit(solution)/shard_map/ppermute | solution.py:298
  35.1 2.8 %collective-permute-start.12 = (bf16[192,1024]{1,0:T(8,128)(2,1)S(1)}, bf16[192,1024]{1,0:T(8,128)(2,1)S(1)}, u32[]{:S(2)}, u32[]{:S(2)}) collective-permute-start(bf16[192,1024]{1,0:T(8,128)(2,1)S(1)} %after.6.last), channel_id=1, source_target_pairs={{0,1},{1,0},{2,3},{3,2},{4,5},{5,4},{6,7},{7,6},{8,9},{9,8},{10,11... | collective-permute-start | bytes 1179656 | tf_op jit(solution)/shard_map/ppermute | solution.py:298
  43.4 1.2 %collective-permute-start.15 = (f32[4,768]{1,0:T(4,128)S(1)}, f32[4,768]{1,0:T(4,128)S(1)}, u32[]{:S(2)}, u32[]{:S(2)}) collective-permute-start(f32[4,768]{1,0:T(4,128)S(1)} %get-tuple-element.30), channel_id=1, source_target_pairs={{0,1},{1,0},{2,3},{3,2},{4,5},{5,4},{6,7},{7,6},{8,9},{9,8},{10,11... | collective-permute-start | bytes 36872 | tf_op jit(solution)/shard_map/ppermute | solution.py:298
  44.6 5.6 %collective-permute-start.18 = (f32[4,768]{1,0:T(4,128)S(1)}, f32[4,768]{1,0:T(4,128)S(1)}, u32[]{:S(2)}, u32[]{:S(2)}) collective-permute-start(f32[4,768]{1,0:T(4,128)S(1)} %log_add_fusion.1), channel_id=1, source_target_pairs={{0,6},{1,7},{2,4},{3,5},{4,2},{5,3},{6,0},{7,1},{8,14},{9,15},{10,... | collective-permute-start | bytes 36872 | tf_op jit(solution)/shard_map/ppermute | solution.py:298
  48.3 4.6 %collective-permute-start.17 = (f32[4,768]{1,0:T(4,128)S(1)}, f32[4,768]{1,0:T(4,128)S(1)}, u32[]{:S(2)}, u32[]{:S(2)}) collective-permute-start(f32[4,768]{1,0:T(4,128)S(1)} %log_add_fusion.1), channel_id=1, source_target_pairs={{0,4},{1,5},{2,6},{3,7},{4,0},{5,1},{6,2},{7,3},{8,12},{9,13},{10,... | collective-permute-start | bytes 36872 | tf_op jit(solution)/shard_map/ppermute | solution.py:298
  48.3 4.6 %collective-permute-start.16 = (f32[4,768]{1,0:T(4,128)S(1)}, f32[4,768]{1,0:T(4,128)S(1)}, u32[]{:S(2)}, u32[]{:S(2)}) collective-permute-start(f32[4,768]{1,0:T(4,128)S(1)} %log_add_fusion.1), channel_id=1, source_target_pairs={{0,2},{1,3},{2,0},{3,1},{4,6},{5,7},{6,4},{7,5},{8,10},{9,11},{10,... | collective-permute-start | bytes 36872 | tf_op jit(solution)/shard_map/ppermute | solution.py:298
  52.9 4.7 %collective-permute-start.21 = (f32[4,768]{1,0:T(4,128)S(1)}, f32[4,768]{1,0:T(4,128)S(1)}, u32[]{:S(2)}, u32[]{:S(2)}) collective-permute-start(f32[4,768]{1,0:T(4,128)S(1)} %log_add_fusion), channel_id=1, source_target_pairs={{0,24},{1,25},{2,26},{3,27},{4,28},{5,29},{6,30},{7,31},{8,16},{9,... | collective-permute-start | bytes 36872 | tf_op jit(solution)/shard_map/ppermute | solution.py:298
  54.4 3.7 %collective-permute-start.20 = (f32[4,768]{1,0:T(4,128)S(1)}, f32[4,768]{1,0:T(4,128)S(1)}, u32[]{:S(2)}, u32[]{:S(2)}) collective-permute-start(f32[4,768]{1,0:T(4,128)S(1)} %log_add_fusion), channel_id=1, source_target_pairs={{0,16},{1,17},{2,18},{3,19},{4,20},{5,21},{6,22},{7,23},{8,24},{9,... | collective-permute-start | bytes 36872 | tf_op jit(solution)/shard_map/ppermute | solution.py:298
  56.0 3.7 %collective-permute-start.19 = (f32[4,768]{1,0:T(4,128)S(1)}, f32[4,768]{1,0:T(4,128)S(1)}, u32[]{:S(2)}, u32[]{:S(2)}) collective-permute-start(f32[4,768]{1,0:T(4,128)S(1)} %log_add_fusion), channel_id=1, source_target_pairs={{0,8},{1,9},{2,10},{3,11},{4,12},{5,13},{6,14},{7,15},{8,0},{9,1},... | collective-permute-start | bytes 36872 | tf_op jit(solution)/shard_map/ppermute | solution.py:298
